TPU v7x, 128 devices: a whole 4x4x4 slice. The times are simulated.
128 devices in a mesh: seq: 32 (over z, x, core), head: 4 (over y).
Axes of the slice: x: 4, y: 4, z: 4, core: 2. Of those that a mesh axis runs over, the one named last changes fastest.
Arguments:
- query_heads: bfloat16 [4, 4, 64, 192], P(None, None, 'head'), may hold values from -6 to 6
- up_keys: bfloat16 [64, 128, 512], P('head'), may hold values from -0.5 to 0.5
- up_values: bfloat16 [64, 512, 128], P('head'), may hold values from -0.25 to 0.25
- latent_cache: bfloat16 [4, 262144, 576], P(None, ('seq', 'head')), may hold values from -120 to 120
- new_latent: bfloat16 [4, 4, 576], replicated, may hold values from -24 to 24
- context_lengths: int32 [4], replicated, may hold values from 32768 to 262144, as said below
- positions: int32 [4], replicated, may hold values from 0 to 262143
Outputs:
- attended: bfloat16 [4, 4, 64, 128], P(None, None, 'head')
Inputs may be any that keep to these rules, and one draw needn't show every extreme that they name: `context_lengths`: some request uses all 262144 cached positions.
All inputs are finite; a program needn't handle non-finite values.
Results may differ from a plain program's by a relative error of at most 0.019.
The roundings to bfloat16 on the way count: a program that leaves them out, or rounds other values in their place, can miss the bound.
Values may be sent and summed in bfloat16 or wider, within the bound.
No kernel may reach another device: no remote copies, remote signals or barrier semaphores. Data moves between devices by JAX's collectives and lax.ppermute only.
A program may use at most 512 MiB of HBM per device.

v0:
```python
import jax
import jax.numpy as jnp
from jax import lax
from jax.sharding import PartitionSpec as P

rope_base = 50000.0
masked_score = -1e30


def rotate(values, where_at):
    halfway = values.shape[-1] // 2
    counter = jnp.arange(halfway, dtype=jnp.float32)
    inverse = jnp.power(jnp.float32(rope_base), -2.0 * counter / values.shape[-1])
    angles = where_at.astype(jnp.float32)[..., None] * inverse
    cosine = jnp.cos(angles)
    sine_part = jnp.sin(angles)
    leading = values[..., :halfway]
    trailing = values[..., halfway:]
    return jnp.concatenate(
        [leading * cosine - trailing * sine_part, trailing * cosine + leading * sine_part], axis=-1
    )


def build_new_keys(new_latent, pos_grid, latent_width):
    rotated = rotate(new_latent[..., latent_width:].astype(jnp.float32), pos_grid).astype(
        jnp.bfloat16
    )
    return jnp.concatenate([new_latent[..., :latent_width], rotated], axis=-1)


def own_heads(values, heads_own):
    start_head = lax.axis_index("head") * heads_own
    return lax.dynamic_slice_in_dim(values, start_head, heads_own, axis=2)


def project_values(latents, values_float):
    return jnp.einsum("bshc,hcv->bshv", latents, values_float, precision=lax.Precision.HIGHEST)


def on_device(
    query_heads, up_keys, up_values, latent_cache, new_latent, context_lengths, positions
):
    step_count, requests, heads_own, query_width = query_heads.shape
    nope_width = up_keys.shape[1]
    latent_width = up_keys.shape[2]
    cache_rows = latent_cache.shape[1]
    softmax_scale = float(query_width) ** (-0.5)
    values_float = up_values.astype(jnp.float32)
    pos_grid = positions[None, :] + jnp.arange(step_count, dtype=jnp.int32)[:, None]
    query_latent = jnp.einsum(
        "sbhn,hnc->sbhc", query_heads[..., :nope_width], up_keys, preferred_element_type=jnp.float32
    ).astype(jnp.bfloat16)
    query_rope = rotate(
        query_heads[..., nope_width:].astype(jnp.float32), pos_grid[:, :, None]
    ).astype(jnp.bfloat16)
    own_queries = jnp.concatenate([query_latent, query_rope], axis=-1)
    new_keys = build_new_keys(new_latent, pos_grid, latent_width)
    all_queries = lax.all_gather(own_queries, "head", axis=2, tiled=True)
    head_count = all_queries.shape[2]
    device_slot = lax.axis_index("seq") * lax.axis_size("head") + lax.axis_index("head")
    row_numbers = device_slot * cache_rows + jnp.arange(cache_rows, dtype=jnp.int32)

    def local_part(request_item):
        queries, cache_keys, length = request_item
        query_rows = queries.reshape(step_count * head_count, queries.shape[-1])
        scores = (
            jnp.einsum("qc,kc->qk", query_rows, cache_keys, preferred_element_type=jnp.float32)
            * softmax_scale
        )
        visible = (row_numbers < length)[None, :]
        scores = jnp.where(visible, scores, masked_score)
        highest = jnp.max(scores, axis=1)
        weights = jnp.where(visible, jnp.exp(scores - highest[:, None]), 0.0)
        weight_sum = jnp.sum(weights, axis=1)
        weighted = jnp.dot(
            weights.astype(jnp.bfloat16),
            cache_keys[:, :latent_width],
            preferred_element_type=jnp.float32,
        )
        return (highest, weight_sum, weighted)

    highest, weight_sum, weighted = lax.map(
        local_part, (jnp.swapaxes(all_queries, 0, 1), latent_cache, context_lengths)
    )
    highest = highest.reshape(requests, step_count, head_count)
    weight_sum = weight_sum.reshape(requests, step_count, head_count)
    weighted = weighted.reshape(requests, step_count, head_count, latent_width)
    projected_first = False
    global_peak = lax.pmax(highest, ("seq", "head"))
    rescale = jnp.exp(highest - global_peak)
    summed_weight, summed_latent = lax.psum(
        (weight_sum * rescale, weighted * rescale[..., None]), ("seq", "head")
    )
    peak_own = own_heads(global_peak, heads_own)
    sum_own = own_heads(summed_weight, heads_own)
    mixed_own = own_heads(summed_latent, heads_own)
    new_scores = (
        jnp.einsum("sbhc,tbc->bsht", own_queries, new_keys, preferred_element_type=jnp.float32)
        * softmax_scale
    )
    step_index = jnp.arange(step_count, dtype=jnp.int32)
    causal = (step_index[None, :] <= step_index[:, None])[None, :, None, :]
    new_scores = jnp.where(causal, new_scores, masked_score)
    overall = jnp.maximum(peak_own, jnp.max(new_scores, axis=3))
    carried = jnp.exp(peak_own - overall)
    new_weights = jnp.where(causal, jnp.exp(new_scores - overall[..., None]), 0.0)
    denominator = sum_own * carried + jnp.sum(new_weights, axis=3)
    new_term = jnp.einsum(
        "bsht,tbc->bshc",
        new_weights.astype(jnp.bfloat16),
        new_keys[..., :latent_width],
        preferred_element_type=jnp.float32,
    )
    latent_out = (mixed_own * carried[..., None] + new_term) / denominator[..., None]
    result = project_values(latent_out, values_float)
    return jnp.swapaxes(result, 0, 1).astype(jnp.bfloat16)


def solution(mesh):
    in_specs = (
        P(None, None, "head", None),
        P("head", None, None),
        P("head", None, None),
        P(None, ("seq", "head"), None),
        P(),
        P(),
        P(),
    )
    out_specs = P(None, None, "head", None)
    return jax.shard_map(
        on_device, mesh=mesh, in_specs=in_specs, out_specs=out_specs, check_vma=False
    )
```

profile of v0, /device:TPU:1, one launch (start us, length us, event | category | flops | bytes accessed | tf_op | source)
XLA Modules:
  0.0 295.1 jit_solution(13216804307365831924)
XLA Ops:
  6.6 1.0 slice.28
  7.5 0.8 slice.27
  9.1 0.7 add_convert_fusion.2
  10.6 0.9 pad_maximum_fusion
  11.6 27.0 %all-gather.2.cloned.1.call-done = bf16[4,4,64,576]{3,1,0,2:T(4,128)(2,1)} async-done(((bf16[4,4,16,576]{3,1,0,2:T(4,128)(2,1)}), bf16[4,4,64,576]{3,1,0,2:T(4,128)(2,1)}) %all-gather.2.cloned.1.call-update) | async-done | bytes 1179664 | tf_op jit(solution)/shard_map/all_gather | solution.py:58
  38.7 1.6 copy.25
  40.3 26.1 %while.15 = (s32[]{:T(128)}, f32[4,256]{1,0:T(4,128)S(1)}, f32[4,256]{1,0:T(4,128)S(1)}, f32[4,256,512]{2,1,0:T(8,128)}, s32[4]{0:T(128)S(1)}, /*index=5*/bf16[4...) while((s32[]{:T(128)}, f32[4,256]{1,0:T(4,128)S(1)}, ...), condition=%wide.region_3.4_spmd.clone, body=%wide.region_0.3_spmd.clone.sunk | while | flops 1145572864 | bytes 16892552 | solution.py:82
  41.6 1.8 dynamic-slice_bitcast_fusion.2
  43.5 1.1 fusion.74
  44.6 1.6 fusion.76
  48.2 1.8 dynamic-slice_bitcast_fusion.2
  50.0 1.1 fusion.74
  51.1 1.6 fusion.76
  54.7 1.8 dynamic-slice_bitcast_fusion.2
  56.6 1.1 fusion.74
  57.7 1.6 fusion.76
  61.2 1.8 dynamic-slice_bitcast_fusion.2
  63.1 1.1 fusion.74
  64.2 1.6 fusion.76
  66.5 66.3 %pmax.7 = f32[4,4,64]{2,1,0:T(4,128)S(1)} all-reduce(f32[4,4,64]{2,1,0:T(4,128)S(1)} %reshape.95), channel_id=1, replica_groups=mesh['seq'=32,'head'=4] {'seq','head'}, use_global_device_ids=true, to_apply=%region_4.5 | all-reduce | flops 1024 | bytes 8192 | tf_op jit(solution)/shard_map/pmax | solution.py:89
  133.0 4.3 %copy_multiply_fusion = f32[4,4,64,512]{3,1,0,2:T(4,128)} fusion(f32[4,4,64,512]{3,2,1,0:T(8,128)} %bitcast.70, f32[4,4,64]{1,0,2:T(4,128)S(1)} %copy.26), kind=kLoop, calls=%fused_computation.21 | loop fusion | flops 524288 | bytes 4198400 | tf_op jit(solution)/shard_map/mul | solution.py:92
  138.9 63.7 %psum.15 = f32[4,4,64]{2,1,0:T(4,128)S(1)} all-reduce(f32[4,4,64]{2,1,0:T(4,128)S(1)} %bitcast.77), channel_id=1, replica_groups=mesh['seq'=32,'head'=4] {'seq','head'}, use_global_device_ids=true, to_apply=%region_7.8 | all-reduce | flops 1024 | bytes 8192 | tf_op jit(solution)/shard_map/psum | solution.py:91
  203.5 81.0 %all-reduce.2.cloned.1.call-done = f32[4,4,64,512]{3,1,0,2:T(4,128)} async-done(((f32[4,4,64,512]{3,1,0,2:T(4,128)}), f32[4,4,64,512]{3,1,0,2:T(4,128)}) %all-reduce.2.cloned.1.call-update) | async-done | bytes 2097168 | tf_op jit(solution)/shard_map/psum | solution.py:91
  284.4 3.1 %fusion.31 = bf16[4,4,16,128]{3,0,1,2:T(4,128)(2,1)S(1)} fusion(bf16[16,512,128]{2,1,0:T(8,128)(2,1)} %param.11, f32[4,4,16,512]{3,2,1,0:T(8,128)S(1)} %fusion.48, f32[4,4,64,512]{3,1,0,2:T(4,128)} %all-reduce.2.cloned.1.call-done, s32[]{:T(128)S(6)} %select_n.19, f32[4,4,16]{1,0,2:T(4,128)S(1)} %copy.32, f32[4,4,16]{1,0,2:T(4,128)S(1)} %copy.31), kind=kOutput, calls=%fused_computation.25 | convolution fusion | flops 201752576 | bytes 3213316 | tf_op jit(solution)/shard_map/bshc,hcv->bshv/dot_general | solution.py:37
  (63 shorter events, 12.7 us)
Async XLA Ops:
  6.5 3.5 %copy-start = (bf16[16,128,512]{2,1,0:T(8,128)(2,1)S(1)}, bf16[16,128,512]{2,1,0:T(8,128)(2,1)}, u32[]{:S(2)}) copy-start(bf16[16,128,512]{2,1,0:T(8,128)(2,1)} %param.10) | copy-start | bytes 6291460
  6.5 32.1 %all-gather.2.cloned.1.call-start = ((), (), s32[]{:S(2)}) async-start(), calls=%async_computation | async-start | bytes 1638400 | tf_op jit(solution)/shard_map/all_gather | solution.py:58
  10.4 29.8 %copy-start.3 = (s32[4]{0:T(128)S(1)}, s32[4]{0:T(128)}, u32[]{:S(2)}) copy-start(s32[4]{0:T(128)} %param.14) | copy-start | bytes 52
  11.5 272.9 %all-reduce.2.cloned.1.call-start = ((), (), s32[]{:S(2)}) async-start(), calls=%async_computation.1 | async-start | bytes 4194304 | tf_op jit(solution)/shard_map/psum | solution.py:91
  137.4 0.7 copy-start.2
  137.4 1.0 copy-start.1
Sparse Core Ops, SparseCore 0:
  11.7 26.9 all-gather.1
  137.5 146.8 all-reduce.1
where the time goes:
time: 296 us; the launch traced here: 295 us
  blocking collectives  130 us (44%)
  waiting for transfers between devices  108 us (36%)
  local copies, waits for them, and re-layouts  16.7 us (6%)
  matrix products  15.3 us (5%)
  between operations  13.6 us (5%)
  other arithmetic  11.3 us (4%)
    psum x1, waiting for transfers between devices, on_device(): lax.psum((weight_sum * rescale, weighted * rescale[..., None]), ('seq', '...  81 us
    pmax x1, blocking collectives, on_device(): global_peak = lax.pmax(highest, ('seq', 'head'))  66.3 us
    psum x1, blocking collectives, on_device(): lax.psum((weight_sum * rescale, weighted * rescale[..., None]), ('seq', '...  63.7 us
    all_gather x1, waiting for transfers between devices, on_device(): all_queries = lax.all_gather(own_queries, 'head', axis=2, tiled=True)  27 us
    squeeze x4, local copies, waits for them, and re-layouts, on_device(): lax.map(local_part, (jnp.swapaxes(all_queries, 0, 1), latent_cache, conte...  7.31 us
    dot_general x4, matrix products, local_part(): jnp.dot(weights.astype(jnp.bfloat16), cache_keys[:, :latent_width], prefe...  6.35 us
  transfers between devices with their start and end apart: 2, of which 2 were waited for; matrix products, arithmetic and copies ran while one was open for 0% of the time, Pallas kernels for 0%

commit v1 on v0

v1 whole, which is shorter than its diff:
```python
import functools

import jax
import jax.numpy as jnp
from jax import lax
from jax.experimental import pallas as pl
from jax.experimental.pallas import tpu as pltpu
from jax.sharding import Mesh, PartitionSpec as P

rope_base = 50000.0
masked_score = -1e30
lowest_max = -1e29
log2_e = 1.4426950408889634
bf16 = jnp.bfloat16
f32 = jnp.float32


def rope_tables(pos_grid, width):
    counter = jnp.arange(width // 2, dtype=f32)
    inverse = jnp.power(f32(rope_base), -2.0 * counter / width)
    angles = pos_grid.reshape(-1).astype(f32)[:, None] * inverse
    cosine = jnp.cos(angles)
    sine = jnp.sin(angles)
    return jnp.concatenate([cosine, cosine], -1), jnp.concatenate([-sine, sine], -1)


def swap_halves(values):
    half = values.shape[-1] // 2
    return jnp.concatenate([values[..., half:], values[..., :half]], axis=-1)


def queries_kernel(steps, requests, q_ref, up_ref, new_ref, cos_ref, sin_ref, out_ref, keys_ref, q_f32, lat):
    pairs, heads, _ = q_ref.shape
    nope, width = up_ref.shape[1], up_ref.shape[2]
    q_f32[...] = q_ref[:, :, :nope].astype(f32)
    for h in range(heads):
        lat[:, h, :] = jnp.dot(q_f32[:, h, :].astype(bf16), up_ref[h], preferred_element_type=f32)
    cos = cos_ref[...]
    sin = sin_ref[...]
    rope = q_ref[:, :, nope:].astype(f32)
    rope = (rope * cos[:, None, :] + swap_halves(rope) * sin[:, None, :]).astype(bf16)
    for s in range(steps):
        for b in range(requests):
            row = jnp.concatenate([lat[s * requests + b].astype(bf16), rope[s * requests + b]], axis=-1)
            for copy in range(out_ref.shape[0]):
                out_ref[copy, b, s * heads : (s + 1) * heads, :] = row
    new = new_ref[...]
    tail = new[:, width:].astype(f32)
    tail = (tail * cos + swap_halves(tail) * sin).astype(bf16)
    keys_ref[...] = jnp.concatenate([new[:, :width], tail], axis=-1)


def attention_kernel(
    scale, steps, heads, info_ref, q_ref, k_ref, new_ref, out_ref, stat_ref, scores, acc, top, total
):
    owners = q_ref.shape[0]
    rows = owners * q_ref.shape[2]
    cached = k_ref.shape[1]
    width = out_ref.shape[3]
    chunk = 512
    request = info_ref[0] + pl.program_id(0)
    limit = info_ref[3 + request] - info_ref[1]
    queries = q_ref[:, 0].reshape(rows, q_ref.shape[3])

    for c in range(0, cached, chunk):
        scores[:, c : c + chunk] = (
            lax.dot_general(
                queries, k_ref[0, c : c + chunk, :], (((1,), (1,)), ((), ())), preferred_element_type=f32
            )
            * scale
        )

    @pl.when(limit < cached)
    def _():
        column = lax.broadcasted_iota(jnp.int32, (rows, cached), 1)
        scores[...] = jnp.where(column < limit, scores[...], masked_score)

    highest = jnp.maximum(jnp.max(scores[...], axis=1, keepdims=True), lowest_max)
    weight_sum = jnp.zeros((rows, 1), f32)
    for c in range(0, cached, chunk):
        weights = jnp.exp2(scores[:, c : c + chunk] - highest)
        weight_sum += jnp.sum(weights, axis=1, keepdims=True)
        part = jnp.dot(weights.astype(bf16), k_ref[0, c : c + chunk, :width], preferred_element_type=f32)
        if c == 0:
            acc[...] = part
        else:
            acc[...] += part
    top[...] = jnp.broadcast_to(highest, top.shape)
    total[...] = jnp.broadcast_to(weight_sum, total.shape)

    @pl.when(info_ref[2] == request)
    def _():
        fresh = new_ref[0]
        new_scores = (
            lax.dot_general(queries, fresh, (((1,), (1,)), ((), ())), preferred_element_type=f32) * scale
        )
        count = fresh.shape[0]
        column = lax.broadcasted_iota(jnp.int32, (rows, count), 1)
        step = (lax.broadcasted_iota(jnp.int32, (rows, count), 0) // heads) % steps
        visible = (column <= step) & (column < steps)
        new_scores = jnp.where(visible, new_scores, masked_score)
        old = top[:, :1]
        peak = jnp.maximum(old, jnp.max(new_scores, axis=1, keepdims=True))
        carried = jnp.exp2(old - peak)
        new_weights = jnp.exp2(new_scores - peak)
        acc[...] = acc[...] * carried + jnp.dot(
            new_weights.astype(bf16), fresh[:, :width], preferred_element_type=f32
        )
        total[...] = total[...] * carried + jnp.sum(new_weights, axis=1, keepdims=True)
        top[...] = jnp.broadcast_to(peak, top.shape)

    out_ref[...] = acc[...].astype(bf16).reshape(out_ref.shape)
    lane = lax.broadcasted_iota(jnp.int32, top.shape, 1)
    stat_ref[...] = jnp.where(lane == 0, top[...], total[...]).reshape(stat_ref.shape)


def split_stats(peak, weight_sum, rows):
    lane = lax.broadcasted_iota(jnp.int32, (rows, 128), 1)
    first = peak.astype(bf16).astype(f32)
    rest = peak - first
    second = rest.astype(bf16).astype(f32)
    third = rest - second
    sum_first = weight_sum.astype(bf16).astype(f32)
    sum_second = weight_sum - sum_first
    out = jnp.where(lane == 0, first, 0.0)
    out = jnp.where(lane == 1, second, out)
    out = jnp.where(lane == 2, third, out)
    out = jnp.where(lane == 3, sum_first, out)
    return jnp.where(lane == 4, sum_second, out)


def pair_kernel(out_a, stat_a, out_b, stat_b, sent_ref):
    rows = sent_ref.shape[1]
    width = out_a.shape[3]
    sa = stat_a[...].reshape(rows, 128)
    sb = stat_b[...].reshape(rows, 128)
    top_a, sum_a = sa[:, :1], sa[:, 1:2]
    top_b, sum_b = sb[:, :1], sb[:, 1:2]
    peak = jnp.maximum(top_a, top_b)
    wa = jnp.exp2(top_a - peak)
    wb = jnp.exp2(top_b - peak)
    sent_ref[0, :, :width] = (
        out_a[...].reshape(rows, width).astype(f32) * wa + out_b[...].reshape(rows, width).astype(f32) * wb
    ).astype(bf16)
    sent_ref[0, :, width:] = split_stats(peak, sum_a * wa + sum_b * wb, rows).astype(bf16)


def project_kernel(heads, got_ref, up_ref, out_ref, mixed, projected):
    sources, rows, _ = got_ref.shape
    width = up_ref.shape[1]
    tops = []
    sums = []
    for i in range(sources):
        stat = got_ref[i, :, width:].astype(f32)
        tops.append(stat[:, 0:1] + stat[:, 1:2] + stat[:, 2:3])
        sums.append(stat[:, 3:4] + stat[:, 4:5])
    peak = functools.reduce(jnp.maximum, tops)
    weights = [jnp.exp2(t - peak) for t in tops]
    weight_sum = sum(w * s for w, s in zip(weights, sums))
    merged = sum(w * got_ref[i, :, :width].astype(f32) for i, w in enumerate(weights))
    mixed[...] = merged.reshape(mixed.shape)
    stats = split_stats(peak, weight_sum, rows).T[:16].astype(bf16)
    count = rows // heads
    for h in range(heads):
        part = mixed[:, h, :]
        high = part.astype(bf16)
        low = (part - high.astype(f32)).astype(bf16)
        both = jnp.dot(jnp.concatenate([high, low], axis=0), up_ref[h], preferred_element_type=f32)
        projected[:, h, :] = both[:count] + both[count:]
    values = projected[...].reshape(rows, projected.shape[2]).astype(bf16)
    for copy in range(out_ref.shape[0]):
        out_ref[copy, :rows, :] = values
        out_ref[copy, rows:, :] = stats


def finish_kernel(got_ref, out_ref):
    sources = got_ref.shape[0]
    rows = out_ref.shape[0]
    tops = []
    sums = []
    for i in range(sources):
        stat = got_ref[i, rows:, :].astype(f32)
        tops.append(stat[0:1] + stat[1:2] + stat[2:3])
        sums.append(stat[3:4] + stat[4:5])
    tops = jnp.concatenate(tops, axis=0)
    sums = jnp.concatenate(sums, axis=0)
    weights = jnp.exp2(tops - jnp.max(tops, axis=0, keepdims=True))
    weights = weights / jnp.sum(weights * sums, axis=0, keepdims=True)
    spread = jnp.concatenate([weights, jnp.zeros((128 - sources, weights.shape[1]), f32)], axis=0).T
    result = jnp.zeros(out_ref.shape, f32)
    for i in range(sources):
        result += got_ref[i, :rows, :].astype(f32) * spread[:rows, i : i + 1]
    out_ref[...] = result.astype(bf16)


def on_device(
    query_heads, up_keys, up_values, latent_cache, new_latent, context_lengths, positions
):
    steps, requests, heads, query_width = query_heads.shape
    nope = up_keys.shape[1]
    width = up_keys.shape[2]
    key_width = latent_cache.shape[2]
    rope = key_width - width
    value_width = up_values.shape[2]
    cached = latent_cache.shape[1]
    owners = lax.axis_size("head")
    plane = lax.axis_size("z") * lax.axis_size("x")
    pairs = steps * requests
    half = requests // 2
    scale = float(query_width) ** (-0.5) * log2_e

    core = lax.axis_index("core")
    slot = lax.axis_index(("z", "x", "core", "head"))

    pos_grid = positions[None, :] + jnp.arange(steps, dtype=jnp.int32)[:, None]
    cos, sin = rope_tables(pos_grid, rope)
    copies, new_keys = pl.pallas_call(
        functools.partial(queries_kernel, steps, requests),
        out_shape=(
            jax.ShapeDtypeStruct((owners, requests, steps * heads, key_width), bf16),
            jax.ShapeDtypeStruct((pairs, key_width), bf16),
        ),
        scratch_shapes=[
            pltpu.VMEM((pairs, heads, nope), f32),
            pltpu.VMEM((pairs, heads, width), f32),
        ],
        compiler_params=pltpu.CompilerParams(vmem_limit_bytes=32 * 2**20),
        name="queries",
    )(query_heads.reshape(pairs, heads, query_width), up_keys, new_latent.reshape(pairs, key_width), cos, sin)
    new_keys = jnp.swapaxes(new_keys.reshape(steps, requests, key_width), 0, 1)
    new_keys = jnp.pad(new_keys, ((0, 0), (0, 128 - steps), (0, 0)))
    queries = lax.all_to_all(copies, "head", 0, 0, tiled=True)

    slots = plane * 2 * owners
    share = slots // requests
    fresh_for = jnp.where(slot % share == 0, slot // share, -1).astype(jnp.int32)

    def attend(first):
        info = jnp.concatenate(
            [
                jnp.stack([first.astype(jnp.int32), slot.astype(jnp.int32) * cached, fresh_for]),
                context_lengths,
            ]
        )
        rows = owners * steps * heads
        return pl.pallas_call(
            functools.partial(attention_kernel, scale, steps, heads),
            grid_spec=pltpu.PrefetchScalarGridSpec(
                num_scalar_prefetch=1,
                grid=(half,),
                in_specs=[
                    pl.BlockSpec((owners, 1, steps * heads, key_width), lambda i, info: (0, info[0] + i, 0, 0)),
                    pl.BlockSpec((1, cached, key_width), lambda i, info: (info[0] + i, 0, 0)),
                    pl.BlockSpec((1, 128, key_width), lambda i, info: (info[0] + i, 0, 0)),
                ],
                out_specs=[
                    pl.BlockSpec((owners, 1, steps * heads, width), lambda i, info: (0, i, 0, 0)),
                    pl.BlockSpec((owners, 1, steps * heads, 128), lambda i, info: (0, i, 0, 0)),
                ],
                scratch_shapes=[
                    pltpu.VMEM((rows, cached), f32),
                    pltpu.VMEM((rows, width), f32),
                    pltpu.VMEM((rows, 128), f32),
                    pltpu.VMEM((rows, 128), f32),
                ],
            ),
            out_shape=(
                jax.ShapeDtypeStruct((owners, half, steps * heads, width), bf16),
                jax.ShapeDtypeStruct((owners, half, steps * heads, 128), f32),
            ),
            compiler_params=pltpu.CompilerParams(
                vmem_limit_bytes=40 * 2**20, dimension_semantics=("arbitrary",)
            ),
            cost_estimate=pl.CostEstimate(
                flops=2 * half * rows * cached * (key_width + width),
                bytes_accessed=half * cached * 640 * 2,
                transcendentals=half * rows * cached,
            ),
            name="attention",
        )(info, queries, latent_cache, new_keys)

    swap = [(0, 1), (1, 0)]
    out_other, stat_other = attend((1 - core) * half)
    out_a = lax.ppermute(out_other, "core", swap)
    stat_a = lax.ppermute(stat_other, "core", swap)
    out_b, stat_b = attend(core * half)

    chunk = half * steps * heads
    part_spec = pl.BlockSpec((1, half, steps * heads, width), lambda i: (i, 0, 0, 0))
    stat_spec = pl.BlockSpec((1, half, steps * heads, 128), lambda i: (i, 0, 0, 0))
    sent = pl.pallas_call(
        pair_kernel,
        grid=(owners,),
        in_specs=[part_spec, stat_spec, part_spec, stat_spec],
        out_specs=pl.BlockSpec((1, chunk, width + 128), lambda i: (i, 0, 0)),
        out_shape=jax.ShapeDtypeStruct((owners, chunk, width + 128), bf16),
        name="pair_merge",
    )(out_a, stat_a, out_b, stat_b)
    got = lax.all_to_all(sent, "head", 0, 0, tiled=True)

    projected = pl.pallas_call(
        functools.partial(project_kernel, heads),
        out_shape=jax.ShapeDtypeStruct((plane, chunk + 16, value_width), bf16),
        scratch_shapes=[
            pltpu.VMEM((chunk // heads, heads, width), f32),
            pltpu.VMEM((chunk // heads, heads, value_width), f32),
        ],
        compiler_params=pltpu.CompilerParams(vmem_limit_bytes=32 * 2**20),
        name="project",
    )(got, up_values)
    everyone = lax.all_to_all(projected, ("z", "x"), 0, 0, tiled=True)

    own = pl.pallas_call(
        finish_kernel,
        out_shape=jax.ShapeDtypeStruct((chunk, value_width), bf16),
        name="finish",
    )(everyone)
    theirs = lax.ppermute(own, "core", swap)
    both = jnp.where(core == 0, jnp.stack([own, theirs]), jnp.stack([theirs, own]))
    return jnp.swapaxes(both.reshape(requests, steps, heads, value_width), 0, 1)


def solution(mesh):
    fine = Mesh(mesh.devices.reshape(4, 4, 2, 4), ("z", "x", "core", "head"))
    in_specs = (
        P(None, None, "head", None),
        P("head", None, None),
        P("head", None, None),
        P(None, ("z", "x", "core", "head"), None),
        P(),
        P(),
        P(),
    )
    out_specs = P(None, None, "head", None)
    return jax.shard_map(
        on_device, mesh=fine, in_specs=in_specs, out_specs=out_specs, check_vma=False
    )
```

time: 296 us -> 92.9 us (0.31)
  waiting for transfers between devices: 108 us -> 2.89 us
  blocking collectives: 130 us -> 31.1 us
  Pallas kernels: 0 us -> 19.2 us
  matrix products: 15.3 us -> 0 us
  between operations: 13.6 us -> 0.08 us
  starting transfers between devices: 0.04 us -> 9.92 us
  local copies, waits for them, and re-layouts: 16.7 us -> 26.5 us
  other arithmetic: 11.3 us -> 1.79 us
    psum x1 -> x0, waiting for transfers between devices: 81 us -> none  [on_device(): lax.psum((weight_sum * rescale, weighted * rescale[..., None]), ('seq', '...]
    pmax x1 -> x0, blocking collectives: 66.3 us -> none  [on_device(): global_peak = lax.pmax(highest, ('seq', 'head'))]
    psum x1 -> x0, blocking collectives: 63.7 us -> none  [on_device(): lax.psum((weight_sum * rescale, weighted * rescale[..., None]), ('seq', '...]
    all_to_all x0 -> x2, blocking collectives: none -> 31.1 us  [the longest x1 18.3 us: on_device(): everyone = lax.all_to_all(projected, ('z', 'x'), 0, 0, tiled=True)]
    all_gather x1 -> x0, waiting for transfers between devices: 27 us -> none  [on_device(): all_queries = lax.all_gather(own_queries, 'head', axis=2, tiled=True)]
    unnamed x10 -> x25, local copies, waits for them, and re-layouts: 2.53 us -> 24.1 us
    pallas_call x0 -> x6, Pallas kernels: none -> 19.2 us  [the longest x2 10.2 us: attend(): pl.pallas_call(functools.partial(attention_kernel, scale, steps, heads),...]
    dot_general x12 -> x0, matrix products: 15.3 us -> none  [the longest x4 6.35 us: local_part(): jnp.dot(weights.astype(jnp.bfloat16), cache_keys[:, :latent_width], prefe...]
  transfers between devices with their start and end apart: 2 -> 4, of which waited for: 2 -> 2; matrix products, arithmetic and copies ran while one was open for 0% -> 17% of each run, Pallas kernels for 0% -> 5%
where the time goes in v1:
time: 92.9 us; the launch traced here: 91.5 us
  blocking collectives  31.1 us (33%)
  local copies, waits for them, and re-layouts  26.5 us (29%)
  Pallas kernels  19.2 us (21%)
  starting transfers between devices  9.92 us (11%)
  waiting for transfers between devices  2.89 us (3%)
  other arithmetic  1.79 us (2%)
    unnamed x25, local copies, waits for them, and re-layouts  24.1 us
    all_to_all x1, blocking collectives, on_device(): everyone = lax.all_to_all(projected, ('z', 'x'), 0, 0, tiled=True)  18.3 us
    all_to_all x1, blocking collectives, on_device(): got = lax.all_to_all(sent, 'head', 0, 0, tiled=True)  12.8 us
    pallas_call x2, Pallas kernels, attend(): pl.pallas_call(functools.partial(attention_kernel, scale, steps, heads),...  10.2 us
    all_to_all x1, starting transfers between devices, on_device(): queries = lax.all_to_all(copies, 'head', 0, 0, tiled=True)  5.01 us
    pallas_call x1, Pallas kernels, on_device(): pl.pallas_call(pair_kernel, grid=(owners,), in_specs=[part_spec, stat_spe...  3.89 us
    ppermute x1, starting transfers between devices, on_device(): theirs = lax.ppermute(own, 'core', swap)  3.04 us
    pallas_call x1, Pallas kernels, on_device(): pl.pallas_call(finish_kernel, out_shape=jax.ShapeDtypeStruct((chunk, valu...  2.22 us
  transfers between devices with their start and end apart: 4, of which 2 were waited for; matrix products, arithmetic and copies ran while one was open for 17% of the time, Pallas kernels for 5%

profile of v1, /device:TPU:1, one launch (start us, length us, event | category | flops | bytes accessed | tf_op | source)
XLA Modules:
  0.0 91.5 jit_solution(2109993394151685492)
XLA Ops:
  0.8 0.7 reshape.36.new_ref
  1.7 1.6 %copy-done.4 = bf16[16,128,512]{2,1,0:T(8,128)(2,1)S(1)} copy-done((bf16[16,128,512]{2,1,0:T(8,128)(2,1)S(1)}, bf16[16,128,512]{2,1,0:T(8,128)(2,1)}, u32[]{:S(2)}) %copy-start.4) | copy-done | bytes 2097176
  3.3 0.9 copy-done.8
  4.2 1.6 %queries.1 = (bf16[4,4,64,576]{3,2,1,0:T(8,128)(2,1)}, bf16[16,576]{1,0:T(8,128)(2,1)S(1)}) custom-call(bf16[16,16,192]{2,1,0:T(8,128)(2,1)S(1)} %bitcast.14, bf16[16,128,512]{2,1,0:T(8,128)(2,1)S(1)} %copy-done.4, bf16[16,576]{1,0:T(8,128)(2,1)S(1)} %reshape.36.new_ref, f32[16,64]{1,0:T(8,128)S(1)} %get-tuple-element.22.cos_ref, ...), custom_call_target="tpu_custom_call" | custom-call | tf_op jit(solution)/shard_map/queries/pallas_call | solution.py:217
  5.8 5.0 %all-to-all-start = ((bf16[4,4,64,576]{3,2,1,0:T(8,128)(2,1)}), bf16[4,4,64,576]{3,2,1,0:T(8,128)(2,1)S(1)}, u32[]{:S(2)}, u32[]{:S(2)}) async-start(bf16[4,4,64,576]{3,2,1,0:T(8,128)(2,1)} %get-tuple-element.11), calls=%async_computation | async-start | bytes 2621440 | tf_op jit(solution)/shard_map/all_to_all | solution.py:232
  10.8 14.2 %copy.12.k_ref = bf16[4,2048,576]{2,1,0:T(8,128)(2,1)} copy(bf16[4,2048,576]{1,2,0:T(8,128)(2,1)} %param.10) | data formatting | bytes 18874368 | tf_op args[3]
  25.0 0.9 pad.4.new_ref
  26.0 1.8 %all-to-all-done.q_ref = bf16[4,4,64,576]{3,2,1,0:T(8,128)(2,1)S(1)} async-done(((bf16[4,4,64,576]{3,2,1,0:T(8,128)(2,1)}), bf16[4,4,64,576]{3,2,1,0:T(8,128)(2,1)S(1)}, u32[]{:S(2)}, u32[]{:S(2)}) %all-to-all-start) | async-done | bytes 1179680 | tf_op jit(solution)/shard_map/all_to_all | solution.py:232
  27.8 4.0 %copy-done = bf16[4,2048,576]{2,1,0:T(8,128)(2,1)S(1)} copy-done((bf16[4,2048,576]{2,1,0:T(8,128)(2,1)S(1)}, bf16[4,2048,576]{2,1,0:T(8,128)(2,1)}, u32[]{:S(2)}) %copy-start) | copy-done | bytes 9437208
  31.8 1.1 %copy-done.2 = bf16[4,128,576]{2,1,0:T(8,128)(2,1)S(1)} copy-done((bf16[4,128,576]{2,1,0:T(8,128)(2,1)S(1)}, bf16[4,128,576]{2,1,0:T(8,128)(2,1)}, u32[]{:S(2)}) %copy-start.2) | copy-done | bytes 589848
  32.9 5.4 %attention.2 = (bf16[4,2,64,512]{3,2,1,0:T(8,128)(2,1)S(1)}, f32[4,2,64,128]{3,2,1,0:T(8,128)}) custom-call(s32[7]{0:T(128)S(1)} %get-tuple-element.21.info_ref, bf16[4,4,64,576]{3,2,1,0:T(8,128)(2,1)S(1)} %all-to-all-done.q_ref, bf16[4,2048,576]{2,1,0:T(8,128)(2,1)S(1)} %copy-done, bf16[4,128,576]{2,1,0:T(8,128)(2,1)S(1)} %copy-done.2), custom_call_target="tpu_custom_call" | custom-call | flops 2281701376 | bytes 5242880 | tf_op jit(solution)/shard_map/attention/pallas_call | solution.py:246
  38.3 1.9 %collective-permute-start = (bf16[4,2,64,512]{3,2,1,0:T(8,128)(2,1)S(1)}, bf16[4,2,64,512]{3,2,1,0:T(8,128)(2,1)S(1)}, u32[]{:S(2)}, u32[]{:S(2)}) collective-permute-start(bf16[4,2,64,512]{3,2,1,0:T(8,128)(2,1)S(1)} %get-tuple-element.13), channel_id=1, source_target_pairs={{0,4},{4,0},{1,5},{5,1},{2,6},{6,2},{3,7},{7,3},{8,12},{12,8},{9,1... | collective-permute-start | bytes 1572872 | tf_op jit(solution)/shard_map/ppermute | solution.py:284
  40.2 4.8 %attention.3 = (bf16[4,2,64,512]{3,2,1,0:T(8,128)(2,1)S(1)}, f32[4,2,64,128]{3,2,1,0:T(8,128)S(1)}) custom-call(s32[7]{0:T(128)S(1)} %get-tuple-element.20.info_ref, bf16[4,4,64,576]{3,2,1,0:T(8,128)(2,1)S(1)} %all-to-all-done.q_ref, bf16[4,2048,576]{2,1,0:T(8,128)(2,1)S(1)} %copy-done.1, bf16[4,128,576]{2,1,0:T(8,128)(2,1)S(1)} %copy-done.3), custom_call_target="tpu_custom_call" | custom-call | flops 2281701376 | bytes 5242880 | tf_op jit(solution)/shard_map/attention/pallas_call | solution.py:246
  45.0 0.8 copy-done.6
  45.8 0.7 copy-done.7
  46.5 0.8 copy-done.9
  47.4 3.9 %pair_merge.1 = bf16[4,128,640]{2,1,0:T(8,128)(2,1)} custom-call(bf16[4,2,64,512]{3,2,1,0:T(8,128)(2,1)} %copy-done.9, f32[4,2,64,128]{3,2,1,0:T(8,128)} %copy-done.10, bf16[4,2,64,512]{3,2,1,0:T(8,128)(2,1)} %copy-done.6, f32[4,2,64,128]{3,2,1,0:T(8,128)} %copy-done.7), custom_call_target="tpu_custom_call" | custom-call | tf_op jit(solution)/shard_map/pair_merge/pallas_call | solution.py:291
  51.3 12.8 %all_to_all.15.got_ref = bf16[4,128,640]{2,1,0:T(8,128)(2,1)S(1)} all-to-all(bf16[4,128,640]{2,1,0:T(8,128)(2,1)} %pair_merge.1), channel_id=1, replica_groups=mesh['z'=4,'x'=4,'core'=2,'head'=4] {'head'}, dimensions={0} | all-to-all | bytes 1310720 | tf_op jit(solution)/shard_map/all_to_all | solution.py:299
  64.0 1.3 %project.1 = bf16[16,144,128]{2,1,0:T(8,128)(2,1)S(1)} custom-call(bf16[4,128,640]{2,1,0:T(8,128)(2,1)S(1)} %all_to_all.15.got_ref, bf16[16,512,128]{2,1,0:T(8,128)(2,1)S(1)} %copy-done.5), custom_call_target="tpu_custom_call" | custom-call | tf_op jit(solution)/shard_map/project/pallas_call | solution.py:301
  65.4 18.3 %all_to_all.16.got_ref = bf16[16,144,128]{2,1,0:T(8,128)(2,1)} all-to-all(bf16[16,144,128]{2,1,0:T(8,128)(2,1)S(1)} %project.1), channel_id=1, replica_groups=mesh['z'=4,'x'=4,'core'=2,'head'=4] {'z','x'}, dimensions={0} | all-to-all | bytes 1179648 | tf_op jit(solution)/shard_map/all_to_all | solution.py:311
  83.7 2.2 %finish.1 = bf16[128,128]{1,0:T(8,128)(2,1)} custom-call(bf16[16,144,128]{2,1,0:T(8,128)(2,1)} %all_to_all.16.got_ref), custom_call_target="tpu_custom_call" | custom-call | tf_op jit(solution)/shard_map/finish/pallas_call | solution.py:313
  86.0 3.0 %collective-permute-start.2 = (bf16[128,128]{1,0:T(8,128)(2,1)}, bf16[128,128]{1,0:T(8,128)(2,1)S(1)}, u32[]{:S(2)}, u32[]{:S(2)}) collective-permute-start(bf16[128,128]{1,0:T(8,128)(2,1)} %finish.1), channel_id=1, source_target_pairs={{0,4},{4,0},{1,5},{5,1},{2,6},{6,2},{3,7},{7,3},{8,12},{12,8},{9,1... | collective-permute-start | bytes 98312 | tf_op jit(solution)/shard_map/ppermute | solution.py:318
  89.0 1.1 %collective-permute-done.2 = bf16[128,128]{1,0:T(8,128)(2,1)S(1)} collective-permute-done((bf16[128,128]{1,0:T(8,128)(2,1)}, bf16[128,128]{1,0:T(8,128)(2,1)S(1)}, u32[]{:S(2)}, u32[]{:S(2)}) %collective-permute-start.2) | collective-permute-done | bytes 32800 | tf_op jit(solution)/shard_map/ppermute | solution.py:318
  90.1 0.8 maximum_select_fusion
  (29 shorter events, 1.8 us)
Async XLA Ops:
  1.7 1.6 %copy-start.4 = (bf16[16,128,512]{2,1,0:T(8,128)(2,1)S(1)}, bf16[16,128,512]{2,1,0:T(8,128)(2,1)}, u32[]{:S(2)}) copy-start(bf16[16,128,512]{2,1,0:T(8,128)(2,1)} %up_ref.2) | copy-start | bytes 6291460
  3.3 0.9 copy-start.8
  5.8 22.0 %all-to-all-start = ((bf16[4,4,64,576]{3,2,1,0:T(8,128)(2,1)}), bf16[4,4,64,576]{3,2,1,0:T(8,128)(2,1)S(1)}, u32[]{:S(2)}, u32[]{:S(2)}) async-start(bf16[4,4,64,576]{3,2,1,0:T(8,128)(2,1)} %get-tuple-element.11), calls=%async_computation | async-start | bytes 2621440 | tf_op jit(solution)/shard_map/all_to_all | solution.py:232
  10.8 15.1 %copy-start.11 = (s32[4]{0:T(128)S(1)}, s32[4]{0:T(128)}, u32[]{:S(2)}) copy-start(s32[4]{0:T(128)} %param.12) | copy-start | bytes 52
  27.8 4.0 %copy-start = (bf16[4,2048,576]{2,1,0:T(8,128)(2,1)S(1)}, bf16[4,2048,576]{2,1,0:T(8,128)(2,1)}, u32[]{:S(2)}) copy-start(bf16[4,2048,576]{2,1,0:T(8,128)(2,1)} %copy.12.k_ref) | copy-start | bytes 28311556
  31.8 1.1 %copy-start.2 = (bf16[4,128,576]{2,1,0:T(8,128)(2,1)S(1)}, bf16[4,128,576]{2,1,0:T(8,128)(2,1)}, u32[]{:S(2)}) copy-start(bf16[4,128,576]{2,1,0:T(8,128)(2,1)} %pad.4.new_ref) | copy-start | bytes 1769476
  32.9 7.3 %copy-start.1 = (bf16[4,2048,576]{2,1,0:T(8,128)(2,1)S(1)}, bf16[4,2048,576]{2,1,0:T(8,128)(2,1)}, u32[]{:S(2)}) copy-start(bf16[4,2048,576]{2,1,0:T(8,128)(2,1)} %copy.12.k_ref) | copy-start | bytes 28311556
  32.9 7.3 %copy-start.3 = (bf16[4,128,576]{2,1,0:T(8,128)(2,1)S(1)}, bf16[4,128,576]{2,1,0:T(8,128)(2,1)}, u32[]{:S(2)}) copy-start(bf16[4,128,576]{2,1,0:T(8,128)(2,1)} %pad.4.new_ref) | copy-start | bytes 1769476
  38.3 8.2 %collective-permute-start = (bf16[4,2,64,512]{3,2,1,0:T(8,128)(2,1)S(1)}, bf16[4,2,64,512]{3,2,1,0:T(8,128)(2,1)S(1)}, u32[]{:S(2)}, u32[]{:S(2)}) collective-permute-start(bf16[4,2,64,512]{3,2,1,0:T(8,128)(2,1)S(1)} %get-tuple-element.13), channel_id=1, source_target_pairs={{0,4},{4,0},{1,5},{5,1},{2,6},{6,2},{3,7},{7,3},{8,12},{12,8},{9,1... | collective-permute-start | bytes 1572872 | tf_op jit(solution)/shard_map/ppermute | solution.py:284
  40.1 6.3 %collective-permute-start.1 = (f32[4,2,64,128]{3,2,1,0:T(8,128)}, f32[4,2,64,128]{3,2,1,0:T(8,128)S(1)}, u32[]{:S(2)}, u32[]{:S(2)}) collective-permute-start(f32[4,2,64,128]{3,2,1,0:T(8,128)} %get-tuple-element.14), channel_id=1, source_target_pairs={{0,4},{4,0},{1,5},{5,1},{2,6},{6,2},{3,7},{7,3},{8,12},{12,8},{9,1... | collective-permute-start | bytes 786440 | tf_op jit(solution)/shard_map/ppermute | solution.py:285
  44.9 0.8 copy-start.6
  45.8 0.7 copy-start.7
  46.5 17.6 %copy-start.5 = (bf16[16,512,128]{2,1,0:T(8,128)(2,1)S(1)}, bf16[16,512,128]{2,1,0:T(8,128)(2,1)}, u32[]{:S(2)}) copy-start(bf16[16,512,128]{2,1,0:T(8,128)(2,1)} %up_ref.3) | copy-start | bytes 6291460
  46.5 0.9 copy-start.10
  46.5 0.8 copy-start.9
  86.0 4.1 %collective-permute-start.2 = (bf16[128,128]{1,0:T(8,128)(2,1)}, bf16[128,128]{1,0:T(8,128)(2,1)S(1)}, u32[]{:S(2)}, u32[]{:S(2)}) collective-permute-start(bf16[128,128]{1,0:T(8,128)(2,1)} %finish.1), channel_id=1, source_target_pairs={{0,4},{4,0},{1,5},{5,1},{2,6},{6,2},{3,7},{7,3},{8,12},{12,8},{9,1... | collective-permute-start | bytes 98312 | tf_op jit(solution)/shard_map/ppermute | solution.py:318

commit v2 on v1

v2 whole, which is shorter than its diff:
```python
import functools

import jax
import jax.numpy as jnp
from jax import lax
from jax.experimental import pallas as pl
from jax.experimental.pallas import tpu as pltpu
from jax.sharding import Mesh, PartitionSpec as P

rope_base = 50000.0
masked_score = -1e30
lowest_max = -1e29
log2_e = 1.4426950408889634
bf16 = jnp.bfloat16
f32 = jnp.float32


def swap_halves(values):
    half = values.shape[-1] // 2
    return jnp.concatenate([values[..., half:], values[..., :half]], axis=-1)


def rope_tables(positions_ref, steps, width):
    requests = positions_ref.shape[0]
    pairs = steps * requests
    half = width // 2
    row = lax.broadcasted_iota(jnp.int32, (pairs, width), 0)
    lane = lax.broadcasted_iota(jnp.int32, (pairs, width), 1)
    where_at = row // requests
    for b in range(requests):
        where_at += jnp.where(row % requests == b, positions_ref[b], 0)
    counter = lax.broadcasted_iota(jnp.int32, (1, width), 1) % half
    inverse = jnp.zeros((1, width), f32)
    for i in range(half):
        inverse = jnp.where(counter == i, f32(rope_base ** (-2.0 * i / width)), inverse)
    angles = where_at.astype(f32) * inverse
    return jnp.cos(angles), jnp.where(lane < half, -1.0, 1.0) * jnp.sin(angles)


def queries_kernel(steps, positions_ref, q_ref, up_ref, new_ref, out_ref, keys_ref, q_f32, lat):
    pairs, heads, _ = q_ref.shape
    requests = pairs // steps
    nope, width = up_ref.shape[1], up_ref.shape[2]
    q_f32[...] = q_ref[:, :, :nope].astype(f32)
    for h in range(heads):
        lat[:, h, :] = jnp.dot(q_f32[:, h, :].astype(bf16), up_ref[h], preferred_element_type=f32)
    cos, sin = rope_tables(positions_ref, steps, new_ref.shape[1] - width)
    rope = q_ref[:, :, nope:].astype(f32)
    rope = (rope * cos[:, None, :] + swap_halves(rope) * sin[:, None, :]).astype(bf16)
    for s in range(steps):
        for b in range(requests):
            row = jnp.concatenate([lat[s * requests + b].astype(bf16), rope[s * requests + b]], axis=-1)
            for copy in range(out_ref.shape[0]):
                out_ref[copy, b, s * heads : (s + 1) * heads, :] = row
    new = new_ref[...]
    tail = new[:, width:].astype(f32)
    tail = (tail * cos + swap_halves(tail) * sin).astype(bf16)
    keys_ref[...] = jnp.concatenate([new[:, :width], tail], axis=-1)


def attention_kernel(
    scale, steps, heads, info_ref, q_ref, k_ref, new_ref, out_ref, stat_ref, acc, *scores
):
    owners, requests = q_ref.shape[:2]
    rows = owners * q_ref.shape[2]
    key_width, cached = k_ref.shape[1:]
    width = out_ref.shape[3]
    chunk = 1024
    count = out_ref.shape[1]
    lane = lax.broadcasted_iota(jnp.int32, (rows, 128), 1)

    tops = []
    for i in range(count):
        request = info_ref[0] + i
        limit = info_ref[3 + request] - info_ref[1]
        queries = q_ref[:, request].reshape(rows, key_width)
        top = jnp.full((rows, 128), lowest_max, f32)
        for c in range(0, cached, chunk):
            part = jnp.dot(queries, k_ref[request, :, c : c + chunk], preferred_element_type=f32) * scale
            column = lax.broadcasted_iota(jnp.int32, (1, chunk), 1) + c
            part = jnp.where(column < limit, part, masked_score)
            scores[i][:, c : c + chunk] = part
            for at in range(0, chunk, 128):
                top = jnp.maximum(top, part[:, at : at + 128])
        tops.append(jnp.max(top, axis=1, keepdims=True))

    for i in range(count):
        request = info_ref[0] + i
        total = jnp.zeros((rows, 128), f32)
        for c in range(0, cached, chunk):
            weights = jnp.exp2(scores[i][:, c : c + chunk] - tops[i])
            for at in range(0, chunk, 128):
                total = total + weights[:, at : at + 128]
            part = lax.dot_general(
                weights.astype(bf16),
                k_ref[request, :width, c : c + chunk],
                (((1,), (1,)), ((), ())),
                preferred_element_type=f32,
            )
            mixed = part if c == 0 else mixed + part
        total = jnp.sum(total, axis=1, keepdims=True)
        out_ref[:, i] = mixed.astype(bf16).reshape(owners, -1, width)
        stat_ref[:, i] = jnp.where(lane == 0, tops[i], total).reshape(owners, -1, 128)

        @pl.when(info_ref[2] == request)
        def _():
            acc[...] = mixed

    for i in range(count):
        request = info_ref[0] + i

        @pl.when(info_ref[2] == request)
        def _():
            queries = q_ref[:, request].reshape(rows, key_width)
            fresh = new_ref[...]
            new_scores = (
                lax.dot_general(queries, fresh, (((1,), (1,)), ((), ())), preferred_element_type=f32) * scale
            )
            shape = (rows, fresh.shape[0])
            key = lax.broadcasted_iota(jnp.int32, shape, 1)
            step = (lax.broadcasted_iota(jnp.int32, shape, 0) // heads) % steps
            visible = (key % requests == request) & (key // requests <= step)
            new_scores = jnp.where(visible, new_scores, masked_score)
            old = stat_ref[:, i].reshape(rows, 128)
            top, total = old[:, :1], old[:, 1:2]
            peak = jnp.maximum(top, jnp.max(new_scores, axis=1, keepdims=True))
            carried = jnp.exp2(top - peak)
            new_weights = jnp.exp2(new_scores - peak)
            mixed = acc[...] * carried + jnp.dot(
                new_weights.astype(bf16), fresh[:, :width], preferred_element_type=f32
            )
            total = total * carried + jnp.sum(new_weights, axis=1, keepdims=True)
            out_ref[:, i] = mixed.astype(bf16).reshape(owners, -1, width)
            stat_ref[:, i] = jnp.where(lane == 0, peak, total).reshape(owners, -1, 128)


def split_stats(peak, weight_sum, rows):
    lane = lax.broadcasted_iota(jnp.int32, (rows, 128), 1)
    first = peak.astype(bf16).astype(f32)
    rest = peak - first
    second = rest.astype(bf16).astype(f32)
    third = rest - second
    sum_first = weight_sum.astype(bf16).astype(f32)
    sum_second = weight_sum - sum_first
    out = jnp.where(lane == 0, first, 0.0)
    out = jnp.where(lane == 1, second, out)
    out = jnp.where(lane == 2, third, out)
    out = jnp.where(lane == 3, sum_first, out)
    return jnp.where(lane == 4, sum_second, out)


def pair_kernel(out_a, stat_a, out_b, stat_b, sent_ref):
    owners, rows, _ = sent_ref.shape
    width = out_a.shape[3]
    for owner in range(owners):
        sa = stat_a[owner].reshape(rows, 128)
        sb = stat_b[owner].reshape(rows, 128)
        top_a, sum_a = sa[:, :1], sa[:, 1:2]
        top_b, sum_b = sb[:, :1], sb[:, 1:2]
        peak = jnp.maximum(top_a, top_b)
        wa = jnp.exp2(top_a - peak)
        wb = jnp.exp2(top_b - peak)
        part_a = out_a[owner].reshape(rows, width).astype(f32)
        part_b = out_b[owner].reshape(rows, width).astype(f32)
        sent_ref[owner, :, :width] = (part_a * wa + part_b * wb).astype(bf16)
        sent_ref[owner, :, width:] = split_stats(peak, sum_a * wa + sum_b * wb, rows).astype(bf16)


def project_kernel(heads, got_ref, up_ref, out_ref, mixed, projected):
    sources, rows, _ = got_ref.shape
    width = up_ref.shape[1]
    tops = []
    sums = []
    for i in range(sources):
        stat = got_ref[i, :, width:].astype(f32)
        tops.append(stat[:, 0:1] + stat[:, 1:2] + stat[:, 2:3])
        sums.append(stat[:, 3:4] + stat[:, 4:5])
    peak = functools.reduce(jnp.maximum, tops)
    weights = [jnp.exp2(t - peak) for t in tops]
    weight_sum = sum(w * s for w, s in zip(weights, sums))
    merged = sum(w * got_ref[i, :, :width].astype(f32) for i, w in enumerate(weights))
    mixed[...] = merged.reshape(mixed.shape)
    stats = split_stats(peak, weight_sum, rows).T[:16].astype(bf16)
    count = rows // heads
    for h in range(heads):
        part = mixed[:, h, :]
        high = part.astype(bf16)
        low = (part - high.astype(f32)).astype(bf16)
        both = jnp.dot(jnp.concatenate([high, low], axis=0), up_ref[h], preferred_element_type=f32)
        projected[:, h, :] = both[:count] + both[count:]
    values = projected[...].reshape(rows, projected.shape[2]).astype(bf16)
    for copy in range(out_ref.shape[0]):
        out_ref[copy, :rows, :] = values
        out_ref[copy, rows:, :] = stats


def finish_kernel(got_ref, out_ref):
    sources = got_ref.shape[0]
    rows = out_ref.shape[0] * out_ref.shape[1] * out_ref.shape[2]
    tops = []
    sums = []
    for i in range(sources):
        stat = got_ref[i, rows:, :].astype(f32)
        tops.append(stat[0:1] + stat[1:2] + stat[2:3])
        sums.append(stat[3:4] + stat[4:5])
    tops = jnp.concatenate(tops, axis=0)
    sums = jnp.concatenate(sums, axis=0)
    weights = jnp.exp2(tops - jnp.max(tops, axis=0, keepdims=True))
    weights = weights / jnp.sum(weights * sums, axis=0, keepdims=True)
    spread = jnp.concatenate([weights, jnp.zeros((128 - sources, weights.shape[1]), f32)], axis=0).T
    result = jnp.zeros((rows, got_ref.shape[2]), f32)
    for i in range(sources):
        result += got_ref[i, :rows, :].astype(f32) * spread[:rows, i : i + 1]
    half, steps = out_ref.shape[1], out_ref.shape[0]
    result = result.astype(bf16).reshape(half, steps, *out_ref.shape[2:])
    for b in range(half):
        out_ref[:, b] = result[b]


def place_kernel(info_ref, own_ref, other_ref, out_ref):
    half = own_ref.shape[1]
    first = info_ref[0]
    out_ref[:, pl.ds(first, half)] = own_ref[...]
    out_ref[:, pl.ds(half - first, half)] = other_ref[...]


def on_device(
    query_heads, up_keys, up_values, latent_cache, new_latent, context_lengths, positions
):
    steps, requests, heads, query_width = query_heads.shape
    nope = up_keys.shape[1]
    width = up_keys.shape[2]
    key_width = latent_cache.shape[2]
    rope = key_width - width
    value_width = up_values.shape[2]
    cached = latent_cache.shape[1]
    owners = lax.axis_size("head")
    plane = lax.axis_size("z") * lax.axis_size("x")
    pairs = steps * requests
    half = requests // 2
    scale = float(query_width) ** (-0.5) * log2_e

    core = lax.axis_index("core")
    slot = lax.axis_index(("z", "x", "core", "head"))

    vmem = pl.BlockSpec(memory_space=pltpu.VMEM)
    smem = pl.BlockSpec(memory_space=pltpu.SMEM)
    small = pltpu.CompilerParams(vmem_limit_bytes=12 * 2**20)
    copies, new_keys = pl.pallas_call(
        functools.partial(queries_kernel, steps),
        in_specs=[smem, vmem, vmem, vmem],
        out_specs=[vmem, vmem],
        out_shape=(
            jax.ShapeDtypeStruct((owners, requests, steps * heads, key_width), bf16),
            jax.ShapeDtypeStruct((pairs, key_width), bf16),
        ),
        scratch_shapes=[
            pltpu.VMEM((pairs, heads, nope), f32),
            pltpu.VMEM((pairs, heads, width), f32),
        ],
        compiler_params=small,
        name="queries",
    )(positions, query_heads.reshape(pairs, heads, query_width), up_keys, new_latent.reshape(pairs, key_width))
    queries = lax.all_to_all(copies, "head", 0, 0, tiled=True)
    cache = jnp.swapaxes(latent_cache, 1, 2)

    slots = plane * 2 * owners
    share = slots // requests
    fresh_for = jnp.where(slot % share == 0, slot // share, -1).astype(jnp.int32)

    def attend(first):
        info = jnp.concatenate(
            [
                jnp.stack([first.astype(jnp.int32), slot.astype(jnp.int32) * cached, fresh_for]),
                context_lengths,
            ]
        )
        rows = owners * steps * heads
        return pl.pallas_call(
            functools.partial(attention_kernel, scale, steps, heads),
            in_specs=[smem, vmem, vmem, vmem],
            out_specs=[vmem, vmem],
            scratch_shapes=[pltpu.VMEM((rows, width), f32)] + [pltpu.VMEM((rows, cached), f32)] * half,
            out_shape=(
                jax.ShapeDtypeStruct((owners, half, steps * heads, width), bf16),
                jax.ShapeDtypeStruct((owners, half, steps * heads, 128), f32),
            ),
            compiler_params=pltpu.CompilerParams(vmem_limit_bytes=20 * 2**20),
            cost_estimate=pl.CostEstimate(
                flops=2 * half * rows * cached * (key_width + width),
                bytes_accessed=half * cached * key_width * 2,
                transcendentals=half * rows * cached,
            ),
            name="attention",
        )(info, queries, cache, new_keys)

    swap = [(0, 1), (1, 0)]
    out_other, stat_other = attend((1 - core) * half)
    out_a = lax.ppermute(out_other, "core", swap)
    stat_a = lax.ppermute(stat_other, "core", swap)
    out_b, stat_b = attend(core * half)

    chunk = half * steps * heads
    sent = pl.pallas_call(
        pair_kernel,
        in_specs=[vmem] * 4,
        out_specs=vmem,
        out_shape=jax.ShapeDtypeStruct((owners, chunk, width + 128), bf16),
        compiler_params=small,
        name="pair_merge",
    )(out_a, stat_a, out_b, stat_b)
    got = lax.all_to_all(sent, "head", 0, 0, tiled=True)

    projected = pl.pallas_call(
        functools.partial(project_kernel, heads),
        in_specs=[vmem] * 2,
        out_specs=vmem,
        out_shape=jax.ShapeDtypeStruct((plane, chunk + 16, value_width), bf16),
        scratch_shapes=[
            pltpu.VMEM((chunk // heads, heads, width), f32),
            pltpu.VMEM((chunk // heads, heads, value_width), f32),
        ],
        compiler_params=small,
        name="project",
    )(got, up_values)
    everyone = lax.all_to_all(projected, ("z", "x"), 0, 0, tiled=True)

    own = pl.pallas_call(
        finish_kernel,
        in_specs=[vmem],
        out_specs=vmem,
        out_shape=jax.ShapeDtypeStruct((steps, half, heads, value_width), bf16),
        compiler_params=small,
        name="finish",
    )(everyone)
    theirs = lax.ppermute(own, "core", swap)
    return pl.pallas_call(
        place_kernel,
        in_specs=[smem, vmem, vmem],
        out_specs=vmem,
        out_shape=jax.ShapeDtypeStruct((steps, requests, heads, value_width), bf16),
        compiler_params=small,
        name="place",
    )((core * half).astype(jnp.int32).reshape(1), own, theirs)


def solution(mesh):
    fine = Mesh(mesh.devices.reshape(4, 4, 2, 4), ("z", "x", "core", "head"))
    in_specs = (
        P(None, None, "head", None),
        P("head", None, None),
        P("head", None, None),
        P(None, ("z", "x", "core", "head"), None),
        P(),
        P(),
        P(),
    )
    out_specs = P(None, None, "head", None)
    return jax.shard_map(
        on_device, mesh=fine, in_specs=in_specs, out_specs=out_specs, check_vma=False
    )
```

time: 92.9 us -> 80.3 us (0.86)
  local copies, waits for them, and re-layouts: 26.5 us -> 7.58 us
  waiting for transfers between devices: 2.89 us -> 17.8 us
  Pallas kernels: 19.2 us -> 13.6 us
  other arithmetic: 1.79 us -> 0.08 us
    unnamed x25 -> x14, local copies, waits for them, and re-layouts: 24.1 us -> 6.84 us
    all_to_all x1, waiting for transfers between devices: 1.82 us -> 16.9 us  [on_device(): queries = lax.all_to_all(copies, 'head', 0, 0, tiled=True)]
    pallas_call x4 -> x5, Pallas kernels: 9.03 us -> 5.44 us  [the longest x1 2.19 us: on_device(): pl.pallas_call(functools.partial(queries_kernel, steps), in_specs=[smem,...]
    pallas_call x2, Pallas kernels: 10.2 us -> 8.16 us  [attend(): pl.pallas_call(functools.partial(attention_kernel, scale, steps, heads),...]
  transfers between devices with their start and end apart: 4 -> 4, of which waited for: 2 -> 2; matrix products, arithmetic and copies ran while one was open for 17% -> 0% of each run, Pallas kernels for 5% -> 5%
where the time goes in v2:
time: 80.3 us; the launch traced here: 79.9 us
  blocking collectives  31.4 us (39%)
  waiting for transfers between devices  17.8 us (22%)
  Pallas kernels  13.6 us (17%)
  starting transfers between devices  9.33 us (12%)
  local copies, waits for them, and re-layouts  7.58 us (9%)
    all_to_all x1, blocking collectives, on_device(): everyone = lax.all_to_all(projected, ('z', 'x'), 0, 0, tiled=True)  19.3 us
    all_to_all x1, waiting for transfers between devices, on_device(): queries = lax.all_to_all(copies, 'head', 0, 0, tiled=True)  16.9 us
    all_to_all x1, blocking collectives, on_device(): got = lax.all_to_all(sent, 'head', 0, 0, tiled=True)  12.2 us
    pallas_call x2, Pallas kernels, attend(): pl.pallas_call(functools.partial(attention_kernel, scale, steps, heads),...  8.16 us
    unnamed x14, local copies, waits for them, and re-layouts  6.84 us
    all_to_all x1, starting transfers between devices, on_device(): queries = lax.all_to_all(copies, 'head', 0, 0, tiled=True)  5.01 us
    ppermute x1, starting transfers between devices, on_device(): theirs = lax.ppermute(own, 'core', swap)  2.28 us
    pallas_call x1, Pallas kernels, on_device(): pl.pallas_call(functools.partial(queries_kernel, steps), in_specs=[smem,...  2.19 us
  transfers between devices with their start and end apart: 4, of which 2 were waited for; matrix products, arithmetic and copies ran while one was open for 0% of the time, Pallas kernels for 5%

profile of v2, /device:TPU:1, one launch (start us, length us, event | category | flops | bytes accessed | tf_op | source)
XLA Modules:
  0.0 79.9 jit_solution(9931466036541714)
XLA Ops:
  0.0 0.7 reshape.11.new_ref
  0.7 0.0 copy-start.2
  0.8 1.6 %copy-done.2 = bf16[16,128,512]{2,1,0:T(8,128)(2,1)S(1)} copy-done((bf16[16,128,512]{2,1,0:T(8,128)(2,1)S(1)}, bf16[16,128,512]{2,1,0:T(8,128)(2,1)}, u32[]{:S(2)}) %copy-start.2) | copy-done | bytes 2097176
  2.3 0.9 %copy-done.4 = bf16[4,4,16,192]{3,2,1,0:T(8,128)(2,1)S(1)} copy-done((bf16[4,4,16,192]{3,2,1,0:T(8,128)(2,1)S(1)}, bf16[4,4,16,192]{3,2,1,0:T(8,128)(2,1)}, u32[]{:S(2)}) %copy-start.4) | copy-done | bytes 98328
  3.2 0.7 copy-done.5
  3.9 2.2 %queries.1 = (bf16[4,4,64,576]{3,2,1,0:T(8,128)(2,1)}, bf16[16,576]{1,0:T(8,128)(2,1)S(1)}) custom-call(s32[4]{0:T(128)S(1)} %copy-done.5, bf16[16,16,192]{2,1,0:T(8,128)(2,1)S(1)} %bitcast.8, bf16[16,128,512]{2,1,0:T(8,128)(2,1)S(1)} %copy-done.2, bf16[16,576]{1,0:T(8,128)(2,1)S(1)} %reshape.11.new_ref), custom_call_target="tpu_custom_call" | custom-call | tf_op jit(solution)/shard_map/queries/pallas_call | solution.py:249
  6.1 5.0 %all-to-all-start = ((bf16[4,4,64,576]{3,2,1,0:T(8,128)(2,1)}), bf16[4,4,64,576]{3,2,1,0:T(8,128)(2,1)S(1)}, u32[]{:S(2)}, u32[]{:S(2)}) async-start(bf16[4,4,64,576]{3,2,1,0:T(8,128)(2,1)} %get-tuple-element.11), calls=%async_computation | async-start | bytes 2621440 | tf_op jit(solution)/shard_map/all_to_all | solution.py:264
  11.1 0.1 add_add_fusion.1
  11.2 16.9 %all-to-all-done.q_ref = bf16[4,4,64,576]{3,2,1,0:T(8,128)(2,1)S(1)} async-done(((bf16[4,4,64,576]{3,2,1,0:T(8,128)(2,1)}), bf16[4,4,64,576]{3,2,1,0:T(8,128)(2,1)S(1)}, u32[]{:S(2)}, u32[]{:S(2)}) %all-to-all-start) | async-done | bytes 1179680 | tf_op jit(solution)/shard_map/all_to_all | solution.py:264
  28.1 3.7 %copy-done = bf16[4,2048,576]{1,2,0:T(8,128)(2,1)S(1)} copy-done((bf16[4,2048,576]{1,2,0:T(8,128)(2,1)S(1)}, bf16[4,2048,576]{1,2,0:T(8,128)(2,1)}, u32[]{:S(2)}) %copy-start) | copy-done | bytes 9437208
  31.8 4.1 %attention.2 = (bf16[4,2,64,512]{3,2,1,0:T(8,128)(2,1)S(1)}, f32[4,2,64,128]{3,2,1,0:T(8,128)S(1)}) custom-call(s32[7]{0:T(128)S(1)} %get-tuple-element.18.info_ref, bf16[4,4,64,576]{3,2,1,0:T(8,128)(2,1)S(1)} %all-to-all-done.q_ref, bf16[4,576,2048]{2,1,0:T(8,128)(2,1)S(1)} %bitcast.6, bf16[16,576]{1,0:T(8,128)(2,1)S(1)} %get-tuple-element.12.new_ref), custom_call_target="tpu_custom_call" | custom-call | flops 2281701376 | bytes 4718592 | tf_op jit(solution)/shard_map/attention/pallas_call | solution.py:279
  35.9 1.9 %collective-permute-start = (bf16[4,2,64,512]{3,2,1,0:T(8,128)(2,1)S(1)}, bf16[4,2,64,512]{3,2,1,0:T(8,128)(2,1)S(1)}, u32[]{:S(2)}, u32[]{:S(2)}) collective-permute-start(bf16[4,2,64,512]{3,2,1,0:T(8,128)(2,1)S(1)} %get-tuple-element.13), channel_id=1, source_target_pairs={{0,4},{4,0},{1,5},{5,1},{2,6},{6,2},{3,7},{7,3},{8,12},{12,8},{9,1... | collective-permute-start | bytes 1572872 | tf_op jit(solution)/shard_map/ppermute | solution.py:299
  37.8 0.1 collective-permute-start.1
  37.9 4.1 %attention.3 = (bf16[4,2,64,512]{3,2,1,0:T(8,128)(2,1)S(1)}, f32[4,2,64,128]{3,2,1,0:T(8,128)S(1)}) custom-call(s32[7]{0:T(128)S(1)} %get-tuple-element.17.info_ref, bf16[4,4,64,576]{3,2,1,0:T(8,128)(2,1)S(1)} %all-to-all-done.q_ref, bf16[4,576,2048]{2,1,0:T(8,128)(2,1)S(1)} %bitcast.7, bf16[16,576]{1,0:T(8,128)(2,1)S(1)} %get-tuple-element.12.new_ref), custom_call_target="tpu_custom_call" | custom-call | flops 2281701376 | bytes 4718592 | tf_op jit(solution)/shard_map/attention/pallas_call | solution.py:279
  42.0 0.0 copy-start.3
  42.0 0.0 collective-permute-done.out_a
  42.0 0.7 pair_merge.1
  42.8 12.2 %all_to_all.15.got_ref = bf16[4,128,640]{2,1,0:T(8,128)(2,1)S(1)} all-to-all(bf16[4,128,640]{2,1,0:T(8,128)(2,1)S(1)} %pair_merge.1), channel_id=1, replica_groups=mesh['z'=4,'x'=4,'core'=2,'head'=4] {'head'}, dimensions={0} | all-to-all | bytes 1310720 | tf_op jit(solution)/shard_map/all_to_all | solution.py:312
  54.9 1.3 %project.1 = bf16[16,144,128]{2,1,0:T(8,128)(2,1)S(1)} custom-call(bf16[4,128,640]{2,1,0:T(8,128)(2,1)S(1)} %all_to_all.15.got_ref, bf16[16,512,128]{2,1,0:T(8,128)(2,1)S(1)} %copy-done.3), custom_call_target="tpu_custom_call" | custom-call | tf_op jit(solution)/shard_map/project/pallas_call | solution.py:314
  56.3 19.3 %all_to_all.16.got_ref = bf16[16,144,128]{2,1,0:T(8,128)(2,1)S(1)} all-to-all(bf16[16,144,128]{2,1,0:T(8,128)(2,1)S(1)} %project.1), channel_id=1, replica_groups=mesh['z'=4,'x'=4,'core'=2,'head'=4] {'z','x'}, dimensions={0} | all-to-all | bytes 1179648 | tf_op jit(solution)/shard_map/all_to_all | solution.py:326
  75.5 0.5 finish.1.own_ref
  76.1 2.3 %collective-permute-start.2 = (bf16[4,2,16,128]{3,2,1,0:T(8,128)(2,1)S(1)}, bf16[4,2,16,128]{3,2,1,0:T(8,128)(2,1)S(1)}, u32[]{:S(2)}, u32[]{:S(2)}) collective-permute-start(bf16[4,2,16,128]{3,2,1,0:T(8,128)(2,1)S(1)} %finish.1.own_ref), channel_id=1, source_target_pairs={{0,4},{4,0},{1,5},{5,1},{2,6},{6,2},{3,7},{7,3},{8,12},{12,8},{9,1... | collective-permute-start | bytes 98312 | tf_op jit(solution)/shard_map/ppermute | solution.py:336
  78.4 0.9 %collective-permute-done.2.other_ref = bf16[4,2,16,128]{3,2,1,0:T(8,128)(2,1)S(1)} collective-permute-done((bf16[4,2,16,128]{3,2,1,0:T(8,128)(2,1)S(1)}, bf16[4,2,16,128]{3,2,1,0:T(8,128)(2,1)S(1)}, u32[]{:S(2)}, u32[]{:S(2)}) %collective-permute-start.2) | collective-permute-done | bytes 32800 | tf_op jit(solution)/shard_map/ppermute | solution.py:336
  79.2 0.6 place.1
  (9 shorter events, 0.0 us)
Async XLA Ops:
  0.7 1.6 %copy-start.2 = (bf16[16,128,512]{2,1,0:T(8,128)(2,1)S(1)}, bf16[16,128,512]{2,1,0:T(8,128)(2,1)}, u32[]{:S(2)}) copy-start(bf16[16,128,512]{2,1,0:T(8,128)(2,1)} %up_ref.2) | copy-start | bytes 6291460
  2.3 0.9 %copy-start.4 = (bf16[4,4,16,192]{3,2,1,0:T(8,128)(2,1)S(1)}, bf16[4,4,16,192]{3,2,1,0:T(8,128)(2,1)}, u32[]{:S(2)}) copy-start(bf16[4,4,16,192]{3,2,1,0:T(8,128)(2,1)} %param.7) | copy-start | bytes 294916
  3.2 0.7 copy-start.5
  3.9 7.2 %copy-start.6 = (s32[4]{0:T(128)S(1)}, s32[4]{0:T(128)}, u32[]{:S(2)}) copy-start(s32[4]{0:T(128)} %param.12) | copy-start | bytes 52
  6.1 22.0 %all-to-all-start = ((bf16[4,4,64,576]{3,2,1,0:T(8,128)(2,1)}), bf16[4,4,64,576]{3,2,1,0:T(8,128)(2,1)S(1)}, u32[]{:S(2)}, u32[]{:S(2)}) async-start(bf16[4,4,64,576]{3,2,1,0:T(8,128)(2,1)} %get-tuple-element.11), calls=%async_computation | async-start | bytes 2621440 | tf_op jit(solution)/shard_map/all_to_all | solution.py:264
  28.1 3.7 %copy-start = (bf16[4,2048,576]{1,2,0:T(8,128)(2,1)S(1)}, bf16[4,2048,576]{1,2,0:T(8,128)(2,1)}, u32[]{:S(2)}) copy-start(bf16[4,2048,576]{1,2,0:T(8,128)(2,1)} %param.10) | copy-start | bytes 28311556
  31.8 6.1 %copy-start.1 = (bf16[4,2048,576]{1,2,0:T(8,128)(2,1)S(1)}, bf16[4,2048,576]{1,2,0:T(8,128)(2,1)}, u32[]{:S(2)}) copy-start(bf16[4,2048,576]{1,2,0:T(8,128)(2,1)} %param.10) | copy-start | bytes 28311556
  35.9 6.2 %collective-permute-start = (bf16[4,2,64,512]{3,2,1,0:T(8,128)(2,1)S(1)}, bf16[4,2,64,512]{3,2,1,0:T(8,128)(2,1)S(1)}, u32[]{:S(2)}, u32[]{:S(2)}) collective-permute-start(bf16[4,2,64,512]{3,2,1,0:T(8,128)(2,1)S(1)} %get-tuple-element.13), channel_id=1, source_target_pairs={{0,4},{4,0},{1,5},{5,1},{2,6},{6,2},{3,7},{7,3},{8,12},{12,8},{9,1... | collective-permute-start | bytes 1572872 | tf_op jit(solution)/shard_map/ppermute | solution.py:299
  37.8 4.2 %collective-permute-start.1 = (f32[4,2,64,128]{3,2,1,0:T(8,128)S(1)}, f32[4,2,64,128]{3,2,1,0:T(8,128)S(1)}, u32[]{:S(2)}, u32[]{:S(2)}) collective-permute-start(f32[4,2,64,128]{3,2,1,0:T(8,128)S(1)} %get-tuple-element.14), channel_id=1, source_target_pairs={{0,4},{4,0},{1,5},{5,1},{2,6},{6,2},{3,7},{7,3},{8,12},{12,8},{9,1... | collective-permute-start | bytes 786440 | tf_op jit(solution)/shard_map/ppermute | solution.py:300
  42.0 12.9 %copy-start.3 = (bf16[16,512,128]{2,1,0:T(8,128)(2,1)S(1)}, bf16[16,512,128]{2,1,0:T(8,128)(2,1)}, u32[]{:S(2)}) copy-start(bf16[16,512,128]{2,1,0:T(8,128)(2,1)} %up_ref.3) | copy-start | bytes 6291460
  76.1 3.1 %collective-permute-start.2 = (bf16[4,2,16,128]{3,2,1,0:T(8,128)(2,1)S(1)}, bf16[4,2,16,128]{3,2,1,0:T(8,128)(2,1)S(1)}, u32[]{:S(2)}, u32[]{:S(2)}) collective-permute-start(bf16[4,2,16,128]{3,2,1,0:T(8,128)(2,1)S(1)} %finish.1.own_ref), channel_id=1, source_target_pairs={{0,4},{4,0},{1,5},{5,1},{2,6},{6,2},{3,7},{7,3},{8,12},{12,8},{9,1... | collective-permute-start | bytes 98312 | tf_op jit(solution)/shard_map/ppermute | solution.py:336

commit v3 on v2

--- a/solution.py
+++ b/solution.py
@@ -37,33 +37,72 @@
     return jnp.cos(angles), jnp.where(lane < half, -1.0, 1.0) * jnp.sin(angles)
 
 
-def queries_kernel(steps, positions_ref, q_ref, up_ref, new_ref, out_ref, keys_ref, q_f32, lat):
-    pairs, heads, _ = q_ref.shape
+def queries_kernel(
+    steps, info_ref, positions_hbm, q_hbm, up_hbm, new_hbm, own_ref, sent_ref, keys_ref, positions, q, up, new, lat, sems
+):
+    pairs, heads, _ = q.shape
     requests = pairs // steps
-    nope, width = up_ref.shape[1], up_ref.shape[2]
-    q_f32[...] = q_ref[:, :, :nope].astype(f32)
-    for h in range(heads):
-        lat[:, h, :] = jnp.dot(q_f32[:, h, :].astype(bf16), up_ref[h], preferred_element_type=f32)
-    cos, sin = rope_tables(positions_ref, steps, new_ref.shape[1] - width)
-    rope = q_ref[:, :, nope:].astype(f32)
+    nope, width = up.shape[1], up.shape[2]
+    key_width = new.shape[2]
+    fetches = [
+        pltpu.make_async_copy(positions_hbm, positions, sems.at[0]),
+        pltpu.make_async_copy(q_hbm, q, sems.at[1]),
+        pltpu.make_async_copy(new_hbm, new, sems.at[2]),
+    ]
+    groups = 4
+    share = heads // groups
+    for g in range(groups):
+        at = pl.ds(g * share, share)
+        fetches.append(pltpu.make_async_copy(up_hbm.at[at], up.at[at], sems.at[3 + g]))
+    for fetch in fetches:
+        fetch.start()
+    own_ref[:, :, key_width:] = jnp.zeros(own_ref.shape[:2] + (own_ref.shape[2] - key_width,), bf16)
+    fetches[0].wait()
+    cos, sin = rope_tables(positions, steps, key_width - width)
+    fetches[1].wait()
+    rope = q[:, :, nope:].astype(f32)
     rope = (rope * cos[:, None, :] + swap_halves(rope) * sin[:, None, :]).astype(bf16)
     for s in range(steps):
         for b in range(requests):
-            row = jnp.concatenate([lat[s * requests + b].astype(bf16), rope[s * requests + b]], axis=-1)
-            for copy in range(out_ref.shape[0]):
-                out_ref[copy, b, s * heads : (s + 1) * heads, :] = row
-    new = new_ref[...]
-    tail = new[:, width:].astype(f32)
-    tail = (tail * cos + swap_halves(tail) * sin).astype(bf16)
-    keys_ref[...] = jnp.concatenate([new[:, :width], tail], axis=-1)
+            own_ref[b, s * heads : (s + 1) * heads, width:key_width] = rope[s * requests + b]
+    fetches[2].wait()
+    for t in range(steps):
+        at = slice(t * requests, (t + 1) * requests)
+        tail = new[t, :, width:].astype(f32)
+        tail = tail * cos[at] + swap_halves(tail) * sin[at]
+        keys_ref[t] = jnp.concatenate([new[t, :, :width], tail.astype(bf16)], axis=-1)
+    q_f32 = q[:, :, :nope].astype(f32)
+    for h in range(heads):
+        if h % share == 0:
+            fetches[3 + h // share].wait()
+        lat[:, h, :] = jnp.dot(q_f32[:, h, :].astype(bf16), up[h], preferred_element_type=f32)
+    for s in range(steps):
+        for b in range(requests):
+            own_ref[b, s * heads : (s + 1) * heads, :width] = lat[s * requests + b].astype(bf16)
+    sent_ref[...] = own_ref[pl.ds(info_ref[0], sent_ref.shape[0])]
+
+
+def stage_kernel(cache_hbm, out_ref, sems):
+    copies = []
+    for i in range(out_ref.shape[0]):
+        copies.append(pltpu.make_async_copy(cache_hbm.at[i], out_ref.at[i], sems.at[i]))
+    for copy in copies:
+        copy.start()
+    for copy in copies:
+        copy.wait()
 
 
 def attention_kernel(
-    scale, steps, heads, info_ref, q_ref, k_ref, new_ref, out_ref, stat_ref, acc, *scores
+    scale, steps, heads, info_ref, own_ref, q1_ref, q2_ref, q3_ref, k_ref, new_ref, out_ref, stat_ref, q_ref, acc, *scores
 ):
-    owners, requests = q_ref.shape[:2]
+    owners = q_ref.shape[1]
+    requests = own_ref.shape[0]
     rows = owners * q_ref.shape[2]
     key_width, cached = k_ref.shape[1:]
+    q_ref[:, 0] = own_ref[pl.ds(info_ref[0], q_ref.shape[0])]
+    q_ref[:, 1] = q1_ref[...]
+    q_ref[:, 2] = q2_ref[...]
+    q_ref[:, 3] = q3_ref[...]
     width = out_ref.shape[3]
     chunk = 1024
     count = out_ref.shape[1]
@@ -73,7 +112,7 @@
     for i in range(count):
         request = info_ref[0] + i
         limit = info_ref[3 + request] - info_ref[1]
-        queries = q_ref[:, request].reshape(rows, key_width)
+        queries = q_ref[i].reshape(rows, -1)[:, :key_width]
         top = jnp.full((rows, 128), lowest_max, f32)
         for c in range(0, cached, chunk):
             part = jnp.dot(queries, k_ref[request, :, c : c + chunk], preferred_element_type=f32) * scale
@@ -111,7 +150,7 @@
 
         @pl.when(info_ref[2] == request)
         def _():
-            queries = q_ref[:, request].reshape(rows, key_width)
+            queries = q_ref[i].reshape(rows, -1)[:, :key_width]
             fresh = new_ref[...]
             new_scores = (
                 lax.dot_general(queries, fresh, (((1,), (1,)), ((), ())), preferred_element_type=f32) * scale
@@ -149,10 +188,10 @@
     return jnp.where(lane == 4, sum_second, out)
 
 
-def pair_kernel(out_a, stat_a, out_b, stat_b, sent_ref):
-    owners, rows, _ = sent_ref.shape
+def pair_kernel(out_a, stat_a, out_b, stat_b, *sent_refs):
+    rows = sent_refs[0].shape[0]
     width = out_a.shape[3]
-    for owner in range(owners):
+    for owner, sent_ref in enumerate(sent_refs):
         sa = stat_a[owner].reshape(rows, 128)
         sb = stat_b[owner].reshape(rows, 128)
         top_a, sum_a = sa[:, :1], sa[:, 1:2]
@@ -162,23 +201,24 @@
         wb = jnp.exp2(top_b - peak)
         part_a = out_a[owner].reshape(rows, width).astype(f32)
         part_b = out_b[owner].reshape(rows, width).astype(f32)
-        sent_ref[owner, :, :width] = (part_a * wa + part_b * wb).astype(bf16)
-        sent_ref[owner, :, width:] = split_stats(peak, sum_a * wa + sum_b * wb, rows).astype(bf16)
-
-
-def project_kernel(heads, got_ref, up_ref, out_ref, mixed, projected):
-    sources, rows, _ = got_ref.shape
+        sent_ref[:, :width] = (part_a * wa + part_b * wb).astype(bf16)
+        sent_ref[:, width:] = split_stats(peak, sum_a * wa + sum_b * wb, rows).astype(bf16)
+
+
+def project_kernel(heads, own_ref, got1_ref, got2_ref, got3_ref, up_ref, out_ref, mixed, projected):
+    parts = (own_ref, got1_ref, got2_ref, got3_ref)
+    rows = own_ref.shape[0]
     width = up_ref.shape[1]
     tops = []
     sums = []
-    for i in range(sources):
-        stat = got_ref[i, :, width:].astype(f32)
+    for part in parts:
+        stat = part[:, width:].astype(f32)
         tops.append(stat[:, 0:1] + stat[:, 1:2] + stat[:, 2:3])
         sums.append(stat[:, 3:4] + stat[:, 4:5])
     peak = functools.reduce(jnp.maximum, tops)
     weights = [jnp.exp2(t - peak) for t in tops]
     weight_sum = sum(w * s for w, s in zip(weights, sums))
-    merged = sum(w * got_ref[i, :, :width].astype(f32) for i, w in enumerate(weights))
+    merged = sum(w * part[:, :width].astype(f32) for w, part in zip(weights, parts))
     mixed[...] = merged.reshape(mixed.shape)
     stats = split_stats(peak, weight_sum, rows).T[:16].astype(bf16)
     count = rows // heads
@@ -246,29 +286,54 @@
     vmem = pl.BlockSpec(memory_space=pltpu.VMEM)
     smem = pl.BlockSpec(memory_space=pltpu.SMEM)
     small = pltpu.CompilerParams(vmem_limit_bytes=12 * 2**20)
-    copies, new_keys = pl.pallas_call(
+    anywhere = pl.BlockSpec(memory_space=pl.ANY)
+    wide = 640
+    other_first = ((1 - core) * half).astype(jnp.int32)
+    own_queries, sent_queries, new_keys = pl.pallas_call(
         functools.partial(queries_kernel, steps),
-        in_specs=[smem, vmem, vmem, vmem],
-        out_specs=[vmem, vmem],
+        in_specs=[smem] + [anywhere] * 4,
+        out_specs=[vmem, vmem, vmem],
         out_shape=(
-            jax.ShapeDtypeStruct((owners, requests, steps * heads, key_width), bf16),
-            jax.ShapeDtypeStruct((pairs, key_width), bf16),
+            jax.ShapeDtypeStruct((requests, steps * heads, wide), bf16),
+            jax.ShapeDtypeStruct((half, steps * heads, wide), bf16),
+            jax.ShapeDtypeStruct((steps, requests, key_width), bf16),
         ),
         scratch_shapes=[
-            pltpu.VMEM((pairs, heads, nope), f32),
+            pltpu.SMEM((requests,), jnp.int32),
+            pltpu.VMEM((pairs, heads, query_width), bf16),
+            pltpu.VMEM(up_keys.shape, bf16),
+            pltpu.VMEM(new_latent.shape, bf16),
             pltpu.VMEM((pairs, heads, width), f32),
+            pltpu.SemaphoreType.DMA((7,)),
         ],
-        compiler_params=small,
+        compiler_params=pltpu.CompilerParams(vmem_limit_bytes=56 * 2**20),
         name="queries",
-    )(positions, query_heads.reshape(pairs, heads, query_width), up_keys, new_latent.reshape(pairs, key_width))
-    queries = lax.all_to_all(copies, "head", 0, 0, tiled=True)
-    cache = jnp.swapaxes(latent_cache, 1, 2)
+    )(other_first.reshape(1), positions, query_heads.reshape(pairs, heads, query_width), up_keys, new_latent)
+    new_keys = new_keys.reshape(pairs, key_width)
+
+    def over_head(array, k):
+        return lax.ppermute(array, "head", [(i, i ^ k) for i in range(owners)])
+
+    swap = [(0, 1), (1, 0)]
+    partners = (1, 3, 2)
+    got = [over_head(sent_queries, k) for k in partners]
+    cache = pl.pallas_call(
+        stage_kernel,
+        in_specs=[anywhere],
+        out_specs=vmem,
+        out_shape=jax.ShapeDtypeStruct((requests, key_width, cached), bf16),
+        scratch_shapes=[pltpu.SemaphoreType.DMA((requests,))],
+        compiler_params=pltpu.CompilerParams(vmem_limit_bytes=16 * 2**20),
+        cost_estimate=pl.CostEstimate(flops=0, bytes_accessed=2 * requests * key_width * cached, transcendentals=0),
+        name="stage",
+    )(jnp.swapaxes(latent_cache, 1, 2))
+    passed = [lax.ppermute(g, "core", swap) for g in got]
 
     slots = plane * 2 * owners
     share = slots // requests
     fresh_for = jnp.where(slot % share == 0, slot // share, -1).astype(jnp.int32)
 
-    def attend(first):
+    def attend(first, got):
         info = jnp.concatenate(
             [
                 jnp.stack([first.astype(jnp.int32), slot.astype(jnp.int32) * cached, fresh_for]),
@@ -278,9 +343,10 @@
         rows = owners * steps * heads
         return pl.pallas_call(
             functools.partial(attention_kernel, scale, steps, heads),
-            in_specs=[smem, vmem, vmem, vmem],
+            in_specs=[smem] + [vmem] * 6,
             out_specs=[vmem, vmem],
-            scratch_shapes=[pltpu.VMEM((rows, width), f32)] + [pltpu.VMEM((rows, cached), f32)] * half,
+            scratch_shapes=[pltpu.VMEM((half, owners, steps * heads, wide), bf16), pltpu.VMEM((rows, width), f32)]
+            + [pltpu.VMEM((rows, cached), f32)] * half,
             out_shape=(
                 jax.ShapeDtypeStruct((owners, half, steps * heads, width), bf16),
                 jax.ShapeDtypeStruct((owners, half, steps * heads, 128), f32),
@@ -292,28 +358,27 @@
                 transcendentals=half * rows * cached,
             ),
             name="attention",
-        )(info, queries, cache, new_keys)
-
-    swap = [(0, 1), (1, 0)]
-    out_other, stat_other = attend((1 - core) * half)
+        )(info, own_queries, *got, cache, new_keys)
+
+    out_other, stat_other = attend(other_first, got)
     out_a = lax.ppermute(out_other, "core", swap)
     stat_a = lax.ppermute(stat_other, "core", swap)
-    out_b, stat_b = attend(core * half)
+    out_b, stat_b = attend(core * half, passed)
 
     chunk = half * steps * heads
     sent = pl.pallas_call(
         pair_kernel,
         in_specs=[vmem] * 4,
-        out_specs=vmem,
-        out_shape=jax.ShapeDtypeStruct((owners, chunk, width + 128), bf16),
+        out_specs=[vmem] * owners,
+        out_shape=[jax.ShapeDtypeStruct((chunk, width + 128), bf16)] * owners,
         compiler_params=small,
         name="pair_merge",
     )(out_a, stat_a, out_b, stat_b)
-    got = lax.all_to_all(sent, "head", 0, 0, tiled=True)
+    arrived = [over_head(array, k) for array, k in zip(sent[1:], partners)]
 
     projected = pl.pallas_call(
         functools.partial(project_kernel, heads),
-        in_specs=[vmem] * 2,
+        in_specs=[vmem] * 5,
         out_specs=vmem,
         out_shape=jax.ShapeDtypeStruct((plane, chunk + 16, value_width), bf16),
         scratch_shapes=[
@@ -322,7 +387,7 @@
         ],
         compiler_params=small,
         name="project",
-    )(got, up_values)
+    )(sent[0], *arrived, up_values)
     everyone = lax.all_to_all(projected, ("z", "x"), 0, 0, tiled=True)
 
     own = pl.pallas_call(

time: 80.3 us -> 67.6 us (0.84)
  blocking collectives: 31.4 us -> 18.2 us
  waiting for transfers between devices: 17.8 us -> 9.67 us
  local copies, waits for them, and re-layouts: 7.58 us -> 11.8 us
  starting transfers between devices: 9.33 us -> 12.7 us
  Pallas kernels: 13.6 us -> 14.8 us
    all_to_all x1 -> x0, waiting for transfers between devices: 16.9 us -> none  [on_device(): queries = lax.all_to_all(copies, 'head', 0, 0, tiled=True)]
    all_to_all x1 -> x0, blocking collectives: 12.2 us -> none  [on_device(): got = lax.all_to_all(sent, 'head', 0, 0, tiled=True)]
    ppermute x0 -> x9, waiting for transfers between devices: none -> 8.81 us  [the longest x6 7.59 us: over_head(): return lax.ppermute(array, 'head', [(i, i ^ k) for i in range(owners)])]
    ppermute x0 -> x9, starting transfers between devices: none -> 8.79 us  [the longest x6 8.19 us: over_head(): return lax.ppermute(array, 'head', [(i, i ^ k) for i in range(owners)])]
    all_to_all x1 -> x0, starting transfers between devices: 5.01 us -> none  [on_device(): queries = lax.all_to_all(copies, 'head', 0, 0, tiled=True)]
    unnamed x14 -> x12, local copies, waits for them, and re-layouts: 6.84 us -> 11 us
    pallas_call x2 -> x3, Pallas kernels: 2.93 us -> 4.18 us  [the longest x1 2.78 us: on_device(): pl.pallas_call(functools.partial(queries_kernel, steps), in_specs=[smem]...]
    all_to_all x1, blocking collectives: 19.3 us -> 18.2 us  [on_device(): everyone = lax.all_to_all(projected, ('z', 'x'), 0, 0, tiled=True)]
  transfers between devices with their start and end apart: 4 -> 12, of which waited for: 2 -> 7; matrix products, arithmetic and copies ran while one was open for 0% -> 1% of each run, Pallas kernels for 5% -> 7%
where the time goes in v3:
time: 67.6 us; the launch traced here: 67.3 us
  blocking collectives  18.2 us (27%)
  Pallas kernels  14.8 us (22%)
  starting transfers between devices  12.7 us (19%)
  local copies, waits for them, and re-layouts  11.8 us (17%)
  waiting for transfers between devices  9.67 us (14%)
    all_to_all x1, blocking collectives, on_device(): everyone = lax.all_to_all(projected, ('z', 'x'), 0, 0, tiled=True)  18.2 us
    unnamed x12, local copies, waits for them, and re-layouts  11 us
    ppermute x6, starting transfers between devices, over_head(): return lax.ppermute(array, 'head', [(i, i ^ k) for i in range(owners)])  8.19 us
    pallas_call x2, Pallas kernels, attend(): pl.pallas_call(functools.partial(attention_kernel, scale, steps, heads),...  8.05 us
    ppermute x6, waiting for transfers between devices, over_head(): return lax.ppermute(array, 'head', [(i, i ^ k) for i in range(owners)])  7.59 us
    pallas_call x1, Pallas kernels, on_device(): pl.pallas_call(functools.partial(queries_kernel, steps), in_specs=[smem]...  2.78 us
    ppermute x1, starting transfers between devices, on_device(): theirs = lax.ppermute(own, 'core', swap)  2.14 us
    pallas_call x1, Pallas kernels, on_device(): pl.pallas_call(functools.partial(project_kernel, heads), in_specs=[vmem]...  1.38 us
  transfers between devices with their start and end apart: 12, of which 7 were waited for; matrix products, arithmetic and copies ran while one was open for 1% of the time, Pallas kernels for 7%

profile of v3, /device:TPU:1, one launch (start us, length us, event | category | flops | bytes accessed | tf_op | source)
XLA Modules:
  0.0 67.3 jit_solution(6597614565871242537)
XLA Ops:
  0.0 2.8 %queries.1 = (bf16[4,64,640]{2,1,0:T(8,128)(2,1)}, bf16[2,64,640]{2,1,0:T(8,128)(2,1)}, bf16[4,4,576]{2,1,0:T(4,128)(2,1)}) custom-call(s32[1]{0:T(128)} %bitcast.1.info_ref, s32[4]{0:T(128)} %positions_hbm.1, bf16[16,16,192]{2,1,0:T(8,128)(2,1)} %bitcast.7, bf16[16,128,512]{2,1,0:T(8,128)(2,1)} %up_hbm.1, bf16[4,4,576]{2,1,0:T(4,128)(2,1)} %new_hbm.1), custom_call_target="tpu_custom_call" | custom-call | tf_op jit(solution)/shard_map/queries/pallas_call | solution.py:292
  2.8 2.2 %collective-permute-start = (bf16[2,64,640]{2,1,0:T(8,128)(2,1)}, bf16[2,64,640]{2,1,0:T(8,128)(2,1)S(1)}, u32[]{:S(2)}, u32[]{:S(2)}) collective-permute-start(bf16[2,64,640]{2,1,0:T(8,128)(2,1)} %get-tuple-element.17), channel_id=1, source_target_pairs={{0,1},{1,0},{2,3},{3,2},{4,5},{5,4},{6,7},{7,6},{8,9},{9,8},{10,11... | collective-permute-start | bytes 491528 | tf_op jit(solution)/shard_map/ppermute | solution.py:315
  5.0 1.9 %collective-permute-start.1 = (bf16[2,64,640]{2,1,0:T(8,128)(2,1)}, bf16[2,64,640]{2,1,0:T(8,128)(2,1)S(1)}, u32[]{:S(2)}, u32[]{:S(2)}) collective-permute-start(bf16[2,64,640]{2,1,0:T(8,128)(2,1)} %get-tuple-element.17), channel_id=1, source_target_pairs={{0,3},{1,2},{2,1},{3,0},{4,7},{5,6},{6,5},{7,4},{8,11},{9,10},{10,... | collective-permute-start | bytes 491528 | tf_op jit(solution)/shard_map/ppermute | solution.py:315
  6.9 0.7 %collective-permute-start.2 = (bf16[2,64,640]{2,1,0:T(8,128)(2,1)}, bf16[2,64,640]{2,1,0:T(8,128)(2,1)S(1)}, u32[]{:S(2)}, u32[]{:S(2)}) collective-permute-start(bf16[2,64,640]{2,1,0:T(8,128)(2,1)} %get-tuple-element.17), channel_id=1, source_target_pairs={{0,2},{1,3},{2,0},{3,1},{4,6},{5,7},{6,4},{7,5},{8,10},{9,11},{10,... | collective-permute-start | bytes 491528 | tf_op jit(solution)/shard_map/ppermute | solution.py:315
  7.6 0.7 %reshape.12.new_ref = bf16[16,576]{1,0:T(8,128)(2,1)S(1)} reshape(bf16[4,4,576]{2,1,0:T(4,128)(2,1)} %get-tuple-element.18) | data formatting | bytes 36864 | tf_op jit(solution)/shard_map/reshape | solution.py:312
  8.4 3.7 %copy-done.2 = bf16[4,2048,576]{1,2,0:T(8,128)(2,1)S(1)} copy-done((bf16[4,2048,576]{1,2,0:T(8,128)(2,1)S(1)}, bf16[4,2048,576]{1,2,0:T(8,128)(2,1)}, u32[]{:S(2)}) %copy-start.2) | copy-done | bytes 9437208
  12.0 0.7 stage.1.k_ref
  12.7 3.7 %copy-done = bf16[4,576,2048]{2,1,0:T(8,128)(2,1)} copy-done((bf16[4,576,2048]{2,1,0:T(8,128)(2,1)}, bf16[4,576,2048]{2,1,0:T(8,128)(2,1)S(1)}, u32[]{:S(2)}) %copy-start) | copy-done | bytes 9437208
  16.5 3.7 %copy-done.1 = bf16[4,576,2048]{2,1,0:T(8,128)(2,1)S(1)} copy-done((bf16[4,576,2048]{2,1,0:T(8,128)(2,1)S(1)}, bf16[4,576,2048]{2,1,0:T(8,128)(2,1)}, u32[]{:S(2)}) %copy-start.1) | copy-done | bytes 9437208
  20.2 4.0 %attention.2 = (bf16[4,2,64,512]{3,2,1,0:T(8,128)(2,1)S(1)}, f32[4,2,64,128]{3,2,1,0:T(8,128)S(1)}) custom-call(s32[7]{0:T(128)S(1)} %get-tuple-element.28.info_ref, bf16[4,64,640]{2,1,0:T(8,128)(2,1)S(1)} %copy-done.4, bf16[2,64,640]{2,1,0:T(8,128)(2,1)S(1)} %collective-permute-done.q1_ref, bf16[2,64,640]{2,1,0:T(8,128)(2,1)S(1)} %collective-permute-done.1.q2_ref, ...), custom_call_target="tpu_custom_call" | custom-call | flops 2281701376 | bytes 4718592 | tf_op jit(solution)/shard_map/attention/pallas_call | solution.py:344
  24.2 1.3 %collective-permute-start.3 = (bf16[4,2,64,512]{3,2,1,0:T(8,128)(2,1)S(1)}, bf16[4,2,64,512]{3,2,1,0:T(8,128)(2,1)S(1)}, u32[]{:S(2)}, u32[]{:S(2)}) collective-permute-start(bf16[4,2,64,512]{3,2,1,0:T(8,128)(2,1)S(1)} %get-tuple-element.19), channel_id=1, source_target_pairs={{0,4},{4,0},{1,5},{5,1},{2,6},{6,2},{3,7},{7,3},{8,12},{12,8},{9,1... | collective-permute-start | bytes 1572872 | tf_op jit(solution)/shard_map/ppermute | solution.py:364
  26.6 0.7 %collective-permute-done.5.q1_ref = bf16[2,64,640]{2,1,0:T(8,128)(2,1)S(1)} collective-permute-done((bf16[2,64,640]{2,1,0:T(8,128)(2,1)S(1)}, bf16[2,64,640]{2,1,0:T(8,128)(2,1)S(1)}, u32[]{:S(2)}, u32[]{:S(2)}) %collective-permute-start.5) | collective-permute-done | bytes 163872 | tf_op jit(solution)/shard_map/ppermute | solution.py:330
  27.8 4.0 %attention.3 = (bf16[4,2,64,512]{3,2,1,0:T(8,128)(2,1)S(1)}, f32[4,2,64,128]{3,2,1,0:T(8,128)S(1)}) custom-call(s32[7]{0:T(128)S(1)} %get-tuple-element.27.info_ref, bf16[4,64,640]{2,1,0:T(8,128)(2,1)S(1)} %copy-done.4, bf16[2,64,640]{2,1,0:T(8,128)(2,1)S(1)} %collective-permute-done.5.q1_ref, bf16[2,64,640]{2,1,0:T(8,128)(2,1)S(1)} %collective-permute-done.6.q2_ref, ...), custom_call_target="tpu_custom_call" | custom-call | flops 2281701376 | bytes 4718592 | tf_op jit(solution)/shard_map/attention/pallas_call | solution.py:344
  31.8 0.7 %pair_merge.1 = (bf16[128,640]{1,0:T(8,128)(2,1)S(1)}, bf16[128,640]{1,0:T(8,128)(2,1)S(1)}, bf16[128,640]{1,0:T(8,128)(2,1)S(1)}, bf16[128,640]{1,0:T(8,128)(2,1)S(1)}) custom-call(bf16[4,2,64,512]{3,2,1,0:T(8,128)(2,1)S(1)} %collective-permute-done.3.out_a, f32[4,2,64,128]{3,2,1,0:T(8,128)S(1)} %collective-permute-done.4.stat_a, ...), custom_call_target="tpu_custom_call" | custom-call | tf_op jit(solution)/shard_map/pair_merge/pallas_call | solution.py:369
  32.6 2.6 %collective-permute-start.10 = (bf16[128,640]{1,0:T(8,128)(2,1)S(1)}, bf16[128,640]{1,0:T(8,128)(2,1)S(1)}, u32[]{:S(2)}, u32[]{:S(2)}) collective-permute-start(bf16[128,640]{1,0:T(8,128)(2,1)S(1)} %get-tuple-element.26), channel_id=1, source_target_pairs={{0,2},{1,3},{2,0},{3,1},{4,6},{5,7},{6,4},{7,5},{8,10},{9,11},{10,... | collective-permute-start | bytes 491528 | tf_op jit(solution)/shard_map/ppermute | solution.py:315
  35.9 2.8 %collective-permute-done.10.got3_ref = bf16[128,640]{1,0:T(8,128)(2,1)S(1)} collective-permute-done((bf16[128,640]{1,0:T(8,128)(2,1)S(1)}, bf16[128,640]{1,0:T(8,128)(2,1)S(1)}, u32[]{:S(2)}, u32[]{:S(2)}) %collective-permute-start.10) | collective-permute-done | bytes 163872 | tf_op jit(solution)/shard_map/ppermute | solution.py:315
  38.7 4.3 %collective-permute-done.8.got1_ref = bf16[128,640]{1,0:T(8,128)(2,1)S(1)} collective-permute-done((bf16[128,640]{1,0:T(8,128)(2,1)S(1)}, bf16[128,640]{1,0:T(8,128)(2,1)S(1)}, u32[]{:S(2)}, u32[]{:S(2)}) %collective-permute-start.8) | collective-permute-done | bytes 163872 | tf_op jit(solution)/shard_map/ppermute | solution.py:315
  43.1 0.5 collective-permute-done.9.got2_ref
  43.5 1.4 %project.1 = bf16[16,144,128]{2,1,0:T(8,128)(2,1)S(1)} custom-call(bf16[128,640]{1,0:T(8,128)(2,1)S(1)} %get-tuple-element.23.own_ref, bf16[128,640]{1,0:T(8,128)(2,1)S(1)} %collective-permute-done.8.got1_ref, bf16[128,640]{1,0:T(8,128)(2,1)S(1)} %collective-permute-done.9.got2_ref, bf16[128,640]{1,0:T(8,128)(2,1)S(1)} %collective-permute-done.10.got3_ref, ...), custom_call_target="tpu_custom_call" | custom-call | tf_op jit(solution)/shard_map/project/pallas_call | solution.py:379
  44.9 18.2 %all_to_all.5.got_ref = bf16[16,144,128]{2,1,0:T(8,128)(2,1)S(1)} all-to-all(bf16[16,144,128]{2,1,0:T(8,128)(2,1)S(1)} %project.1), channel_id=1, replica_groups=mesh['z'=4,'x'=4,'core'=2,'head'=4] {'z','x'}, dimensions={0} | all-to-all | bytes 1179648 | tf_op jit(solution)/shard_map/all_to_all | solution.py:391
  63.1 0.5 finish.1.own_ref
  63.7 2.1 %collective-permute-start.11 = (bf16[4,2,16,128]{3,2,1,0:T(8,128)(2,1)S(1)}, bf16[4,2,16,128]{3,2,1,0:T(8,128)(2,1)S(1)}, u32[]{:S(2)}, u32[]{:S(2)}) collective-permute-start(bf16[4,2,16,128]{3,2,1,0:T(8,128)(2,1)S(1)} %finish.1.own_ref), channel_id=1, source_target_pairs={{0,4},{4,0},{1,5},{5,1},{2,6},{6,2},{3,7},{7,3},{8,12},{12,8},{9,1... | collective-permute-start | bytes 98312 | tf_op jit(solution)/shard_map/ppermute | solution.py:401
  65.8 0.9 %collective-permute-done.11.other_ref = bf16[4,2,16,128]{3,2,1,0:T(8,128)(2,1)S(1)} collective-permute-done((bf16[4,2,16,128]{3,2,1,0:T(8,128)(2,1)S(1)}, bf16[4,2,16,128]{3,2,1,0:T(8,128)(2,1)S(1)}, u32[]{:S(2)}, u32[]{:S(2)}) %collective-permute-start.11) | collective-permute-done | bytes 32800 | tf_op jit(solution)/shard_map/ppermute | solution.py:401
  66.7 0.6 place.1
  (23 shorter events, 2.4 us)
Async XLA Ops:
  2.8 13.7 %collective-permute-start = (bf16[2,64,640]{2,1,0:T(8,128)(2,1)}, bf16[2,64,640]{2,1,0:T(8,128)(2,1)S(1)}, u32[]{:S(2)}, u32[]{:S(2)}) collective-permute-start(bf16[2,64,640]{2,1,0:T(8,128)(2,1)} %get-tuple-element.17), channel_id=1, source_target_pairs={{0,1},{1,0},{2,3},{3,2},{4,5},{5,4},{6,7},{7,6},{8,9},{9,8},{10,11... | collective-permute-start | bytes 491528 | tf_op jit(solution)/shard_map/ppermute | solution.py:315
  5.0 11.5 %collective-permute-start.1 = (bf16[2,64,640]{2,1,0:T(8,128)(2,1)}, bf16[2,64,640]{2,1,0:T(8,128)(2,1)S(1)}, u32[]{:S(2)}, u32[]{:S(2)}) collective-permute-start(bf16[2,64,640]{2,1,0:T(8,128)(2,1)} %get-tuple-element.17), channel_id=1, source_target_pairs={{0,3},{1,2},{2,1},{3,0},{4,7},{5,6},{6,5},{7,4},{8,11},{9,10},{10,... | collective-permute-start | bytes 491528 | tf_op jit(solution)/shard_map/ppermute | solution.py:315
  6.9 9.6 %collective-permute-start.2 = (bf16[2,64,640]{2,1,0:T(8,128)(2,1)}, bf16[2,64,640]{2,1,0:T(8,128)(2,1)S(1)}, u32[]{:S(2)}, u32[]{:S(2)}) collective-permute-start(bf16[2,64,640]{2,1,0:T(8,128)(2,1)} %get-tuple-element.17), channel_id=1, source_target_pairs={{0,2},{1,3},{2,0},{3,1},{4,6},{5,7},{6,4},{7,5},{8,10},{9,11},{10,... | collective-permute-start | bytes 491528 | tf_op jit(solution)/shard_map/ppermute | solution.py:315
  8.4 3.7 %copy-start.2 = (bf16[4,2048,576]{1,2,0:T(8,128)(2,1)S(1)}, bf16[4,2048,576]{1,2,0:T(8,128)(2,1)}, u32[]{:S(2)}) copy-start(bf16[4,2048,576]{1,2,0:T(8,128)(2,1)} %param.10) | copy-start | bytes 28311556
  12.0 4.4 %copy-start.5 = (s32[4]{0:T(128)S(1)}, s32[4]{0:T(128)}, u32[]{:S(2)}) copy-start(s32[4]{0:T(128)} %param.12) | copy-start | bytes 52
  12.0 4.5 %copy-start.4 = (bf16[4,64,640]{2,1,0:T(8,128)(2,1)S(1)}, bf16[4,64,640]{2,1,0:T(8,128)(2,1)}, u32[]{:S(2)}) copy-start(bf16[4,64,640]{2,1,0:T(8,128)(2,1)} %get-tuple-element.16.own_ref) | copy-start | bytes 983044
  12.7 3.7 %copy-start = (bf16[4,576,2048]{2,1,0:T(8,128)(2,1)}, bf16[4,576,2048]{2,1,0:T(8,128)(2,1)S(1)}, u32[]{:S(2)}) copy-start(bf16[4,576,2048]{2,1,0:T(8,128)(2,1)S(1)} %stage.1.k_ref) | copy-start | bytes 28311556
  16.5 3.7 %copy-start.1 = (bf16[4,576,2048]{2,1,0:T(8,128)(2,1)S(1)}, bf16[4,576,2048]{2,1,0:T(8,128)(2,1)}, u32[]{:S(2)}) copy-start(bf16[4,576,2048]{2,1,0:T(8,128)(2,1)} %copy-done) | copy-start | bytes 28311556
  20.2 23.3 %copy-start.3 = (bf16[16,512,128]{2,1,0:T(8,128)(2,1)S(1)}, bf16[16,512,128]{2,1,0:T(8,128)(2,1)}, u32[]{:S(2)}) copy-start(bf16[16,512,128]{2,1,0:T(8,128)(2,1)} %up_ref.1) | copy-start | bytes 6291460
  24.2 7.6 %collective-permute-start.3 = (bf16[4,2,64,512]{3,2,1,0:T(8,128)(2,1)S(1)}, bf16[4,2,64,512]{3,2,1,0:T(8,128)(2,1)S(1)}, u32[]{:S(2)}, u32[]{:S(2)}) collective-permute-start(bf16[4,2,64,512]{3,2,1,0:T(8,128)(2,1)S(1)} %get-tuple-element.19), channel_id=1, source_target_pairs={{0,4},{4,0},{1,5},{5,1},{2,6},{6,2},{3,7},{7,3},{8,12},{12,8},{9,1... | collective-permute-start | bytes 1572872 | tf_op jit(solution)/shard_map/ppermute | solution.py:364
  25.5 1.8 %collective-permute-start.5 = (bf16[2,64,640]{2,1,0:T(8,128)(2,1)S(1)}, bf16[2,64,640]{2,1,0:T(8,128)(2,1)S(1)}, u32[]{:S(2)}, u32[]{:S(2)}) collective-permute-start(bf16[2,64,640]{2,1,0:T(8,128)(2,1)S(1)} %collective-permute-done.q1_ref), channel_id=1, source_target_pairs={{0,4},{4,0},{1,5},{5,1},{2,6},{6,2},{3,7},{7,3},{8,12},{12,8},{9,1... | collective-permute-start | bytes 491528 | tf_op jit(solution)/shard_map/ppermute | solution.py:330
  25.6 1.9 %collective-permute-start.6 = (bf16[2,64,640]{2,1,0:T(8,128)(2,1)S(1)}, bf16[2,64,640]{2,1,0:T(8,128)(2,1)S(1)}, u32[]{:S(2)}, u32[]{:S(2)}) collective-permute-start(bf16[2,64,640]{2,1,0:T(8,128)(2,1)S(1)} %collective-permute-done.1.q2_ref), channel_id=1, source_target_pairs={{0,4},{4,0},{1,5},{5,1},{2,6},{6,2},{3,7},{7,3},{8,12},{12,8},{9,1... | collective-permute-start | bytes 491528 | tf_op jit(solution)/shard_map/ppermute | solution.py:330
  26.0 1.7 %collective-permute-start.7 = (bf16[2,64,640]{2,1,0:T(8,128)(2,1)S(1)}, bf16[2,64,640]{2,1,0:T(8,128)(2,1)S(1)}, u32[]{:S(2)}, u32[]{:S(2)}) collective-permute-start(bf16[2,64,640]{2,1,0:T(8,128)(2,1)S(1)} %collective-permute-done.2.q3_ref), channel_id=1, source_target_pairs={{0,4},{4,0},{1,5},{5,1},{2,6},{6,2},{3,7},{7,3},{8,12},{12,8},{9,1... | collective-permute-start | bytes 491528 | tf_op jit(solution)/shard_map/ppermute | solution.py:330
  26.1 5.7 %collective-permute-start.4 = (f32[4,2,64,128]{3,2,1,0:T(8,128)S(1)}, f32[4,2,64,128]{3,2,1,0:T(8,128)S(1)}, u32[]{:S(2)}, u32[]{:S(2)}) collective-permute-start(f32[4,2,64,128]{3,2,1,0:T(8,128)S(1)} %get-tuple-element.20), channel_id=1, source_target_pairs={{0,4},{4,0},{1,5},{5,1},{2,6},{6,2},{3,7},{7,3},{8,12},{12,8},{9,1... | collective-permute-start | bytes 786440 | tf_op jit(solution)/shard_map/ppermute | solution.py:365
  32.6 6.2 %collective-permute-start.10 = (bf16[128,640]{1,0:T(8,128)(2,1)S(1)}, bf16[128,640]{1,0:T(8,128)(2,1)S(1)}, u32[]{:S(2)}, u32[]{:S(2)}) collective-permute-start(bf16[128,640]{1,0:T(8,128)(2,1)S(1)} %get-tuple-element.26), channel_id=1, source_target_pairs={{0,2},{1,3},{2,0},{3,1},{4,6},{5,7},{6,4},{7,5},{8,10},{9,11},{10,... | collective-permute-start | bytes 491528 | tf_op jit(solution)/shard_map/ppermute | solution.py:315
  35.2 7.9 %collective-permute-start.8 = (bf16[128,640]{1,0:T(8,128)(2,1)S(1)}, bf16[128,640]{1,0:T(8,128)(2,1)S(1)}, u32[]{:S(2)}, u32[]{:S(2)}) collective-permute-start(bf16[128,640]{1,0:T(8,128)(2,1)S(1)} %get-tuple-element.24), channel_id=1, source_target_pairs={{0,1},{1,0},{2,3},{3,2},{4,5},{5,4},{6,7},{7,6},{8,9},{9,8},{10,11... | collective-permute-start | bytes 491528 | tf_op jit(solution)/shard_map/ppermute | solution.py:315
  35.6 8.0 %collective-permute-start.9 = (bf16[128,640]{1,0:T(8,128)(2,1)S(1)}, bf16[128,640]{1,0:T(8,128)(2,1)S(1)}, u32[]{:S(2)}, u32[]{:S(2)}) collective-permute-start(bf16[128,640]{1,0:T(8,128)(2,1)S(1)} %get-tuple-element.25), channel_id=1, source_target_pairs={{0,3},{1,2},{2,1},{3,0},{4,7},{5,6},{6,5},{7,4},{8,11},{9,10},{10,... | collective-permute-start | bytes 491528 | tf_op jit(solution)/shard_map/ppermute | solution.py:315
  63.7 3.0 %collective-permute-start.11 = (bf16[4,2,16,128]{3,2,1,0:T(8,128)(2,1)S(1)}, bf16[4,2,16,128]{3,2,1,0:T(8,128)(2,1)S(1)}, u32[]{:S(2)}, u32[]{:S(2)}) collective-permute-start(bf16[4,2,16,128]{3,2,1,0:T(8,128)(2,1)S(1)} %finish.1.own_ref), channel_id=1, source_target_pairs={{0,4},{4,0},{1,5},{5,1},{2,6},{6,2},{3,7},{7,3},{8,12},{12,8},{9,1... | collective-permute-start | bytes 98312 | tf_op jit(solution)/shard_map/ppermute | solution.py:401

commit v4 on v3

v4 whole, which is shorter than its diff:
```python
import functools

import jax
import jax.numpy as jnp
from jax import lax
from jax.experimental import pallas as pl
from jax.experimental.pallas import tpu as pltpu
from jax.sharding import Mesh, PartitionSpec as P

rope_base = 50000.0
masked_score = -1e30
lowest_max = -1e29
log2_e = 1.4426950408889634
bf16 = jnp.bfloat16
f32 = jnp.float32


def swap_halves(values):
    half = values.shape[-1] // 2
    return jnp.concatenate([values[..., half:], values[..., :half]], axis=-1)


def rope_tables(positions_ref, steps, width):
    requests = positions_ref.shape[0]
    pairs = steps * requests
    half = width // 2
    row = lax.broadcasted_iota(jnp.int32, (pairs, width), 0)
    lane = lax.broadcasted_iota(jnp.int32, (pairs, width), 1)
    where_at = row // requests
    for b in range(requests):
        where_at += jnp.where(row % requests == b, positions_ref[b], 0)
    counter = lax.broadcasted_iota(jnp.int32, (1, width), 1) % half
    inverse = jnp.zeros((1, width), f32)
    for i in range(half):
        inverse = jnp.where(counter == i, f32(rope_base ** (-2.0 * i / width)), inverse)
    angles = where_at.astype(f32) * inverse
    return jnp.cos(angles), jnp.where(lane < half, -1.0, 1.0) * jnp.sin(angles)


def queries_kernel(
    steps, info_ref, positions_hbm, q_hbm, up_hbm, new_hbm, own_ref, sent_ref, keys_ref, positions, q, up, new, lat, sems
):
    pairs, heads, _ = q.shape
    requests = pairs // steps
    nope, width = up.shape[1], up.shape[2]
    key_width = new.shape[2]
    fetches = [
        pltpu.make_async_copy(positions_hbm, positions, sems.at[0]),
        pltpu.make_async_copy(q_hbm, q, sems.at[1]),
        pltpu.make_async_copy(new_hbm, new, sems.at[2]),
    ]
    groups = 4
    share = heads // groups
    for g in range(groups):
        at = pl.ds(g * share, share)
        fetches.append(pltpu.make_async_copy(up_hbm.at[at], up.at[at], sems.at[3 + g]))
    for fetch in fetches:
        fetch.start()
    own_ref[:, :, key_width:] = jnp.zeros(own_ref.shape[:2] + (own_ref.shape[2] - key_width,), bf16)
    fetches[0].wait()
    cos, sin = rope_tables(positions, steps, key_width - width)
    fetches[1].wait()
    rope = q[:, :, nope:].astype(f32)
    rope = (rope * cos[:, None, :] + swap_halves(rope) * sin[:, None, :]).astype(bf16)
    for s in range(steps):
        for b in range(requests):
            own_ref[b, s * heads : (s + 1) * heads, width:key_width] = rope[s * requests + b]
    fetches[2].wait()
    rows = jnp.concatenate([new[t].astype(f32) for t in range(steps)], axis=0)
    tail = rows[:, width:]
    tail = tail * cos + swap_halves(tail) * sin
    keys_ref[...] = jnp.concatenate([rows[:, :width], tail], axis=-1).astype(bf16)
    q_f32 = q[:, :, :nope].astype(f32)
    for h in range(heads):
        if h % share == 0:
            fetches[3 + h // share].wait()
        lat[:, h, :] = jnp.dot(q_f32[:, h, :].astype(bf16), up[h], preferred_element_type=f32)
    for s in range(steps):
        for b in range(requests):
            own_ref[b, s * heads : (s + 1) * heads, :width] = lat[s * requests + b].astype(bf16)
    sent_ref[...] = own_ref[pl.ds(info_ref[0], sent_ref.shape[0])]


def split_stats(peak, weight_sum, rows):
    lane = lax.broadcasted_iota(jnp.int32, (rows, 128), 1)
    first = peak.astype(bf16).astype(f32)
    rest = peak - first
    second = rest.astype(bf16).astype(f32)
    third = rest - second
    sum_first = weight_sum.astype(bf16).astype(f32)
    sum_second = weight_sum - sum_first
    out = jnp.where(lane == 0, first, 0.0)
    out = jnp.where(lane == 1, second, out)
    out = jnp.where(lane == 2, third, out)
    out = jnp.where(lane == 3, sum_first, out)
    return jnp.where(lane == 4, sum_second, out)


def attention_kernel(
    scale, info_ref, own_ref, q1_ref, q2_ref, q3_ref, cache_hbm, out_ref, q_ref, k_ref, sems, *scores
):
    count, owners, share, _ = q_ref.shape
    rows = owners * share
    key_width, cached = k_ref.shape[1:]
    width = out_ref.shape[2] - 128
    pieces = sems.shape[1]
    piece = cached // pieces
    chunk = 1024
    first = info_ref[0]
    fetches = []
    for i in range(count):
        for p in range(pieces):
            at = pl.ds(p * piece, piece)
            fetches.append(
                pltpu.make_async_copy(cache_hbm.at[first + i, :, at], k_ref.at[i, :, at], sems.at[i, p])
            )
    for fetch in fetches:
        fetch.start()

    q_ref[:, 0] = own_ref[pl.ds(first, count)]
    q_ref[:, 1] = q1_ref[...]
    q_ref[:, 2] = q2_ref[...]
    q_ref[:, 3] = q3_ref[...]

    tops = []
    for i in range(count):
        limit = info_ref[2 + first + i] - info_ref[1]
        queries = q_ref[i].reshape(rows, -1)[:, :key_width]
        top = jnp.full((rows, 128), lowest_max, f32)
        step = piece if i == 0 else cached
        for c in range(0, cached, step):
            for p in range(c // piece, (c + step) // piece):
                fetches[i * pieces + p].wait()
            part = jnp.dot(queries, k_ref[i, :, c : c + step], preferred_element_type=f32) * scale
            column = lax.broadcasted_iota(jnp.int32, (1, step), 1) + c
            part = jnp.where(column < limit, part, masked_score)
            scores[i][:, c : c + step] = part
            for at in range(0, step, 128):
                top = jnp.maximum(top, part[:, at : at + 128])
        tops.append(jnp.max(top, axis=1, keepdims=True))

    for i in range(count):
        total = jnp.zeros((rows, 128), f32)
        for c in range(0, cached, chunk):
            weights = jnp.exp2(scores[i][:, c : c + chunk] - tops[i])
            for at in range(0, chunk, 128):
                total = total + weights[:, at : at + 128]
            part = lax.dot_general(
                weights.astype(bf16),
                k_ref[i, :width, c : c + chunk],
                (((1,), (1,)), ((), ())),
                preferred_element_type=f32,
            )
            mixed = part if c == 0 else mixed + part
        total = jnp.sum(total, axis=1, keepdims=True)
        at = slice(i * share, (i + 1) * share)
        out_ref[:, at, :width] = mixed.astype(bf16).reshape(owners, share, width)
        out_ref[:, at, width:] = split_stats(tops[i], total, rows).astype(bf16).reshape(owners, share, 128)


def fresh_kernel(scale, steps, heads, info_ref, own_ref, new_ref, out_ref):
    requests, share, _ = own_ref.shape
    key_width = new_ref.shape[1]
    width = out_ref.shape[1] - 128
    fresh = new_ref[...]
    shape = (share, fresh.shape[0])
    key = lax.broadcasted_iota(jnp.int32, shape, 1)
    step = (lax.broadcasted_iota(jnp.int32, shape, 0) // heads) % steps
    counted = info_ref[1] == 1
    for i in range(out_ref.shape[0] // share):
        request = info_ref[0] + i
        scores = (
            lax.dot_general(
                own_ref[request][:, :key_width], fresh, (((1,), (1,)), ((), ())), preferred_element_type=f32
            )
            * scale
        )
        visible = (key % requests == request) & (key // requests <= step) & counted
        scores = jnp.where(visible, scores, masked_score)
        top = jnp.maximum(jnp.max(scores, axis=1, keepdims=True), lowest_max)
        weights = jnp.exp2(scores - top)
        total = jnp.sum(weights, axis=1, keepdims=True)
        mixed = jnp.dot(weights.astype(bf16), fresh[:, :width], preferred_element_type=f32)
        at = slice(i * share, (i + 1) * share)
        out_ref[at, :width] = mixed.astype(bf16)
        out_ref[at, width:] = split_stats(top, total, share).astype(bf16)


def merge_parts(parts, width):
    tops = []
    sums = []
    for part in parts:
        stat = part[:, width:].astype(f32)
        tops.append(stat[:, 0:1] + stat[:, 1:2] + stat[:, 2:3])
        sums.append(stat[:, 3:4] + stat[:, 4:5])
    peak = functools.reduce(jnp.maximum, tops)
    weights = [jnp.exp2(t - peak) for t in tops]
    weight_sum = sum(w * s for w, s in zip(weights, sums))
    merged = sum(w * part[:, :width].astype(f32) for w, part in zip(weights, parts))
    return merged, peak, weight_sum


def pair_kernel(a_ref, b_ref, *sent_refs):
    rows = sent_refs[0].shape[0]
    width = a_ref.shape[2] - 128
    for owner, sent_ref in enumerate(sent_refs):
        merged, peak, weight_sum = merge_parts((a_ref[owner], b_ref[owner]), width)
        sent_ref[:, :width] = merged.astype(bf16)
        sent_ref[:, width:] = split_stats(peak, weight_sum, rows).astype(bf16)


def project_kernel(heads, *refs):
    *parts, up_ref, out_ref, mixed, projected = refs
    rows = parts[0].shape[0]
    merged, peak, weight_sum = merge_parts([part[...] for part in parts], up_ref.shape[1])
    mixed[...] = merged.reshape(mixed.shape)
    stats = split_stats(peak, weight_sum, rows).T[:16].astype(bf16)
    count = rows // heads
    for h in range(heads):
        part = mixed[:, h, :]
        high = part.astype(bf16)
        low = (part - high.astype(f32)).astype(bf16)
        both = jnp.dot(jnp.concatenate([high, low], axis=0), up_ref[h], preferred_element_type=f32)
        projected[:, h, :] = both[:count] + both[count:]
    values = projected[...].reshape(rows, projected.shape[2]).astype(bf16)
    out_ref[:rows, :] = values
    out_ref[rows:, :] = stats


def merge_rows(parts, rows):
    tops = []
    sums = []
    for part in parts:
        stat = part[rows:, :].astype(f32)
        tops.append(stat[0:1] + stat[1:2] + stat[2:3])
        sums.append(stat[3:4] + stat[4:5])
    tops = jnp.concatenate(tops, axis=0)
    peak = jnp.max(tops, axis=0, keepdims=True)
    weights = jnp.exp2(tops - peak)
    weight_sum = jnp.sum(weights * jnp.concatenate(sums, axis=0), axis=0, keepdims=True)
    return weights, peak, weight_sum


def weigh(parts, weights, rows):
    spread = jnp.concatenate([weights, jnp.zeros((128 - len(parts), weights.shape[1]), f32)], axis=0).T
    return sum(part[:rows, :].astype(f32) * spread[:rows, i : i + 1] for i, part in enumerate(parts))


def middle_kernel(*refs):
    *parts, out_ref = refs
    parts = [part[...] for part in parts]
    rows = out_ref.shape[0] - 16
    weights, peak, weight_sum = merge_rows(parts, rows)
    out_ref[:rows, :] = weigh(parts, weights, rows).astype(bf16)
    line = lax.broadcasted_iota(jnp.int32, (16, weights.shape[1]), 0)
    first = peak.astype(bf16).astype(f32)
    second = (peak - first).astype(bf16).astype(f32)
    sum_first = weight_sum.astype(bf16).astype(f32)
    stats = jnp.where(line == 0, first, 0.0)
    stats = jnp.where(line == 1, second, stats)
    stats = jnp.where(line == 2, peak - first - second, stats)
    stats = jnp.where(line == 3, sum_first, stats)
    out_ref[rows:, :] = jnp.where(line == 4, weight_sum - sum_first, stats).astype(bf16)


def finish_kernel(*refs):
    *parts, out_ref = refs
    parts = [part[...] for part in parts]
    steps, half = out_ref.shape[:2]
    rows = steps * half * out_ref.shape[2]
    weights, _, weight_sum = merge_rows(parts, rows)
    result = weigh(parts, weights / weight_sum, rows)
    result = result.astype(bf16).reshape(half, steps, *out_ref.shape[2:])
    for b in range(half):
        out_ref[:, b] = result[b]


def place_kernel(info_ref, own_ref, other_ref, out_ref):
    half = own_ref.shape[1]
    first = info_ref[0]
    out_ref[:, pl.ds(first, half)] = own_ref[...]
    out_ref[:, pl.ds(half - first, half)] = other_ref[...]


def on_device(
    query_heads, up_keys, up_values, latent_cache, new_latent, context_lengths, positions
):
    steps, requests, heads, query_width = query_heads.shape
    nope = up_keys.shape[1]
    width = up_keys.shape[2]
    key_width = latent_cache.shape[2]
    rope = key_width - width
    value_width = up_values.shape[2]
    cached = latent_cache.shape[1]
    owners = lax.axis_size("head")
    plane = lax.axis_size("z") * lax.axis_size("x")
    pairs = steps * requests
    half = requests // 2
    scale = float(query_width) ** (-0.5) * log2_e

    core = lax.axis_index("core")
    slot = lax.axis_index(("z", "x", "core", "head"))

    vmem = pl.BlockSpec(memory_space=pltpu.VMEM)
    smem = pl.BlockSpec(memory_space=pltpu.SMEM)
    small = pltpu.CompilerParams(vmem_limit_bytes=12 * 2**20)
    anywhere = pl.BlockSpec(memory_space=pltpu.HBM)
    wide = 640
    in_hbm = functools.partial(pltpu.with_memory_space_constraint, memory_space=pltpu.HBM)
    other_first = ((1 - core) * half).astype(jnp.int32)
    own_queries, sent_queries, new_keys = pl.pallas_call(
        functools.partial(queries_kernel, steps),
        in_specs=[smem] + [anywhere] * 4,
        out_specs=[vmem, vmem, vmem],
        out_shape=(
            jax.ShapeDtypeStruct((requests, steps * heads, wide), bf16),
            jax.ShapeDtypeStruct((half, steps * heads, wide), bf16),
            jax.ShapeDtypeStruct((pairs, key_width), bf16),
        ),
        scratch_shapes=[
            pltpu.SMEM((requests,), jnp.int32),
            pltpu.VMEM((pairs, heads, query_width), bf16),
            pltpu.VMEM(up_keys.shape, bf16),
            pltpu.VMEM(new_latent.shape, bf16),
            pltpu.VMEM((pairs, heads, width), f32),
            pltpu.SemaphoreType.DMA((7,)),
        ],
        compiler_params=pltpu.CompilerParams(vmem_limit_bytes=24 * 2**20),
        name="queries",
    )(
        other_first.reshape(1),
        in_hbm(positions),
        in_hbm(query_heads.reshape(pairs, heads, query_width)),
        in_hbm(up_keys),
        in_hbm(new_latent),
    )

    def over_head(array, k):
        return lax.ppermute(array, "head", [(i, i ^ k) for i in range(owners)])

    swap = [(0, 1), (1, 0)]
    partners = (1, 3, 2)
    got = [over_head(sent_queries, k) for k in partners]
    own_first = (core * half).astype(jnp.int32)
    chunk = half * steps * heads
    at_origin = (lax.axis_index(("z", "x")) == 0).astype(jnp.int32)
    fresh = pl.pallas_call(
        functools.partial(fresh_kernel, scale, steps, heads),
        in_specs=[smem, vmem, vmem],
        out_specs=vmem,
        out_shape=jax.ShapeDtypeStruct((chunk, width + 128), bf16),
        compiler_params=small,
        cost_estimate=pl.CostEstimate(flops=10**9, bytes_accessed=4 * 10**6, transcendentals=0),
        name="fresh",
    )(jnp.stack([own_first, at_origin]), own_queries, new_keys)
    cache = in_hbm(jnp.swapaxes(latent_cache, 1, 2))
    passed = [lax.ppermute(g, "core", swap) for g in got]

    rows = owners * steps * heads

    def attend(first, got):
        info = jnp.concatenate([jnp.stack([first, slot.astype(jnp.int32) * cached]), context_lengths])
        return pl.pallas_call(
            functools.partial(attention_kernel, scale),
            in_specs=[smem] + [vmem] * 4 + [anywhere],
            out_specs=vmem,
            scratch_shapes=[
                pltpu.VMEM((half, owners, steps * heads, wide), bf16),
                pltpu.VMEM((half, key_width, cached), bf16),
                pltpu.SemaphoreType.DMA((half, 4)),
            ]
            + [pltpu.VMEM((rows, cached), f32)] * half,
            out_shape=jax.ShapeDtypeStruct((owners, chunk, width + 128), bf16),
            compiler_params=pltpu.CompilerParams(vmem_limit_bytes=24 * 2**20),
            cost_estimate=pl.CostEstimate(
                flops=2 * half * rows * cached * (key_width + width),
                bytes_accessed=half * cached * key_width * 2,
                transcendentals=half * rows * cached,
            ),
            name="attention",
        )(info, own_queries, *got, cache)

    other_part = lax.ppermute(attend(other_first, got), "core", swap)
    own_part = attend(own_first, passed)
    sent = pl.pallas_call(
        pair_kernel,
        in_specs=[vmem] * 2,
        out_specs=[vmem] * owners,
        out_shape=[jax.ShapeDtypeStruct((chunk, width + 128), bf16)] * owners,
        compiler_params=small,
        name="pair_merge",
    )(other_part, own_part)
    arrived = [over_head(array, k) for array, k in zip(sent[1:], partners)]
    part = pl.pallas_call(
        functools.partial(project_kernel, heads),
        in_specs=[vmem] * 6,
        out_specs=vmem,
        out_shape=jax.ShapeDtypeStruct((chunk + 16, value_width), bf16),
        scratch_shapes=[
            pltpu.VMEM((chunk // heads, heads, width), f32),
            pltpu.VMEM((chunk // heads, heads, value_width), f32),
        ],
        compiler_params=small,
        name="project",
    )(sent[0], *arrived, fresh, up_values)

    def over_plane(array, k):
        return lax.ppermute(array, ("z", "x"), [(i, i ^ k) for i in range(plane)])

    part = pl.pallas_call(
        middle_kernel,
        in_specs=[vmem] * 4,
        out_specs=vmem,
        out_shape=jax.ShapeDtypeStruct(part.shape, bf16),
        compiler_params=small,
        name="middle_merge",
    )(part, *[over_plane(part, k) for k in (1, 4, 5)])
    own = pl.pallas_call(
        finish_kernel,
        in_specs=[vmem] * 4,
        out_specs=vmem,
        out_shape=jax.ShapeDtypeStruct((steps, half, heads, value_width), bf16),
        compiler_params=small,
        name="finish",
    )(part, *[over_plane(part, k) for k in (3, 12, 15)])
    theirs = lax.ppermute(own, "core", swap)
    return pl.pallas_call(
        place_kernel,
        in_specs=[smem, vmem, vmem],
        out_specs=vmem,
        out_shape=jax.ShapeDtypeStruct((steps, requests, heads, value_width), bf16),
        compiler_params=small,
        name="place",
    )(own_first.reshape(1), own, theirs)


def solution(mesh):
    fine = Mesh(mesh.devices.reshape(4, 4, 2, 4), ("z", "x", "core", "head"))
    in_specs = (
        P(None, None, "head", None),
        P("head", None, None),
        P("head", None, None),
        P(None, ("z", "x", "core", "head"), None),
        P(),
        P(),
        P(),
    )
    out_specs = P(None, None, "head", None)
    return jax.shard_map(
        on_device, mesh=fine, in_specs=in_specs, out_specs=out_specs, check_vma=False
    )
```

time: 67.6 us -> 64.2 us (0.950)
  blocking collectives: 18.2 us -> 0 us
  waiting for transfers between devices: 9.67 us -> 22.4 us
  local copies, waits for them, and re-layouts: 11.8 us -> 0.01 us
  starting transfers between devices: 12.7 us -> 23 us
  Pallas kernels: 14.8 us -> 18.5 us
    all_to_all x1 -> x0, blocking collectives: 18.2 us -> none  [on_device(): everyone = lax.all_to_all(projected, ('z', 'x'), 0, 0, tiled=True)]
    unnamed x12 -> x4, local copies, waits for them, and re-layouts: 11 us -> 0.01 us
    ppermute x2 -> x7, starting transfers between devices: 1.74 us -> 10.4 us  [the longest x6 8.92 us: over_plane(): return lax.ppermute(array, ('z', 'x'), [(i, i ^ k) for i in range(plane)])]
    ppermute x2 -> x7, waiting for transfers between devices: 0.01 us -> 6.64 us  [the longest x6 6.63 us: over_plane(): return lax.ppermute(array, ('z', 'x'), [(i, i ^ k) for i in range(plane)])]
    ppermute x6, waiting for transfers between devices: 7.59 us -> 13.1 us  [over_head(): return lax.ppermute(array, 'head', [(i, i ^ k) for i in range(owners)])]
    pallas_call x5 -> x6, Pallas kernels: 9.99 us -> 14.5 us  [the longest x2 11.9 us: attend(): pl.pallas_call(functools.partial(attention_kernel, scale), in_specs=[smem...]
    ppermute x1, starting transfers between devices: 2.14 us -> 3.71 us  [on_device(): theirs = lax.ppermute(own, 'core', swap)]
    pallas_call x1, Pallas kernels: 2.78 us -> 2.02 us  [on_device(): pl.pallas_call(functools.partial(queries_kernel, steps), in_specs=[smem]...]
  transfers between devices with their start and end apart: 12 -> 17, of which waited for: 7 -> 13; matrix products, arithmetic and copies ran while one was open for 1% -> 0% of each run, Pallas kernels for 7% -> 11%
where the time goes in v4:
time: 64.2 us; the launch traced here: 64.1 us
  starting transfers between devices  23 us (36%)
  waiting for transfers between devices  22.4 us (35%)
  Pallas kernels  18.5 us (29%)
    ppermute x6, waiting for transfers between devices, over_head(): return lax.ppermute(array, 'head', [(i, i ^ k) for i in range(owners)])  13.1 us
    pallas_call x2, Pallas kernels, attend(): pl.pallas_call(functools.partial(attention_kernel, scale), in_specs=[smem...  11.9 us
    ppermute x6, starting transfers between devices, over_plane(): return lax.ppermute(array, ('z', 'x'), [(i, i ^ k) for i in range(plane)])  8.92 us
    ppermute x6, starting transfers between devices, over_head(): return lax.ppermute(array, 'head', [(i, i ^ k) for i in range(owners)])  8.24 us
    ppermute x6, waiting for transfers between devices, over_plane(): return lax.ppermute(array, ('z', 'x'), [(i, i ^ k) for i in range(plane)])  6.63 us
    ppermute x1, starting transfers between devices, on_device(): theirs = lax.ppermute(own, 'core', swap)  3.71 us
    pallas_call x1, Pallas kernels, on_device(): pl.pallas_call(functools.partial(queries_kernel, steps), in_specs=[smem]...  2.02 us
    ppermute x3, waiting for transfers between devices, on_device(): passed = [lax.ppermute(g, 'core', swap) for g in got]  1.82 us
  transfers between devices with their start and end apart: 17, of which 13 were waited for; matrix products, arithmetic and copies ran while one was open for 0% of the time, Pallas kernels for 11%

profile of v4, /device:TPU:1, one launch (start us, length us, event | category | flops | bytes accessed | tf_op | source)
XLA Modules:
  0.0 64.1 jit_solution(564290231309175866)
XLA Ops:
  0.0 2.0 %queries.1 = (bf16[4,64,640]{2,1,0:T(8,128)(2,1)S(1)}, bf16[2,64,640]{2,1,0:T(8,128)(2,1)S(1)}, bf16[16,576]{1,0:T(8,128)(2,1)S(1)}) custom-call(s32[1]{0:T(128)} %bitcast.1.info_ref, s32[4]{0:T(128)} %positions_hbm.1, bf16[16,16,192]{2,1,0:T(8,128)(2,1)} %bitcast.8, bf16[16,128,512]{2,1,0:T(8,128)(2,1)} %up_hbm.1, bf16[4,4,576]{2,1,0:T(4,128)(2,1)} %new_hbm.1), custom_call_target="tpu_custom_call" | custom-call | tf_op jit(solution)/shard_map/queries/pallas_call | solution.py:311
  2.0 3.8 %collective-permute-start.2 = (bf16[2,64,640]{2,1,0:T(8,128)(2,1)S(1)}, bf16[2,64,640]{2,1,0:T(8,128)(2,1)S(1)}, u32[]{:S(2)}, u32[]{:S(2)}) collective-permute-start(bf16[2,64,640]{2,1,0:T(8,128)(2,1)S(1)} %get-tuple-element.13), channel_id=1, source_target_pairs={{0,2},{1,3},{2,0},{3,1},{4,6},{5,7},{6,4},{7,5},{8,10},{9,11},{10,... | collective-permute-start | bytes 491528 | tf_op jit(solution)/shard_map/ppermute | solution.py:339
  6.7 2.8 %collective-permute-done.2.q3_ref = bf16[2,64,640]{2,1,0:T(8,128)(2,1)S(1)} collective-permute-done((bf16[2,64,640]{2,1,0:T(8,128)(2,1)S(1)}, bf16[2,64,640]{2,1,0:T(8,128)(2,1)S(1)}, u32[]{:S(2)}, u32[]{:S(2)}) %collective-permute-start.2) | collective-permute-done | bytes 163872 | tf_op jit(solution)/shard_map/ppermute | solution.py:339
  9.5 4.0 %collective-permute-done.1.q2_ref = bf16[2,64,640]{2,1,0:T(8,128)(2,1)S(1)} collective-permute-done((bf16[2,64,640]{2,1,0:T(8,128)(2,1)S(1)}, bf16[2,64,640]{2,1,0:T(8,128)(2,1)S(1)}, u32[]{:S(2)}, u32[]{:S(2)}) %collective-permute-start.1) | collective-permute-done | bytes 163872 | tf_op jit(solution)/shard_map/ppermute | solution.py:339
  13.5 5.9 %attention.2 = bf16[4,128,640]{2,1,0:T(8,128)(2,1)S(1)} custom-call(s32[6]{0:T(128)S(1)} %get-tuple-element.20.info_ref, bf16[4,64,640]{2,1,0:T(8,128)(2,1)S(1)} %get-tuple-element.12.own_ref, bf16[2,64,640]{2,1,0:T(8,128)(2,1)S(1)} %collective-permute-done.q1_ref, bf16[2,64,640]{2,1,0:T(8,128)(2,1)S(1)} %collective-permute-done.1.q2_ref, ...), custom_call_target="tpu_custom_call" | custom-call | flops 2281701376 | bytes 4718592 | tf_op jit(solution)/shard_map/attention/pallas_call | solution.py:363
  19.5 1.5 %collective-permute-start.3 = (bf16[4,128,640]{2,1,0:T(8,128)(2,1)S(1)}, bf16[4,128,640]{2,1,0:T(8,128)(2,1)S(1)}, u32[]{:S(2)}, u32[]{:S(2)}) collective-permute-start(bf16[4,128,640]{2,1,0:T(8,128)(2,1)S(1)} %attention.2), channel_id=1, source_target_pairs={{0,4},{4,0},{1,5},{5,1},{2,6},{6,2},{3,7},{7,3},{8,12},{12,8},{9,1... | collective-permute-start | bytes 1966088 | tf_op jit(solution)/shard_map/ppermute | solution.py:383
  21.6 1.4 %collective-permute-done.6.q3_ref = bf16[2,64,640]{2,1,0:T(8,128)(2,1)S(1)} collective-permute-done((bf16[2,64,640]{2,1,0:T(8,128)(2,1)S(1)}, bf16[2,64,640]{2,1,0:T(8,128)(2,1)S(1)}, u32[]{:S(2)}, u32[]{:S(2)}) %collective-permute-start.6) | collective-permute-done | bytes 163872 | tf_op jit(solution)/shard_map/ppermute | solution.py:357
  23.4 5.9 %attention.3.b_ref = bf16[4,128,640]{2,1,0:T(8,128)(2,1)S(1)} custom-call(s32[6]{0:T(128)S(1)} %get-tuple-element.19.info_ref, bf16[4,64,640]{2,1,0:T(8,128)(2,1)S(1)} %get-tuple-element.12.own_ref, bf16[2,64,640]{2,1,0:T(8,128)(2,1)S(1)} %collective-permute-done.4.q1_ref, bf16[2,64,640]{2,1,0:T(8,128)(2,1)S(1)} %collective-permute-done.5.q2_ref, ...), custom_call_target="tpu_custom_call" | custom-call | flops 2281701376 | bytes 4718592 | tf_op jit(solution)/shard_map/attention/pallas_call | solution.py:363
  29.4 0.9 %pair_merge.1 = (bf16[128,640]{1,0:T(8,128)(2,1)S(1)}, bf16[128,640]{1,0:T(8,128)(2,1)S(1)}, bf16[128,640]{1,0:T(8,128)(2,1)S(1)}, bf16[128,640]{1,0:T(8,128)(2,1)S(1)}) custom-call(bf16[4,128,640]{2,1,0:T(8,128)(2,1)S(1)} %collective-permute-done.3.a_ref, bf16[4,128,640]{2,1,0:T(8,128)(2,1)S(1)} %attention.3.b_ref), custom_call_target="tpu_custom_call" | custom-call | tf_op jit(solution)/shard_map/pair_merge/pallas_call | solution.py:385
  30.3 1.2 %collective-permute-start.7 = (bf16[128,640]{1,0:T(8,128)(2,1)S(1)}, bf16[128,640]{1,0:T(8,128)(2,1)S(1)}, u32[]{:S(2)}, u32[]{:S(2)}) collective-permute-start(bf16[128,640]{1,0:T(8,128)(2,1)S(1)} %get-tuple-element.15), channel_id=1, source_target_pairs={{0,1},{1,0},{2,3},{3,2},{4,5},{5,4},{6,7},{7,6},{8,9},{9,8},{10,11... | collective-permute-start | bytes 491528 | tf_op jit(solution)/shard_map/ppermute | solution.py:339
  31.4 1.4 %collective-permute-start.8 = (bf16[128,640]{1,0:T(8,128)(2,1)S(1)}, bf16[128,640]{1,0:T(8,128)(2,1)S(1)}, u32[]{:S(2)}, u32[]{:S(2)}) collective-permute-start(bf16[128,640]{1,0:T(8,128)(2,1)S(1)} %get-tuple-element.16), channel_id=1, source_target_pairs={{0,3},{1,2},{2,1},{3,0},{4,7},{5,6},{6,5},{7,4},{8,11},{9,10},{10,... | collective-permute-start | bytes 491528 | tf_op jit(solution)/shard_map/ppermute | solution.py:339
  32.8 1.1 %collective-permute-start.9 = (bf16[128,640]{1,0:T(8,128)(2,1)S(1)}, bf16[128,640]{1,0:T(8,128)(2,1)S(1)}, u32[]{:S(2)}, u32[]{:S(2)}) collective-permute-start(bf16[128,640]{1,0:T(8,128)(2,1)S(1)} %get-tuple-element.17), channel_id=1, source_target_pairs={{0,2},{1,3},{2,0},{3,1},{4,6},{5,7},{6,4},{7,5},{8,10},{9,11},{10,... | collective-permute-start | bytes 491528 | tf_op jit(solution)/shard_map/ppermute | solution.py:339
  34.0 1.1 %fresh.1.refs_4_ = bf16[128,640]{1,0:T(8,128)(2,1)S(1)} custom-call(s32[2]{0:T(128)S(1)} %pad_add_fusion.info_ref, bf16[4,64,640]{2,1,0:T(8,128)(2,1)S(1)} %get-tuple-element.12.own_ref, bf16[16,576]{1,0:T(8,128)(2,1)S(1)} %get-tuple-element.18.new_ref), custom_call_target="tpu_custom_call" | custom-call | flops 1000000000 | bytes 4000000 | tf_op jit(solution)/shard_map/fresh/pallas_call | solution.py:347
  35.7 3.6 %collective-permute-done.8.refs_2_ = bf16[128,640]{1,0:T(8,128)(2,1)S(1)} collective-permute-done((bf16[128,640]{1,0:T(8,128)(2,1)S(1)}, bf16[128,640]{1,0:T(8,128)(2,1)S(1)}, u32[]{:S(2)}, u32[]{:S(2)}) %collective-permute-start.8) | collective-permute-done | bytes 163872 | tf_op jit(solution)/shard_map/ppermute | solution.py:339
  39.4 2.0 %collective-permute-done.9.refs_3_ = bf16[128,640]{1,0:T(8,128)(2,1)S(1)} collective-permute-done((bf16[128,640]{1,0:T(8,128)(2,1)S(1)}, bf16[128,640]{1,0:T(8,128)(2,1)S(1)}, u32[]{:S(2)}, u32[]{:S(2)}) %collective-permute-start.9) | collective-permute-done | bytes 163872 | tf_op jit(solution)/shard_map/ppermute | solution.py:339
  41.4 1.4 %project.1.refs_0_ = bf16[144,128]{1,0:T(8,128)(2,1)S(1)} custom-call(bf16[128,640]{1,0:T(8,128)(2,1)S(1)} %get-tuple-element.14.refs_0_, bf16[128,640]{1,0:T(8,128)(2,1)S(1)} %collective-permute-done.7.refs_1_, bf16[128,640]{1,0:T(8,128)(2,1)S(1)} %collective-permute-done.8.refs_2_, bf16[128,640]{1,0:T(8,128)(2,1)S(1)} %collective-permute-done.9.refs_3_, ...), custom_call_target="tpu_custom_call" | custom-call | tf_op jit(solution)/shard_map/project/pallas_call | solution.py:394
  42.8 2.6 %collective-permute-start.12 = (bf16[144,128]{1,0:T(8,128)(2,1)S(1)}, bf16[144,128]{1,0:T(8,128)(2,1)S(1)}, u32[]{:S(2)}, u32[]{:S(2)}) collective-permute-start(bf16[144,128]{1,0:T(8,128)(2,1)S(1)} %project.1.refs_0_), channel_id=1, source_target_pairs={{0,40},{8,32},{16,56},{24,48},{32,8},{40,0},{48,24},{56,16},{64,10... | collective-permute-start | bytes 110600 | tf_op jit(solution)/shard_map/ppermute | solution.py:408
  45.8 1.0 %collective-permute-done.12.refs_3_ = bf16[144,128]{1,0:T(8,128)(2,1)S(1)} collective-permute-done((bf16[144,128]{1,0:T(8,128)(2,1)S(1)}, bf16[144,128]{1,0:T(8,128)(2,1)S(1)}, u32[]{:S(2)}, u32[]{:S(2)}) %collective-permute-start.12) | collective-permute-done | bytes 36896 | tf_op jit(solution)/shard_map/ppermute | solution.py:408
  46.8 1.9 %collective-permute-done.11.refs_2_ = bf16[144,128]{1,0:T(8,128)(2,1)S(1)} collective-permute-done((bf16[144,128]{1,0:T(8,128)(2,1)S(1)}, bf16[144,128]{1,0:T(8,128)(2,1)S(1)}, u32[]{:S(2)}, u32[]{:S(2)}) %collective-permute-start.11) | collective-permute-done | bytes 36896 | tf_op jit(solution)/shard_map/ppermute | solution.py:408
  49.0 5.1 %collective-permute-start.15 = (bf16[144,128]{1,0:T(8,128)(2,1)S(1)}, bf16[144,128]{1,0:T(8,128)(2,1)S(1)}, u32[]{:S(2)}, u32[]{:S(2)}) collective-permute-start(bf16[144,128]{1,0:T(8,128)(2,1)S(1)} %middle_merge.1.refs_0_), channel_id=1, source_target_pairs={{0,120},{8,112},{16,104},{24,96},{32,88},{40,80},{48,72},{56,64},{... | collective-permute-start | bytes 110600 | tf_op jit(solution)/shard_map/ppermute | solution.py:408
  54.0 0.8 %collective-permute-start.13 = (bf16[144,128]{1,0:T(8,128)(2,1)S(1)}, bf16[144,128]{1,0:T(8,128)(2,1)S(1)}, u32[]{:S(2)}, u32[]{:S(2)}) collective-permute-start(bf16[144,128]{1,0:T(8,128)(2,1)S(1)} %middle_merge.1.refs_0_), channel_id=1, source_target_pairs={{0,24},{8,16},{16,8},{24,0},{32,56},{40,48},{48,40},{56,32},{64,88... | collective-permute-start | bytes 110600 | tf_op jit(solution)/shard_map/ppermute | solution.py:408
  55.4 3.2 %collective-permute-done.14.refs_2_ = bf16[144,128]{1,0:T(8,128)(2,1)S(1)} collective-permute-done((bf16[144,128]{1,0:T(8,128)(2,1)S(1)}, bf16[144,128]{1,0:T(8,128)(2,1)S(1)}, u32[]{:S(2)}, u32[]{:S(2)}) %collective-permute-start.14) | collective-permute-done | bytes 36896 | tf_op jit(solution)/shard_map/ppermute | solution.py:408
  58.9 3.7 %collective-permute-start.16 = (bf16[4,2,16,128]{3,2,1,0:T(8,128)(2,1)S(1)}, bf16[4,2,16,128]{3,2,1,0:T(8,128)(2,1)S(1)}, u32[]{:S(2)}, u32[]{:S(2)}) collective-permute-start(bf16[4,2,16,128]{3,2,1,0:T(8,128)(2,1)S(1)} %finish.1.own_ref), channel_id=1, source_target_pairs={{0,4},{4,0},{1,5},{5,1},{2,6},{6,2},{3,7},{7,3},{8,12},{12,8},{9,1... | collective-permute-start | bytes 98312 | tf_op jit(solution)/shard_map/ppermute | solution.py:426
  62.6 0.9 %collective-permute-done.16.other_ref = bf16[4,2,16,128]{3,2,1,0:T(8,128)(2,1)S(1)} collective-permute-done((bf16[4,2,16,128]{3,2,1,0:T(8,128)(2,1)S(1)}, bf16[4,2,16,128]{3,2,1,0:T(8,128)(2,1)S(1)}, u32[]{:S(2)}, u32[]{:S(2)}) %collective-permute-start.16) | collective-permute-done | bytes 32800 | tf_op jit(solution)/shard_map/ppermute | solution.py:426
  (25 shorter events, 4.7 us)
Async XLA Ops:
  0.0 6.6 %copy-start.1 = (s32[4]{0:T(128)S(1)}, s32[4]{0:T(128)}, u32[]{:S(2)}) copy-start(s32[4]{0:T(128)} %param.12) | copy-start | bytes 52
  2.0 7.5 %collective-permute-start.2 = (bf16[2,64,640]{2,1,0:T(8,128)(2,1)S(1)}, bf16[2,64,640]{2,1,0:T(8,128)(2,1)S(1)}, u32[]{:S(2)}, u32[]{:S(2)}) collective-permute-start(bf16[2,64,640]{2,1,0:T(8,128)(2,1)S(1)} %get-tuple-element.13), channel_id=1, source_target_pairs={{0,2},{1,3},{2,0},{3,1},{4,6},{5,7},{6,4},{7,5},{8,10},{9,11},{10,... | collective-permute-start | bytes 491528 | tf_op jit(solution)/shard_map/ppermute | solution.py:339
  5.9 7.6 %collective-permute-start.1 = (bf16[2,64,640]{2,1,0:T(8,128)(2,1)S(1)}, bf16[2,64,640]{2,1,0:T(8,128)(2,1)S(1)}, u32[]{:S(2)}, u32[]{:S(2)}) collective-permute-start(bf16[2,64,640]{2,1,0:T(8,128)(2,1)S(1)} %get-tuple-element.13), channel_id=1, source_target_pairs={{0,3},{1,2},{2,1},{3,0},{4,7},{5,6},{6,5},{7,4},{8,11},{9,10},{10,... | collective-permute-start | bytes 491528 | tf_op jit(solution)/shard_map/ppermute | solution.py:339
  6.6 6.9 %collective-permute-start = (bf16[2,64,640]{2,1,0:T(8,128)(2,1)S(1)}, bf16[2,64,640]{2,1,0:T(8,128)(2,1)S(1)}, u32[]{:S(2)}, u32[]{:S(2)}) collective-permute-start(bf16[2,64,640]{2,1,0:T(8,128)(2,1)S(1)} %get-tuple-element.13), channel_id=1, source_target_pairs={{0,1},{1,0},{2,3},{3,2},{4,5},{5,4},{6,7},{7,6},{8,9},{9,8},{10,11... | collective-permute-start | bytes 491528 | tf_op jit(solution)/shard_map/ppermute | solution.py:339
  19.5 9.9 %collective-permute-start.3 = (bf16[4,128,640]{2,1,0:T(8,128)(2,1)S(1)}, bf16[4,128,640]{2,1,0:T(8,128)(2,1)S(1)}, u32[]{:S(2)}, u32[]{:S(2)}) collective-permute-start(bf16[4,128,640]{2,1,0:T(8,128)(2,1)S(1)} %attention.2), channel_id=1, source_target_pairs={{0,4},{4,0},{1,5},{5,1},{2,6},{6,2},{3,7},{7,3},{8,12},{12,8},{9,1... | collective-permute-start | bytes 1966088 | tf_op jit(solution)/shard_map/ppermute | solution.py:383
  21.0 2.0 %collective-permute-start.6 = (bf16[2,64,640]{2,1,0:T(8,128)(2,1)S(1)}, bf16[2,64,640]{2,1,0:T(8,128)(2,1)S(1)}, u32[]{:S(2)}, u32[]{:S(2)}) collective-permute-start(bf16[2,64,640]{2,1,0:T(8,128)(2,1)S(1)} %collective-permute-done.2.q3_ref), channel_id=1, source_target_pairs={{0,4},{4,0},{1,5},{5,1},{2,6},{6,2},{3,7},{7,3},{8,12},{12,8},{9,1... | collective-permute-start | bytes 491528 | tf_op jit(solution)/shard_map/ppermute | solution.py:357
  21.1 2.1 %collective-permute-start.5 = (bf16[2,64,640]{2,1,0:T(8,128)(2,1)S(1)}, bf16[2,64,640]{2,1,0:T(8,128)(2,1)S(1)}, u32[]{:S(2)}, u32[]{:S(2)}) collective-permute-start(bf16[2,64,640]{2,1,0:T(8,128)(2,1)S(1)} %collective-permute-done.1.q2_ref), channel_id=1, source_target_pairs={{0,4},{4,0},{1,5},{5,1},{2,6},{6,2},{3,7},{7,3},{8,12},{12,8},{9,1... | collective-permute-start | bytes 491528 | tf_op jit(solution)/shard_map/ppermute | solution.py:357
  21.5 1.9 %collective-permute-start.4 = (bf16[2,64,640]{2,1,0:T(8,128)(2,1)S(1)}, bf16[2,64,640]{2,1,0:T(8,128)(2,1)S(1)}, u32[]{:S(2)}, u32[]{:S(2)}) collective-permute-start(bf16[2,64,640]{2,1,0:T(8,128)(2,1)S(1)} %collective-permute-done.q1_ref), channel_id=1, source_target_pairs={{0,4},{4,0},{1,5},{5,1},{2,6},{6,2},{3,7},{7,3},{8,12},{12,8},{9,1... | collective-permute-start | bytes 491528 | tf_op jit(solution)/shard_map/ppermute | solution.py:357
  30.2 11.2 %copy-start = (bf16[16,512,128]{2,1,0:T(8,128)(2,1)S(1)}, bf16[16,512,128]{2,1,0:T(8,128)(2,1)}, u32[]{:S(2)}) copy-start(bf16[16,512,128]{2,1,0:T(8,128)(2,1)} %refs_5_.1) | copy-start | bytes 6291460
  30.3 5.5 %collective-permute-start.7 = (bf16[128,640]{1,0:T(8,128)(2,1)S(1)}, bf16[128,640]{1,0:T(8,128)(2,1)S(1)}, u32[]{:S(2)}, u32[]{:S(2)}) collective-permute-start(bf16[128,640]{1,0:T(8,128)(2,1)S(1)} %get-tuple-element.15), channel_id=1, source_target_pairs={{0,1},{1,0},{2,3},{3,2},{4,5},{5,4},{6,7},{7,6},{8,9},{9,8},{10,11... | collective-permute-start | bytes 491528 | tf_op jit(solution)/shard_map/ppermute | solution.py:339
  31.4 8.0 %collective-permute-start.8 = (bf16[128,640]{1,0:T(8,128)(2,1)S(1)}, bf16[128,640]{1,0:T(8,128)(2,1)S(1)}, u32[]{:S(2)}, u32[]{:S(2)}) collective-permute-start(bf16[128,640]{1,0:T(8,128)(2,1)S(1)} %get-tuple-element.16), channel_id=1, source_target_pairs={{0,3},{1,2},{2,1},{3,0},{4,7},{5,6},{6,5},{7,4},{8,11},{9,10},{10,... | collective-permute-start | bytes 491528 | tf_op jit(solution)/shard_map/ppermute | solution.py:339
  32.8 8.6 %collective-permute-start.9 = (bf16[128,640]{1,0:T(8,128)(2,1)S(1)}, bf16[128,640]{1,0:T(8,128)(2,1)S(1)}, u32[]{:S(2)}, u32[]{:S(2)}) collective-permute-start(bf16[128,640]{1,0:T(8,128)(2,1)S(1)} %get-tuple-element.17), channel_id=1, source_target_pairs={{0,2},{1,3},{2,0},{3,1},{4,6},{5,7},{6,4},{7,5},{8,10},{9,11},{10,... | collective-permute-start | bytes 491528 | tf_op jit(solution)/shard_map/ppermute | solution.py:339
  42.8 4.0 %collective-permute-start.12 = (bf16[144,128]{1,0:T(8,128)(2,1)S(1)}, bf16[144,128]{1,0:T(8,128)(2,1)S(1)}, u32[]{:S(2)}, u32[]{:S(2)}) collective-permute-start(bf16[144,128]{1,0:T(8,128)(2,1)S(1)} %project.1.refs_0_), channel_id=1, source_target_pairs={{0,40},{8,32},{16,56},{24,48},{32,8},{40,0},{48,24},{56,16},{64,10... | collective-permute-start | bytes 110600 | tf_op jit(solution)/shard_map/ppermute | solution.py:408
  45.4 3.3 %collective-permute-start.11 = (bf16[144,128]{1,0:T(8,128)(2,1)S(1)}, bf16[144,128]{1,0:T(8,128)(2,1)S(1)}, u32[]{:S(2)}, u32[]{:S(2)}) collective-permute-start(bf16[144,128]{1,0:T(8,128)(2,1)S(1)} %project.1.refs_0_), channel_id=1, source_target_pairs={{0,32},{8,40},{16,48},{24,56},{32,0},{40,8},{48,16},{56,24},{64,96... | collective-permute-start | bytes 110600 | tf_op jit(solution)/shard_map/ppermute | solution.py:408
  45.4 3.3 %collective-permute-start.10 = (bf16[144,128]{1,0:T(8,128)(2,1)S(1)}, bf16[144,128]{1,0:T(8,128)(2,1)S(1)}, u32[]{:S(2)}, u32[]{:S(2)}) collective-permute-start(bf16[144,128]{1,0:T(8,128)(2,1)S(1)} %project.1.refs_0_), channel_id=1, source_target_pairs={{0,8},{8,0},{16,24},{24,16},{32,40},{40,32},{48,56},{56,48},{64,72... | collective-permute-start | bytes 110600 | tf_op jit(solution)/shard_map/ppermute | solution.py:408
  49.0 6.4 %collective-permute-start.15 = (bf16[144,128]{1,0:T(8,128)(2,1)S(1)}, bf16[144,128]{1,0:T(8,128)(2,1)S(1)}, u32[]{:S(2)}, u32[]{:S(2)}) collective-permute-start(bf16[144,128]{1,0:T(8,128)(2,1)S(1)} %middle_merge.1.refs_0_), channel_id=1, source_target_pairs={{0,120},{8,112},{16,104},{24,96},{32,88},{40,80},{48,72},{56,64},{... | collective-permute-start | bytes 110600 | tf_op jit(solution)/shard_map/ppermute | solution.py:408
  54.0 4.6 %collective-permute-start.14 = (bf16[144,128]{1,0:T(8,128)(2,1)S(1)}, bf16[144,128]{1,0:T(8,128)(2,1)S(1)}, u32[]{:S(2)}, u32[]{:S(2)}) collective-permute-start(bf16[144,128]{1,0:T(8,128)(2,1)S(1)} %middle_merge.1.refs_0_), channel_id=1, source_target_pairs={{0,96},{8,104},{16,112},{24,120},{32,64},{40,72},{48,80},{56,88},{... | collective-permute-start | bytes 110600 | tf_op jit(solution)/shard_map/ppermute | solution.py:408
  54.0 4.6 %collective-permute-start.13 = (bf16[144,128]{1,0:T(8,128)(2,1)S(1)}, bf16[144,128]{1,0:T(8,128)(2,1)S(1)}, u32[]{:S(2)}, u32[]{:S(2)}) collective-permute-start(bf16[144,128]{1,0:T(8,128)(2,1)S(1)} %middle_merge.1.refs_0_), channel_id=1, source_target_pairs={{0,24},{8,16},{16,8},{24,0},{32,56},{40,48},{48,40},{56,32},{64,88... | collective-permute-start | bytes 110600 | tf_op jit(solution)/shard_map/ppermute | solution.py:408
  58.9 4.6 %collective-permute-start.16 = (bf16[4,2,16,128]{3,2,1,0:T(8,128)(2,1)S(1)}, bf16[4,2,16,128]{3,2,1,0:T(8,128)(2,1)S(1)}, u32[]{:S(2)}, u32[]{:S(2)}) collective-permute-start(bf16[4,2,16,128]{3,2,1,0:T(8,128)(2,1)S(1)} %finish.1.own_ref), channel_id=1, source_target_pairs={{0,4},{4,0},{1,5},{5,1},{2,6},{6,2},{3,7},{7,3},{8,12},{12,8},{9,1... | collective-permute-start | bytes 98312 | tf_op jit(solution)/shard_map/ppermute | solution.py:426

commit v5 on v4

--- a/solution.py
+++ b/solution.py
@@ -96,27 +96,23 @@
     return jnp.where(lane == 4, sum_second, out)
 
 
-def attention_kernel(
-    scale, info_ref, own_ref, q1_ref, q2_ref, q3_ref, cache_hbm, out_ref, q_ref, k_ref, sems, *scores
-):
+def stage_kernel(cache_hbm, out_ref, sems):
+    copies = []
+    for i in range(out_ref.shape[0]):
+        copies.append(pltpu.make_async_copy(cache_hbm.at[i], out_ref.at[i], sems.at[i]))
+    for copy in copies:
+        copy.start()
+    for copy in copies:
+        copy.wait()
+
+
+def attention_kernel(scale, info_ref, own_ref, q1_ref, q2_ref, q3_ref, k_ref, out_ref, q_ref, *scores):
     count, owners, share, _ = q_ref.shape
     rows = owners * share
     key_width, cached = k_ref.shape[1:]
     width = out_ref.shape[2] - 128
-    pieces = sems.shape[1]
-    piece = cached // pieces
     chunk = 1024
     first = info_ref[0]
-    fetches = []
-    for i in range(count):
-        for p in range(pieces):
-            at = pl.ds(p * piece, piece)
-            fetches.append(
-                pltpu.make_async_copy(cache_hbm.at[first + i, :, at], k_ref.at[i, :, at], sems.at[i, p])
-            )
-    for fetch in fetches:
-        fetch.start()
-
     q_ref[:, 0] = own_ref[pl.ds(first, count)]
     q_ref[:, 1] = q1_ref[...]
     q_ref[:, 2] = q2_ref[...]
@@ -127,15 +123,13 @@
         limit = info_ref[2 + first + i] - info_ref[1]
         queries = q_ref[i].reshape(rows, -1)[:, :key_width]
         top = jnp.full((rows, 128), lowest_max, f32)
-        step = piece if i == 0 else cached
-        for c in range(0, cached, step):
-            for p in range(c // piece, (c + step) // piece):
-                fetches[i * pieces + p].wait()
-            part = jnp.dot(queries, k_ref[i, :, c : c + step], preferred_element_type=f32) * scale
-            column = lax.broadcasted_iota(jnp.int32, (1, step), 1) + c
+        for c in range(0, cached, chunk):
+            keys = k_ref[first + i, :, c : c + chunk]
+            part = jnp.dot(queries, keys, preferred_element_type=f32) * scale
+            column = lax.broadcasted_iota(jnp.int32, (1, chunk), 1) + c
             part = jnp.where(column < limit, part, masked_score)
-            scores[i][:, c : c + step] = part
-            for at in range(0, step, 128):
+            scores[i][:, c : c + chunk] = part
+            for at in range(0, chunk, 128):
                 top = jnp.maximum(top, part[:, at : at + 128])
         tops.append(jnp.max(top, axis=1, keepdims=True))
 
@@ -147,7 +141,7 @@
                 total = total + weights[:, at : at + 128]
             part = lax.dot_general(
                 weights.astype(bf16),
-                k_ref[i, :width, c : c + chunk],
+                k_ref[first + i, :width, c : c + chunk],
                 (((1,), (1,)), ((), ())),
                 preferred_element_type=f32,
             )
@@ -353,8 +347,20 @@
         cost_estimate=pl.CostEstimate(flops=10**9, bytes_accessed=4 * 10**6, transcendentals=0),
         name="fresh",
     )(jnp.stack([own_first, at_origin]), own_queries, new_keys)
-    cache = in_hbm(jnp.swapaxes(latent_cache, 1, 2))
+    cache = pl.pallas_call(
+        stage_kernel,
+        in_specs=[anywhere],
+        out_specs=vmem,
+        out_shape=pltpu.VMEM((requests, key_width, cached), bf16),
+        scratch_shapes=[pltpu.SemaphoreType.DMA((requests,))],
+        compiler_params=small,
+        cost_estimate=pl.CostEstimate(flops=0, bytes_accessed=2 * requests * key_width * cached, transcendentals=0),
+        name="stage",
+    )(in_hbm(jnp.swapaxes(latent_cache, 1, 2)))
+    cache = pltpu.with_memory_space_constraint(cache, memory_space=pltpu.VMEM)
+    got[2], cache = lax.optimization_barrier((got[2], cache))
     passed = [lax.ppermute(g, "core", swap) for g in got]
+    got, passed = lax.optimization_barrier((got, passed))
 
     rows = owners * steps * heads
 
@@ -362,12 +368,10 @@
         info = jnp.concatenate([jnp.stack([first, slot.astype(jnp.int32) * cached]), context_lengths])
         return pl.pallas_call(
             functools.partial(attention_kernel, scale),
-            in_specs=[smem] + [vmem] * 4 + [anywhere],
+            in_specs=[smem] + [vmem] * 5,
             out_specs=vmem,
             scratch_shapes=[
                 pltpu.VMEM((half, owners, steps * heads, wide), bf16),
-                pltpu.VMEM((half, key_width, cached), bf16),
-                pltpu.SemaphoreType.DMA((half, 4)),
             ]
             + [pltpu.VMEM((rows, cached), f32)] * half,
             out_shape=jax.ShapeDtypeStruct((owners, chunk, width + 128), bf16),

time: 64.2 us -> 72.4 us (1.13)
  local copies, waits for them, and re-layouts: 0.01 us -> 12.6 us
  waiting for transfers between devices: 22.4 us -> 17.3 us
    unnamed x4 -> x14, local copies, waits for them, and re-layouts: 0.01 us -> 12.6 us
    ppermute x6, waiting for transfers between devices: 13.1 us -> 6.4 us  [over_head(): return lax.ppermute(array, 'head', [(i, i ^ k) for i in range(owners)])]
    pallas_call x0 -> x1, Pallas kernels: none -> 3.81 us  [on_device(): pl.pallas_call(stage_kernel, in_specs=[anywhere], out_specs=vmem, out_sha...]
    pallas_call x2, Pallas kernels: 11.9 us -> 8.67 us  [attend(): pl.pallas_call(functools.partial(attention_kernel, scale), in_specs=[smem...]
    ppermute x6, waiting for transfers between devices: 6.63 us -> 9.05 us  [over_plane(): return lax.ppermute(array, ('z', 'x'), [(i, i ^ k) for i in range(plane)])]
    ppermute x1, starting transfers between devices: 1.51 us -> 0.28 us  [on_device(): other_part = lax.ppermute(attend(other_first, got), 'core', swap)]
    ppermute x3, starting transfers between devices: 0.6 us -> 1.75 us  [on_device(): passed = [lax.ppermute(g, 'core', swap) for g in got]]
    ppermute x6, starting transfers between devices: 8.92 us -> 8.08 us  [over_plane(): return lax.ppermute(array, ('z', 'x'), [(i, i ^ k) for i in range(plane)])]
  transfers between devices with their start and end apart: 17 -> 17, of which waited for: 13 -> 11; matrix products, arithmetic and copies ran while one was open for 0% -> 0% of each run, Pallas kernels for 11% -> 12%
where the time goes in v5:
time: 72.4 us; the launch traced here: 72.2 us
  starting transfers between devices  22.9 us (32%)
  Pallas kernels  19.1 us (26%)
  waiting for transfers between devices  17.3 us (24%)
  local copies, waits for them, and re-layouts  12.6 us (17%)
    unnamed x14, local copies, waits for them, and re-layouts  12.6 us
    ppermute x6, waiting for transfers between devices, over_plane(): return lax.ppermute(array, ('z', 'x'), [(i, i ^ k) for i in range(plane)])  9.05 us
    pallas_call x2, Pallas kernels, attend(): pl.pallas_call(functools.partial(attention_kernel, scale), in_specs=[smem...  8.67 us
    ppermute x6, starting transfers between devices, over_head(): return lax.ppermute(array, 'head', [(i, i ^ k) for i in range(owners)])  8.44 us
    ppermute x6, starting transfers between devices, over_plane(): return lax.ppermute(array, ('z', 'x'), [(i, i ^ k) for i in range(plane)])  8.08 us
    ppermute x6, waiting for transfers between devices, over_head(): return lax.ppermute(array, 'head', [(i, i ^ k) for i in range(owners)])  6.4 us
    ppermute x1, starting transfers between devices, on_device(): theirs = lax.ppermute(own, 'core', swap)  4.37 us
    pallas_call x1, Pallas kernels, on_device(): pl.pallas_call(stage_kernel, in_specs=[anywhere], out_specs=vmem, out_sha...  3.81 us
  transfers between devices with their start and end apart: 17, of which 11 were waited for; matrix products, arithmetic and copies ran while one was open for 0% of the time, Pallas kernels for 12%

profile of v5, /device:TPU:1, one launch (start us, length us, event | category | flops | bytes accessed | tf_op | source)
XLA Modules:
  0.0 72.2 jit_solution(13697145091921905572)
XLA Ops:
  0.0 2.0 %queries.1 = (bf16[4,64,640]{2,1,0:T(8,128)(2,1)S(1)}, bf16[2,64,640]{2,1,0:T(8,128)(2,1)S(1)}, bf16[16,576]{1,0:T(8,128)(2,1)S(1)}) custom-call(s32[1]{0:T(128)} %bitcast.1.info_ref, s32[4]{0:T(128)} %positions_hbm.1, bf16[16,16,192]{2,1,0:T(8,128)(2,1)} %bitcast.7, bf16[16,128,512]{2,1,0:T(8,128)(2,1)} %up_hbm.1, bf16[4,4,576]{2,1,0:T(4,128)(2,1)} %new_hbm.1), custom_call_target="tpu_custom_call" | custom-call | tf_op jit(solution)/shard_map/queries/pallas_call | solution.py:305
  2.0 3.8 %collective-permute-start.2 = (bf16[2,64,640]{2,1,0:T(8,128)(2,1)S(1)}, bf16[2,64,640]{2,1,0:T(8,128)(2,1)S(1)}, u32[]{:S(2)}, u32[]{:S(2)}) collective-permute-start(bf16[2,64,640]{2,1,0:T(8,128)(2,1)S(1)} %get-tuple-element.21), channel_id=1, source_target_pairs={{0,2},{1,3},{2,0},{3,1},{4,6},{5,7},{6,4},{7,5},{8,10},{9,11},{10,... | collective-permute-start | bytes 491528 | tf_op jit(solution)/shard_map/ppermute | solution.py:333
  6.6 3.8 %stage.1.k_ref = bf16[4,576,2048]{2,1,0:T(8,128)(2,1)S(1)} custom-call(bf16[4,576,2048]{2,1,0:T(8,128)(2,1)} %bitcast.6), custom_call_target="tpu_custom_call" | custom-call | bytes 9437184 | tf_op jit(solution)/shard_map/stage/pallas_call | solution.py:350
  10.5 3.7 %copy-done = bf16[4,576,2048]{2,1,0:T(8,128)(2,1)} copy-done((bf16[4,576,2048]{2,1,0:T(8,128)(2,1)}, bf16[4,576,2048]{2,1,0:T(8,128)(2,1)S(1)}, u32[]{:S(2)}) %copy-start) | copy-done | bytes 9437208
  14.1 1.2 %collective-permute-start.5 = (bf16[2,64,640]{2,1,0:T(8,128)(2,1)S(1)}, bf16[2,64,640]{2,1,0:T(8,128)(2,1)S(1)}, u32[]{:S(2)}, u32[]{:S(2)}) collective-permute-start(bf16[2,64,640]{2,1,0:T(8,128)(2,1)S(1)} %collective-permute-done.2.q3_ref), channel_id=1, source_target_pairs={{0,4},{4,0},{1,5},{5,1},{2,6},{6,2},{3,7},{7,3},{8,12},{12,8},{9,1... | collective-permute-start | bytes 491528 | tf_op jit(solution)/shard_map/ppermute | solution.py:362
  17.7 3.7 %copy-done.1 = bf16[4,576,2048]{2,1,0:T(8,128)(2,1)S(1)} copy-done((bf16[4,576,2048]{2,1,0:T(8,128)(2,1)S(1)}, bf16[4,576,2048]{2,1,0:T(8,128)(2,1)}, u32[]{:S(2)}) %copy-start.1) | copy-done | bytes 9437208
  21.4 4.7 %attention.2 = bf16[4,128,640]{2,1,0:T(8,128)(2,1)} custom-call(s32[6]{0:T(128)S(1)} %get-tuple-element.36.info_ref, bf16[4,64,640]{2,1,0:T(8,128)(2,1)S(1)} %get-tuple-element.20.own_ref, bf16[2,64,640]{2,1,0:T(8,128)(2,1)S(1)} %collective-permute-done.q1_ref, bf16[2,64,640]{2,1,0:T(8,128)(2,1)S(1)} %collective-permute-done.1.q2_ref, ...), custom_call_target="tpu_custom_call" | custom-call | flops 2281701376 | bytes 4718592 | tf_op jit(solution)/shard_map/attention/pallas_call | solution.py:369
  26.4 3.7 %copy-done.2 = bf16[4,576,2048]{2,1,0:T(8,128)(2,1)S(1)} copy-done((bf16[4,576,2048]{2,1,0:T(8,128)(2,1)S(1)}, bf16[4,576,2048]{2,1,0:T(8,128)(2,1)}, u32[]{:S(2)}) %copy-start.2) | copy-done | bytes 9437208
  31.0 3.9 %attention.3.b_ref = bf16[4,128,640]{2,1,0:T(8,128)(2,1)S(1)} custom-call(s32[6]{0:T(128)S(1)} %get-tuple-element.35.info_ref, bf16[4,64,640]{2,1,0:T(8,128)(2,1)S(1)} %get-tuple-element.20.own_ref, bf16[2,64,640]{2,1,0:T(8,128)(2,1)S(1)} %collective-permute-done.3.q1_ref, bf16[2,64,640]{2,1,0:T(8,128)(2,1)S(1)} %copy-done.5, ...), custom_call_target="tpu_custom_call" | custom-call | flops 2281701376 | bytes 4718592 | tf_op jit(solution)/shard_map/attention/pallas_call | solution.py:369
  35.8 1.2 %collective-permute-start.7 = (bf16[128,640]{1,0:T(8,128)(2,1)S(1)}, bf16[128,640]{1,0:T(8,128)(2,1)S(1)}, u32[]{:S(2)}, u32[]{:S(2)}) collective-permute-start(bf16[128,640]{1,0:T(8,128)(2,1)S(1)} %get-tuple-element.31), channel_id=1, source_target_pairs={{0,1},{1,0},{2,3},{3,2},{4,5},{5,4},{6,7},{7,6},{8,9},{9,8},{10,11... | collective-permute-start | bytes 491528 | tf_op jit(solution)/shard_map/ppermute | solution.py:333
  37.0 1.9 %collective-permute-start.8 = (bf16[128,640]{1,0:T(8,128)(2,1)S(1)}, bf16[128,640]{1,0:T(8,128)(2,1)S(1)}, u32[]{:S(2)}, u32[]{:S(2)}) collective-permute-start(bf16[128,640]{1,0:T(8,128)(2,1)S(1)} %get-tuple-element.32), channel_id=1, source_target_pairs={{0,3},{1,2},{2,1},{3,0},{4,7},{5,6},{6,5},{7,4},{8,11},{9,10},{10,... | collective-permute-start | bytes 491528 | tf_op jit(solution)/shard_map/ppermute | solution.py:333
  39.7 1.1 %fresh.1.refs_4_ = bf16[128,640]{1,0:T(8,128)(2,1)S(1)} custom-call(s32[2]{0:T(128)S(1)} %pad_add_fusion.info_ref, bf16[4,64,640]{2,1,0:T(8,128)(2,1)S(1)} %get-tuple-element.20.own_ref, bf16[16,576]{1,0:T(8,128)(2,1)S(1)} %get-tuple-element.34.new_ref), custom_call_target="tpu_custom_call" | custom-call | flops 1000000000 | bytes 4000000 | tf_op jit(solution)/shard_map/fresh/pallas_call | solution.py:341
  41.4 3.9 %collective-permute-done.8.refs_2_ = bf16[128,640]{1,0:T(8,128)(2,1)S(1)} collective-permute-done((bf16[128,640]{1,0:T(8,128)(2,1)S(1)}, bf16[128,640]{1,0:T(8,128)(2,1)S(1)}, u32[]{:S(2)}, u32[]{:S(2)}) %collective-permute-start.8) | collective-permute-done | bytes 163872 | tf_op jit(solution)/shard_map/ppermute | solution.py:333
  45.4 1.9 %collective-permute-done.9.refs_3_ = bf16[128,640]{1,0:T(8,128)(2,1)S(1)} collective-permute-done((bf16[128,640]{1,0:T(8,128)(2,1)S(1)}, bf16[128,640]{1,0:T(8,128)(2,1)S(1)}, u32[]{:S(2)}, u32[]{:S(2)}) %collective-permute-start.9) | collective-permute-done | bytes 163872 | tf_op jit(solution)/shard_map/ppermute | solution.py:333
  47.3 1.4 %project.1.refs_0_ = bf16[144,128]{1,0:T(8,128)(2,1)S(1)} custom-call(bf16[128,640]{1,0:T(8,128)(2,1)S(1)} %get-tuple-element.30.refs_0_, bf16[128,640]{1,0:T(8,128)(2,1)S(1)} %collective-permute-done.7.refs_1_, bf16[128,640]{1,0:T(8,128)(2,1)S(1)} %collective-permute-done.8.refs_2_, bf16[128,640]{1,0:T(8,128)(2,1)S(1)} %collective-permute-done.9.refs_3_, ...), custom_call_target="tpu_custom_call" | custom-call | tf_op jit(solution)/shard_map/project/pallas_call | solution.py:398
  48.6 1.3 %collective-permute-start.10 = (bf16[144,128]{1,0:T(8,128)(2,1)S(1)}, bf16[144,128]{1,0:T(8,128)(2,1)S(1)}, u32[]{:S(2)}, u32[]{:S(2)}) collective-permute-start(bf16[144,128]{1,0:T(8,128)(2,1)S(1)} %project.1.refs_0_), channel_id=1, source_target_pairs={{0,8},{8,0},{16,24},{24,16},{32,40},{40,32},{48,56},{56,48},{64,72... | collective-permute-start | bytes 110600 | tf_op jit(solution)/shard_map/ppermute | solution.py:412
  49.9 1.6 %collective-permute-start.11 = (bf16[144,128]{1,0:T(8,128)(2,1)S(1)}, bf16[144,128]{1,0:T(8,128)(2,1)S(1)}, u32[]{:S(2)}, u32[]{:S(2)}) collective-permute-start(bf16[144,128]{1,0:T(8,128)(2,1)S(1)} %project.1.refs_0_), channel_id=1, source_target_pairs={{0,32},{8,40},{16,48},{24,56},{32,0},{40,8},{48,16},{56,24},{64,96... | collective-permute-start | bytes 110600 | tf_op jit(solution)/shard_map/ppermute | solution.py:412
  51.6 1.6 %collective-permute-done.11.refs_2_ = bf16[144,128]{1,0:T(8,128)(2,1)S(1)} collective-permute-done((bf16[144,128]{1,0:T(8,128)(2,1)S(1)}, bf16[144,128]{1,0:T(8,128)(2,1)S(1)}, u32[]{:S(2)}, u32[]{:S(2)}) %collective-permute-start.11) | collective-permute-done | bytes 36896 | tf_op jit(solution)/shard_map/ppermute | solution.py:412
  53.2 2.1 %collective-permute-done.12.refs_3_ = bf16[144,128]{1,0:T(8,128)(2,1)S(1)} collective-permute-done((bf16[144,128]{1,0:T(8,128)(2,1)S(1)}, bf16[144,128]{1,0:T(8,128)(2,1)S(1)}, u32[]{:S(2)}, u32[]{:S(2)}) %collective-permute-start.12) | collective-permute-done | bytes 36896 | tf_op jit(solution)/shard_map/ppermute | solution.py:412
  55.5 2.1 %collective-permute-start.13 = (bf16[144,128]{1,0:T(8,128)(2,1)S(1)}, bf16[144,128]{1,0:T(8,128)(2,1)S(1)}, u32[]{:S(2)}, u32[]{:S(2)}) collective-permute-start(bf16[144,128]{1,0:T(8,128)(2,1)S(1)} %middle_merge.1.refs_0_), channel_id=1, source_target_pairs={{0,24},{8,16},{16,8},{24,0},{32,56},{40,48},{48,40},{56,32},{64,88... | collective-permute-start | bytes 110600 | tf_op jit(solution)/shard_map/ppermute | solution.py:412
  57.7 2.2 %collective-permute-start.14 = (bf16[144,128]{1,0:T(8,128)(2,1)S(1)}, bf16[144,128]{1,0:T(8,128)(2,1)S(1)}, u32[]{:S(2)}, u32[]{:S(2)}) collective-permute-start(bf16[144,128]{1,0:T(8,128)(2,1)S(1)} %middle_merge.1.refs_0_), channel_id=1, source_target_pairs={{0,96},{8,104},{16,112},{24,120},{32,64},{40,72},{48,80},{56,88},{... | collective-permute-start | bytes 110600 | tf_op jit(solution)/shard_map/ppermute | solution.py:412
  60.7 1.0 %collective-permute-done.14.refs_2_ = bf16[144,128]{1,0:T(8,128)(2,1)S(1)} collective-permute-done((bf16[144,128]{1,0:T(8,128)(2,1)S(1)}, bf16[144,128]{1,0:T(8,128)(2,1)S(1)}, u32[]{:S(2)}, u32[]{:S(2)}) %collective-permute-start.14) | collective-permute-done | bytes 36896 | tf_op jit(solution)/shard_map/ppermute | solution.py:412
  61.7 4.4 %collective-permute-done.15.refs_3_ = bf16[144,128]{1,0:T(8,128)(2,1)S(1)} collective-permute-done((bf16[144,128]{1,0:T(8,128)(2,1)S(1)}, bf16[144,128]{1,0:T(8,128)(2,1)S(1)}, u32[]{:S(2)}, u32[]{:S(2)}) %collective-permute-start.15) | collective-permute-done | bytes 36896 | tf_op jit(solution)/shard_map/ppermute | solution.py:412
  66.3 4.4 %collective-permute-start.16 = (bf16[4,2,16,128]{3,2,1,0:T(8,128)(2,1)S(1)}, bf16[4,2,16,128]{3,2,1,0:T(8,128)(2,1)S(1)}, u32[]{:S(2)}, u32[]{:S(2)}) collective-permute-start(bf16[4,2,16,128]{3,2,1,0:T(8,128)(2,1)S(1)} %finish.1.own_ref), channel_id=1, source_target_pairs={{0,4},{4,0},{1,5},{5,1},{2,6},{6,2},{3,7},{7,3},{8,12},{12,8},{9,1... | collective-permute-start | bytes 98312 | tf_op jit(solution)/shard_map/ppermute | solution.py:430
  (36 shorter events, 9.4 us)
Async XLA Ops:
  2.0 12.1 %collective-permute-start.2 = (bf16[2,64,640]{2,1,0:T(8,128)(2,1)S(1)}, bf16[2,64,640]{2,1,0:T(8,128)(2,1)S(1)}, u32[]{:S(2)}, u32[]{:S(2)}) collective-permute-start(bf16[2,64,640]{2,1,0:T(8,128)(2,1)S(1)} %get-tuple-element.21), channel_id=1, source_target_pairs={{0,2},{1,3},{2,0},{3,1},{4,6},{5,7},{6,4},{7,5},{8,10},{9,11},{10,... | collective-permute-start | bytes 491528 | tf_op jit(solution)/shard_map/ppermute | solution.py:333
  5.8 9.5 %collective-permute-start = (bf16[2,64,640]{2,1,0:T(8,128)(2,1)S(1)}, bf16[2,64,640]{2,1,0:T(8,128)(2,1)S(1)}, u32[]{:S(2)}, u32[]{:S(2)}) collective-permute-start(bf16[2,64,640]{2,1,0:T(8,128)(2,1)S(1)} %get-tuple-element.21), channel_id=1, source_target_pairs={{0,1},{1,0},{2,3},{3,2},{4,5},{5,4},{6,7},{7,6},{8,9},{9,8},{10,11... | collective-permute-start | bytes 491528 | tf_op jit(solution)/shard_map/ppermute | solution.py:333
  6.2 9.2 %collective-permute-start.1 = (bf16[2,64,640]{2,1,0:T(8,128)(2,1)S(1)}, bf16[2,64,640]{2,1,0:T(8,128)(2,1)S(1)}, u32[]{:S(2)}, u32[]{:S(2)}) collective-permute-start(bf16[2,64,640]{2,1,0:T(8,128)(2,1)S(1)} %get-tuple-element.21), channel_id=1, source_target_pairs={{0,3},{1,2},{2,1},{3,0},{4,7},{5,6},{6,5},{7,4},{8,11},{9,10},{10,... | collective-permute-start | bytes 491528 | tf_op jit(solution)/shard_map/ppermute | solution.py:333
  6.6 9.3 %copy-start.6 = (s32[4]{0:T(128)S(1)}, s32[4]{0:T(128)}, u32[]{:S(2)}) copy-start(s32[4]{0:T(128)} %param.12) | copy-start | bytes 52
  10.4 3.7 %copy-start = (bf16[4,576,2048]{2,1,0:T(8,128)(2,1)}, bf16[4,576,2048]{2,1,0:T(8,128)(2,1)S(1)}, u32[]{:S(2)}) copy-start(bf16[4,576,2048]{2,1,0:T(8,128)(2,1)S(1)} %stage.1.k_ref) | copy-start | bytes 28311556
  14.1 2.3 %collective-permute-start.5 = (bf16[2,64,640]{2,1,0:T(8,128)(2,1)S(1)}, bf16[2,64,640]{2,1,0:T(8,128)(2,1)S(1)}, u32[]{:S(2)}, u32[]{:S(2)}) collective-permute-start(bf16[2,64,640]{2,1,0:T(8,128)(2,1)S(1)} %collective-permute-done.2.q3_ref), channel_id=1, source_target_pairs={{0,4},{4,0},{1,5},{5,1},{2,6},{6,2},{3,7},{7,3},{8,12},{12,8},{9,1... | collective-permute-start | bytes 491528 | tf_op jit(solution)/shard_map/ppermute | solution.py:362
  15.4 1.4 %collective-permute-start.3 = (bf16[2,64,640]{2,1,0:T(8,128)(2,1)S(1)}, bf16[2,64,640]{2,1,0:T(8,128)(2,1)S(1)}, u32[]{:S(2)}, u32[]{:S(2)}) collective-permute-start(bf16[2,64,640]{2,1,0:T(8,128)(2,1)S(1)} %collective-permute-done.q1_ref), channel_id=1, source_target_pairs={{0,4},{4,0},{1,5},{5,1},{2,6},{6,2},{3,7},{7,3},{8,12},{12,8},{9,1... | collective-permute-start | bytes 491528 | tf_op jit(solution)/shard_map/ppermute | solution.py:362
  15.5 1.5 %collective-permute-start.4 = (bf16[2,64,640]{2,1,0:T(8,128)(2,1)S(1)}, bf16[2,64,640]{2,1,0:T(8,128)(2,1)S(1)}, u32[]{:S(2)}, u32[]{:S(2)}) collective-permute-start(bf16[2,64,640]{2,1,0:T(8,128)(2,1)S(1)} %collective-permute-done.1.q2_ref), channel_id=1, source_target_pairs={{0,4},{4,0},{1,5},{5,1},{2,6},{6,2},{3,7},{7,3},{8,12},{12,8},{9,1... | collective-permute-start | bytes 491528 | tf_op jit(solution)/shard_map/ppermute | solution.py:362
  17.0 0.7 copy-start.4
  17.7 3.7 %copy-start.1 = (bf16[4,576,2048]{2,1,0:T(8,128)(2,1)S(1)}, bf16[4,576,2048]{2,1,0:T(8,128)(2,1)}, u32[]{:S(2)}) copy-start(bf16[4,576,2048]{2,1,0:T(8,128)(2,1)} %copy-done) | copy-start | bytes 28311556
  21.4 25.9 %copy-start.3 = (bf16[16,512,128]{2,1,0:T(8,128)(2,1)S(1)}, bf16[16,512,128]{2,1,0:T(8,128)(2,1)}, u32[]{:S(2)}) copy-start(bf16[16,512,128]{2,1,0:T(8,128)(2,1)} %refs_5_.1) | copy-start | bytes 6291460
  26.1 8.8 %collective-permute-start.6 = (bf16[4,128,640]{2,1,0:T(8,128)(2,1)}, bf16[4,128,640]{2,1,0:T(8,128)(2,1)S(1)}, u32[]{:S(2)}, u32[]{:S(2)}) collective-permute-start(bf16[4,128,640]{2,1,0:T(8,128)(2,1)} %attention.2), channel_id=1, source_target_pairs={{0,4},{4,0},{1,5},{5,1},{2,6},{6,2},{3,7},{7,3},{8,12},{12,8},{9,1... | collective-permute-start | bytes 1966088 | tf_op jit(solution)/shard_map/ppermute | solution.py:387
  26.4 3.7 %copy-start.2 = (bf16[4,576,2048]{2,1,0:T(8,128)(2,1)S(1)}, bf16[4,576,2048]{2,1,0:T(8,128)(2,1)}, u32[]{:S(2)}) copy-start(bf16[4,576,2048]{2,1,0:T(8,128)(2,1)} %copy-done) | copy-start | bytes 28311556
  30.1 0.9 %copy-start.5 = (bf16[2,64,640]{2,1,0:T(8,128)(2,1)S(1)}, bf16[2,64,640]{2,1,0:T(8,128)(2,1)}, u32[]{:S(2)}) copy-start(bf16[2,64,640]{2,1,0:T(8,128)(2,1)} %copy-done.4) | copy-start | bytes 491524
  35.8 5.6 %collective-permute-start.7 = (bf16[128,640]{1,0:T(8,128)(2,1)S(1)}, bf16[128,640]{1,0:T(8,128)(2,1)S(1)}, u32[]{:S(2)}, u32[]{:S(2)}) collective-permute-start(bf16[128,640]{1,0:T(8,128)(2,1)S(1)} %get-tuple-element.31), channel_id=1, source_target_pairs={{0,1},{1,0},{2,3},{3,2},{4,5},{5,4},{6,7},{7,6},{8,9},{9,8},{10,11... | collective-permute-start | bytes 491528 | tf_op jit(solution)/shard_map/ppermute | solution.py:333
  37.0 8.3 %collective-permute-start.8 = (bf16[128,640]{1,0:T(8,128)(2,1)S(1)}, bf16[128,640]{1,0:T(8,128)(2,1)S(1)}, u32[]{:S(2)}, u32[]{:S(2)}) collective-permute-start(bf16[128,640]{1,0:T(8,128)(2,1)S(1)} %get-tuple-element.32), channel_id=1, source_target_pairs={{0,3},{1,2},{2,1},{3,0},{4,7},{5,6},{6,5},{7,4},{8,11},{9,10},{10,... | collective-permute-start | bytes 491528 | tf_op jit(solution)/shard_map/ppermute | solution.py:333
  38.9 8.3 %collective-permute-start.9 = (bf16[128,640]{1,0:T(8,128)(2,1)S(1)}, bf16[128,640]{1,0:T(8,128)(2,1)S(1)}, u32[]{:S(2)}, u32[]{:S(2)}) collective-permute-start(bf16[128,640]{1,0:T(8,128)(2,1)S(1)} %get-tuple-element.33), channel_id=1, source_target_pairs={{0,2},{1,3},{2,0},{3,1},{4,6},{5,7},{6,4},{7,5},{8,10},{9,11},{10,... | collective-permute-start | bytes 491528 | tf_op jit(solution)/shard_map/ppermute | solution.py:333
  48.6 2.9 %collective-permute-start.10 = (bf16[144,128]{1,0:T(8,128)(2,1)S(1)}, bf16[144,128]{1,0:T(8,128)(2,1)S(1)}, u32[]{:S(2)}, u32[]{:S(2)}) collective-permute-start(bf16[144,128]{1,0:T(8,128)(2,1)S(1)} %project.1.refs_0_), channel_id=1, source_target_pairs={{0,8},{8,0},{16,24},{24,16},{32,40},{40,32},{48,56},{56,48},{64,72... | collective-permute-start | bytes 110600 | tf_op jit(solution)/shard_map/ppermute | solution.py:412
  49.9 3.3 %collective-permute-start.11 = (bf16[144,128]{1,0:T(8,128)(2,1)S(1)}, bf16[144,128]{1,0:T(8,128)(2,1)S(1)}, u32[]{:S(2)}, u32[]{:S(2)}) collective-permute-start(bf16[144,128]{1,0:T(8,128)(2,1)S(1)} %project.1.refs_0_), channel_id=1, source_target_pairs={{0,32},{8,40},{16,48},{24,56},{32,0},{40,8},{48,16},{56,24},{64,96... | collective-permute-start | bytes 110600 | tf_op jit(solution)/shard_map/ppermute | solution.py:412
  51.6 3.7 %collective-permute-start.12 = (bf16[144,128]{1,0:T(8,128)(2,1)S(1)}, bf16[144,128]{1,0:T(8,128)(2,1)S(1)}, u32[]{:S(2)}, u32[]{:S(2)}) collective-permute-start(bf16[144,128]{1,0:T(8,128)(2,1)S(1)} %project.1.refs_0_), channel_id=1, source_target_pairs={{0,40},{8,32},{16,56},{24,48},{32,8},{40,0},{48,24},{56,16},{64,10... | collective-permute-start | bytes 110600 | tf_op jit(solution)/shard_map/ppermute | solution.py:412
  55.5 5.2 %collective-permute-start.13 = (bf16[144,128]{1,0:T(8,128)(2,1)S(1)}, bf16[144,128]{1,0:T(8,128)(2,1)S(1)}, u32[]{:S(2)}, u32[]{:S(2)}) collective-permute-start(bf16[144,128]{1,0:T(8,128)(2,1)S(1)} %middle_merge.1.refs_0_), channel_id=1, source_target_pairs={{0,24},{8,16},{16,8},{24,0},{32,56},{40,48},{48,40},{56,32},{64,88... | collective-permute-start | bytes 110600 | tf_op jit(solution)/shard_map/ppermute | solution.py:412
  57.7 4.0 %collective-permute-start.14 = (bf16[144,128]{1,0:T(8,128)(2,1)S(1)}, bf16[144,128]{1,0:T(8,128)(2,1)S(1)}, u32[]{:S(2)}, u32[]{:S(2)}) collective-permute-start(bf16[144,128]{1,0:T(8,128)(2,1)S(1)} %middle_merge.1.refs_0_), channel_id=1, source_target_pairs={{0,96},{8,104},{16,112},{24,120},{32,64},{40,72},{48,80},{56,88},{... | collective-permute-start | bytes 110600 | tf_op jit(solution)/shard_map/ppermute | solution.py:412
  59.9 6.1 %collective-permute-start.15 = (bf16[144,128]{1,0:T(8,128)(2,1)S(1)}, bf16[144,128]{1,0:T(8,128)(2,1)S(1)}, u32[]{:S(2)}, u32[]{:S(2)}) collective-permute-start(bf16[144,128]{1,0:T(8,128)(2,1)S(1)} %middle_merge.1.refs_0_), channel_id=1, source_target_pairs={{0,120},{8,112},{16,104},{24,96},{32,88},{40,80},{48,72},{56,64},{... | collective-permute-start | bytes 110600 | tf_op jit(solution)/shard_map/ppermute | solution.py:412
  66.3 5.2 %collective-permute-start.16 = (bf16[4,2,16,128]{3,2,1,0:T(8,128)(2,1)S(1)}, bf16[4,2,16,128]{3,2,1,0:T(8,128)(2,1)S(1)}, u32[]{:S(2)}, u32[]{:S(2)}) collective-permute-start(bf16[4,2,16,128]{3,2,1,0:T(8,128)(2,1)S(1)} %finish.1.own_ref), channel_id=1, source_target_pairs={{0,4},{4,0},{1,5},{5,1},{2,6},{6,2},{3,7},{7,3},{8,12},{12,8},{9,1... | collective-permute-start | bytes 98312 | tf_op jit(solution)/shard_map/ppermute | solution.py:430

commit v6 on v5

--- a/solution.py
+++ b/solution.py
@@ -96,23 +96,37 @@
     return jnp.where(lane == 4, sum_second, out)
 
 
-def stage_kernel(cache_hbm, out_ref, sems):
+def stage_kernel(info_ref, cache_hbm, out_ref, sems):
     copies = []
     for i in range(out_ref.shape[0]):
-        copies.append(pltpu.make_async_copy(cache_hbm.at[i], out_ref.at[i], sems.at[i]))
+        copies.append(pltpu.make_async_copy(cache_hbm.at[info_ref[0] + i], out_ref.at[i], sems.at[i]))
     for copy in copies:
         copy.start()
     for copy in copies:
         copy.wait()
 
 
-def attention_kernel(scale, info_ref, own_ref, q1_ref, q2_ref, q3_ref, k_ref, out_ref, q_ref, *scores):
+def first_attention_kernel(
+    scale, info_ref, own_ref, q1_ref, q2_ref, q3_ref, k_ref, cache_hbm, out_ref, next_ref, q_ref, sems, *scores
+):
+    copies = []
+    for i in range(next_ref.shape[0]):
+        source = cache_hbm.at[info_ref[1] + i]
+        copies.append(pltpu.make_async_copy(source, next_ref.at[i], sems.at[i]))
+    for copy in copies:
+        copy.start()
+    attention_kernel(scale, 0, info_ref, own_ref, q1_ref, q2_ref, q3_ref, k_ref, out_ref, q_ref, *scores)
+    for copy in copies:
+        copy.wait()
+
+
+def attention_kernel(scale, which, info_ref, own_ref, q1_ref, q2_ref, q3_ref, k_ref, out_ref, q_ref, *scores):
     count, owners, share, _ = q_ref.shape
     rows = owners * share
     key_width, cached = k_ref.shape[1:]
     width = out_ref.shape[2] - 128
     chunk = 1024
-    first = info_ref[0]
+    first = info_ref[which]
     q_ref[:, 0] = own_ref[pl.ds(first, count)]
     q_ref[:, 1] = q1_ref[...]
     q_ref[:, 2] = q2_ref[...]
@@ -120,11 +134,11 @@
 
     tops = []
     for i in range(count):
-        limit = info_ref[2 + first + i] - info_ref[1]
+        limit = info_ref[4 + first + i] - info_ref[2]
         queries = q_ref[i].reshape(rows, -1)[:, :key_width]
         top = jnp.full((rows, 128), lowest_max, f32)
         for c in range(0, cached, chunk):
-            keys = k_ref[first + i, :, c : c + chunk]
+            keys = k_ref[i, :, c : c + chunk]
             part = jnp.dot(queries, keys, preferred_element_type=f32) * scale
             column = lax.broadcasted_iota(jnp.int32, (1, chunk), 1) + c
             part = jnp.where(column < limit, part, masked_score)
@@ -141,7 +155,7 @@
                 total = total + weights[:, at : at + 128]
             part = lax.dot_general(
                 weights.astype(bf16),
-                k_ref[first + i, :width, c : c + chunk],
+                k_ref[i, :width, c : c + chunk],
                 (((1,), (1,)), ((), ())),
                 preferred_element_type=f32,
             )
@@ -160,9 +174,9 @@
     shape = (share, fresh.shape[0])
     key = lax.broadcasted_iota(jnp.int32, shape, 1)
     step = (lax.broadcasted_iota(jnp.int32, shape, 0) // heads) % steps
-    counted = info_ref[1] == 1
+    counted = info_ref[3] == 1
     for i in range(out_ref.shape[0] // share):
-        request = info_ref[0] + i
+        request = info_ref[1] + i
         scores = (
             lax.dot_general(
                 own_ref[request][:, :key_width], fresh, (((1,), (1,)), ((), ())), preferred_element_type=f32
@@ -271,7 +285,7 @@
 
 def place_kernel(info_ref, own_ref, other_ref, out_ref):
     half = own_ref.shape[1]
-    first = info_ref[0]
+    first = info_ref[1]
     out_ref[:, pl.ds(first, half)] = own_ref[...]
     out_ref[:, pl.ds(half - first, half)] = other_ref[...]
 
@@ -301,7 +315,11 @@
     anywhere = pl.BlockSpec(memory_space=pltpu.HBM)
     wide = 640
     in_hbm = functools.partial(pltpu.with_memory_space_constraint, memory_space=pltpu.HBM)
-    other_first = ((1 - core) * half).astype(jnp.int32)
+    own_first = core * half
+    at_origin = lax.axis_index(("z", "x")) == 0
+    info = jnp.stack([half - own_first, own_first, slot * cached, at_origin])
+    info = jnp.concatenate([info.astype(jnp.int32), context_lengths])
+    chunk = half * steps * heads
     own_queries, sent_queries, new_keys = pl.pallas_call(
         functools.partial(queries_kernel, steps),
         in_specs=[smem] + [anywhere] * 4,
@@ -322,7 +340,7 @@
         compiler_params=pltpu.CompilerParams(vmem_limit_bytes=24 * 2**20),
         name="queries",
     )(
-        other_first.reshape(1),
+        info,
         in_hbm(positions),
         in_hbm(query_heads.reshape(pairs, heads, query_width)),
         in_hbm(up_keys),
@@ -335,9 +353,6 @@
     swap = [(0, 1), (1, 0)]
     partners = (1, 3, 2)
     got = [over_head(sent_queries, k) for k in partners]
-    own_first = (core * half).astype(jnp.int32)
-    chunk = half * steps * heads
-    at_origin = (lax.axis_index(("z", "x")) == 0).astype(jnp.int32)
     fresh = pl.pallas_call(
         functools.partial(fresh_kernel, scale, steps, heads),
         in_specs=[smem, vmem, vmem],
@@ -346,46 +361,50 @@
         compiler_params=small,
         cost_estimate=pl.CostEstimate(flops=10**9, bytes_accessed=4 * 10**6, transcendentals=0),
         name="fresh",
-    )(jnp.stack([own_first, at_origin]), own_queries, new_keys)
-    cache = pl.pallas_call(
+    )(info, own_queries, new_keys)
+    cache = in_hbm(jnp.swapaxes(latent_cache, 1, 2))
+    staged_shape = pltpu.VMEM((half, key_width, cached), bf16)
+    in_vmem = functools.partial(pltpu.with_memory_space_constraint, memory_space=pltpu.VMEM)
+    staged = pl.pallas_call(
         stage_kernel,
-        in_specs=[anywhere],
-        out_specs=vmem,
-        out_shape=pltpu.VMEM((requests, key_width, cached), bf16),
-        scratch_shapes=[pltpu.SemaphoreType.DMA((requests,))],
-        compiler_params=small,
-        cost_estimate=pl.CostEstimate(flops=0, bytes_accessed=2 * requests * key_width * cached, transcendentals=0),
+        in_specs=[smem, anywhere],
+        out_specs=vmem,
+        out_shape=staged_shape,
+        scratch_shapes=[pltpu.SemaphoreType.DMA((half,))],
+        compiler_params=small,
+        cost_estimate=pl.CostEstimate(flops=0, bytes_accessed=2 * half * key_width * cached, transcendentals=0),
         name="stage",
-    )(in_hbm(jnp.swapaxes(latent_cache, 1, 2)))
-    cache = pltpu.with_memory_space_constraint(cache, memory_space=pltpu.VMEM)
-    got[2], cache = lax.optimization_barrier((got[2], cache))
+    )(info, cache)
+    got[2], staged = lax.optimization_barrier((got[2], staged))
     passed = [lax.ppermute(g, "core", swap) for g in got]
     got, passed = lax.optimization_barrier((got, passed))
 
     rows = owners * steps * heads
 
-    def attend(first, got):
-        info = jnp.concatenate([jnp.stack([first, slot.astype(jnp.int32) * cached]), context_lengths])
+    def attend(got, keys, is_first):
+        part_shape = jax.ShapeDtypeStruct((owners, chunk, width + 128), bf16)
+        scratch = [pltpu.VMEM((half, owners, steps * heads, wide), bf16)]
+        scores = [pltpu.VMEM((rows, cached), f32)] * half
         return pl.pallas_call(
-            functools.partial(attention_kernel, scale),
-            in_specs=[smem] + [vmem] * 5,
-            out_specs=vmem,
-            scratch_shapes=[
-                pltpu.VMEM((half, owners, steps * heads, wide), bf16),
-            ]
-            + [pltpu.VMEM((rows, cached), f32)] * half,
-            out_shape=jax.ShapeDtypeStruct((owners, chunk, width + 128), bf16),
-            compiler_params=pltpu.CompilerParams(vmem_limit_bytes=24 * 2**20),
+            functools.partial(first_attention_kernel, scale)
+            if is_first
+            else functools.partial(attention_kernel, scale, 1),
+            in_specs=[smem] + [vmem] * 5 + [anywhere] * is_first,
+            out_specs=[vmem] * 2 if is_first else vmem,
+            scratch_shapes=scratch + [pltpu.SemaphoreType.DMA((half,))] * is_first + scores,
+            out_shape=[part_shape, staged_shape] if is_first else part_shape,
+            compiler_params=pltpu.CompilerParams(vmem_limit_bytes=18 * 2**20),
             cost_estimate=pl.CostEstimate(
                 flops=2 * half * rows * cached * (key_width + width),
                 bytes_accessed=half * cached * key_width * 2,
                 transcendentals=half * rows * cached,
             ),
             name="attention",
-        )(info, own_queries, *got, cache)
-
-    other_part = lax.ppermute(attend(other_first, got), "core", swap)
-    own_part = attend(own_first, passed)
+        )(info, own_queries, *got, in_vmem(keys), *[cache] * is_first)
+
+    other_part, staged = attend(got, staged, True)
+    other_part = lax.ppermute(other_part, "core", swap)
+    own_part = attend(passed, staged, False)
     sent = pl.pallas_call(
         pair_kernel,
         in_specs=[vmem] * 2,
@@ -435,7 +454,7 @@
         out_shape=jax.ShapeDtypeStruct((steps, requests, heads, value_width), bf16),
         compiler_params=small,
         name="place",
-    )(own_first.reshape(1), own, theirs)
+    )(info, own, theirs)
 
 
 def solution(mesh):

time: 72.4 us -> 66.2 us (0.914)
  local copies, waits for them, and re-layouts: 12.6 us -> 0.74 us
  starting transfers between devices: 22.9 us -> 25 us
  waiting for transfers between devices: 17.3 us -> 19.3 us
  Pallas kernels: 19.1 us -> 21 us
    unnamed x14 -> x2, local copies, waits for them, and re-layouts: 12.6 us -> 0.01 us
    ppermute x3, starting transfers between devices: 1.75 us -> 4.08 us  [on_device(): passed = [lax.ppermute(g, 'core', swap) for g in got]]
    ppermute x6, waiting for transfers between devices: 6.4 us -> 7.88 us  [over_head(): return lax.ppermute(array, 'head', [(i, i ^ k) for i in range(owners)])]
    pallas_call x3, Pallas kernels: 12.5 us -> 13.3 us  [the longest x2 10.4 us: attend(): pl.pallas_call(functools.partial(first_attention_kernel, scale) if is_fir...]
    concatenate x0 -> x1, local copies, waits for them, and re-layouts: none -> 0.73 us  [on_device(): info = jnp.concatenate([info.astype(jnp.int32), context_lengths])]
where the time goes in v6:
time: 66.2 us; the launch traced here: 66.1 us
  starting transfers between devices  25 us (38%)
  Pallas kernels  21 us (32%)
  waiting for transfers between devices  19.3 us (29%)
  local copies, waits for them, and re-layouts  0.74 us (1%)
    pallas_call x2, Pallas kernels, attend(): pl.pallas_call(functools.partial(first_attention_kernel, scale) if is_fir...  10.4 us
    ppermute x6, waiting for transfers between devices, over_plane(): return lax.ppermute(array, ('z', 'x'), [(i, i ^ k) for i in range(plane)])  9.13 us
    ppermute x6, starting transfers between devices, over_plane(): return lax.ppermute(array, ('z', 'x'), [(i, i ^ k) for i in range(plane)])  8.07 us
    ppermute x6, starting transfers between devices, over_head(): return lax.ppermute(array, 'head', [(i, i ^ k) for i in range(owners)])  8 us
    ppermute x6, waiting for transfers between devices, over_head(): return lax.ppermute(array, 'head', [(i, i ^ k) for i in range(owners)])  7.88 us
    ppermute x1, starting transfers between devices, on_device(): theirs = lax.ppermute(own, 'core', swap)  4.57 us
    ppermute x3, starting transfers between devices, on_device(): passed = [lax.ppermute(g, 'core', swap) for g in got]  4.08 us
    pallas_call x1, Pallas kernels, on_device(): pl.pallas_call(stage_kernel, in_specs=[smem, anywhere], out_specs=vmem, o...  2.94 us
  transfers between devices with their start and end apart: 17, of which 11 were waited for; matrix products, arithmetic and copies ran while one was open for 0% of the time, Pallas kernels for 12%

profile of v6, /device:TPU:1, one launch (start us, length us, event | category | flops | bytes accessed | tf_op | source)
XLA Modules:
  0.0 66.1 jit_solution(3132394455428824924)
XLA Ops:
  0.7 2.6 %queries.1 = (bf16[4,64,640]{2,1,0:T(8,128)(2,1)S(1)}, bf16[2,64,640]{2,1,0:T(8,128)(2,1)S(1)}, bf16[16,576]{1,0:T(8,128)(2,1)S(1)}) custom-call(s32[8]{0:T(128)S(1)} %concatenate.3.info_ref, s32[4]{0:T(128)} %positions_hbm.1, bf16[16,16,192]{2,1,0:T(8,128)(2,1)} %bitcast.8, bf16[16,128,512]{2,1,0:T(8,128)(2,1)} %up_hbm.1, bf16[4,4,576]{2,1,0:T(4,128)(2,1)} %new_hbm.1), custom_call_target="tpu_custom_call" | custom-call | tf_op jit(solution)/shard_map/queries/pallas_call | solution.py:323
  3.3 3.8 %collective-permute-start.2 = (bf16[2,64,640]{2,1,0:T(8,128)(2,1)S(1)}, bf16[2,64,640]{2,1,0:T(8,128)(2,1)S(1)}, u32[]{:S(2)}, u32[]{:S(2)}) collective-permute-start(bf16[2,64,640]{2,1,0:T(8,128)(2,1)S(1)} %get-tuple-element.23), channel_id=1, source_target_pairs={{0,2},{1,3},{2,0},{3,1},{4,6},{5,7},{6,4},{7,5},{8,10},{9,11},{10,... | collective-permute-start | bytes 491528 | tf_op jit(solution)/shard_map/ppermute | solution.py:351
  7.9 2.9 %stage.1.k_ref = bf16[2,576,2048]{2,1,0:T(8,128)(2,1)S(1)} custom-call(s32[8]{0:T(128)S(1)} %concatenate.3.info_ref, bf16[4,576,2048]{2,1,0:T(8,128)(2,1)} %bitcast.6), custom_call_target="tpu_custom_call" | custom-call | bytes 4718592 | tf_op jit(solution)/shard_map/stage/pallas_call | solution.py:368
  10.9 2.5 %collective-permute-start.5 = (bf16[2,64,640]{2,1,0:T(8,128)(2,1)S(1)}, bf16[2,64,640]{2,1,0:T(8,128)(2,1)S(1)}, u32[]{:S(2)}, u32[]{:S(2)}) collective-permute-start(bf16[2,64,640]{2,1,0:T(8,128)(2,1)S(1)} %collective-permute-done.2.q3_ref), channel_id=1, source_target_pairs={{0,4},{4,0},{1,5},{5,1},{2,6},{6,2},{3,7},{7,3},{8,12},{12,8},{9,1... | collective-permute-start | bytes 491528 | tf_op jit(solution)/shard_map/ppermute | solution.py:379
  13.4 1.3 %collective-permute-done.q1_ref = bf16[2,64,640]{2,1,0:T(8,128)(2,1)S(1)} collective-permute-done((bf16[2,64,640]{2,1,0:T(8,128)(2,1)S(1)}, bf16[2,64,640]{2,1,0:T(8,128)(2,1)S(1)}, u32[]{:S(2)}, u32[]{:S(2)}) %collective-permute-start) | collective-permute-done | bytes 163872 | tf_op jit(solution)/shard_map/ppermute | solution.py:351
  14.7 1.5 %collective-permute-start.3 = (bf16[2,64,640]{2,1,0:T(8,128)(2,1)S(1)}, bf16[2,64,640]{2,1,0:T(8,128)(2,1)S(1)}, u32[]{:S(2)}, u32[]{:S(2)}) collective-permute-start(bf16[2,64,640]{2,1,0:T(8,128)(2,1)S(1)} %collective-permute-done.q1_ref), channel_id=1, source_target_pairs={{0,4},{4,0},{1,5},{5,1},{2,6},{6,2},{3,7},{7,3},{8,12},{12,8},{9,1... | collective-permute-start | bytes 491528 | tf_op jit(solution)/shard_map/ppermute | solution.py:379
  17.6 6.3 %attention.2 = (bf16[4,128,640]{2,1,0:T(8,128)(2,1)S(1)}, bf16[2,576,2048]{2,1,0:T(8,128)(2,1)S(1)}) custom-call(s32[8]{0:T(128)S(1)} %concatenate.3.info_ref, bf16[4,64,640]{2,1,0:T(8,128)(2,1)S(1)} %get-tuple-element.22.own_ref, bf16[2,64,640]{2,1,0:T(8,128)(2,1)S(1)} %collective-permute-done.q1_ref, ...), custom_call_target="tpu_custom_call" | custom-call | flops 2281701376 | bytes 4718592 | tf_op jit(solution)/shard_map/attention/pallas_call | solution.py:388
  24.2 4.1 %attention.3.b_ref = bf16[4,128,640]{2,1,0:T(8,128)(2,1)S(1)} custom-call(s32[8]{0:T(128)S(1)} %concatenate.3.info_ref, bf16[4,64,640]{2,1,0:T(8,128)(2,1)S(1)} %get-tuple-element.22.own_ref, bf16[2,64,640]{2,1,0:T(8,128)(2,1)S(1)} %collective-permute-done.3.q1_ref, bf16[2,64,640]{2,1,0:T(8,128)(2,1)S(1)} %collective-permute-done.4.q2_ref, ...), custom_call_target="tpu_custom_call" | custom-call | flops 2281701376 | bytes 4718592 | tf_op jit(solution)/shard_map/attention/pallas_call | solution.py:388
  29.2 1.2 %collective-permute-start.7 = (bf16[128,640]{1,0:T(8,128)(2,1)S(1)}, bf16[128,640]{1,0:T(8,128)(2,1)S(1)}, u32[]{:S(2)}, u32[]{:S(2)}) collective-permute-start(bf16[128,640]{1,0:T(8,128)(2,1)S(1)} %get-tuple-element.35), channel_id=1, source_target_pairs={{0,1},{1,0},{2,3},{3,2},{4,5},{5,4},{6,7},{7,6},{8,9},{9,8},{10,11... | collective-permute-start | bytes 491528 | tf_op jit(solution)/shard_map/ppermute | solution.py:351
  30.3 1.5 %collective-permute-start.8 = (bf16[128,640]{1,0:T(8,128)(2,1)S(1)}, bf16[128,640]{1,0:T(8,128)(2,1)S(1)}, u32[]{:S(2)}, u32[]{:S(2)}) collective-permute-start(bf16[128,640]{1,0:T(8,128)(2,1)S(1)} %get-tuple-element.36), channel_id=1, source_target_pairs={{0,3},{1,2},{2,1},{3,0},{4,7},{5,6},{6,5},{7,4},{8,11},{9,10},{10,... | collective-permute-start | bytes 491528 | tf_op jit(solution)/shard_map/ppermute | solution.py:351
  32.6 1.1 %fresh.1.refs_4_ = bf16[128,640]{1,0:T(8,128)(2,1)S(1)} custom-call(s32[8]{0:T(128)S(1)} %concatenate.3.info_ref, bf16[4,64,640]{2,1,0:T(8,128)(2,1)S(1)} %get-tuple-element.22.own_ref, bf16[16,576]{1,0:T(8,128)(2,1)S(1)} %get-tuple-element.38.new_ref), custom_call_target="tpu_custom_call" | custom-call | flops 1000000000 | bytes 4000000 | tf_op jit(solution)/shard_map/fresh/pallas_call | solution.py:356
  34.8 3.6 %collective-permute-done.8.refs_2_ = bf16[128,640]{1,0:T(8,128)(2,1)S(1)} collective-permute-done((bf16[128,640]{1,0:T(8,128)(2,1)S(1)}, bf16[128,640]{1,0:T(8,128)(2,1)S(1)}, u32[]{:S(2)}, u32[]{:S(2)}) %collective-permute-start.8) | collective-permute-done | bytes 163872 | tf_op jit(solution)/shard_map/ppermute | solution.py:351
  38.4 2.0 %collective-permute-done.9.refs_3_ = bf16[128,640]{1,0:T(8,128)(2,1)S(1)} collective-permute-done((bf16[128,640]{1,0:T(8,128)(2,1)S(1)}, bf16[128,640]{1,0:T(8,128)(2,1)S(1)}, u32[]{:S(2)}, u32[]{:S(2)}) %collective-permute-start.9) | collective-permute-done | bytes 163872 | tf_op jit(solution)/shard_map/ppermute | solution.py:351
  40.3 1.4 %project.1.refs_0_ = bf16[144,128]{1,0:T(8,128)(2,1)S(1)} custom-call(bf16[128,640]{1,0:T(8,128)(2,1)S(1)} %get-tuple-element.34.refs_0_, bf16[128,640]{1,0:T(8,128)(2,1)S(1)} %collective-permute-done.7.refs_1_, bf16[128,640]{1,0:T(8,128)(2,1)S(1)} %collective-permute-done.8.refs_2_, bf16[128,640]{1,0:T(8,128)(2,1)S(1)} %collective-permute-done.9.refs_3_, ...), custom_call_target="tpu_custom_call" | custom-call | tf_op jit(solution)/shard_map/project/pallas_call | solution.py:417
  41.7 1.3 %collective-permute-start.10 = (bf16[144,128]{1,0:T(8,128)(2,1)S(1)}, bf16[144,128]{1,0:T(8,128)(2,1)S(1)}, u32[]{:S(2)}, u32[]{:S(2)}) collective-permute-start(bf16[144,128]{1,0:T(8,128)(2,1)S(1)} %project.1.refs_0_), channel_id=1, source_target_pairs={{0,8},{8,0},{16,24},{24,16},{32,40},{40,32},{48,56},{56,48},{64,72... | collective-permute-start | bytes 110600 | tf_op jit(solution)/shard_map/ppermute | solution.py:431
  43.0 1.6 %collective-permute-start.11 = (bf16[144,128]{1,0:T(8,128)(2,1)S(1)}, bf16[144,128]{1,0:T(8,128)(2,1)S(1)}, u32[]{:S(2)}, u32[]{:S(2)}) collective-permute-start(bf16[144,128]{1,0:T(8,128)(2,1)S(1)} %project.1.refs_0_), channel_id=1, source_target_pairs={{0,32},{8,40},{16,48},{24,56},{32,0},{40,8},{48,16},{56,24},{64,96... | collective-permute-start | bytes 110600 | tf_op jit(solution)/shard_map/ppermute | solution.py:431
  44.6 1.3 %collective-permute-done.11.refs_2_ = bf16[144,128]{1,0:T(8,128)(2,1)S(1)} collective-permute-done((bf16[144,128]{1,0:T(8,128)(2,1)S(1)}, bf16[144,128]{1,0:T(8,128)(2,1)S(1)}, u32[]{:S(2)}, u32[]{:S(2)}) %collective-permute-start.11) | collective-permute-done | bytes 36896 | tf_op jit(solution)/shard_map/ppermute | solution.py:431
  46.0 2.4 %collective-permute-done.12.refs_3_ = bf16[144,128]{1,0:T(8,128)(2,1)S(1)} collective-permute-done((bf16[144,128]{1,0:T(8,128)(2,1)S(1)}, bf16[144,128]{1,0:T(8,128)(2,1)S(1)}, u32[]{:S(2)}, u32[]{:S(2)}) %collective-permute-start.12) | collective-permute-done | bytes 36896 | tf_op jit(solution)/shard_map/ppermute | solution.py:431
  48.6 2.2 %collective-permute-start.13 = (bf16[144,128]{1,0:T(8,128)(2,1)S(1)}, bf16[144,128]{1,0:T(8,128)(2,1)S(1)}, u32[]{:S(2)}, u32[]{:S(2)}) collective-permute-start(bf16[144,128]{1,0:T(8,128)(2,1)S(1)} %middle_merge.1.refs_0_), channel_id=1, source_target_pairs={{0,24},{8,16},{16,8},{24,0},{32,56},{40,48},{48,40},{56,32},{64,88... | collective-permute-start | bytes 110600 | tf_op jit(solution)/shard_map/ppermute | solution.py:431
  50.9 2.2 %collective-permute-start.14 = (bf16[144,128]{1,0:T(8,128)(2,1)S(1)}, bf16[144,128]{1,0:T(8,128)(2,1)S(1)}, u32[]{:S(2)}, u32[]{:S(2)}) collective-permute-start(bf16[144,128]{1,0:T(8,128)(2,1)S(1)} %middle_merge.1.refs_0_), channel_id=1, source_target_pairs={{0,96},{8,104},{16,112},{24,120},{32,64},{40,72},{48,80},{56,88},{... | collective-permute-start | bytes 110600 | tf_op jit(solution)/shard_map/ppermute | solution.py:431
  53.8 1.1 %collective-permute-done.14.refs_2_ = bf16[144,128]{1,0:T(8,128)(2,1)S(1)} collective-permute-done((bf16[144,128]{1,0:T(8,128)(2,1)S(1)}, bf16[144,128]{1,0:T(8,128)(2,1)S(1)}, u32[]{:S(2)}, u32[]{:S(2)}) %collective-permute-start.14) | collective-permute-done | bytes 36896 | tf_op jit(solution)/shard_map/ppermute | solution.py:431
  54.9 4.3 %collective-permute-done.15.refs_3_ = bf16[144,128]{1,0:T(8,128)(2,1)S(1)} collective-permute-done((bf16[144,128]{1,0:T(8,128)(2,1)S(1)}, bf16[144,128]{1,0:T(8,128)(2,1)S(1)}, u32[]{:S(2)}, u32[]{:S(2)}) %collective-permute-start.15) | collective-permute-done | bytes 36896 | tf_op jit(solution)/shard_map/ppermute | solution.py:431
  59.5 4.6 %collective-permute-start.16 = (bf16[4,2,16,128]{3,2,1,0:T(8,128)(2,1)S(1)}, bf16[4,2,16,128]{3,2,1,0:T(8,128)(2,1)S(1)}, u32[]{:S(2)}, u32[]{:S(2)}) collective-permute-start(bf16[4,2,16,128]{3,2,1,0:T(8,128)(2,1)S(1)} %finish.1.own_ref), channel_id=1, source_target_pairs={{0,4},{4,0},{1,5},{5,1},{2,6},{6,2},{3,7},{7,3},{8,12},{12,8},{9,1... | collective-permute-start | bytes 98312 | tf_op jit(solution)/shard_map/ppermute | solution.py:449
  64.9 1.2 %place.1 = bf16[4,4,16,128]{3,2,1,0:T(8,128)(2,1)} custom-call(s32[8]{0:T(128)S(1)} %concatenate.3.info_ref, bf16[4,2,16,128]{3,2,1,0:T(8,128)(2,1)S(1)} %finish.1.own_ref, bf16[4,2,16,128]{3,2,1,0:T(8,128)(2,1)S(1)} %collective-permute-done.16.other_ref), custom_call_target="tpu_custom_call" | custom-call | tf_op jit(solution)/shard_map/place/pallas_call | solution.py:450
  (23 shorter events, 8.0 us)
Async XLA Ops:
  3.3 7.5 %collective-permute-start.2 = (bf16[2,64,640]{2,1,0:T(8,128)(2,1)S(1)}, bf16[2,64,640]{2,1,0:T(8,128)(2,1)S(1)}, u32[]{:S(2)}, u32[]{:S(2)}) collective-permute-start(bf16[2,64,640]{2,1,0:T(8,128)(2,1)S(1)} %get-tuple-element.23), channel_id=1, source_target_pairs={{0,2},{1,3},{2,0},{3,1},{4,6},{5,7},{6,4},{7,5},{8,10},{9,11},{10,... | collective-permute-start | bytes 491528 | tf_op jit(solution)/shard_map/ppermute | solution.py:351
  7.1 7.5 %collective-permute-start = (bf16[2,64,640]{2,1,0:T(8,128)(2,1)S(1)}, bf16[2,64,640]{2,1,0:T(8,128)(2,1)S(1)}, u32[]{:S(2)}, u32[]{:S(2)}) collective-permute-start(bf16[2,64,640]{2,1,0:T(8,128)(2,1)S(1)} %get-tuple-element.23), channel_id=1, source_target_pairs={{0,1},{1,0},{2,3},{3,2},{4,5},{5,4},{6,7},{7,6},{8,9},{9,8},{10,11... | collective-permute-start | bytes 491528 | tf_op jit(solution)/shard_map/ppermute | solution.py:351
  7.5 8.7 %collective-permute-start.1 = (bf16[2,64,640]{2,1,0:T(8,128)(2,1)S(1)}, bf16[2,64,640]{2,1,0:T(8,128)(2,1)S(1)}, u32[]{:S(2)}, u32[]{:S(2)}) collective-permute-start(bf16[2,64,640]{2,1,0:T(8,128)(2,1)S(1)} %get-tuple-element.23), channel_id=1, source_target_pairs={{0,3},{1,2},{2,1},{3,0},{4,7},{5,6},{6,5},{7,4},{8,11},{9,10},{10,... | collective-permute-start | bytes 491528 | tf_op jit(solution)/shard_map/ppermute | solution.py:351
  10.9 5.4 %collective-permute-start.5 = (bf16[2,64,640]{2,1,0:T(8,128)(2,1)S(1)}, bf16[2,64,640]{2,1,0:T(8,128)(2,1)S(1)}, u32[]{:S(2)}, u32[]{:S(2)}) collective-permute-start(bf16[2,64,640]{2,1,0:T(8,128)(2,1)S(1)} %collective-permute-done.2.q3_ref), channel_id=1, source_target_pairs={{0,4},{4,0},{1,5},{5,1},{2,6},{6,2},{3,7},{7,3},{8,12},{12,8},{9,1... | collective-permute-start | bytes 491528 | tf_op jit(solution)/shard_map/ppermute | solution.py:379
  14.7 2.6 %collective-permute-start.3 = (bf16[2,64,640]{2,1,0:T(8,128)(2,1)S(1)}, bf16[2,64,640]{2,1,0:T(8,128)(2,1)S(1)}, u32[]{:S(2)}, u32[]{:S(2)}) collective-permute-start(bf16[2,64,640]{2,1,0:T(8,128)(2,1)S(1)} %collective-permute-done.q1_ref), channel_id=1, source_target_pairs={{0,4},{4,0},{1,5},{5,1},{2,6},{6,2},{3,7},{7,3},{8,12},{12,8},{9,1... | collective-permute-start | bytes 491528 | tf_op jit(solution)/shard_map/ppermute | solution.py:379
  16.2 1.4 %collective-permute-start.4 = (bf16[2,64,640]{2,1,0:T(8,128)(2,1)S(1)}, bf16[2,64,640]{2,1,0:T(8,128)(2,1)S(1)}, u32[]{:S(2)}, u32[]{:S(2)}) collective-permute-start(bf16[2,64,640]{2,1,0:T(8,128)(2,1)S(1)} %collective-permute-done.1.q2_ref), channel_id=1, source_target_pairs={{0,4},{4,0},{1,5},{5,1},{2,6},{6,2},{3,7},{7,3},{8,12},{12,8},{9,1... | collective-permute-start | bytes 491528 | tf_op jit(solution)/shard_map/ppermute | solution.py:379
  23.9 4.4 %collective-permute-start.6 = (bf16[4,128,640]{2,1,0:T(8,128)(2,1)S(1)}, bf16[4,128,640]{2,1,0:T(8,128)(2,1)S(1)}, u32[]{:S(2)}, u32[]{:S(2)}) collective-permute-start(bf16[4,128,640]{2,1,0:T(8,128)(2,1)S(1)} %get-tuple-element.29), channel_id=1, source_target_pairs={{0,4},{4,0},{1,5},{5,1},{2,6},{6,2},{3,7},{7,3},{8,12},{12,8},{9,1... | collective-permute-start | bytes 1966088 | tf_op jit(solution)/shard_map/ppermute | solution.py:406
  24.2 16.1 %copy-start = (bf16[16,512,128]{2,1,0:T(8,128)(2,1)S(1)}, bf16[16,512,128]{2,1,0:T(8,128)(2,1)}, u32[]{:S(2)}) copy-start(bf16[16,512,128]{2,1,0:T(8,128)(2,1)} %refs_5_.1) | copy-start | bytes 6291460
  29.2 5.6 %collective-permute-start.7 = (bf16[128,640]{1,0:T(8,128)(2,1)S(1)}, bf16[128,640]{1,0:T(8,128)(2,1)S(1)}, u32[]{:S(2)}, u32[]{:S(2)}) collective-permute-start(bf16[128,640]{1,0:T(8,128)(2,1)S(1)} %get-tuple-element.35), channel_id=1, source_target_pairs={{0,1},{1,0},{2,3},{3,2},{4,5},{5,4},{6,7},{7,6},{8,9},{9,8},{10,11... | collective-permute-start | bytes 491528 | tf_op jit(solution)/shard_map/ppermute | solution.py:351
  30.3 8.0 %collective-permute-start.8 = (bf16[128,640]{1,0:T(8,128)(2,1)S(1)}, bf16[128,640]{1,0:T(8,128)(2,1)S(1)}, u32[]{:S(2)}, u32[]{:S(2)}) collective-permute-start(bf16[128,640]{1,0:T(8,128)(2,1)S(1)} %get-tuple-element.36), channel_id=1, source_target_pairs={{0,3},{1,2},{2,1},{3,0},{4,7},{5,6},{6,5},{7,4},{8,11},{9,10},{10,... | collective-permute-start | bytes 491528 | tf_op jit(solution)/shard_map/ppermute | solution.py:351
  31.9 8.5 %collective-permute-start.9 = (bf16[128,640]{1,0:T(8,128)(2,1)S(1)}, bf16[128,640]{1,0:T(8,128)(2,1)S(1)}, u32[]{:S(2)}, u32[]{:S(2)}) collective-permute-start(bf16[128,640]{1,0:T(8,128)(2,1)S(1)} %get-tuple-element.37), channel_id=1, source_target_pairs={{0,2},{1,3},{2,0},{3,1},{4,6},{5,7},{6,4},{7,5},{8,10},{9,11},{10,... | collective-permute-start | bytes 491528 | tf_op jit(solution)/shard_map/ppermute | solution.py:351
  41.7 2.9 %collective-permute-start.10 = (bf16[144,128]{1,0:T(8,128)(2,1)S(1)}, bf16[144,128]{1,0:T(8,128)(2,1)S(1)}, u32[]{:S(2)}, u32[]{:S(2)}) collective-permute-start(bf16[144,128]{1,0:T(8,128)(2,1)S(1)} %project.1.refs_0_), channel_id=1, source_target_pairs={{0,8},{8,0},{16,24},{24,16},{32,40},{40,32},{48,56},{56,48},{64,72... | collective-permute-start | bytes 110600 | tf_op jit(solution)/shard_map/ppermute | solution.py:431
  43.0 3.0 %collective-permute-start.11 = (bf16[144,128]{1,0:T(8,128)(2,1)S(1)}, bf16[144,128]{1,0:T(8,128)(2,1)S(1)}, u32[]{:S(2)}, u32[]{:S(2)}) collective-permute-start(bf16[144,128]{1,0:T(8,128)(2,1)S(1)} %project.1.refs_0_), channel_id=1, source_target_pairs={{0,32},{8,40},{16,48},{24,56},{32,0},{40,8},{48,16},{56,24},{64,96... | collective-permute-start | bytes 110600 | tf_op jit(solution)/shard_map/ppermute | solution.py:431
  44.6 3.7 %collective-permute-start.12 = (bf16[144,128]{1,0:T(8,128)(2,1)S(1)}, bf16[144,128]{1,0:T(8,128)(2,1)S(1)}, u32[]{:S(2)}, u32[]{:S(2)}) collective-permute-start(bf16[144,128]{1,0:T(8,128)(2,1)S(1)} %project.1.refs_0_), channel_id=1, source_target_pairs={{0,40},{8,32},{16,56},{24,48},{32,8},{40,0},{48,24},{56,16},{64,10... | collective-permute-start | bytes 110600 | tf_op jit(solution)/shard_map/ppermute | solution.py:431
  48.6 5.2 %collective-permute-start.13 = (bf16[144,128]{1,0:T(8,128)(2,1)S(1)}, bf16[144,128]{1,0:T(8,128)(2,1)S(1)}, u32[]{:S(2)}, u32[]{:S(2)}) collective-permute-start(bf16[144,128]{1,0:T(8,128)(2,1)S(1)} %middle_merge.1.refs_0_), channel_id=1, source_target_pairs={{0,24},{8,16},{16,8},{24,0},{32,56},{40,48},{48,40},{56,32},{64,88... | collective-permute-start | bytes 110600 | tf_op jit(solution)/shard_map/ppermute | solution.py:431
  50.9 4.0 %collective-permute-start.14 = (bf16[144,128]{1,0:T(8,128)(2,1)S(1)}, bf16[144,128]{1,0:T(8,128)(2,1)S(1)}, u32[]{:S(2)}, u32[]{:S(2)}) collective-permute-start(bf16[144,128]{1,0:T(8,128)(2,1)S(1)} %middle_merge.1.refs_0_), channel_id=1, source_target_pairs={{0,96},{8,104},{16,112},{24,120},{32,64},{40,72},{48,80},{56,88},{... | collective-permute-start | bytes 110600 | tf_op jit(solution)/shard_map/ppermute | solution.py:431
  53.1 6.1 %collective-permute-start.15 = (bf16[144,128]{1,0:T(8,128)(2,1)S(1)}, bf16[144,128]{1,0:T(8,128)(2,1)S(1)}, u32[]{:S(2)}, u32[]{:S(2)}) collective-permute-start(bf16[144,128]{1,0:T(8,128)(2,1)S(1)} %middle_merge.1.refs_0_), channel_id=1, source_target_pairs={{0,120},{8,112},{16,104},{24,96},{32,88},{40,80},{48,72},{56,64},{... | collective-permute-start | bytes 110600 | tf_op jit(solution)/shard_map/ppermute | solution.py:431
  59.5 5.4 %collective-permute-start.16 = (bf16[4,2,16,128]{3,2,1,0:T(8,128)(2,1)S(1)}, bf16[4,2,16,128]{3,2,1,0:T(8,128)(2,1)S(1)}, u32[]{:S(2)}, u32[]{:S(2)}) collective-permute-start(bf16[4,2,16,128]{3,2,1,0:T(8,128)(2,1)S(1)} %finish.1.own_ref), channel_id=1, source_target_pairs={{0,4},{4,0},{1,5},{5,1},{2,6},{6,2},{3,7},{7,3},{8,12},{12,8},{9,1... | collective-permute-start | bytes 98312 | tf_op jit(solution)/shard_map/ppermute | solution.py:449

commit v7 on v5

--- a/solution.py
+++ b/solution.py
@@ -38,7 +38,25 @@
 
 
 def queries_kernel(
-    steps, info_ref, positions_hbm, q_hbm, up_hbm, new_hbm, own_ref, sent_ref, keys_ref, positions, q, up, new, lat, sems
+    steps,
+    info_ref,
+    row_ref,
+    positions_hbm,
+    lengths_hbm,
+    q_hbm,
+    up_hbm,
+    new_hbm,
+    own_ref,
+    sent_ref,
+    keys_ref,
+    limits_ref,
+    positions,
+    lengths,
+    q,
+    up,
+    new,
+    lat,
+    sems,
 ):
     pairs, heads, _ = q.shape
     requests = pairs // steps
@@ -48,12 +66,13 @@
         pltpu.make_async_copy(positions_hbm, positions, sems.at[0]),
         pltpu.make_async_copy(q_hbm, q, sems.at[1]),
         pltpu.make_async_copy(new_hbm, new, sems.at[2]),
+        pltpu.make_async_copy(lengths_hbm, lengths, sems.at[3]),
     ]
     groups = 4
     share = heads // groups
     for g in range(groups):
         at = pl.ds(g * share, share)
-        fetches.append(pltpu.make_async_copy(up_hbm.at[at], up.at[at], sems.at[3 + g]))
+        fetches.append(pltpu.make_async_copy(up_hbm.at[at], up.at[at], sems.at[4 + g]))
     for fetch in fetches:
         fetch.start()
     own_ref[:, :, key_width:] = jnp.zeros(own_ref.shape[:2] + (own_ref.shape[2] - key_width,), bf16)
@@ -65,6 +84,12 @@
     for s in range(steps):
         for b in range(requests):
             own_ref[b, s * heads : (s + 1) * heads, width:key_width] = rope[s * requests + b]
+    fetches[3].wait()
+    line = lax.broadcasted_iota(jnp.int32, limits_ref.shape, 0)
+    limits = jnp.zeros(limits_ref.shape, jnp.int32)
+    for b in range(requests):
+        limits = jnp.where(line == b, lengths[b] - row_ref[0], limits)
+    limits_ref[...] = limits
     fetches[2].wait()
     rows = jnp.concatenate([new[t].astype(f32) for t in range(steps)], axis=0)
     tail = rows[:, width:]
@@ -73,7 +98,7 @@
     q_f32 = q[:, :, :nope].astype(f32)
     for h in range(heads):
         if h % share == 0:
-            fetches[3 + h // share].wait()
+            fetches[4 + h // share].wait()
         lat[:, h, :] = jnp.dot(q_f32[:, h, :].astype(bf16), up[h], preferred_element_type=f32)
     for s in range(steps):
         for b in range(requests):
@@ -96,23 +121,24 @@
     return jnp.where(lane == 4, sum_second, out)
 
 
-def stage_kernel(cache_hbm, out_ref, sems):
+def stage_kernel(info_ref, cache_hbm, out_ref, sems):
     copies = []
     for i in range(out_ref.shape[0]):
-        copies.append(pltpu.make_async_copy(cache_hbm.at[i], out_ref.at[i], sems.at[i]))
+        copies.append(pltpu.make_async_copy(cache_hbm.at[info_ref[0] + i], out_ref.at[i], sems.at[i]))
     for copy in copies:
         copy.start()
     for copy in copies:
         copy.wait()
 
 
-def attention_kernel(scale, info_ref, own_ref, q1_ref, q2_ref, q3_ref, k_ref, out_ref, q_ref, *scores):
+def attention_kernel(scale, info_ref, limits_ref, own_ref, q1_ref, q2_ref, q3_ref, k_ref, out_ref, q_ref, *scores):
     count, owners, share, _ = q_ref.shape
     rows = owners * share
     key_width, cached = k_ref.shape[1:]
     width = out_ref.shape[2] - 128
     chunk = 1024
     first = info_ref[0]
+    base = first if k_ref.shape[0] > count else 0
     q_ref[:, 0] = own_ref[pl.ds(first, count)]
     q_ref[:, 1] = q1_ref[...]
     q_ref[:, 2] = q2_ref[...]
@@ -120,11 +146,11 @@
 
     tops = []
     for i in range(count):
-        limit = info_ref[2 + first + i] - info_ref[1]
+        limit = limits_ref[pl.ds(first + i, 1), :1]
         queries = q_ref[i].reshape(rows, -1)[:, :key_width]
         top = jnp.full((rows, 128), lowest_max, f32)
         for c in range(0, cached, chunk):
-            keys = k_ref[first + i, :, c : c + chunk]
+            keys = k_ref[base + i, :, c : c + chunk]
             part = jnp.dot(queries, keys, preferred_element_type=f32) * scale
             column = lax.broadcasted_iota(jnp.int32, (1, chunk), 1) + c
             part = jnp.where(column < limit, part, masked_score)
@@ -141,7 +167,7 @@
                 total = total + weights[:, at : at + 128]
             part = lax.dot_general(
                 weights.astype(bf16),
-                k_ref[first + i, :width, c : c + chunk],
+                k_ref[base + i, :width, c : c + chunk],
                 (((1,), (1,)), ((), ())),
                 preferred_element_type=f32,
             )
@@ -152,7 +178,7 @@
         out_ref[:, at, width:] = split_stats(tops[i], total, rows).astype(bf16).reshape(owners, share, 128)
 
 
-def fresh_kernel(scale, steps, heads, info_ref, own_ref, new_ref, out_ref):
+def fresh_kernel(scale, steps, heads, info_ref, place_ref, own_ref, new_ref, out_ref):
     requests, share, _ = own_ref.shape
     key_width = new_ref.shape[1]
     width = out_ref.shape[1] - 128
@@ -160,7 +186,7 @@
     shape = (share, fresh.shape[0])
     key = lax.broadcasted_iota(jnp.int32, shape, 1)
     step = (lax.broadcasted_iota(jnp.int32, shape, 0) // heads) % steps
-    counted = info_ref[1] == 1
+    counted = place_ref[0] == 0
     for i in range(out_ref.shape[0] // share):
         request = info_ref[0] + i
         scores = (
@@ -301,29 +327,38 @@
     anywhere = pl.BlockSpec(memory_space=pltpu.HBM)
     wide = 640
     in_hbm = functools.partial(pltpu.with_memory_space_constraint, memory_space=pltpu.HBM)
-    other_first = ((1 - core) * half).astype(jnp.int32)
-    own_queries, sent_queries, new_keys = pl.pallas_call(
+    core32 = core.astype(jnp.int32)
+    own_first = (core32 * half).reshape(1)
+    other_first = (half - core32 * half).reshape(1)
+    first_row = (slot.astype(jnp.int32) * cached).reshape(1)
+    place = lax.axis_index(("z", "x")).astype(jnp.int32).reshape(1)
+    chunk = half * steps * heads
+    own_queries, sent_queries, new_keys, limits = pl.pallas_call(
         functools.partial(queries_kernel, steps),
-        in_specs=[smem] + [anywhere] * 4,
-        out_specs=[vmem, vmem, vmem],
+        in_specs=[smem] * 2 + [anywhere] * 5,
+        out_specs=[vmem] * 4,
         out_shape=(
             jax.ShapeDtypeStruct((requests, steps * heads, wide), bf16),
             jax.ShapeDtypeStruct((half, steps * heads, wide), bf16),
             jax.ShapeDtypeStruct((pairs, key_width), bf16),
+            jax.ShapeDtypeStruct((8, 128), jnp.int32),
         ),
         scratch_shapes=[
+            pltpu.SMEM((requests,), jnp.int32),
             pltpu.SMEM((requests,), jnp.int32),
             pltpu.VMEM((pairs, heads, query_width), bf16),
             pltpu.VMEM(up_keys.shape, bf16),
             pltpu.VMEM(new_latent.shape, bf16),
             pltpu.VMEM((pairs, heads, width), f32),
-            pltpu.SemaphoreType.DMA((7,)),
+            pltpu.SemaphoreType.DMA((8,)),
         ],
         compiler_params=pltpu.CompilerParams(vmem_limit_bytes=24 * 2**20),
         name="queries",
     )(
-        other_first.reshape(1),
+        other_first,
+        first_row,
         in_hbm(positions),
+        in_hbm(context_lengths),
         in_hbm(query_heads.reshape(pairs, heads, query_width)),
         in_hbm(up_keys),
         in_hbm(new_latent),
@@ -335,57 +370,53 @@
     swap = [(0, 1), (1, 0)]
     partners = (1, 3, 2)
     got = [over_head(sent_queries, k) for k in partners]
-    own_first = (core * half).astype(jnp.int32)
-    chunk = half * steps * heads
-    at_origin = (lax.axis_index(("z", "x")) == 0).astype(jnp.int32)
     fresh = pl.pallas_call(
         functools.partial(fresh_kernel, scale, steps, heads),
-        in_specs=[smem, vmem, vmem],
+        in_specs=[smem, smem, vmem, vmem],
         out_specs=vmem,
         out_shape=jax.ShapeDtypeStruct((chunk, width + 128), bf16),
         compiler_params=small,
         cost_estimate=pl.CostEstimate(flops=10**9, bytes_accessed=4 * 10**6, transcendentals=0),
         name="fresh",
-    )(jnp.stack([own_first, at_origin]), own_queries, new_keys)
-    cache = pl.pallas_call(
+    )(own_first, place, own_queries, new_keys)
+    cache = jnp.swapaxes(latent_cache, 1, 2)
+    staged_shape = pltpu.VMEM((half, key_width, cached), bf16)
+    in_vmem = functools.partial(pltpu.with_memory_space_constraint, memory_space=pltpu.VMEM)
+    staged = pl.pallas_call(
         stage_kernel,
-        in_specs=[anywhere],
-        out_specs=vmem,
-        out_shape=pltpu.VMEM((requests, key_width, cached), bf16),
-        scratch_shapes=[pltpu.SemaphoreType.DMA((requests,))],
-        compiler_params=small,
-        cost_estimate=pl.CostEstimate(flops=0, bytes_accessed=2 * requests * key_width * cached, transcendentals=0),
+        in_specs=[smem, anywhere],
+        out_specs=vmem,
+        out_shape=staged_shape,
+        scratch_shapes=[pltpu.SemaphoreType.DMA((half,))],
+        compiler_params=small,
+        cost_estimate=pl.CostEstimate(flops=0, bytes_accessed=2 * half * key_width * cached, transcendentals=0),
         name="stage",
-    )(in_hbm(jnp.swapaxes(latent_cache, 1, 2)))
-    cache = pltpu.with_memory_space_constraint(cache, memory_space=pltpu.VMEM)
-    got[2], cache = lax.optimization_barrier((got[2], cache))
+    )(other_first, in_hbm(cache))
+    got[2], staged = lax.optimization_barrier((got[2], staged))
     passed = [lax.ppermute(g, "core", swap) for g in got]
     got, passed = lax.optimization_barrier((got, passed))
 
     rows = owners * steps * heads
 
-    def attend(first, got):
-        info = jnp.concatenate([jnp.stack([first, slot.astype(jnp.int32) * cached]), context_lengths])
+    def attend(first, got, keys):
         return pl.pallas_call(
             functools.partial(attention_kernel, scale),
-            in_specs=[smem] + [vmem] * 5,
+            in_specs=[smem] + [vmem] * 6,
             out_specs=vmem,
-            scratch_shapes=[
-                pltpu.VMEM((half, owners, steps * heads, wide), bf16),
-            ]
+            scratch_shapes=[pltpu.VMEM((half, owners, steps * heads, wide), bf16)]
             + [pltpu.VMEM((rows, cached), f32)] * half,
             out_shape=jax.ShapeDtypeStruct((owners, chunk, width + 128), bf16),
-            compiler_params=pltpu.CompilerParams(vmem_limit_bytes=24 * 2**20),
+            compiler_params=pltpu.CompilerParams(vmem_limit_bytes=18 * 2**20),
             cost_estimate=pl.CostEstimate(
                 flops=2 * half * rows * cached * (key_width + width),
                 bytes_accessed=half * cached * key_width * 2,
                 transcendentals=half * rows * cached,
             ),
             name="attention",
-        )(info, own_queries, *got, cache)
-
-    other_part = lax.ppermute(attend(other_first, got), "core", swap)
-    own_part = attend(own_first, passed)
+        )(first, limits, own_queries, *got, keys)
+
+    other_part = lax.ppermute(attend(other_first, got, in_vmem(staged)), "core", swap)
+    own_part = attend(own_first, passed, cache)
     sent = pl.pallas_call(
         pair_kernel,
         in_specs=[vmem] * 2,
@@ -418,7 +449,7 @@
         out_shape=jax.ShapeDtypeStruct(part.shape, bf16),
         compiler_params=small,
         name="middle_merge",
-    )(part, *[over_plane(part, k) for k in (1, 4, 5)])
+    )(part, *[over_plane(part, k) for k in (5, 4, 1)])
     own = pl.pallas_call(
         finish_kernel,
         in_specs=[vmem] * 4,
@@ -426,7 +457,7 @@
         out_shape=jax.ShapeDtypeStruct((steps, half, heads, value_width), bf16),
         compiler_params=small,
         name="finish",
-    )(part, *[over_plane(part, k) for k in (3, 12, 15)])
+    )(part, *[over_plane(part, k) for k in (15, 12, 3)])
     theirs = lax.ppermute(own, "core", swap)
     return pl.pallas_call(
         place_kernel,
@@ -435,7 +466,7 @@
         out_shape=jax.ShapeDtypeStruct((steps, requests, heads, value_width), bf16),
         compiler_params=small,
         name="place",
-    )(own_first.reshape(1), own, theirs)
+    )(own_first, own, theirs)
 
 
 def solution(mesh):

time: 72.4 us -> 59.4 us (0.82)
  local copies, waits for them, and re-layouts: 12.6 us -> 0.02 us
  Pallas kernels: 19.1 us -> 16.2 us
  waiting for transfers between devices: 17.3 us -> 20 us
    unnamed x14 -> x8, local copies, waits for them, and re-layouts: 12.6 us -> 0.02 us
    ppermute x6, waiting for transfers between devices: 6.4 us -> 11.4 us  [over_head(): return lax.ppermute(array, 'head', [(i, i ^ k) for i in range(owners)])]
    ppermute x6, waiting for transfers between devices: 9.05 us -> 6.56 us  [over_plane(): return lax.ppermute(array, ('z', 'x'), [(i, i ^ k) for i in range(plane)])]
    pallas_call x2, Pallas kernels: 8.67 us -> 7.06 us  [attend(): pl.pallas_call(functools.partial(attention_kernel, scale), in_specs=[smem...]
    pallas_call x1, Pallas kernels: 3.81 us -> 2.54 us  [on_device(): pl.pallas_call(stage_kernel, in_specs=[smem, anywhere], out_specs=vmem, o...]
    ppermute x6, starting transfers between devices: 8.08 us -> 8.96 us  [over_plane(): return lax.ppermute(array, ('z', 'x'), [(i, i ^ k) for i in range(plane)])]
  transfers between devices with their start and end apart: 17 -> 17, of which waited for: 11 -> 13; matrix products, arithmetic and copies ran while one was open for 0% -> 0% of each run, Pallas kernels for 12% -> 11%
where the time goes in v7:
time: 59.4 us; the launch traced here: 59.2 us
  starting transfers between devices  23 us (39%)
  waiting for transfers between devices  20 us (34%)
  Pallas kernels  16.2 us (27%)
    ppermute x6, waiting for transfers between devices, over_head(): return lax.ppermute(array, 'head', [(i, i ^ k) for i in range(owners)])  11.4 us
    ppermute x6, starting transfers between devices, over_plane(): return lax.ppermute(array, ('z', 'x'), [(i, i ^ k) for i in range(plane)])  8.96 us
    ppermute x6, starting transfers between devices, over_head(): return lax.ppermute(array, 'head', [(i, i ^ k) for i in range(owners)])  7.88 us
    pallas_call x2, Pallas kernels, attend(): pl.pallas_call(functools.partial(attention_kernel, scale), in_specs=[smem...  7.06 us
    ppermute x6, waiting for transfers between devices, over_plane(): return lax.ppermute(array, ('z', 'x'), [(i, i ^ k) for i in range(plane)])  6.56 us
    ppermute x1, starting transfers between devices, on_device(): theirs = lax.ppermute(own, 'core', swap)  3.71 us
    pallas_call x1, Pallas kernels, on_device(): pl.pallas_call(stage_kernel, in_specs=[smem, anywhere], out_specs=vmem, o...  2.54 us
    ppermute x3, starting transfers between devices, on_device(): passed = [lax.ppermute(g, 'core', swap) for g in got]  2.06 us
  transfers between devices with their start and end apart: 17, of which 13 were waited for; matrix products, arithmetic and copies ran while one was open for 0% of the time, Pallas kernels for 11%

profile of v7, /device:TPU:1, one launch (start us, length us, event | category | flops | bytes accessed | tf_op | source)
XLA Modules:
  0.0 59.2 jit_solution(5143332003718246804)
XLA Ops:
  0.0 2.0 %queries.1 = (bf16[4,64,640]{2,1,0:T(8,128)(2,1)S(1)}, bf16[2,64,640]{2,1,0:T(8,128)(2,1)S(1)}, bf16[16,576]{1,0:T(8,128)(2,1)S(1)}, s32[8,128]{1,0:T(8,128)S(1)}) custom-call(s32[1]{0:T(128)} %bitcast.1.info_ref, s32[1]{0:T(128)} %bitcast.2.row_ref, s32[4]{0:T(128)} %positions_hbm.1, s32[4]{0:T(128)} %lengths_hbm.1, bf16[16,16,192]{2,1,0:T(8,128)(2,1)} %bitcast.10, ...), custom_call_target="tpu_custom_call" | custom-call | tf_op jit(solution)/shard_map/queries/pallas_call | solution.py:336
  2.0 3.8 %collective-permute-start.2 = (bf16[2,64,640]{2,1,0:T(8,128)(2,1)S(1)}, bf16[2,64,640]{2,1,0:T(8,128)(2,1)S(1)}, u32[]{:S(2)}, u32[]{:S(2)}) collective-permute-start(bf16[2,64,640]{2,1,0:T(8,128)(2,1)S(1)} %get-tuple-element.23), channel_id=1, source_target_pairs={{0,2},{1,3},{2,0},{3,1},{4,6},{5,7},{6,4},{7,5},{8,10},{9,11},{10,... | collective-permute-start | bytes 491528 | tf_op jit(solution)/shard_map/ppermute | solution.py:368
  6.6 2.5 %stage.1.k_ref = bf16[2,576,2048]{2,1,0:T(8,128)(2,1)S(1)} custom-call(s32[1]{0:T(128)} %bitcast.1.info_ref, bf16[4,576,2048]{2,1,0:T(8,128)(2,1)} %bitcast.6), custom_call_target="tpu_custom_call" | custom-call | bytes 4718592 | tf_op jit(solution)/shard_map/stage/pallas_call | solution.py:385
  9.5 3.9 %collective-permute-done.q1_ref = bf16[2,64,640]{2,1,0:T(8,128)(2,1)S(1)} collective-permute-done((bf16[2,64,640]{2,1,0:T(8,128)(2,1)S(1)}, bf16[2,64,640]{2,1,0:T(8,128)(2,1)S(1)}, u32[]{:S(2)}, u32[]{:S(2)}) %collective-permute-start) | collective-permute-done | bytes 163872 | tf_op jit(solution)/shard_map/ppermute | solution.py:368
  13.4 1.5 %collective-permute-start.3 = (bf16[2,64,640]{2,1,0:T(8,128)(2,1)S(1)}, bf16[2,64,640]{2,1,0:T(8,128)(2,1)S(1)}, u32[]{:S(2)}, u32[]{:S(2)}) collective-permute-start(bf16[2,64,640]{2,1,0:T(8,128)(2,1)S(1)} %collective-permute-done.q1_ref), channel_id=1, source_target_pairs={{0,4},{4,0},{1,5},{5,1},{2,6},{6,2},{3,7},{7,3},{8,12},{12,8},{9,1... | collective-permute-start | bytes 491528 | tf_op jit(solution)/shard_map/ppermute | solution.py:396
  16.6 3.5 %attention.2 = bf16[4,128,640]{2,1,0:T(8,128)(2,1)S(1)} custom-call(s32[1]{0:T(128)} %bitcast.1.info_ref, s32[8,128]{1,0:T(8,128)S(1)} %get-tuple-element.21.limits_ref, bf16[4,64,640]{2,1,0:T(8,128)(2,1)S(1)} %get-tuple-element.22.own_ref, bf16[2,64,640]{2,1,0:T(8,128)(2,1)S(1)} %collective-permute-done.q1_ref, ...), custom_call_target="tpu_custom_call" | custom-call | flops 2281701376 | bytes 4718592 | tf_op jit(solution)/shard_map/attention/pallas_call | solution.py:402
  20.5 3.5 %attention.3.b_ref = bf16[4,128,640]{2,1,0:T(8,128)(2,1)S(1)} custom-call(s32[1]{0:T(128)} %bitcast.info_ref, s32[8,128]{1,0:T(8,128)S(1)} %get-tuple-element.21.limits_ref, bf16[4,64,640]{2,1,0:T(8,128)(2,1)S(1)} %get-tuple-element.22.own_ref, bf16[2,64,640]{2,1,0:T(8,128)(2,1)S(1)} %collective-permute-done.3.q1_ref, ...), custom_call_target="tpu_custom_call" | custom-call | flops 2281701376 | bytes 4718592 | tf_op jit(solution)/shard_map/attention/pallas_call | solution.py:402
  24.0 1.5 %pair_merge.1 = (bf16[128,640]{1,0:T(8,128)(2,1)S(1)}, bf16[128,640]{1,0:T(8,128)(2,1)}, bf16[128,640]{1,0:T(8,128)(2,1)S(1)}, bf16[128,640]{1,0:T(8,128)(2,1)S(1)}) custom-call(bf16[4,128,640]{2,1,0:T(8,128)(2,1)S(1)} %collective-permute-done.6.a_ref, bf16[4,128,640]{2,1,0:T(8,128)(2,1)S(1)} %attention.3.b_ref), custom_call_target="tpu_custom_call" | custom-call | tf_op jit(solution)/shard_map/pair_merge/pallas_call | solution.py:420
  25.5 1.1 %collective-permute-start.7 = (bf16[128,640]{1,0:T(8,128)(2,1)}, bf16[128,640]{1,0:T(8,128)(2,1)S(1)}, u32[]{:S(2)}, u32[]{:S(2)}) collective-permute-start(bf16[128,640]{1,0:T(8,128)(2,1)} %get-tuple-element.33), channel_id=1, source_target_pairs={{0,1},{1,0},{2,3},{3,2},{4,5},{5,4},{6,7},{7,6},{8,9},{9,8},{10,11... | collective-permute-start | bytes 491528 | tf_op jit(solution)/shard_map/ppermute | solution.py:368
  26.6 1.5 %collective-permute-start.8 = (bf16[128,640]{1,0:T(8,128)(2,1)S(1)}, bf16[128,640]{1,0:T(8,128)(2,1)S(1)}, u32[]{:S(2)}, u32[]{:S(2)}) collective-permute-start(bf16[128,640]{1,0:T(8,128)(2,1)S(1)} %get-tuple-element.34), channel_id=1, source_target_pairs={{0,3},{1,2},{2,1},{3,0},{4,7},{5,6},{6,5},{7,4},{8,11},{9,10},{10,... | collective-permute-start | bytes 491528 | tf_op jit(solution)/shard_map/ppermute | solution.py:368
  28.1 0.7 %collective-permute-start.9 = (bf16[128,640]{1,0:T(8,128)(2,1)S(1)}, bf16[128,640]{1,0:T(8,128)(2,1)S(1)}, u32[]{:S(2)}, u32[]{:S(2)}) collective-permute-start(bf16[128,640]{1,0:T(8,128)(2,1)S(1)} %get-tuple-element.35), channel_id=1, source_target_pairs={{0,2},{1,3},{2,0},{3,1},{4,6},{5,7},{6,4},{7,5},{8,10},{9,11},{10,... | collective-permute-start | bytes 491528 | tf_op jit(solution)/shard_map/ppermute | solution.py:368
  29.4 1.9 %collective-permute-done.7.refs_1_ = bf16[128,640]{1,0:T(8,128)(2,1)S(1)} collective-permute-done((bf16[128,640]{1,0:T(8,128)(2,1)}, bf16[128,640]{1,0:T(8,128)(2,1)S(1)}, u32[]{:S(2)}, u32[]{:S(2)}) %collective-permute-start.7) | collective-permute-done | bytes 163872 | tf_op jit(solution)/shard_map/ppermute | solution.py:368
  31.3 1.8 %collective-permute-done.8.refs_2_ = bf16[128,640]{1,0:T(8,128)(2,1)S(1)} collective-permute-done((bf16[128,640]{1,0:T(8,128)(2,1)S(1)}, bf16[128,640]{1,0:T(8,128)(2,1)S(1)}, u32[]{:S(2)}, u32[]{:S(2)}) %collective-permute-start.8) | collective-permute-done | bytes 163872 | tf_op jit(solution)/shard_map/ppermute | solution.py:368
  33.1 3.5 %collective-permute-done.9.refs_3_ = bf16[128,640]{1,0:T(8,128)(2,1)S(1)} collective-permute-done((bf16[128,640]{1,0:T(8,128)(2,1)S(1)}, bf16[128,640]{1,0:T(8,128)(2,1)S(1)}, u32[]{:S(2)}, u32[]{:S(2)}) %collective-permute-start.9) | collective-permute-done | bytes 163872 | tf_op jit(solution)/shard_map/ppermute | solution.py:368
  36.6 1.4 %project.1.refs_0_ = bf16[144,128]{1,0:T(8,128)(2,1)S(1)} custom-call(bf16[128,640]{1,0:T(8,128)(2,1)S(1)} %get-tuple-element.32.refs_0_, bf16[128,640]{1,0:T(8,128)(2,1)S(1)} %collective-permute-done.7.refs_1_, bf16[128,640]{1,0:T(8,128)(2,1)S(1)} %collective-permute-done.8.refs_2_, bf16[128,640]{1,0:T(8,128)(2,1)S(1)} %collective-permute-done.9.refs_3_, ...), custom_call_target="tpu_custom_call" | custom-call | tf_op jit(solution)/shard_map/project/pallas_call | solution.py:429
  38.0 2.6 %collective-permute-start.10 = (bf16[144,128]{1,0:T(8,128)(2,1)S(1)}, bf16[144,128]{1,0:T(8,128)(2,1)S(1)}, u32[]{:S(2)}, u32[]{:S(2)}) collective-permute-start(bf16[144,128]{1,0:T(8,128)(2,1)S(1)} %project.1.refs_0_), channel_id=1, source_target_pairs={{0,40},{8,32},{16,56},{24,48},{32,8},{40,0},{48,24},{56,16},{64,10... | collective-permute-start | bytes 110600 | tf_op jit(solution)/shard_map/ppermute | solution.py:443
  41.0 1.0 %collective-permute-done.10.refs_1_ = bf16[144,128]{1,0:T(8,128)(2,1)S(1)} collective-permute-done((bf16[144,128]{1,0:T(8,128)(2,1)S(1)}, bf16[144,128]{1,0:T(8,128)(2,1)S(1)}, u32[]{:S(2)}, u32[]{:S(2)}) %collective-permute-start.10) | collective-permute-done | bytes 36896 | tf_op jit(solution)/shard_map/ppermute | solution.py:443
  42.0 1.9 %collective-permute-done.11.refs_2_ = bf16[144,128]{1,0:T(8,128)(2,1)S(1)} collective-permute-done((bf16[144,128]{1,0:T(8,128)(2,1)S(1)}, bf16[144,128]{1,0:T(8,128)(2,1)S(1)}, u32[]{:S(2)}, u32[]{:S(2)}) %collective-permute-start.11) | collective-permute-done | bytes 36896 | tf_op jit(solution)/shard_map/ppermute | solution.py:443
  44.1 5.1 %collective-permute-start.13 = (bf16[144,128]{1,0:T(8,128)(2,1)S(1)}, bf16[144,128]{1,0:T(8,128)(2,1)S(1)}, u32[]{:S(2)}, u32[]{:S(2)}) collective-permute-start(bf16[144,128]{1,0:T(8,128)(2,1)S(1)} %middle_merge.1.refs_0_), channel_id=1, source_target_pairs={{0,120},{8,112},{16,104},{24,96},{32,88},{40,80},{48,72},{56,64},{... | collective-permute-start | bytes 110600 | tf_op jit(solution)/shard_map/ppermute | solution.py:443
  49.2 0.9 %collective-permute-start.15 = (bf16[144,128]{1,0:T(8,128)(2,1)S(1)}, bf16[144,128]{1,0:T(8,128)(2,1)S(1)}, u32[]{:S(2)}, u32[]{:S(2)}) collective-permute-start(bf16[144,128]{1,0:T(8,128)(2,1)S(1)} %middle_merge.1.refs_0_), channel_id=1, source_target_pairs={{0,24},{8,16},{16,8},{24,0},{32,56},{40,48},{48,40},{56,32},{64,88... | collective-permute-start | bytes 110600 | tf_op jit(solution)/shard_map/ppermute | solution.py:443
  50.5 3.2 %collective-permute-done.14.refs_2_ = bf16[144,128]{1,0:T(8,128)(2,1)S(1)} collective-permute-done((bf16[144,128]{1,0:T(8,128)(2,1)S(1)}, bf16[144,128]{1,0:T(8,128)(2,1)S(1)}, u32[]{:S(2)}, u32[]{:S(2)}) %collective-permute-start.14) | collective-permute-done | bytes 36896 | tf_op jit(solution)/shard_map/ppermute | solution.py:443
  54.0 3.7 %collective-permute-start.16 = (bf16[4,2,16,128]{3,2,1,0:T(8,128)(2,1)S(1)}, bf16[4,2,16,128]{3,2,1,0:T(8,128)(2,1)S(1)}, u32[]{:S(2)}, u32[]{:S(2)}) collective-permute-start(bf16[4,2,16,128]{3,2,1,0:T(8,128)(2,1)S(1)} %finish.1.own_ref), channel_id=1, source_target_pairs={{0,4},{4,0},{1,5},{5,1},{2,6},{6,2},{3,7},{7,3},{8,12},{12,8},{9,1... | collective-permute-start | bytes 98312 | tf_op jit(solution)/shard_map/ppermute | solution.py:461
  57.8 0.9 %collective-permute-done.16.other_ref = bf16[4,2,16,128]{3,2,1,0:T(8,128)(2,1)S(1)} collective-permute-done((bf16[4,2,16,128]{3,2,1,0:T(8,128)(2,1)S(1)}, bf16[4,2,16,128]{3,2,1,0:T(8,128)(2,1)S(1)}, u32[]{:S(2)}, u32[]{:S(2)}) %collective-permute-start.16) | collective-permute-done | bytes 32800 | tf_op jit(solution)/shard_map/ppermute | solution.py:461
  58.6 0.6 %place.1 = bf16[4,4,16,128]{3,2,1,0:T(8,128)(2,1)} custom-call(s32[1]{0:T(128)} %bitcast.info_ref, bf16[4,2,16,128]{3,2,1,0:T(8,128)(2,1)S(1)} %finish.1.own_ref, bf16[4,2,16,128]{3,2,1,0:T(8,128)(2,1)S(1)} %collective-permute-done.16.other_ref), custom_call_target="tpu_custom_call" | custom-call | tf_op jit(solution)/shard_map/place/pallas_call | solution.py:462
  (29 shorter events, 5.1 us)
Async XLA Ops:
  2.0 7.5 %collective-permute-start.2 = (bf16[2,64,640]{2,1,0:T(8,128)(2,1)S(1)}, bf16[2,64,640]{2,1,0:T(8,128)(2,1)S(1)}, u32[]{:S(2)}, u32[]{:S(2)}) collective-permute-start(bf16[2,64,640]{2,1,0:T(8,128)(2,1)S(1)} %get-tuple-element.23), channel_id=1, source_target_pairs={{0,2},{1,3},{2,0},{3,1},{4,6},{5,7},{6,4},{7,5},{8,10},{9,11},{10,... | collective-permute-start | bytes 491528 | tf_op jit(solution)/shard_map/ppermute | solution.py:368
  5.9 7.5 %collective-permute-start = (bf16[2,64,640]{2,1,0:T(8,128)(2,1)S(1)}, bf16[2,64,640]{2,1,0:T(8,128)(2,1)S(1)}, u32[]{:S(2)}, u32[]{:S(2)}) collective-permute-start(bf16[2,64,640]{2,1,0:T(8,128)(2,1)S(1)} %get-tuple-element.23), channel_id=1, source_target_pairs={{0,1},{1,0},{2,3},{3,2},{4,5},{5,4},{6,7},{7,6},{8,9},{9,8},{10,11... | collective-permute-start | bytes 491528 | tf_op jit(solution)/shard_map/ppermute | solution.py:368
  6.3 8.7 %collective-permute-start.1 = (bf16[2,64,640]{2,1,0:T(8,128)(2,1)S(1)}, bf16[2,64,640]{2,1,0:T(8,128)(2,1)S(1)}, u32[]{:S(2)}, u32[]{:S(2)}) collective-permute-start(bf16[2,64,640]{2,1,0:T(8,128)(2,1)S(1)} %get-tuple-element.23), channel_id=1, source_target_pairs={{0,3},{1,2},{2,1},{3,0},{4,7},{5,6},{6,5},{7,4},{8,11},{9,10},{10,... | collective-permute-start | bytes 491528 | tf_op jit(solution)/shard_map/ppermute | solution.py:368
  6.6 13.8 %slice-start = ((s8[9437184]{0:T(1024)(128)(4,1)}), s8[4194304]{0:T(1024)(128)(4,1)S(1)}, s32[]{:S(2)}) async-start(s8[9437184]{0:T(1024)(128)(4,1)} %bitcast.7), calls=%async_computation | async-start | bytes 8388608
  6.6 13.8 %slice-start.1 = ((s8[9437184]{0:T(1024)(128)(4,1)}), s8[4194304]{0:T(1024)(128)(4,1)S(1)}, s32[]{:S(2)}) async-start(s8[9437184]{0:T(1024)(128)(4,1)} %bitcast.7), calls=%async_computation.1 | async-start | bytes 8388608
  13.4 2.6 %collective-permute-start.3 = (bf16[2,64,640]{2,1,0:T(8,128)(2,1)S(1)}, bf16[2,64,640]{2,1,0:T(8,128)(2,1)S(1)}, u32[]{:S(2)}, u32[]{:S(2)}) collective-permute-start(bf16[2,64,640]{2,1,0:T(8,128)(2,1)S(1)} %collective-permute-done.q1_ref), channel_id=1, source_target_pairs={{0,4},{4,0},{1,5},{5,1},{2,6},{6,2},{3,7},{7,3},{8,12},{12,8},{9,1... | collective-permute-start | bytes 491528 | tf_op jit(solution)/shard_map/ppermute | solution.py:396
  14.9 1.4 %collective-permute-start.4 = (bf16[2,64,640]{2,1,0:T(8,128)(2,1)S(1)}, bf16[2,64,640]{2,1,0:T(8,128)(2,1)S(1)}, u32[]{:S(2)}, u32[]{:S(2)}) collective-permute-start(bf16[2,64,640]{2,1,0:T(8,128)(2,1)S(1)} %collective-permute-done.1.q2_ref), channel_id=1, source_target_pairs={{0,4},{4,0},{1,5},{5,1},{2,6},{6,2},{3,7},{7,3},{8,12},{12,8},{9,1... | collective-permute-start | bytes 491528 | tf_op jit(solution)/shard_map/ppermute | solution.py:396
  14.9 1.6 %collective-permute-start.5 = (bf16[2,64,640]{2,1,0:T(8,128)(2,1)S(1)}, bf16[2,64,640]{2,1,0:T(8,128)(2,1)S(1)}, u32[]{:S(2)}, u32[]{:S(2)}) collective-permute-start(bf16[2,64,640]{2,1,0:T(8,128)(2,1)S(1)} %collective-permute-done.2.q3_ref), channel_id=1, source_target_pairs={{0,4},{4,0},{1,5},{5,1},{2,6},{6,2},{3,7},{7,3},{8,12},{12,8},{9,1... | collective-permute-start | bytes 491528 | tf_op jit(solution)/shard_map/ppermute | solution.py:396
  16.6 3.9 %slice-start.2 = ((s8[9437184]{0:T(1024)(128)(4,1)}), s8[1048576]{0:T(1024)(128)(4,1)S(1)}, s32[]{:S(2)}) async-start(s8[9437184]{0:T(1024)(128)(4,1)} %bitcast.7), calls=%async_computation.2 | async-start | bytes 2097152
  20.1 3.9 %collective-permute-start.6 = (bf16[4,128,640]{2,1,0:T(8,128)(2,1)S(1)}, bf16[4,128,640]{2,1,0:T(8,128)(2,1)S(1)}, u32[]{:S(2)}, u32[]{:S(2)}) collective-permute-start(bf16[4,128,640]{2,1,0:T(8,128)(2,1)S(1)} %attention.2), channel_id=1, source_target_pairs={{0,4},{4,0},{1,5},{5,1},{2,6},{6,2},{3,7},{7,3},{8,12},{12,8},{9,1... | collective-permute-start | bytes 1966088 | tf_op jit(solution)/shard_map/ppermute | solution.py:418
  24.0 12.6 %copy-start = (bf16[16,512,128]{2,1,0:T(8,128)(2,1)S(1)}, bf16[16,512,128]{2,1,0:T(8,128)(2,1)}, u32[]{:S(2)}) copy-start(bf16[16,512,128]{2,1,0:T(8,128)(2,1)} %refs_5_.1) | copy-start | bytes 6291460
  25.5 5.8 %collective-permute-start.7 = (bf16[128,640]{1,0:T(8,128)(2,1)}, bf16[128,640]{1,0:T(8,128)(2,1)S(1)}, u32[]{:S(2)}, u32[]{:S(2)}) collective-permute-start(bf16[128,640]{1,0:T(8,128)(2,1)} %get-tuple-element.33), channel_id=1, source_target_pairs={{0,1},{1,0},{2,3},{3,2},{4,5},{5,4},{6,7},{7,6},{8,9},{9,8},{10,11... | collective-permute-start | bytes 491528 | tf_op jit(solution)/shard_map/ppermute | solution.py:368
  26.6 6.5 %collective-permute-start.8 = (bf16[128,640]{1,0:T(8,128)(2,1)S(1)}, bf16[128,640]{1,0:T(8,128)(2,1)S(1)}, u32[]{:S(2)}, u32[]{:S(2)}) collective-permute-start(bf16[128,640]{1,0:T(8,128)(2,1)S(1)} %get-tuple-element.34), channel_id=1, source_target_pairs={{0,3},{1,2},{2,1},{3,0},{4,7},{5,6},{6,5},{7,4},{8,11},{9,10},{10,... | collective-permute-start | bytes 491528 | tf_op jit(solution)/shard_map/ppermute | solution.py:368
  28.1 8.5 %collective-permute-start.9 = (bf16[128,640]{1,0:T(8,128)(2,1)S(1)}, bf16[128,640]{1,0:T(8,128)(2,1)S(1)}, u32[]{:S(2)}, u32[]{:S(2)}) collective-permute-start(bf16[128,640]{1,0:T(8,128)(2,1)S(1)} %get-tuple-element.35), channel_id=1, source_target_pairs={{0,2},{1,3},{2,0},{3,1},{4,6},{5,7},{6,4},{7,5},{8,10},{9,11},{10,... | collective-permute-start | bytes 491528 | tf_op jit(solution)/shard_map/ppermute | solution.py:368
  38.0 4.0 %collective-permute-start.10 = (bf16[144,128]{1,0:T(8,128)(2,1)S(1)}, bf16[144,128]{1,0:T(8,128)(2,1)S(1)}, u32[]{:S(2)}, u32[]{:S(2)}) collective-permute-start(bf16[144,128]{1,0:T(8,128)(2,1)S(1)} %project.1.refs_0_), channel_id=1, source_target_pairs={{0,40},{8,32},{16,56},{24,48},{32,8},{40,0},{48,24},{56,16},{64,10... | collective-permute-start | bytes 110600 | tf_op jit(solution)/shard_map/ppermute | solution.py:443
  40.6 3.2 %collective-permute-start.11 = (bf16[144,128]{1,0:T(8,128)(2,1)S(1)}, bf16[144,128]{1,0:T(8,128)(2,1)S(1)}, u32[]{:S(2)}, u32[]{:S(2)}) collective-permute-start(bf16[144,128]{1,0:T(8,128)(2,1)S(1)} %project.1.refs_0_), channel_id=1, source_target_pairs={{0,32},{8,40},{16,48},{24,56},{32,0},{40,8},{48,16},{56,24},{64,96... | collective-permute-start | bytes 110600 | tf_op jit(solution)/shard_map/ppermute | solution.py:443
  40.6 3.2 %collective-permute-start.12 = (bf16[144,128]{1,0:T(8,128)(2,1)S(1)}, bf16[144,128]{1,0:T(8,128)(2,1)S(1)}, u32[]{:S(2)}, u32[]{:S(2)}) collective-permute-start(bf16[144,128]{1,0:T(8,128)(2,1)S(1)} %project.1.refs_0_), channel_id=1, source_target_pairs={{0,8},{8,0},{16,24},{24,16},{32,40},{40,32},{48,56},{56,48},{64,72... | collective-permute-start | bytes 110600 | tf_op jit(solution)/shard_map/ppermute | solution.py:443
  44.1 6.4 %collective-permute-start.13 = (bf16[144,128]{1,0:T(8,128)(2,1)S(1)}, bf16[144,128]{1,0:T(8,128)(2,1)S(1)}, u32[]{:S(2)}, u32[]{:S(2)}) collective-permute-start(bf16[144,128]{1,0:T(8,128)(2,1)S(1)} %middle_merge.1.refs_0_), channel_id=1, source_target_pairs={{0,120},{8,112},{16,104},{24,96},{32,88},{40,80},{48,72},{56,64},{... | collective-permute-start | bytes 110600 | tf_op jit(solution)/shard_map/ppermute | solution.py:443
  49.2 4.6 %collective-permute-start.14 = (bf16[144,128]{1,0:T(8,128)(2,1)S(1)}, bf16[144,128]{1,0:T(8,128)(2,1)S(1)}, u32[]{:S(2)}, u32[]{:S(2)}) collective-permute-start(bf16[144,128]{1,0:T(8,128)(2,1)S(1)} %middle_merge.1.refs_0_), channel_id=1, source_target_pairs={{0,96},{8,104},{16,112},{24,120},{32,64},{40,72},{48,80},{56,88},{... | collective-permute-start | bytes 110600 | tf_op jit(solution)/shard_map/ppermute | solution.py:443
  49.2 4.6 %collective-permute-start.15 = (bf16[144,128]{1,0:T(8,128)(2,1)S(1)}, bf16[144,128]{1,0:T(8,128)(2,1)S(1)}, u32[]{:S(2)}, u32[]{:S(2)}) collective-permute-start(bf16[144,128]{1,0:T(8,128)(2,1)S(1)} %middle_merge.1.refs_0_), channel_id=1, source_target_pairs={{0,24},{8,16},{16,8},{24,0},{32,56},{40,48},{48,40},{56,32},{64,88... | collective-permute-start | bytes 110600 | tf_op jit(solution)/shard_map/ppermute | solution.py:443
  54.0 4.6 %collective-permute-start.16 = (bf16[4,2,16,128]{3,2,1,0:T(8,128)(2,1)S(1)}, bf16[4,2,16,128]{3,2,1,0:T(8,128)(2,1)S(1)}, u32[]{:S(2)}, u32[]{:S(2)}) collective-permute-start(bf16[4,2,16,128]{3,2,1,0:T(8,128)(2,1)S(1)} %finish.1.own_ref), channel_id=1, source_target_pairs={{0,4},{4,0},{1,5},{5,1},{2,6},{6,2},{3,7},{7,3},{8,12},{12,8},{9,1... | collective-permute-start | bytes 98312 | tf_op jit(solution)/shard_map/ppermute | solution.py:461

commit v8 on v7

--- a/solution.py
+++ b/solution.py
@@ -131,7 +131,9 @@
         copy.wait()
 
 
-def attention_kernel(scale, info_ref, limits_ref, own_ref, q1_ref, q2_ref, q3_ref, k_ref, out_ref, q_ref, *scores):
+def attention_kernel(
+    scale, info_ref, core_ref, limits_ref, own_ref, near_ref, passed_ref, far_ref, k_ref, out_ref, q_ref, *scores
+):
     count, owners, share, _ = q_ref.shape
     rows = owners * share
     key_width, cached = k_ref.shape[1:]
@@ -140,9 +142,9 @@
     first = info_ref[0]
     base = first if k_ref.shape[0] > count else 0
     q_ref[:, 0] = own_ref[pl.ds(first, count)]
-    q_ref[:, 1] = q1_ref[...]
-    q_ref[:, 2] = q2_ref[...]
-    q_ref[:, 3] = q3_ref[...]
+    q_ref[:, pl.ds(1 + core_ref[0], 1)] = near_ref[pl.ds(first, count)][:, None]
+    q_ref[:, pl.ds(2 - core_ref[0], 1)] = passed_ref[pl.ds(first, count)][:, None]
+    q_ref[:, 3] = far_ref[...]
 
     tops = []
     for i in range(count):
@@ -369,7 +371,9 @@
 
     swap = [(0, 1), (1, 0)]
     partners = (1, 3, 2)
-    got = [over_head(sent_queries, k) for k in partners]
+    far = over_head(sent_queries, 2)
+    beside = [(c * owners + i, c * owners + (i ^ (1 + 2 * c))) for c in range(2) for i in range(owners)]
+    near = lax.ppermute(own_queries, ("core", "head"), beside)
     fresh = pl.pallas_call(
         functools.partial(fresh_kernel, scale, steps, heads),
         in_specs=[smem, smem, vmem, vmem],
@@ -392,16 +396,16 @@
         cost_estimate=pl.CostEstimate(flops=0, bytes_accessed=2 * half * key_width * cached, transcendentals=0),
         name="stage",
     )(other_first, in_hbm(cache))
-    got[2], staged = lax.optimization_barrier((got[2], staged))
-    passed = [lax.ppermute(g, "core", swap) for g in got]
-    got, passed = lax.optimization_barrier((got, passed))
-
+    near, far, staged = lax.optimization_barrier((near, far, staged))
+    near_passed = lax.ppermute(near, "core", swap)
+    far_passed = lax.ppermute(far, "core", swap)
+    near_passed, far_passed = lax.optimization_barrier((near_passed, far_passed))
     rows = owners * steps * heads
 
-    def attend(first, got, keys):
+    def attend(first, far, keys):
         return pl.pallas_call(
             functools.partial(attention_kernel, scale),
-            in_specs=[smem] + [vmem] * 6,
+            in_specs=[smem] * 2 + [vmem] * 6,
             out_specs=vmem,
             scratch_shapes=[pltpu.VMEM((half, owners, steps * heads, wide), bf16)]
             + [pltpu.VMEM((rows, cached), f32)] * half,
@@ -413,15 +417,15 @@
                 transcendentals=half * rows * cached,
             ),
             name="attention",
-        )(first, limits, own_queries, *got, keys)
-
-    other_part = lax.ppermute(attend(other_first, got, in_vmem(staged)), "core", swap)
-    own_part = attend(own_first, passed, cache)
+        )(first, core32.reshape(1), limits, own_queries, near, near_passed, far, keys)
+
+    other_part = lax.ppermute(attend(other_first, far, in_vmem(staged)), "core", swap)
+    own_part = attend(own_first, far_passed, cache)
     sent = pl.pallas_call(
         pair_kernel,
         in_specs=[vmem] * 2,
         out_specs=[vmem] * owners,
-        out_shape=[jax.ShapeDtypeStruct((chunk, width + 128), bf16)] * owners,
+        out_shape=[pltpu.VMEM((chunk, width + 128), bf16)] * owners,
         compiler_params=small,
         name="pair_merge",
     )(other_part, own_part)
@@ -449,7 +453,7 @@
         out_shape=jax.ShapeDtypeStruct(part.shape, bf16),
         compiler_params=small,
         name="middle_merge",
-    )(part, *[over_plane(part, k) for k in (5, 4, 1)])
+    )(part, *[over_plane(part, k) for k in (1, 3, 2)])
     own = pl.pallas_call(
         finish_kernel,
         in_specs=[vmem] * 4,
@@ -457,7 +461,7 @@
         out_shape=jax.ShapeDtypeStruct((steps, half, heads, value_width), bf16),
         compiler_params=small,
         name="finish",
-    )(part, *[over_plane(part, k) for k in (15, 12, 3)])
+    )(part, *[over_plane(part, k) for k in (4, 12, 8)])
     theirs = lax.ppermute(own, "core", swap)
     return pl.pallas_call(
         place_kernel,

time: 59.4 us -> 61.3 us (1.032)
  starting transfers between devices: 23 us -> 24.4 us
    ppermute x4, starting transfers between devices: 2.41 us -> 7.55 us  [the longest x1 3.64 us: on_device(): near = lax.ppermute(own_queries, ('core', 'head'), beside)]
    ppermute x6 -> x4, starting transfers between devices: 7.88 us -> 3.6 us  [over_head(): return lax.ppermute(array, 'head', [(i, i ^ k) for i in range(owners)])]
    ppermute x1, starting transfers between devices: 3.71 us -> 4.5 us  [on_device(): theirs = lax.ppermute(own, 'core', swap)]
    ppermute x6 -> x4, waiting for transfers between devices: 11.4 us -> 10.9 us  [over_head(): return lax.ppermute(array, 'head', [(i, i ^ k) for i in range(owners)])]
  transfers between devices with their start and end apart: 17 -> 15, of which waited for: 13 -> 10; matrix products, arithmetic and copies ran while one was open for 0% -> 0% of each run, Pallas kernels for 11% -> 11%
where the time goes in v8:
time: 61.3 us; the launch traced here: 61.2 us
  starting transfers between devices  24.4 us (40%)
  waiting for transfers between devices  20.4 us (33%)
  Pallas kernels  16.2 us (26%)
    ppermute x4, waiting for transfers between devices, over_head(): return lax.ppermute(array, 'head', [(i, i ^ k) for i in range(owners)])  10.9 us
    ppermute x6, starting transfers between devices, over_plane(): return lax.ppermute(array, ('z', 'x'), [(i, i ^ k) for i in range(plane)])  8.77 us
    pallas_call x2, Pallas kernels, attend(): pl.pallas_call(functools.partial(attention_kernel, scale), in_specs=[smem...  7.09 us
    ppermute x6, waiting for transfers between devices, over_plane(): return lax.ppermute(array, ('z', 'x'), [(i, i ^ k) for i in range(plane)])  7.01 us
    ppermute x1, starting transfers between devices, on_device(): theirs = lax.ppermute(own, 'core', swap)  4.5 us
    ppermute x1, starting transfers between devices, on_device(): near = lax.ppermute(own_queries, ('core', 'head'), beside)  3.64 us
    ppermute x4, starting transfers between devices, over_head(): return lax.ppermute(array, 'head', [(i, i ^ k) for i in range(owners)])  3.6 us
    ppermute x1, starting transfers between devices, on_device(): near_passed = lax.ppermute(near, 'core', swap)  3.45 us
  transfers between devices with their start and end apart: 15, of which 10 were waited for; matrix products, arithmetic and copies ran while one was open for 0% of the time, Pallas kernels for 11%

profile of v8, /device:TPU:1, one launch (start us, length us, event | category | flops | bytes accessed | tf_op | source)
XLA Modules:
  0.0 61.2 jit_solution(8965784735481403097)
XLA Ops:
  0.0 2.0 %queries.1 = (bf16[4,64,640]{2,1,0:T(8,128)(2,1)S(1)}, bf16[2,64,640]{2,1,0:T(8,128)(2,1)S(1)}, bf16[16,576]{1,0:T(8,128)(2,1)S(1)}, s32[8,128]{1,0:T(8,128)S(1)}) custom-call(s32[1]{0:T(128)} %bitcast.1.info_ref, s32[1]{0:T(128)} %bitcast.3.row_ref, s32[4]{0:T(128)} %positions_hbm.1, s32[4]{0:T(128)} %lengths_hbm.1, bf16[16,16,192]{2,1,0:T(8,128)(2,1)} %bitcast.11, ...), custom_call_target="tpu_custom_call" | custom-call | tf_op jit(solution)/shard_map/queries/pallas_call | solution.py:338
  2.0 3.6 %collective-permute-start = (bf16[4,64,640]{2,1,0:T(8,128)(2,1)S(1)}, bf16[4,64,640]{2,1,0:T(8,128)(2,1)S(1)}, u32[]{:S(2)}, u32[]{:S(2)}) collective-permute-start(bf16[4,64,640]{2,1,0:T(8,128)(2,1)S(1)} %get-tuple-element.19.own_ref), channel_id=1, source_target_pairs={{0,1},{1,0},{2,3},{3,2},{4,7},{5,6},{6,5},{7,4},{8,9},{9,8},{10,11... | collective-permute-start | bytes 983048 | tf_op jit(solution)/shard_map/ppermute | solution.py:376
  6.0 2.5 %stage.1.k_ref = bf16[2,576,2048]{2,1,0:T(8,128)(2,1)S(1)} custom-call(s32[1]{0:T(128)} %bitcast.1.info_ref, bf16[4,576,2048]{2,1,0:T(8,128)(2,1)} %bitcast.7), custom_call_target="tpu_custom_call" | custom-call | bytes 4718592 | tf_op jit(solution)/shard_map/stage/pallas_call | solution.py:389
  8.6 4.5 %collective-permute-done.1.far_ref = bf16[2,64,640]{2,1,0:T(8,128)(2,1)S(1)} collective-permute-done((bf16[2,64,640]{2,1,0:T(8,128)(2,1)S(1)}, bf16[2,64,640]{2,1,0:T(8,128)(2,1)S(1)}, u32[]{:S(2)}, u32[]{:S(2)}) %collective-permute-start.1) | collective-permute-done | bytes 163872 | tf_op jit(solution)/shard_map/ppermute | solution.py:370
  13.2 3.5 %collective-permute-start.2 = (bf16[4,64,640]{2,1,0:T(8,128)(2,1)S(1)}, bf16[4,64,640]{2,1,0:T(8,128)(2,1)S(1)}, u32[]{:S(2)}, u32[]{:S(2)}) collective-permute-start(bf16[4,64,640]{2,1,0:T(8,128)(2,1)S(1)} %collective-permute-done.near_ref), channel_id=1, source_target_pairs={{0,4},{4,0},{1,5},{5,1},{2,6},{6,2},{3,7},{7,3},{8,12},{12,8},{9,1... | collective-permute-start | bytes 983048 | tf_op jit(solution)/shard_map/ppermute | solution.py:400
  16.7 1.5 %collective-permute-done.3.far_ref = bf16[2,64,640]{2,1,0:T(8,128)(2,1)S(1)} collective-permute-done((bf16[2,64,640]{2,1,0:T(8,128)(2,1)S(1)}, bf16[2,64,640]{2,1,0:T(8,128)(2,1)S(1)}, u32[]{:S(2)}, u32[]{:S(2)}) %collective-permute-start.3) | collective-permute-done | bytes 163872 | tf_op jit(solution)/shard_map/ppermute | solution.py:401
  18.2 3.5 %attention.2 = bf16[4,128,640]{2,1,0:T(8,128)(2,1)S(1)} custom-call(s32[1]{0:T(128)} %bitcast.1.info_ref, s32[1]{0:T(128)} %bitcast.2.core_ref, s32[8,128]{1,0:T(8,128)S(1)} %get-tuple-element.18.limits_ref, bf16[4,64,640]{2,1,0:T(8,128)(2,1)S(1)} %get-tuple-element.19.own_ref, bf16[4,64,640]{2,1,0:T(8,128)(2,1)S(1)} %collective-permute-done.near_ref, ...), custom_call_target="tpu_custom_call" | custom-call | flops 2281701376 | bytes 4718592 | tf_op jit(solution)/shard_map/attention/pallas_call | solution.py:406
  22.1 3.6 %attention.3.b_ref = bf16[4,128,640]{2,1,0:T(8,128)(2,1)S(1)} custom-call(s32[1]{0:T(128)} %bitcast.info_ref, s32[1]{0:T(128)} %bitcast.2.core_ref, s32[8,128]{1,0:T(8,128)S(1)} %get-tuple-element.18.limits_ref, bf16[4,64,640]{2,1,0:T(8,128)(2,1)S(1)} %get-tuple-element.19.own_ref, bf16[4,64,640]{2,1,0:T(8,128)(2,1)S(1)} %collective-permute-done.near_ref, ...), custom_call_target="tpu_custom_call" | custom-call | flops 2281701376 | bytes 4718592 | tf_op jit(solution)/shard_map/attention/pallas_call | solution.py:406
  25.7 1.4 %pair_merge.1 = (bf16[128,640]{1,0:T(8,128)(2,1)S(1)}, bf16[128,640]{1,0:T(8,128)(2,1)}, bf16[128,640]{1,0:T(8,128)(2,1)S(1)}, bf16[128,640]{1,0:T(8,128)(2,1)S(1)}) custom-call(bf16[4,128,640]{2,1,0:T(8,128)(2,1)S(1)} %collective-permute-done.4.a_ref, bf16[4,128,640]{2,1,0:T(8,128)(2,1)S(1)} %attention.3.b_ref), custom_call_target="tpu_custom_call" | custom-call | tf_op jit(solution)/shard_map/pair_merge/pallas_call | solution.py:424
  27.8 2.6 %collective-permute-start.7 = (bf16[128,640]{1,0:T(8,128)(2,1)S(1)}, bf16[128,640]{1,0:T(8,128)(2,1)S(1)}, u32[]{:S(2)}, u32[]{:S(2)}) collective-permute-start(bf16[128,640]{1,0:T(8,128)(2,1)S(1)} %get-tuple-element.29), channel_id=1, source_target_pairs={{0,2},{1,3},{2,0},{3,1},{4,6},{5,7},{6,4},{7,5},{8,10},{9,11},{10,... | collective-permute-start | bytes 491528 | tf_op jit(solution)/shard_map/ppermute | solution.py:370
  31.0 2.0 %collective-permute-done.5.refs_1_ = bf16[128,640]{1,0:T(8,128)(2,1)S(1)} collective-permute-done((bf16[128,640]{1,0:T(8,128)(2,1)}, bf16[128,640]{1,0:T(8,128)(2,1)S(1)}, u32[]{:S(2)}, u32[]{:S(2)}) %collective-permute-start.5) | collective-permute-done | bytes 163872 | tf_op jit(solution)/shard_map/ppermute | solution.py:370
  33.1 4.4 %collective-permute-done.6.refs_2_ = bf16[128,640]{1,0:T(8,128)(2,1)S(1)} collective-permute-done((bf16[128,640]{1,0:T(8,128)(2,1)S(1)}, bf16[128,640]{1,0:T(8,128)(2,1)S(1)}, u32[]{:S(2)}, u32[]{:S(2)}) %collective-permute-start.6) | collective-permute-done | bytes 163872 | tf_op jit(solution)/shard_map/ppermute | solution.py:370
  37.4 1.4 %project.1.refs_0_ = bf16[144,128]{1,0:T(8,128)(2,1)S(1)} custom-call(bf16[128,640]{1,0:T(8,128)(2,1)S(1)} %get-tuple-element.26.refs_0_, bf16[128,640]{1,0:T(8,128)(2,1)S(1)} %collective-permute-done.5.refs_1_, bf16[128,640]{1,0:T(8,128)(2,1)S(1)} %collective-permute-done.6.refs_2_, bf16[128,640]{1,0:T(8,128)(2,1)S(1)} %collective-permute-done.7.refs_3_, ...), custom_call_target="tpu_custom_call" | custom-call | tf_op jit(solution)/shard_map/project/pallas_call | solution.py:433
  38.8 1.3 %collective-permute-start.8 = (bf16[144,128]{1,0:T(8,128)(2,1)S(1)}, bf16[144,128]{1,0:T(8,128)(2,1)S(1)}, u32[]{:S(2)}, u32[]{:S(2)}) collective-permute-start(bf16[144,128]{1,0:T(8,128)(2,1)S(1)} %project.1.refs_0_), channel_id=1, source_target_pairs={{0,8},{8,0},{16,24},{24,16},{32,40},{40,32},{48,56},{56,48},{64,72... | collective-permute-start | bytes 110600 | tf_op jit(solution)/shard_map/ppermute | solution.py:447
  40.1 1.8 %collective-permute-start.9 = (bf16[144,128]{1,0:T(8,128)(2,1)S(1)}, bf16[144,128]{1,0:T(8,128)(2,1)S(1)}, u32[]{:S(2)}, u32[]{:S(2)}) collective-permute-start(bf16[144,128]{1,0:T(8,128)(2,1)S(1)} %project.1.refs_0_), channel_id=1, source_target_pairs={{0,24},{8,16},{16,8},{24,0},{32,56},{40,48},{48,40},{56,32},{64,88... | collective-permute-start | bytes 110600 | tf_op jit(solution)/shard_map/ppermute | solution.py:447
  42.5 1.5 %collective-permute-done.9.refs_2_ = bf16[144,128]{1,0:T(8,128)(2,1)S(1)} collective-permute-done((bf16[144,128]{1,0:T(8,128)(2,1)S(1)}, bf16[144,128]{1,0:T(8,128)(2,1)S(1)}, u32[]{:S(2)}, u32[]{:S(2)}) %collective-permute-start.9) | collective-permute-done | bytes 36896 | tf_op jit(solution)/shard_map/ppermute | solution.py:447
  44.1 2.2 %collective-permute-done.10.refs_3_ = bf16[144,128]{1,0:T(8,128)(2,1)S(1)} collective-permute-done((bf16[144,128]{1,0:T(8,128)(2,1)S(1)}, bf16[144,128]{1,0:T(8,128)(2,1)S(1)}, u32[]{:S(2)}, u32[]{:S(2)}) %collective-permute-start.10) | collective-permute-done | bytes 36896 | tf_op jit(solution)/shard_map/ppermute | solution.py:447
  46.6 1.7 %collective-permute-start.11 = (bf16[144,128]{1,0:T(8,128)(2,1)S(1)}, bf16[144,128]{1,0:T(8,128)(2,1)S(1)}, u32[]{:S(2)}, u32[]{:S(2)}) collective-permute-start(bf16[144,128]{1,0:T(8,128)(2,1)S(1)} %middle_merge.1.refs_0_), channel_id=1, source_target_pairs={{0,32},{8,40},{16,48},{24,56},{32,0},{40,8},{48,16},{56,24},{64,96... | collective-permute-start | bytes 110600 | tf_op jit(solution)/shard_map/ppermute | solution.py:447
  48.3 2.2 %collective-permute-start.12 = (bf16[144,128]{1,0:T(8,128)(2,1)S(1)}, bf16[144,128]{1,0:T(8,128)(2,1)S(1)}, u32[]{:S(2)}, u32[]{:S(2)}) collective-permute-start(bf16[144,128]{1,0:T(8,128)(2,1)S(1)} %middle_merge.1.refs_0_), channel_id=1, source_target_pairs={{0,96},{8,104},{16,112},{24,120},{32,64},{40,72},{48,80},{56,88},{... | collective-permute-start | bytes 110600 | tf_op jit(solution)/shard_map/ppermute | solution.py:447
  50.5 1.1 %collective-permute-start.13 = (bf16[144,128]{1,0:T(8,128)(2,1)S(1)}, bf16[144,128]{1,0:T(8,128)(2,1)S(1)}, u32[]{:S(2)}, u32[]{:S(2)}) collective-permute-start(bf16[144,128]{1,0:T(8,128)(2,1)S(1)} %middle_merge.1.refs_0_), channel_id=1, source_target_pairs={{0,64},{8,72},{16,80},{24,88},{32,96},{40,104},{48,112},{56,120},{... | collective-permute-start | bytes 110600 | tf_op jit(solution)/shard_map/ppermute | solution.py:447
  51.6 0.7 %collective-permute-done.12.refs_2_ = bf16[144,128]{1,0:T(8,128)(2,1)S(1)} collective-permute-done((bf16[144,128]{1,0:T(8,128)(2,1)S(1)}, bf16[144,128]{1,0:T(8,128)(2,1)S(1)}, u32[]{:S(2)}, u32[]{:S(2)}) %collective-permute-start.12) | collective-permute-done | bytes 36896 | tf_op jit(solution)/shard_map/ppermute | solution.py:447
  52.3 2.5 %collective-permute-done.13.refs_3_ = bf16[144,128]{1,0:T(8,128)(2,1)S(1)} collective-permute-done((bf16[144,128]{1,0:T(8,128)(2,1)S(1)}, bf16[144,128]{1,0:T(8,128)(2,1)S(1)}, u32[]{:S(2)}, u32[]{:S(2)}) %collective-permute-start.13) | collective-permute-done | bytes 36896 | tf_op jit(solution)/shard_map/ppermute | solution.py:447
  55.2 4.5 %collective-permute-start.14 = (bf16[4,2,16,128]{3,2,1,0:T(8,128)(2,1)S(1)}, bf16[4,2,16,128]{3,2,1,0:T(8,128)(2,1)S(1)}, u32[]{:S(2)}, u32[]{:S(2)}) collective-permute-start(bf16[4,2,16,128]{3,2,1,0:T(8,128)(2,1)S(1)} %finish.1.own_ref), channel_id=1, source_target_pairs={{0,4},{4,0},{1,5},{5,1},{2,6},{6,2},{3,7},{7,3},{8,12},{12,8},{9,1... | collective-permute-start | bytes 98312 | tf_op jit(solution)/shard_map/ppermute | solution.py:465
  59.7 0.9 %collective-permute-done.14.other_ref = bf16[4,2,16,128]{3,2,1,0:T(8,128)(2,1)S(1)} collective-permute-done((bf16[4,2,16,128]{3,2,1,0:T(8,128)(2,1)S(1)}, bf16[4,2,16,128]{3,2,1,0:T(8,128)(2,1)S(1)}, u32[]{:S(2)}, u32[]{:S(2)}) %collective-permute-start.14) | collective-permute-done | bytes 32800 | tf_op jit(solution)/shard_map/ppermute | solution.py:465
  (25 shorter events, 4.1 us)
Async XLA Ops:
  2.0 11.2 %collective-permute-start = (bf16[4,64,640]{2,1,0:T(8,128)(2,1)S(1)}, bf16[4,64,640]{2,1,0:T(8,128)(2,1)S(1)}, u32[]{:S(2)}, u32[]{:S(2)}) collective-permute-start(bf16[4,64,640]{2,1,0:T(8,128)(2,1)S(1)} %get-tuple-element.19.own_ref), channel_id=1, source_target_pairs={{0,1},{1,0},{2,3},{3,2},{4,7},{5,6},{6,5},{7,4},{8,9},{9,8},{10,11... | collective-permute-start | bytes 983048 | tf_op jit(solution)/shard_map/ppermute | solution.py:376
  5.7 7.4 %collective-permute-start.1 = (bf16[2,64,640]{2,1,0:T(8,128)(2,1)S(1)}, bf16[2,64,640]{2,1,0:T(8,128)(2,1)S(1)}, u32[]{:S(2)}, u32[]{:S(2)}) collective-permute-start(bf16[2,64,640]{2,1,0:T(8,128)(2,1)S(1)} %get-tuple-element.20), channel_id=1, source_target_pairs={{0,2},{1,3},{2,0},{3,1},{4,6},{5,7},{6,4},{7,5},{8,10},{9,11},{10,... | collective-permute-start | bytes 491528 | tf_op jit(solution)/shard_map/ppermute | solution.py:370
  6.0 16.1 %slice-start = ((s8[9437184]{0:T(1024)(128)(4,1)}), s8[4194304]{0:T(1024)(128)(4,1)S(1)}, s32[]{:S(2)}) async-start(s8[9437184]{0:T(1024)(128)(4,1)} %bitcast.8), calls=%async_computation | async-start | bytes 8388608
  6.0 16.1 %slice-start.1 = ((s8[9437184]{0:T(1024)(128)(4,1)}), s8[4194304]{0:T(1024)(128)(4,1)S(1)}, s32[]{:S(2)}) async-start(s8[9437184]{0:T(1024)(128)(4,1)} %bitcast.8), calls=%async_computation.1 | async-start | bytes 8388608
  13.2 4.9 %collective-permute-start.2 = (bf16[4,64,640]{2,1,0:T(8,128)(2,1)S(1)}, bf16[4,64,640]{2,1,0:T(8,128)(2,1)S(1)}, u32[]{:S(2)}, u32[]{:S(2)}) collective-permute-start(bf16[4,64,640]{2,1,0:T(8,128)(2,1)S(1)} %collective-permute-done.near_ref), channel_id=1, source_target_pairs={{0,4},{4,0},{1,5},{5,1},{2,6},{6,2},{3,7},{7,3},{8,12},{12,8},{9,1... | collective-permute-start | bytes 983048 | tf_op jit(solution)/shard_map/ppermute | solution.py:400
  16.7 1.5 %collective-permute-start.3 = (bf16[2,64,640]{2,1,0:T(8,128)(2,1)S(1)}, bf16[2,64,640]{2,1,0:T(8,128)(2,1)S(1)}, u32[]{:S(2)}, u32[]{:S(2)}) collective-permute-start(bf16[2,64,640]{2,1,0:T(8,128)(2,1)S(1)} %collective-permute-done.1.far_ref), channel_id=1, source_target_pairs={{0,4},{4,0},{1,5},{5,1},{2,6},{6,2},{3,7},{7,3},{8,12},{12,8},{9,1... | collective-permute-start | bytes 491528 | tf_op jit(solution)/shard_map/ppermute | solution.py:401
  18.2 4.0 %slice-start.2 = ((s8[9437184]{0:T(1024)(128)(4,1)}), s8[1048576]{0:T(1024)(128)(4,1)S(1)}, s32[]{:S(2)}) async-start(s8[9437184]{0:T(1024)(128)(4,1)} %bitcast.8), calls=%async_computation.2 | async-start | bytes 2097152
  21.7 4.1 %collective-permute-start.4 = (bf16[4,128,640]{2,1,0:T(8,128)(2,1)S(1)}, bf16[4,128,640]{2,1,0:T(8,128)(2,1)S(1)}, u32[]{:S(2)}, u32[]{:S(2)}) collective-permute-start(bf16[4,128,640]{2,1,0:T(8,128)(2,1)S(1)} %attention.2), channel_id=1, source_target_pairs={{0,4},{4,0},{1,5},{5,1},{2,6},{6,2},{3,7},{7,3},{8,12},{12,8},{9,1... | collective-permute-start | bytes 1966088 | tf_op jit(solution)/shard_map/ppermute | solution.py:422
  25.7 11.7 %copy-start = (bf16[16,512,128]{2,1,0:T(8,128)(2,1)S(1)}, bf16[16,512,128]{2,1,0:T(8,128)(2,1)}, u32[]{:S(2)}) copy-start(bf16[16,512,128]{2,1,0:T(8,128)(2,1)} %refs_5_.1) | copy-start | bytes 6291460
  27.2 5.9 %collective-permute-start.5 = (bf16[128,640]{1,0:T(8,128)(2,1)}, bf16[128,640]{1,0:T(8,128)(2,1)S(1)}, u32[]{:S(2)}, u32[]{:S(2)}) collective-permute-start(bf16[128,640]{1,0:T(8,128)(2,1)} %get-tuple-element.27), channel_id=1, source_target_pairs={{0,1},{1,0},{2,3},{3,2},{4,5},{5,4},{6,7},{7,6},{8,9},{9,8},{10,11... | collective-permute-start | bytes 491528 | tf_op jit(solution)/shard_map/ppermute | solution.py:370
  27.2 10.2 %collective-permute-start.6 = (bf16[128,640]{1,0:T(8,128)(2,1)S(1)}, bf16[128,640]{1,0:T(8,128)(2,1)S(1)}, u32[]{:S(2)}, u32[]{:S(2)}) collective-permute-start(bf16[128,640]{1,0:T(8,128)(2,1)S(1)} %get-tuple-element.28), channel_id=1, source_target_pairs={{0,3},{1,2},{2,1},{3,0},{4,7},{5,6},{6,5},{7,4},{8,11},{9,10},{10,... | collective-permute-start | bytes 491528 | tf_op jit(solution)/shard_map/ppermute | solution.py:370
  27.8 9.6 %collective-permute-start.7 = (bf16[128,640]{1,0:T(8,128)(2,1)S(1)}, bf16[128,640]{1,0:T(8,128)(2,1)S(1)}, u32[]{:S(2)}, u32[]{:S(2)}) collective-permute-start(bf16[128,640]{1,0:T(8,128)(2,1)S(1)} %get-tuple-element.29), channel_id=1, source_target_pairs={{0,2},{1,3},{2,0},{3,1},{4,6},{5,7},{6,4},{7,5},{8,10},{9,11},{10,... | collective-permute-start | bytes 491528 | tf_op jit(solution)/shard_map/ppermute | solution.py:370
  38.8 3.7 %collective-permute-start.8 = (bf16[144,128]{1,0:T(8,128)(2,1)S(1)}, bf16[144,128]{1,0:T(8,128)(2,1)S(1)}, u32[]{:S(2)}, u32[]{:S(2)}) collective-permute-start(bf16[144,128]{1,0:T(8,128)(2,1)S(1)} %project.1.refs_0_), channel_id=1, source_target_pairs={{0,8},{8,0},{16,24},{24,16},{32,40},{40,32},{48,56},{56,48},{64,72... | collective-permute-start | bytes 110600 | tf_op jit(solution)/shard_map/ppermute | solution.py:447
  40.1 4.0 %collective-permute-start.9 = (bf16[144,128]{1,0:T(8,128)(2,1)S(1)}, bf16[144,128]{1,0:T(8,128)(2,1)S(1)}, u32[]{:S(2)}, u32[]{:S(2)}) collective-permute-start(bf16[144,128]{1,0:T(8,128)(2,1)S(1)} %project.1.refs_0_), channel_id=1, source_target_pairs={{0,24},{8,16},{16,8},{24,0},{32,56},{40,48},{48,40},{56,32},{64,88... | collective-permute-start | bytes 110600 | tf_op jit(solution)/shard_map/ppermute | solution.py:447
  41.9 4.4 %collective-permute-start.10 = (bf16[144,128]{1,0:T(8,128)(2,1)S(1)}, bf16[144,128]{1,0:T(8,128)(2,1)S(1)}, u32[]{:S(2)}, u32[]{:S(2)}) collective-permute-start(bf16[144,128]{1,0:T(8,128)(2,1)S(1)} %project.1.refs_0_), channel_id=1, source_target_pairs={{0,16},{8,24},{16,0},{24,8},{32,48},{40,56},{48,32},{56,40},{64,80... | collective-permute-start | bytes 110600 | tf_op jit(solution)/shard_map/ppermute | solution.py:447
  46.6 5.0 %collective-permute-start.11 = (bf16[144,128]{1,0:T(8,128)(2,1)S(1)}, bf16[144,128]{1,0:T(8,128)(2,1)S(1)}, u32[]{:S(2)}, u32[]{:S(2)}) collective-permute-start(bf16[144,128]{1,0:T(8,128)(2,1)S(1)} %middle_merge.1.refs_0_), channel_id=1, source_target_pairs={{0,32},{8,40},{16,48},{24,56},{32,0},{40,8},{48,16},{56,24},{64,96... | collective-permute-start | bytes 110600 | tf_op jit(solution)/shard_map/ppermute | solution.py:447
  48.3 4.0 %collective-permute-start.12 = (bf16[144,128]{1,0:T(8,128)(2,1)S(1)}, bf16[144,128]{1,0:T(8,128)(2,1)S(1)}, u32[]{:S(2)}, u32[]{:S(2)}) collective-permute-start(bf16[144,128]{1,0:T(8,128)(2,1)S(1)} %middle_merge.1.refs_0_), channel_id=1, source_target_pairs={{0,96},{8,104},{16,112},{24,120},{32,64},{40,72},{48,80},{56,88},{... | collective-permute-start | bytes 110600 | tf_op jit(solution)/shard_map/ppermute | solution.py:447
  50.5 4.3 %collective-permute-start.13 = (bf16[144,128]{1,0:T(8,128)(2,1)S(1)}, bf16[144,128]{1,0:T(8,128)(2,1)S(1)}, u32[]{:S(2)}, u32[]{:S(2)}) collective-permute-start(bf16[144,128]{1,0:T(8,128)(2,1)S(1)} %middle_merge.1.refs_0_), channel_id=1, source_target_pairs={{0,64},{8,72},{16,80},{24,88},{32,96},{40,104},{48,112},{56,120},{... | collective-permute-start | bytes 110600 | tf_op jit(solution)/shard_map/ppermute | solution.py:447
  55.2 5.4 %collective-permute-start.14 = (bf16[4,2,16,128]{3,2,1,0:T(8,128)(2,1)S(1)}, bf16[4,2,16,128]{3,2,1,0:T(8,128)(2,1)S(1)}, u32[]{:S(2)}, u32[]{:S(2)}) collective-permute-start(bf16[4,2,16,128]{3,2,1,0:T(8,128)(2,1)S(1)} %finish.1.own_ref), channel_id=1, source_target_pairs={{0,4},{4,0},{1,5},{5,1},{2,6},{6,2},{3,7},{7,3},{8,12},{12,8},{9,1... | collective-permute-start | bytes 98312 | tf_op jit(solution)/shard_map/ppermute | solution.py:465

commit v9 on v7

--- a/solution.py
+++ b/solution.py
@@ -40,7 +40,9 @@
 def queries_kernel(
     steps,
     info_ref,
+    own_first_ref,
     row_ref,
+    place_ref,
     positions_hbm,
     lengths_hbm,
     q_hbm,
@@ -89,7 +91,7 @@
     limits = jnp.zeros(limits_ref.shape, jnp.int32)
     for b in range(requests):
         limits = jnp.where(line == b, lengths[b] - row_ref[0], limits)
-    limits_ref[...] = limits
+    limits_ref[...] = jnp.where(line == requests, place_ref[0], limits)
     fetches[2].wait()
     rows = jnp.concatenate([new[t].astype(f32) for t in range(steps)], axis=0)
     tail = rows[:, width:]
@@ -178,7 +180,7 @@
         out_ref[:, at, width:] = split_stats(tops[i], total, rows).astype(bf16).reshape(owners, share, 128)
 
 
-def fresh_kernel(scale, steps, heads, info_ref, place_ref, own_ref, new_ref, out_ref):
+def fresh_kernel(scale, steps, heads, info_ref, limits_ref, own_ref, new_ref, out_ref):
     requests, share, _ = own_ref.shape
     key_width = new_ref.shape[1]
     width = out_ref.shape[1] - 128
@@ -186,7 +188,7 @@
     shape = (share, fresh.shape[0])
     key = lax.broadcasted_iota(jnp.int32, shape, 1)
     step = (lax.broadcasted_iota(jnp.int32, shape, 0) // heads) % steps
-    counted = place_ref[0] == 0
+    counted = limits_ref[requests : requests + 1, :1] == 0
     for i in range(out_ref.shape[0] // share):
         request = info_ref[0] + i
         scores = (
@@ -335,7 +337,7 @@
     chunk = half * steps * heads
     own_queries, sent_queries, new_keys, limits = pl.pallas_call(
         functools.partial(queries_kernel, steps),
-        in_specs=[smem] * 2 + [anywhere] * 5,
+        in_specs=[smem] * 4 + [anywhere] * 5,
         out_specs=[vmem] * 4,
         out_shape=(
             jax.ShapeDtypeStruct((requests, steps * heads, wide), bf16),
@@ -356,7 +358,9 @@
         name="queries",
     )(
         other_first,
+        own_first,
         first_row,
+        place,
         in_hbm(positions),
         in_hbm(context_lengths),
         in_hbm(query_heads.reshape(pairs, heads, query_width)),
@@ -368,17 +372,17 @@
         return lax.ppermute(array, "head", [(i, i ^ k) for i in range(owners)])
 
     swap = [(0, 1), (1, 0)]
-    partners = (1, 3, 2)
+    partners = (2, 3, 1)
     got = [over_head(sent_queries, k) for k in partners]
     fresh = pl.pallas_call(
         functools.partial(fresh_kernel, scale, steps, heads),
-        in_specs=[smem, smem, vmem, vmem],
+        in_specs=[smem, vmem, vmem, vmem],
         out_specs=vmem,
         out_shape=jax.ShapeDtypeStruct((chunk, width + 128), bf16),
         compiler_params=small,
         cost_estimate=pl.CostEstimate(flops=10**9, bytes_accessed=4 * 10**6, transcendentals=0),
         name="fresh",
-    )(own_first, place, own_queries, new_keys)
+    )(own_first, limits, own_queries, new_keys)
     cache = jnp.swapaxes(latent_cache, 1, 2)
     staged_shape = pltpu.VMEM((half, key_width, cached), bf16)
     in_vmem = functools.partial(pltpu.with_memory_space_constraint, memory_space=pltpu.VMEM)
@@ -392,7 +396,7 @@
         cost_estimate=pl.CostEstimate(flops=0, bytes_accessed=2 * half * key_width * cached, transcendentals=0),
         name="stage",
     )(other_first, in_hbm(cache))
-    got[2], staged = lax.optimization_barrier((got[2], staged))
+    got[0], staged = lax.optimization_barrier((got[0], staged))
     passed = [lax.ppermute(g, "core", swap) for g in got]
     got, passed = lax.optimization_barrier((got, passed))
 
@@ -449,7 +453,7 @@
         out_shape=jax.ShapeDtypeStruct(part.shape, bf16),
         compiler_params=small,
         name="middle_merge",
-    )(part, *[over_plane(part, k) for k in (5, 4, 1)])
+    )(part, *[over_plane(part, k) for k in (2, 3, 1)])
     own = pl.pallas_call(
         finish_kernel,
         in_specs=[vmem] * 4,
@@ -457,7 +461,7 @@
         out_shape=jax.ShapeDtypeStruct((steps, half, heads, value_width), bf16),
         compiler_params=small,
         name="finish",
-    )(part, *[over_plane(part, k) for k in (15, 12, 3)])
+    )(part, *[over_plane(part, k) for k in (8, 12, 4)])
     theirs = lax.ppermute(own, "core", swap)
     return pl.pallas_call(
         place_kernel,

time: 59.4 us -> 57.4 us (0.966)
  waiting for transfers between devices: 20 us -> 17.8 us
  starting transfers between devices: 23 us -> 23.7 us
    ppermute x6, waiting for transfers between devices: 11.4 us -> 9.37 us  [over_head(): return lax.ppermute(array, 'head', [(i, i ^ k) for i in range(owners)])]
    ppermute x3, starting transfers between devices: 2.06 us -> 3.35 us  [on_device(): passed = [lax.ppermute(g, 'core', swap) for g in got]]
    ppermute x6, starting transfers between devices: 8.96 us -> 8.1 us  [over_plane(): return lax.ppermute(array, ('z', 'x'), [(i, i ^ k) for i in range(plane)])]
  transfers between devices with their start and end apart: 17 -> 17, of which waited for: 13 -> 11; matrix products, arithmetic and copies ran while one was open for 0% -> 0% of each run, Pallas kernels for 11% -> 12%
where the time goes in v9:
time: 57.4 us; the launch traced here: 57.3 us
  starting transfers between devices  23.7 us (41%)
  waiting for transfers between devices  17.8 us (31%)
  Pallas kernels  15.7 us (27%)
    ppermute x6, waiting for transfers between devices, over_head(): return lax.ppermute(array, 'head', [(i, i ^ k) for i in range(owners)])  9.37 us
    ppermute x6, starting transfers between devices, over_head(): return lax.ppermute(array, 'head', [(i, i ^ k) for i in range(owners)])  8.24 us
    ppermute x6, starting transfers between devices, over_plane(): return lax.ppermute(array, ('z', 'x'), [(i, i ^ k) for i in range(plane)])  8.1 us
    pallas_call x2, Pallas kernels, attend(): pl.pallas_call(functools.partial(attention_kernel, scale), in_specs=[smem...  7.05 us
    ppermute x6, waiting for transfers between devices, over_plane(): return lax.ppermute(array, ('z', 'x'), [(i, i ^ k) for i in range(plane)])  6.52 us
    ppermute x1, starting transfers between devices, on_device(): theirs = lax.ppermute(own, 'core', swap)  3.61 us
    ppermute x3, starting transfers between devices, on_device(): passed = [lax.ppermute(g, 'core', swap) for g in got]  3.35 us
    pallas_call x1, Pallas kernels, on_device(): pl.pallas_call(stage_kernel, in_specs=[smem, anywhere], out_specs=vmem, o...  2.54 us
  transfers between devices with their start and end apart: 17, of which 11 were waited for; matrix products, arithmetic and copies ran while one was open for 0% of the time, Pallas kernels for 12%

profile of v9, /device:TPU:1, one launch (start us, length us, event | category | flops | bytes accessed | tf_op | source)
XLA Modules:
  0.0 57.3 jit_solution(10412333376180163930)
XLA Ops:
  0.0 2.0 %queries.1 = (bf16[4,64,640]{2,1,0:T(8,128)(2,1)S(1)}, bf16[2,64,640]{2,1,0:T(8,128)(2,1)S(1)}, bf16[16,576]{1,0:T(8,128)(2,1)S(1)}, s32[8,128]{1,0:T(8,128)S(1)}) custom-call(s32[1]{0:T(128)} %bitcast.1.info_ref, s32[1]{0:T(128)} %bitcast.own_first_ref.info_ref, s32[1]{0:T(128)} %bitcast.2.row_ref, s32[1]{0:T(128)} %bitcast.3.place_ref, s32[4]{0:T(128)} %positions_hbm.1, ...), custom_call_target="tpu_custom_call" | custom-call | tf_op jit(solution)/shard_map/queries/pallas_call | solution.py:338
  2.0 3.8 %collective-permute-start = (bf16[2,64,640]{2,1,0:T(8,128)(2,1)S(1)}, bf16[2,64,640]{2,1,0:T(8,128)(2,1)S(1)}, u32[]{:S(2)}, u32[]{:S(2)}) collective-permute-start(bf16[2,64,640]{2,1,0:T(8,128)(2,1)S(1)} %get-tuple-element.23), channel_id=1, source_target_pairs={{0,2},{1,3},{2,0},{3,1},{4,6},{5,7},{6,4},{7,5},{8,10},{9,11},{10,... | collective-permute-start | bytes 491528 | tf_op jit(solution)/shard_map/ppermute | solution.py:372
  5.9 0.8 %collective-permute-start.1 = (bf16[2,64,640]{2,1,0:T(8,128)(2,1)S(1)}, bf16[2,64,640]{2,1,0:T(8,128)(2,1)S(1)}, u32[]{:S(2)}, u32[]{:S(2)}) collective-permute-start(bf16[2,64,640]{2,1,0:T(8,128)(2,1)S(1)} %get-tuple-element.23), channel_id=1, source_target_pairs={{0,3},{1,2},{2,1},{3,0},{4,7},{5,6},{6,5},{7,4},{8,11},{9,10},{10,... | collective-permute-start | bytes 491528 | tf_op jit(solution)/shard_map/ppermute | solution.py:372
  6.6 2.5 %stage.1.k_ref = bf16[2,576,2048]{2,1,0:T(8,128)(2,1)S(1)} custom-call(s32[1]{0:T(128)} %bitcast.1.info_ref, bf16[4,576,2048]{2,1,0:T(8,128)(2,1)} %bitcast.6), custom_call_target="tpu_custom_call" | custom-call | bytes 4718592 | tf_op jit(solution)/shard_map/stage/pallas_call | solution.py:389
  9.5 1.9 %collective-permute-start.3 = (bf16[2,64,640]{2,1,0:T(8,128)(2,1)S(1)}, bf16[2,64,640]{2,1,0:T(8,128)(2,1)S(1)}, u32[]{:S(2)}, u32[]{:S(2)}) collective-permute-start(bf16[2,64,640]{2,1,0:T(8,128)(2,1)S(1)} %collective-permute-done.q1_ref), channel_id=1, source_target_pairs={{0,4},{4,0},{1,5},{5,1},{2,6},{6,2},{3,7},{7,3},{8,12},{12,8},{9,1... | collective-permute-start | bytes 491528 | tf_op jit(solution)/shard_map/ppermute | solution.py:400
  11.4 2.1 %collective-permute-done.1.q2_ref = bf16[2,64,640]{2,1,0:T(8,128)(2,1)S(1)} collective-permute-done((bf16[2,64,640]{2,1,0:T(8,128)(2,1)S(1)}, bf16[2,64,640]{2,1,0:T(8,128)(2,1)S(1)}, u32[]{:S(2)}, u32[]{:S(2)}) %collective-permute-start.1) | collective-permute-done | bytes 163872 | tf_op jit(solution)/shard_map/ppermute | solution.py:372
  13.5 1.0 %collective-permute-start.4 = (bf16[2,64,640]{2,1,0:T(8,128)(2,1)S(1)}, bf16[2,64,640]{2,1,0:T(8,128)(2,1)S(1)}, u32[]{:S(2)}, u32[]{:S(2)}) collective-permute-start(bf16[2,64,640]{2,1,0:T(8,128)(2,1)S(1)} %collective-permute-done.1.q2_ref), channel_id=1, source_target_pairs={{0,4},{4,0},{1,5},{5,1},{2,6},{6,2},{3,7},{7,3},{8,12},{12,8},{9,1... | collective-permute-start | bytes 491528 | tf_op jit(solution)/shard_map/ppermute | solution.py:400
  16.0 3.5 %attention.2 = bf16[4,128,640]{2,1,0:T(8,128)(2,1)S(1)} custom-call(s32[1]{0:T(128)} %bitcast.1.info_ref, s32[8,128]{1,0:T(8,128)S(1)} %get-tuple-element.21.limits_ref, bf16[4,64,640]{2,1,0:T(8,128)(2,1)S(1)} %get-tuple-element.22.own_ref, bf16[2,64,640]{2,1,0:T(8,128)(2,1)S(1)} %collective-permute-done.q1_ref, ...), custom_call_target="tpu_custom_call" | custom-call | flops 2281701376 | bytes 4718592 | tf_op jit(solution)/shard_map/attention/pallas_call | solution.py:406
  20.0 3.5 %attention.3.b_ref = bf16[4,128,640]{2,1,0:T(8,128)(2,1)S(1)} custom-call(s32[1]{0:T(128)} %bitcast.own_first_ref.info_ref, s32[8,128]{1,0:T(8,128)S(1)} %get-tuple-element.21.limits_ref, bf16[4,64,640]{2,1,0:T(8,128)(2,1)S(1)} %get-tuple-element.22.own_ref, bf16[2,64,640]{2,1,0:T(8,128)(2,1)S(1)} %collective-permute-done.3.q1_ref, ...), custom_call_target="tpu_custom_call" | custom-call | flops 2281701376 | bytes 4718592 | tf_op jit(solution)/shard_map/attention/pallas_call | solution.py:406
  23.5 0.9 %pair_merge.1 = (bf16[128,640]{1,0:T(8,128)(2,1)S(1)}, bf16[128,640]{1,0:T(8,128)(2,1)S(1)}, bf16[128,640]{1,0:T(8,128)(2,1)S(1)}, bf16[128,640]{1,0:T(8,128)(2,1)S(1)}) custom-call(bf16[4,128,640]{2,1,0:T(8,128)(2,1)S(1)} %collective-permute-done.6.a_ref, bf16[4,128,640]{2,1,0:T(8,128)(2,1)S(1)} %attention.3.b_ref), custom_call_target="tpu_custom_call" | custom-call | tf_op jit(solution)/shard_map/pair_merge/pallas_call | solution.py:424
  24.4 2.1 %collective-permute-start.7 = (bf16[128,640]{1,0:T(8,128)(2,1)S(1)}, bf16[128,640]{1,0:T(8,128)(2,1)S(1)}, u32[]{:S(2)}, u32[]{:S(2)}) collective-permute-start(bf16[128,640]{1,0:T(8,128)(2,1)S(1)} %get-tuple-element.33), channel_id=1, source_target_pairs={{0,2},{1,3},{2,0},{3,1},{4,6},{5,7},{6,4},{7,5},{8,10},{9,11},{10,... | collective-permute-start | bytes 491528 | tf_op jit(solution)/shard_map/ppermute | solution.py:372
  26.5 1.6 %collective-permute-start.8 = (bf16[128,640]{1,0:T(8,128)(2,1)S(1)}, bf16[128,640]{1,0:T(8,128)(2,1)S(1)}, u32[]{:S(2)}, u32[]{:S(2)}) collective-permute-start(bf16[128,640]{1,0:T(8,128)(2,1)S(1)} %get-tuple-element.34), channel_id=1, source_target_pairs={{0,3},{1,2},{2,1},{3,0},{4,7},{5,6},{6,5},{7,4},{8,11},{9,10},{10,... | collective-permute-start | bytes 491528 | tf_op jit(solution)/shard_map/ppermute | solution.py:372
  28.6 3.0 %collective-permute-done.7.refs_1_ = bf16[128,640]{1,0:T(8,128)(2,1)S(1)} collective-permute-done((bf16[128,640]{1,0:T(8,128)(2,1)S(1)}, bf16[128,640]{1,0:T(8,128)(2,1)S(1)}, u32[]{:S(2)}, u32[]{:S(2)}) %collective-permute-start.7) | collective-permute-done | bytes 163872 | tf_op jit(solution)/shard_map/ppermute | solution.py:372
  31.7 4.0 %collective-permute-done.8.refs_2_ = bf16[128,640]{1,0:T(8,128)(2,1)S(1)} collective-permute-done((bf16[128,640]{1,0:T(8,128)(2,1)S(1)}, bf16[128,640]{1,0:T(8,128)(2,1)S(1)}, u32[]{:S(2)}, u32[]{:S(2)}) %collective-permute-start.8) | collective-permute-done | bytes 163872 | tf_op jit(solution)/shard_map/ppermute | solution.py:372
  35.6 1.4 %project.1.refs_0_ = bf16[144,128]{1,0:T(8,128)(2,1)S(1)} custom-call(bf16[128,640]{1,0:T(8,128)(2,1)S(1)} %get-tuple-element.32.refs_0_, bf16[128,640]{1,0:T(8,128)(2,1)S(1)} %collective-permute-done.7.refs_1_, bf16[128,640]{1,0:T(8,128)(2,1)S(1)} %collective-permute-done.8.refs_2_, bf16[128,640]{1,0:T(8,128)(2,1)S(1)} %collective-permute-done.9.refs_3_, ...), custom_call_target="tpu_custom_call" | custom-call | tf_op jit(solution)/shard_map/project/pallas_call | solution.py:433
  37.0 2.8 %collective-permute-start.10 = (bf16[144,128]{1,0:T(8,128)(2,1)S(1)}, bf16[144,128]{1,0:T(8,128)(2,1)S(1)}, u32[]{:S(2)}, u32[]{:S(2)}) collective-permute-start(bf16[144,128]{1,0:T(8,128)(2,1)S(1)} %project.1.refs_0_), channel_id=1, source_target_pairs={{0,16},{8,24},{16,0},{24,8},{32,48},{40,56},{48,32},{56,40},{64,80... | collective-permute-start | bytes 110600 | tf_op jit(solution)/shard_map/ppermute | solution.py:447
  39.8 0.9 %collective-permute-start.11 = (bf16[144,128]{1,0:T(8,128)(2,1)S(1)}, bf16[144,128]{1,0:T(8,128)(2,1)S(1)}, u32[]{:S(2)}, u32[]{:S(2)}) collective-permute-start(bf16[144,128]{1,0:T(8,128)(2,1)S(1)} %project.1.refs_0_), channel_id=1, source_target_pairs={{0,24},{8,16},{16,8},{24,0},{32,56},{40,48},{48,40},{56,32},{64,88... | collective-permute-start | bytes 110600 | tf_op jit(solution)/shard_map/ppermute | solution.py:447
  40.7 0.7 %collective-permute-done.10.refs_1_ = bf16[144,128]{1,0:T(8,128)(2,1)S(1)} collective-permute-done((bf16[144,128]{1,0:T(8,128)(2,1)S(1)}, bf16[144,128]{1,0:T(8,128)(2,1)S(1)}, u32[]{:S(2)}, u32[]{:S(2)}) %collective-permute-start.10) | collective-permute-done | bytes 36896 | tf_op jit(solution)/shard_map/ppermute | solution.py:447
  41.4 2.4 %collective-permute-done.11.refs_2_ = bf16[144,128]{1,0:T(8,128)(2,1)S(1)} collective-permute-done((bf16[144,128]{1,0:T(8,128)(2,1)S(1)}, bf16[144,128]{1,0:T(8,128)(2,1)S(1)}, u32[]{:S(2)}, u32[]{:S(2)}) %collective-permute-start.11) | collective-permute-done | bytes 36896 | tf_op jit(solution)/shard_map/ppermute | solution.py:447
  44.1 3.7 %collective-permute-start.13 = (bf16[144,128]{1,0:T(8,128)(2,1)S(1)}, bf16[144,128]{1,0:T(8,128)(2,1)S(1)}, u32[]{:S(2)}, u32[]{:S(2)}) collective-permute-start(bf16[144,128]{1,0:T(8,128)(2,1)S(1)} %middle_merge.1.refs_0_), channel_id=1, source_target_pairs={{0,64},{8,72},{16,80},{24,88},{32,96},{40,104},{48,112},{56,120},{... | collective-permute-start | bytes 110600 | tf_op jit(solution)/shard_map/ppermute | solution.py:447
  49.2 2.8 %collective-permute-done.14.refs_2_ = bf16[144,128]{1,0:T(8,128)(2,1)S(1)} collective-permute-done((bf16[144,128]{1,0:T(8,128)(2,1)S(1)}, bf16[144,128]{1,0:T(8,128)(2,1)S(1)}, u32[]{:S(2)}, u32[]{:S(2)}) %collective-permute-start.14) | collective-permute-done | bytes 36896 | tf_op jit(solution)/shard_map/ppermute | solution.py:447
  52.2 3.6 %collective-permute-start.16 = (bf16[4,2,16,128]{3,2,1,0:T(8,128)(2,1)S(1)}, bf16[4,2,16,128]{3,2,1,0:T(8,128)(2,1)S(1)}, u32[]{:S(2)}, u32[]{:S(2)}) collective-permute-start(bf16[4,2,16,128]{3,2,1,0:T(8,128)(2,1)S(1)} %finish.1.own_ref), channel_id=1, source_target_pairs={{0,4},{4,0},{1,5},{5,1},{2,6},{6,2},{3,7},{7,3},{8,12},{12,8},{9,1... | collective-permute-start | bytes 98312 | tf_op jit(solution)/shard_map/ppermute | solution.py:465
  55.8 0.9 %collective-permute-done.16.other_ref = bf16[4,2,16,128]{3,2,1,0:T(8,128)(2,1)S(1)} collective-permute-done((bf16[4,2,16,128]{3,2,1,0:T(8,128)(2,1)S(1)}, bf16[4,2,16,128]{3,2,1,0:T(8,128)(2,1)S(1)}, u32[]{:S(2)}, u32[]{:S(2)}) %collective-permute-start.16) | collective-permute-done | bytes 32800 | tf_op jit(solution)/shard_map/ppermute | solution.py:465
  56.7 0.6 %place.1 = bf16[4,4,16,128]{3,2,1,0:T(8,128)(2,1)} custom-call(s32[1]{0:T(128)} %bitcast.own_first_ref.info_ref, bf16[4,2,16,128]{3,2,1,0:T(8,128)(2,1)S(1)} %finish.1.own_ref, bf16[4,2,16,128]{3,2,1,0:T(8,128)(2,1)S(1)} %collective-permute-done.16.other_ref), custom_call_target="tpu_custom_call" | custom-call | tf_op jit(solution)/shard_map/place/pallas_call | solution.py:466
  (29 shorter events, 4.8 us)
Async XLA Ops:
  2.0 7.5 %collective-permute-start = (bf16[2,64,640]{2,1,0:T(8,128)(2,1)S(1)}, bf16[2,64,640]{2,1,0:T(8,128)(2,1)S(1)}, u32[]{:S(2)}, u32[]{:S(2)}) collective-permute-start(bf16[2,64,640]{2,1,0:T(8,128)(2,1)S(1)} %get-tuple-element.23), channel_id=1, source_target_pairs={{0,2},{1,3},{2,0},{3,1},{4,6},{5,7},{6,4},{7,5},{8,10},{9,11},{10,... | collective-permute-start | bytes 491528 | tf_op jit(solution)/shard_map/ppermute | solution.py:372
  5.9 7.6 %collective-permute-start.1 = (bf16[2,64,640]{2,1,0:T(8,128)(2,1)S(1)}, bf16[2,64,640]{2,1,0:T(8,128)(2,1)S(1)}, u32[]{:S(2)}, u32[]{:S(2)}) collective-permute-start(bf16[2,64,640]{2,1,0:T(8,128)(2,1)S(1)} %get-tuple-element.23), channel_id=1, source_target_pairs={{0,3},{1,2},{2,1},{3,0},{4,7},{5,6},{6,5},{7,4},{8,11},{9,10},{10,... | collective-permute-start | bytes 491528 | tf_op jit(solution)/shard_map/ppermute | solution.py:372
  6.6 7.9 %collective-permute-start.2 = (bf16[2,64,640]{2,1,0:T(8,128)(2,1)S(1)}, bf16[2,64,640]{2,1,0:T(8,128)(2,1)S(1)}, u32[]{:S(2)}, u32[]{:S(2)}) collective-permute-start(bf16[2,64,640]{2,1,0:T(8,128)(2,1)S(1)} %get-tuple-element.23), channel_id=1, source_target_pairs={{0,1},{1,0},{2,3},{3,2},{4,5},{5,4},{6,7},{7,6},{8,9},{9,8},{10,11... | collective-permute-start | bytes 491528 | tf_op jit(solution)/shard_map/ppermute | solution.py:372
  6.6 13.3 %slice-start = ((s8[9437184]{0:T(1024)(128)(4,1)}), s8[4194304]{0:T(1024)(128)(4,1)S(1)}, s32[]{:S(2)}) async-start(s8[9437184]{0:T(1024)(128)(4,1)} %bitcast.7), calls=%async_computation | async-start | bytes 8388608
  6.6 13.3 %slice-start.1 = ((s8[9437184]{0:T(1024)(128)(4,1)}), s8[4194304]{0:T(1024)(128)(4,1)S(1)}, s32[]{:S(2)}) async-start(s8[9437184]{0:T(1024)(128)(4,1)} %bitcast.7), calls=%async_computation.1 | async-start | bytes 8388608
  9.5 5.4 %collective-permute-start.3 = (bf16[2,64,640]{2,1,0:T(8,128)(2,1)S(1)}, bf16[2,64,640]{2,1,0:T(8,128)(2,1)S(1)}, u32[]{:S(2)}, u32[]{:S(2)}) collective-permute-start(bf16[2,64,640]{2,1,0:T(8,128)(2,1)S(1)} %collective-permute-done.q1_ref), channel_id=1, source_target_pairs={{0,4},{4,0},{1,5},{5,1},{2,6},{6,2},{3,7},{7,3},{8,12},{12,8},{9,1... | collective-permute-start | bytes 491528 | tf_op jit(solution)/shard_map/ppermute | solution.py:400
  13.5 2.1 %collective-permute-start.4 = (bf16[2,64,640]{2,1,0:T(8,128)(2,1)S(1)}, bf16[2,64,640]{2,1,0:T(8,128)(2,1)S(1)}, u32[]{:S(2)}, u32[]{:S(2)}) collective-permute-start(bf16[2,64,640]{2,1,0:T(8,128)(2,1)S(1)} %collective-permute-done.1.q2_ref), channel_id=1, source_target_pairs={{0,4},{4,0},{1,5},{5,1},{2,6},{6,2},{3,7},{7,3},{8,12},{12,8},{9,1... | collective-permute-start | bytes 491528 | tf_op jit(solution)/shard_map/ppermute | solution.py:400
  14.5 1.4 %collective-permute-start.5 = (bf16[2,64,640]{2,1,0:T(8,128)(2,1)S(1)}, bf16[2,64,640]{2,1,0:T(8,128)(2,1)S(1)}, u32[]{:S(2)}, u32[]{:S(2)}) collective-permute-start(bf16[2,64,640]{2,1,0:T(8,128)(2,1)S(1)} %collective-permute-done.2.q3_ref), channel_id=1, source_target_pairs={{0,4},{4,0},{1,5},{5,1},{2,6},{6,2},{3,7},{7,3},{8,12},{12,8},{9,1... | collective-permute-start | bytes 491528 | tf_op jit(solution)/shard_map/ppermute | solution.py:400
  16.0 4.0 %slice-start.2 = ((s8[9437184]{0:T(1024)(128)(4,1)}), s8[1048576]{0:T(1024)(128)(4,1)S(1)}, s32[]{:S(2)}) async-start(s8[9437184]{0:T(1024)(128)(4,1)} %bitcast.7), calls=%async_computation.2 | async-start | bytes 2097152
  19.5 4.0 %collective-permute-start.6 = (bf16[4,128,640]{2,1,0:T(8,128)(2,1)S(1)}, bf16[4,128,640]{2,1,0:T(8,128)(2,1)S(1)}, u32[]{:S(2)}, u32[]{:S(2)}) collective-permute-start(bf16[4,128,640]{2,1,0:T(8,128)(2,1)S(1)} %attention.2), channel_id=1, source_target_pairs={{0,4},{4,0},{1,5},{5,1},{2,6},{6,2},{3,7},{7,3},{8,12},{12,8},{9,1... | collective-permute-start | bytes 1966088 | tf_op jit(solution)/shard_map/ppermute | solution.py:422
  23.5 12.1 %copy-start = (bf16[16,512,128]{2,1,0:T(8,128)(2,1)S(1)}, bf16[16,512,128]{2,1,0:T(8,128)(2,1)}, u32[]{:S(2)}) copy-start(bf16[16,512,128]{2,1,0:T(8,128)(2,1)} %refs_5_.1) | copy-start | bytes 6291460
  24.4 7.2 %collective-permute-start.7 = (bf16[128,640]{1,0:T(8,128)(2,1)S(1)}, bf16[128,640]{1,0:T(8,128)(2,1)S(1)}, u32[]{:S(2)}, u32[]{:S(2)}) collective-permute-start(bf16[128,640]{1,0:T(8,128)(2,1)S(1)} %get-tuple-element.33), channel_id=1, source_target_pairs={{0,2},{1,3},{2,0},{3,1},{4,6},{5,7},{6,4},{7,5},{8,10},{9,11},{10,... | collective-permute-start | bytes 491528 | tf_op jit(solution)/shard_map/ppermute | solution.py:372
  26.5 9.1 %collective-permute-start.8 = (bf16[128,640]{1,0:T(8,128)(2,1)S(1)}, bf16[128,640]{1,0:T(8,128)(2,1)S(1)}, u32[]{:S(2)}, u32[]{:S(2)}) collective-permute-start(bf16[128,640]{1,0:T(8,128)(2,1)S(1)} %get-tuple-element.34), channel_id=1, source_target_pairs={{0,3},{1,2},{2,1},{3,0},{4,7},{5,6},{6,5},{7,4},{8,11},{9,10},{10,... | collective-permute-start | bytes 491528 | tf_op jit(solution)/shard_map/ppermute | solution.py:372
  28.0 7.6 %collective-permute-start.9 = (bf16[128,640]{1,0:T(8,128)(2,1)S(1)}, bf16[128,640]{1,0:T(8,128)(2,1)S(1)}, u32[]{:S(2)}, u32[]{:S(2)}) collective-permute-start(bf16[128,640]{1,0:T(8,128)(2,1)S(1)} %get-tuple-element.35), channel_id=1, source_target_pairs={{0,1},{1,0},{2,3},{3,2},{4,5},{5,4},{6,7},{7,6},{8,9},{9,8},{10,11... | collective-permute-start | bytes 491528 | tf_op jit(solution)/shard_map/ppermute | solution.py:372
  37.0 4.4 %collective-permute-start.10 = (bf16[144,128]{1,0:T(8,128)(2,1)S(1)}, bf16[144,128]{1,0:T(8,128)(2,1)S(1)}, u32[]{:S(2)}, u32[]{:S(2)}) collective-permute-start(bf16[144,128]{1,0:T(8,128)(2,1)S(1)} %project.1.refs_0_), channel_id=1, source_target_pairs={{0,16},{8,24},{16,0},{24,8},{32,48},{40,56},{48,32},{56,40},{64,80... | collective-permute-start | bytes 110600 | tf_op jit(solution)/shard_map/ppermute | solution.py:447
  39.8 4.0 %collective-permute-start.11 = (bf16[144,128]{1,0:T(8,128)(2,1)S(1)}, bf16[144,128]{1,0:T(8,128)(2,1)S(1)}, u32[]{:S(2)}, u32[]{:S(2)}) collective-permute-start(bf16[144,128]{1,0:T(8,128)(2,1)S(1)} %project.1.refs_0_), channel_id=1, source_target_pairs={{0,24},{8,16},{16,8},{24,0},{32,56},{40,48},{48,40},{56,32},{64,88... | collective-permute-start | bytes 110600 | tf_op jit(solution)/shard_map/ppermute | solution.py:447
  40.7 3.2 %collective-permute-start.12 = (bf16[144,128]{1,0:T(8,128)(2,1)S(1)}, bf16[144,128]{1,0:T(8,128)(2,1)S(1)}, u32[]{:S(2)}, u32[]{:S(2)}) collective-permute-start(bf16[144,128]{1,0:T(8,128)(2,1)S(1)} %project.1.refs_0_), channel_id=1, source_target_pairs={{0,8},{8,0},{16,24},{24,16},{32,40},{40,32},{48,56},{56,48},{64,72... | collective-permute-start | bytes 110600 | tf_op jit(solution)/shard_map/ppermute | solution.py:447
  44.1 5.0 %collective-permute-start.13 = (bf16[144,128]{1,0:T(8,128)(2,1)S(1)}, bf16[144,128]{1,0:T(8,128)(2,1)S(1)}, u32[]{:S(2)}, u32[]{:S(2)}) collective-permute-start(bf16[144,128]{1,0:T(8,128)(2,1)S(1)} %middle_merge.1.refs_0_), channel_id=1, source_target_pairs={{0,64},{8,72},{16,80},{24,88},{32,96},{40,104},{48,112},{56,120},{... | collective-permute-start | bytes 110600 | tf_op jit(solution)/shard_map/ppermute | solution.py:447
  47.8 4.1 %collective-permute-start.14 = (bf16[144,128]{1,0:T(8,128)(2,1)S(1)}, bf16[144,128]{1,0:T(8,128)(2,1)S(1)}, u32[]{:S(2)}, u32[]{:S(2)}) collective-permute-start(bf16[144,128]{1,0:T(8,128)(2,1)S(1)} %middle_merge.1.refs_0_), channel_id=1, source_target_pairs={{0,96},{8,104},{16,112},{24,120},{32,64},{40,72},{48,80},{56,88},{... | collective-permute-start | bytes 110600 | tf_op jit(solution)/shard_map/ppermute | solution.py:447
  48.3 3.7 %collective-permute-start.15 = (bf16[144,128]{1,0:T(8,128)(2,1)S(1)}, bf16[144,128]{1,0:T(8,128)(2,1)S(1)}, u32[]{:S(2)}, u32[]{:S(2)}) collective-permute-start(bf16[144,128]{1,0:T(8,128)(2,1)S(1)} %middle_merge.1.refs_0_), channel_id=1, source_target_pairs={{0,32},{8,40},{16,48},{24,56},{32,0},{40,8},{48,16},{56,24},{64,96... | collective-permute-start | bytes 110600 | tf_op jit(solution)/shard_map/ppermute | solution.py:447
  52.2 4.5 %collective-permute-start.16 = (bf16[4,2,16,128]{3,2,1,0:T(8,128)(2,1)S(1)}, bf16[4,2,16,128]{3,2,1,0:T(8,128)(2,1)S(1)}, u32[]{:S(2)}, u32[]{:S(2)}) collective-permute-start(bf16[4,2,16,128]{3,2,1,0:T(8,128)(2,1)S(1)} %finish.1.own_ref), channel_id=1, source_target_pairs={{0,4},{4,0},{1,5},{5,1},{2,6},{6,2},{3,7},{7,3},{8,12},{12,8},{9,1... | collective-permute-start | bytes 98312 | tf_op jit(solution)/shard_map/ppermute | solution.py:465

commit v10 on v9

--- a/solution.py
+++ b/solution.py
@@ -105,7 +105,9 @@
     for s in range(steps):
         for b in range(requests):
             own_ref[b, s * heads : (s + 1) * heads, :width] = lat[s * requests + b].astype(bf16)
-    sent_ref[...] = own_ref[pl.ds(info_ref[0], sent_ref.shape[0])]
+    packed = [own_ref[info_ref[0] + i] for i in range(sent_ref.shape[1] // key_width)]
+    latents = [row[:, :width] for row in packed]
+    sent_ref[...] = jnp.concatenate(latents + [row[:, width:key_width] for row in packed], axis=-1)
 
 
 def split_stats(peak, weight_sum, rows):
@@ -133,6 +135,18 @@
         copy.wait()
 
 
+def stat_rows(peak, weight_sum):
+    line = lax.broadcasted_iota(jnp.int32, (16, peak.shape[1]), 0)
+    first = peak.astype(bf16).astype(f32)
+    second = (peak - first).astype(bf16).astype(f32)
+    sum_first = weight_sum.astype(bf16).astype(f32)
+    stats = jnp.where(line == 0, first, 0.0)
+    stats = jnp.where(line == 1, second, stats)
+    stats = jnp.where(line == 2, peak - first - second, stats)
+    stats = jnp.where(line == 3, sum_first, stats)
+    return jnp.where(line == 4, weight_sum - sum_first, stats).astype(bf16)
+
+
 def attention_kernel(scale, info_ref, limits_ref, own_ref, q1_ref, q2_ref, q3_ref, k_ref, out_ref, q_ref, *scores):
     count, owners, share, _ = q_ref.shape
     rows = owners * share
@@ -142,9 +156,12 @@
     first = info_ref[0]
     base = first if k_ref.shape[0] > count else 0
     q_ref[:, 0] = own_ref[pl.ds(first, count)]
-    q_ref[:, 1] = q1_ref[...]
-    q_ref[:, 2] = q2_ref[...]
-    q_ref[:, 3] = q3_ref[...]
+    rope = key_width - width
+    for k, packed_ref in enumerate((q1_ref, q2_ref, q3_ref)):
+        for i in range(count):
+            q_ref[i, 1 + k, :, :width] = packed_ref[:, i * width : (i + 1) * width]
+            at = count * width + i * rope
+            q_ref[i, 1 + k, :, width:key_width] = packed_ref[:, at : at + rope]
 
     tops = []
     for i in range(count):
@@ -183,13 +200,15 @@
 def fresh_kernel(scale, steps, heads, info_ref, limits_ref, own_ref, new_ref, out_ref):
     requests, share, _ = own_ref.shape
     key_width = new_ref.shape[1]
-    width = out_ref.shape[1] - 128
+    width = out_ref.shape[1]
+    requests_rows = out_ref.shape[0] - 16
+    stats = []
     fresh = new_ref[...]
     shape = (share, fresh.shape[0])
     key = lax.broadcasted_iota(jnp.int32, shape, 1)
     step = (lax.broadcasted_iota(jnp.int32, shape, 0) // heads) % steps
     counted = limits_ref[requests : requests + 1, :1] == 0
-    for i in range(out_ref.shape[0] // share):
+    for i in range(requests_rows // share):
         request = info_ref[0] + i
         scores = (
             lax.dot_general(
@@ -203,9 +222,10 @@
         weights = jnp.exp2(scores - top)
         total = jnp.sum(weights, axis=1, keepdims=True)
         mixed = jnp.dot(weights.astype(bf16), fresh[:, :width], preferred_element_type=f32)
-        at = slice(i * share, (i + 1) * share)
-        out_ref[at, :width] = mixed.astype(bf16)
-        out_ref[at, width:] = split_stats(top, total, share).astype(bf16)
+        out_ref[i * share : (i + 1) * share, :] = mixed.astype(bf16)
+        stats.append(split_stats(top, total, share))
+    out_ref[requests_rows:, :] = jnp.zeros((16, width), bf16)
+    out_ref[requests_rows:, :requests_rows] = jnp.concatenate(stats, axis=0).T[:16].astype(bf16)
 
 
 def merge_parts(parts, width):
@@ -223,37 +243,41 @@
 
 
 def pair_kernel(a_ref, b_ref, *sent_refs):
-    rows = sent_refs[0].shape[0]
-    width = a_ref.shape[2] - 128
+    width = sent_refs[0].shape[1]
+    rows = sent_refs[0].shape[0] - 16
     for owner, sent_ref in enumerate(sent_refs):
         merged, peak, weight_sum = merge_parts((a_ref[owner], b_ref[owner]), width)
-        sent_ref[:, :width] = merged.astype(bf16)
-        sent_ref[:, width:] = split_stats(peak, weight_sum, rows).astype(bf16)
+        sent_ref[:rows, :] = merged.astype(bf16)
+        sent_ref[rows:, :] = jnp.zeros((16, width), bf16)
+        sent_ref[rows:, :rows] = split_stats(peak, weight_sum, rows).T[:16].astype(bf16)
 
 
 def project_kernel(heads, *refs):
-    *parts, up_ref, out_ref, mixed, projected = refs
-    rows = parts[0].shape[0]
-    merged, peak, weight_sum = merge_parts([part[...] for part in parts], up_ref.shape[1])
-    mixed[...] = merged.reshape(mixed.shape)
-    stats = split_stats(peak, weight_sum, rows).T[:16].astype(bf16)
-    count = rows // heads
-    for h in range(heads):
-        part = mixed[:, h, :]
-        high = part.astype(bf16)
-        low = (part - high.astype(f32)).astype(bf16)
-        both = jnp.dot(jnp.concatenate([high, low], axis=0), up_ref[h], preferred_element_type=f32)
-        projected[:, h, :] = both[:count] + both[count:]
-    values = projected[...].reshape(rows, projected.shape[2]).astype(bf16)
-    out_ref[:rows, :] = values
-    out_ref[rows:, :] = stats
+    *parts, up_ref, out_ref = refs
+    parts = [part[...] for part in parts]
+    rows = out_ref.shape[0] - 16
+    weights, peak, weight_sum = merge_rows(parts, rows)
+    mixed = weigh(parts, weights, rows)
+    high = mixed.astype(bf16)
+    both = jnp.concatenate([high, (mixed - high.astype(f32)).astype(bf16)], axis=0)
+    value_width = out_ref.shape[1]
+    head = lax.broadcasted_iota(jnp.int32, (rows, value_width), 0) % heads
+    values = jnp.zeros((rows, value_width), f32)
+    for h in range(0, heads, 2):
+        two = jnp.concatenate([up_ref[h], up_ref[h + 1]], axis=1)
+        part = jnp.dot(both, two, preferred_element_type=f32)
+        part = part[:rows] + part[rows:]
+        values = jnp.where(head == h, part[:, :value_width], values)
+        values = jnp.where(head == h + 1, part[:, value_width:], values)
+    out_ref[:rows, :] = values.astype(bf16)
+    out_ref[rows:, :] = stat_rows(peak, weight_sum)
 
 
 def merge_rows(parts, rows):
     tops = []
     sums = []
     for part in parts:
-        stat = part[rows:, :].astype(f32)
+        stat = part[rows:, :rows].astype(f32)
         tops.append(stat[0:1] + stat[1:2] + stat[2:3])
         sums.append(stat[3:4] + stat[4:5])
     tops = jnp.concatenate(tops, axis=0)
@@ -274,15 +298,7 @@
     rows = out_ref.shape[0] - 16
     weights, peak, weight_sum = merge_rows(parts, rows)
     out_ref[:rows, :] = weigh(parts, weights, rows).astype(bf16)
-    line = lax.broadcasted_iota(jnp.int32, (16, weights.shape[1]), 0)
-    first = peak.astype(bf16).astype(f32)
-    second = (peak - first).astype(bf16).astype(f32)
-    sum_first = weight_sum.astype(bf16).astype(f32)
-    stats = jnp.where(line == 0, first, 0.0)
-    stats = jnp.where(line == 1, second, stats)
-    stats = jnp.where(line == 2, peak - first - second, stats)
-    stats = jnp.where(line == 3, sum_first, stats)
-    out_ref[rows:, :] = jnp.where(line == 4, weight_sum - sum_first, stats).astype(bf16)
+    out_ref[rows:, :] = stat_rows(peak, weight_sum)
 
 
 def finish_kernel(*refs):
@@ -341,7 +357,7 @@
         out_specs=[vmem] * 4,
         out_shape=(
             jax.ShapeDtypeStruct((requests, steps * heads, wide), bf16),
-            jax.ShapeDtypeStruct((half, steps * heads, wide), bf16),
+            jax.ShapeDtypeStruct((steps * heads, half * key_width), bf16),
             jax.ShapeDtypeStruct((pairs, key_width), bf16),
             jax.ShapeDtypeStruct((8, 128), jnp.int32),
         ),
@@ -378,7 +394,7 @@
         functools.partial(fresh_kernel, scale, steps, heads),
         in_specs=[smem, vmem, vmem, vmem],
         out_specs=vmem,
-        out_shape=jax.ShapeDtypeStruct((chunk, width + 128), bf16),
+        out_shape=jax.ShapeDtypeStruct((chunk + 16, width), bf16),
         compiler_params=small,
         cost_estimate=pl.CostEstimate(flops=10**9, bytes_accessed=4 * 10**6, transcendentals=0),
         name="fresh",
@@ -425,7 +441,7 @@
         pair_kernel,
         in_specs=[vmem] * 2,
         out_specs=[vmem] * owners,
-        out_shape=[jax.ShapeDtypeStruct((chunk, width + 128), bf16)] * owners,
+        out_shape=[jax.ShapeDtypeStruct((chunk + 16, width), bf16)] * owners,
         compiler_params=small,
         name="pair_merge",
     )(other_part, own_part)
@@ -435,10 +451,6 @@
         in_specs=[vmem] * 6,
         out_specs=vmem,
         out_shape=jax.ShapeDtypeStruct((chunk + 16, value_width), bf16),
-        scratch_shapes=[
-            pltpu.VMEM((chunk // heads, heads, width), f32),
-            pltpu.VMEM((chunk // heads, heads, value_width), f32),
-        ],
         compiler_params=small,
         name="project",
     )(sent[0], *arrived, fresh, up_values)

time: 57.4 us -> 55.7 us (0.970)
  waiting for transfers between devices: 17.8 us -> 16.3 us
    ppermute x6, waiting for transfers between devices: 9.37 us -> 7.91 us  [over_head(): return lax.ppermute(array, 'head', [(i, i ^ k) for i in range(owners)])]
  transfers between devices with their start and end apart: 17 -> 17, of which waited for: 11 -> 10; matrix products, arithmetic and copies ran while one was open for 0% -> 0% of each run, Pallas kernels for 12% -> 12%
where the time goes in v10:
time: 55.7 us; the launch traced here: 55.6 us
  starting transfers between devices  23.8 us (43%)
  waiting for transfers between devices  16.3 us (29%)
  Pallas kernels  15.5 us (28%)
    ppermute x6, starting transfers between devices, over_head(): return lax.ppermute(array, 'head', [(i, i ^ k) for i in range(owners)])  8.22 us
    ppermute x6, starting transfers between devices, over_plane(): return lax.ppermute(array, ('z', 'x'), [(i, i ^ k) for i in range(plane)])  8.11 us
    ppermute x6, waiting for transfers between devices, over_head(): return lax.ppermute(array, 'head', [(i, i ^ k) for i in range(owners)])  7.91 us
    pallas_call x2, Pallas kernels, attend(): pl.pallas_call(functools.partial(attention_kernel, scale), in_specs=[smem...  7.04 us
    ppermute x6, waiting for transfers between devices, over_plane(): return lax.ppermute(array, ('z', 'x'), [(i, i ^ k) for i in range(plane)])  6.49 us
    ppermute x1, starting transfers between devices, on_device(): theirs = lax.ppermute(own, 'core', swap)  3.61 us
    ppermute x3, starting transfers between devices, on_device(): passed = [lax.ppermute(g, 'core', swap) for g in got]  3.38 us
    pallas_call x1, Pallas kernels, on_device(): pl.pallas_call(stage_kernel, in_specs=[smem, anywhere], out_specs=vmem, o...  2.54 us
  transfers between devices with their start and end apart: 17, of which 10 were waited for; matrix products, arithmetic and copies ran while one was open for 0% of the time, Pallas kernels for 12%

profile of v10, /device:TPU:1, one launch (start us, length us, event | category | flops | bytes accessed | tf_op | source)
XLA Modules:
  0.0 55.6 jit_solution(14753590951069179787)
XLA Ops:
  0.0 2.1 %queries.1 = (bf16[4,64,640]{2,1,0:T(8,128)(2,1)S(1)}, bf16[64,1152]{1,0:T(8,128)(2,1)S(1)}, bf16[16,576]{1,0:T(8,128)(2,1)S(1)}, s32[8,128]{1,0:T(8,128)S(1)}) custom-call(s32[1]{0:T(128)} %bitcast.1.info_ref, s32[1]{0:T(128)} %bitcast.own_first_ref.info_ref, s32[1]{0:T(128)} %bitcast.2.row_ref, s32[1]{0:T(128)} %bitcast.3.place_ref, s32[4]{0:T(128)} %positions_hbm.1, ...), custom_call_target="tpu_custom_call" | custom-call | tf_op jit(solution)/shard_map/queries/pallas_call | solution.py:354
  2.1 3.8 %collective-permute-start = (bf16[64,1152]{1,0:T(8,128)(2,1)S(1)}, bf16[64,1152]{1,0:T(8,128)(2,1)S(1)}, u32[]{:S(2)}, u32[]{:S(2)}) collective-permute-start(bf16[64,1152]{1,0:T(8,128)(2,1)S(1)} %get-tuple-element.23), channel_id=1, source_target_pairs={{0,2},{1,3},{2,0},{3,1},{4,6},{5,7},{6,4},{7,5},{8,10},{9,11},{10,... | collective-permute-start | bytes 442376 | tf_op jit(solution)/shard_map/ppermute | solution.py:388
  5.9 0.8 %collective-permute-start.1 = (bf16[64,1152]{1,0:T(8,128)(2,1)S(1)}, bf16[64,1152]{1,0:T(8,128)(2,1)S(1)}, u32[]{:S(2)}, u32[]{:S(2)}) collective-permute-start(bf16[64,1152]{1,0:T(8,128)(2,1)S(1)} %get-tuple-element.23), channel_id=1, source_target_pairs={{0,3},{1,2},{2,1},{3,0},{4,7},{5,6},{6,5},{7,4},{8,11},{9,10},{10,... | collective-permute-start | bytes 442376 | tf_op jit(solution)/shard_map/ppermute | solution.py:388
  6.7 2.5 %stage.1.k_ref = bf16[2,576,2048]{2,1,0:T(8,128)(2,1)S(1)} custom-call(s32[1]{0:T(128)} %bitcast.1.info_ref, bf16[4,576,2048]{2,1,0:T(8,128)(2,1)} %bitcast.6), custom_call_target="tpu_custom_call" | custom-call | bytes 4718592 | tf_op jit(solution)/shard_map/stage/pallas_call | solution.py:405
  9.3 1.9 %collective-permute-start.3 = (bf16[64,1152]{1,0:T(8,128)(2,1)S(1)}, bf16[64,1152]{1,0:T(8,128)(2,1)S(1)}, u32[]{:S(2)}, u32[]{:S(2)}) collective-permute-start(bf16[64,1152]{1,0:T(8,128)(2,1)S(1)} %collective-permute-done.q1_ref), channel_id=1, source_target_pairs={{0,4},{4,0},{1,5},{5,1},{2,6},{6,2},{3,7},{7,3},{8,12},{12,8},{9,1... | collective-permute-start | bytes 442376 | tf_op jit(solution)/shard_map/ppermute | solution.py:416
  11.1 1.6 %collective-permute-done.1.q2_ref = bf16[64,1152]{1,0:T(8,128)(2,1)S(1)} collective-permute-done((bf16[64,1152]{1,0:T(8,128)(2,1)S(1)}, bf16[64,1152]{1,0:T(8,128)(2,1)S(1)}, u32[]{:S(2)}, u32[]{:S(2)}) %collective-permute-start.1) | collective-permute-done | bytes 147488 | tf_op jit(solution)/shard_map/ppermute | solution.py:388
  12.8 1.1 %collective-permute-start.4 = (bf16[64,1152]{1,0:T(8,128)(2,1)S(1)}, bf16[64,1152]{1,0:T(8,128)(2,1)S(1)}, u32[]{:S(2)}, u32[]{:S(2)}) collective-permute-start(bf16[64,1152]{1,0:T(8,128)(2,1)S(1)} %collective-permute-done.1.q2_ref), channel_id=1, source_target_pairs={{0,4},{4,0},{1,5},{5,1},{2,6},{6,2},{3,7},{7,3},{8,12},{12,8},{9,1... | collective-permute-start | bytes 442376 | tf_op jit(solution)/shard_map/ppermute | solution.py:416
  15.3 3.5 %attention.2 = bf16[4,128,640]{2,1,0:T(8,128)(2,1)S(1)} custom-call(s32[1]{0:T(128)} %bitcast.1.info_ref, s32[8,128]{1,0:T(8,128)S(1)} %get-tuple-element.21.limits_ref, bf16[4,64,640]{2,1,0:T(8,128)(2,1)S(1)} %get-tuple-element.22.own_ref, bf16[64,1152]{1,0:T(8,128)(2,1)S(1)} %collective-permute-done.q1_ref, ...), custom_call_target="tpu_custom_call" | custom-call | flops 2281701376 | bytes 4718592 | tf_op jit(solution)/shard_map/attention/pallas_call | solution.py:422
  19.3 3.5 %attention.3.b_ref = bf16[4,128,640]{2,1,0:T(8,128)(2,1)S(1)} custom-call(s32[1]{0:T(128)} %bitcast.own_first_ref.info_ref, s32[8,128]{1,0:T(8,128)S(1)} %get-tuple-element.21.limits_ref, bf16[4,64,640]{2,1,0:T(8,128)(2,1)S(1)} %get-tuple-element.22.own_ref, bf16[64,1152]{1,0:T(8,128)(2,1)S(1)} %collective-permute-done.3.q1_ref, ...), custom_call_target="tpu_custom_call" | custom-call | flops 2281701376 | bytes 4718592 | tf_op jit(solution)/shard_map/attention/pallas_call | solution.py:422
  22.8 1.0 %pair_merge.1 = (bf16[144,512]{1,0:T(8,128)(2,1)S(1)}, bf16[144,512]{1,0:T(8,128)(2,1)S(1)}, bf16[144,512]{1,0:T(8,128)(2,1)S(1)}, bf16[144,512]{1,0:T(8,128)(2,1)S(1)}) custom-call(bf16[4,128,640]{2,1,0:T(8,128)(2,1)S(1)} %collective-permute-done.6.a_ref, bf16[4,128,640]{2,1,0:T(8,128)(2,1)S(1)} %attention.3.b_ref), custom_call_target="tpu_custom_call" | custom-call | tf_op jit(solution)/shard_map/pair_merge/pallas_call | solution.py:440
  23.8 2.1 %collective-permute-start.7 = (bf16[144,512]{1,0:T(8,128)(2,1)S(1)}, bf16[144,512]{1,0:T(8,128)(2,1)S(1)}, u32[]{:S(2)}, u32[]{:S(2)}) collective-permute-start(bf16[144,512]{1,0:T(8,128)(2,1)S(1)} %get-tuple-element.33), channel_id=1, source_target_pairs={{0,2},{1,3},{2,0},{3,1},{4,6},{5,7},{6,4},{7,5},{8,10},{9,11},{10,... | collective-permute-start | bytes 442376 | tf_op jit(solution)/shard_map/ppermute | solution.py:388
  25.9 1.6 %collective-permute-start.8 = (bf16[144,512]{1,0:T(8,128)(2,1)S(1)}, bf16[144,512]{1,0:T(8,128)(2,1)S(1)}, u32[]{:S(2)}, u32[]{:S(2)}) collective-permute-start(bf16[144,512]{1,0:T(8,128)(2,1)S(1)} %get-tuple-element.34), channel_id=1, source_target_pairs={{0,3},{1,2},{2,1},{3,0},{4,7},{5,6},{6,5},{7,4},{8,11},{9,10},{10,... | collective-permute-start | bytes 442376 | tf_op jit(solution)/shard_map/ppermute | solution.py:388
  28.1 2.6 %collective-permute-done.7.refs_1_ = bf16[144,512]{1,0:T(8,128)(2,1)S(1)} collective-permute-done((bf16[144,512]{1,0:T(8,128)(2,1)S(1)}, bf16[144,512]{1,0:T(8,128)(2,1)S(1)}, u32[]{:S(2)}, u32[]{:S(2)}) %collective-permute-start.7) | collective-permute-done | bytes 147488 | tf_op jit(solution)/shard_map/ppermute | solution.py:388
  30.7 3.6 %collective-permute-done.8.refs_2_ = bf16[144,512]{1,0:T(8,128)(2,1)S(1)} collective-permute-done((bf16[144,512]{1,0:T(8,128)(2,1)S(1)}, bf16[144,512]{1,0:T(8,128)(2,1)S(1)}, u32[]{:S(2)}, u32[]{:S(2)}) %collective-permute-start.8) | collective-permute-done | bytes 147488 | tf_op jit(solution)/shard_map/ppermute | solution.py:388
  34.3 1.0 %project.1.refs_0_ = bf16[144,128]{1,0:T(8,128)(2,1)S(1)} custom-call(bf16[144,512]{1,0:T(8,128)(2,1)S(1)} %get-tuple-element.32.refs_0_, bf16[144,512]{1,0:T(8,128)(2,1)S(1)} %collective-permute-done.7.refs_1_, bf16[144,512]{1,0:T(8,128)(2,1)S(1)} %collective-permute-done.8.refs_2_, bf16[144,512]{1,0:T(8,128)(2,1)S(1)} %collective-permute-done.9.refs_3_, ...), custom_call_target="tpu_custom_call" | custom-call | tf_op jit(solution)/shard_map/project/pallas_call | solution.py:449
  35.3 2.8 %collective-permute-start.10 = (bf16[144,128]{1,0:T(8,128)(2,1)S(1)}, bf16[144,128]{1,0:T(8,128)(2,1)S(1)}, u32[]{:S(2)}, u32[]{:S(2)}) collective-permute-start(bf16[144,128]{1,0:T(8,128)(2,1)S(1)} %project.1.refs_0_), channel_id=1, source_target_pairs={{0,16},{8,24},{16,0},{24,8},{32,48},{40,56},{48,32},{56,40},{64,80... | collective-permute-start | bytes 110600 | tf_op jit(solution)/shard_map/ppermute | solution.py:459
  38.1 0.9 %collective-permute-start.11 = (bf16[144,128]{1,0:T(8,128)(2,1)S(1)}, bf16[144,128]{1,0:T(8,128)(2,1)S(1)}, u32[]{:S(2)}, u32[]{:S(2)}) collective-permute-start(bf16[144,128]{1,0:T(8,128)(2,1)S(1)} %project.1.refs_0_), channel_id=1, source_target_pairs={{0,24},{8,16},{16,8},{24,0},{32,56},{40,48},{48,40},{56,32},{64,88... | collective-permute-start | bytes 110600 | tf_op jit(solution)/shard_map/ppermute | solution.py:459
  39.0 0.7 %collective-permute-done.10.refs_1_ = bf16[144,128]{1,0:T(8,128)(2,1)S(1)} collective-permute-done((bf16[144,128]{1,0:T(8,128)(2,1)S(1)}, bf16[144,128]{1,0:T(8,128)(2,1)S(1)}, u32[]{:S(2)}, u32[]{:S(2)}) %collective-permute-start.10) | collective-permute-done | bytes 36896 | tf_op jit(solution)/shard_map/ppermute | solution.py:459
  39.7 2.4 %collective-permute-done.11.refs_2_ = bf16[144,128]{1,0:T(8,128)(2,1)S(1)} collective-permute-done((bf16[144,128]{1,0:T(8,128)(2,1)S(1)}, bf16[144,128]{1,0:T(8,128)(2,1)S(1)}, u32[]{:S(2)}, u32[]{:S(2)}) %collective-permute-start.11) | collective-permute-done | bytes 36896 | tf_op jit(solution)/shard_map/ppermute | solution.py:459
  42.4 3.7 %collective-permute-start.13 = (bf16[144,128]{1,0:T(8,128)(2,1)S(1)}, bf16[144,128]{1,0:T(8,128)(2,1)S(1)}, u32[]{:S(2)}, u32[]{:S(2)}) collective-permute-start(bf16[144,128]{1,0:T(8,128)(2,1)S(1)} %middle_merge.1.refs_0_), channel_id=1, source_target_pairs={{0,64},{8,72},{16,80},{24,88},{32,96},{40,104},{48,112},{56,120},{... | collective-permute-start | bytes 110600 | tf_op jit(solution)/shard_map/ppermute | solution.py:459
  47.5 2.7 %collective-permute-done.14.refs_2_ = bf16[144,128]{1,0:T(8,128)(2,1)S(1)} collective-permute-done((bf16[144,128]{1,0:T(8,128)(2,1)S(1)}, bf16[144,128]{1,0:T(8,128)(2,1)S(1)}, u32[]{:S(2)}, u32[]{:S(2)}) %collective-permute-start.14) | collective-permute-done | bytes 36896 | tf_op jit(solution)/shard_map/ppermute | solution.py:459
  50.5 3.6 %collective-permute-start.16 = (bf16[4,2,16,128]{3,2,1,0:T(8,128)(2,1)S(1)}, bf16[4,2,16,128]{3,2,1,0:T(8,128)(2,1)S(1)}, u32[]{:S(2)}, u32[]{:S(2)}) collective-permute-start(bf16[4,2,16,128]{3,2,1,0:T(8,128)(2,1)S(1)} %finish.1.own_ref), channel_id=1, source_target_pairs={{0,4},{4,0},{1,5},{5,1},{2,6},{6,2},{3,7},{7,3},{8,12},{12,8},{9,1... | collective-permute-start | bytes 98312 | tf_op jit(solution)/shard_map/ppermute | solution.py:477
  54.1 0.9 %collective-permute-done.16.other_ref = bf16[4,2,16,128]{3,2,1,0:T(8,128)(2,1)S(1)} collective-permute-done((bf16[4,2,16,128]{3,2,1,0:T(8,128)(2,1)S(1)}, bf16[4,2,16,128]{3,2,1,0:T(8,128)(2,1)S(1)}, u32[]{:S(2)}, u32[]{:S(2)}) %collective-permute-start.16) | collective-permute-done | bytes 32800 | tf_op jit(solution)/shard_map/ppermute | solution.py:477
  55.0 0.6 %place.1 = bf16[4,4,16,128]{3,2,1,0:T(8,128)(2,1)} custom-call(s32[1]{0:T(128)} %bitcast.own_first_ref.info_ref, bf16[4,2,16,128]{3,2,1,0:T(8,128)(2,1)S(1)} %finish.1.own_ref, bf16[4,2,16,128]{3,2,1,0:T(8,128)(2,1)S(1)} %collective-permute-done.16.other_ref), custom_call_target="tpu_custom_call" | custom-call | tf_op jit(solution)/shard_map/place/pallas_call | solution.py:478
  (29 shorter events, 4.4 us)
Async XLA Ops:
  2.1 7.2 %collective-permute-start = (bf16[64,1152]{1,0:T(8,128)(2,1)S(1)}, bf16[64,1152]{1,0:T(8,128)(2,1)S(1)}, u32[]{:S(2)}, u32[]{:S(2)}) collective-permute-start(bf16[64,1152]{1,0:T(8,128)(2,1)S(1)} %get-tuple-element.23), channel_id=1, source_target_pairs={{0,2},{1,3},{2,0},{3,1},{4,6},{5,7},{6,4},{7,5},{8,10},{9,11},{10,... | collective-permute-start | bytes 442376 | tf_op jit(solution)/shard_map/ppermute | solution.py:388
  5.9 6.8 %collective-permute-start.1 = (bf16[64,1152]{1,0:T(8,128)(2,1)S(1)}, bf16[64,1152]{1,0:T(8,128)(2,1)S(1)}, u32[]{:S(2)}, u32[]{:S(2)}) collective-permute-start(bf16[64,1152]{1,0:T(8,128)(2,1)S(1)} %get-tuple-element.23), channel_id=1, source_target_pairs={{0,3},{1,2},{2,1},{3,0},{4,7},{5,6},{6,5},{7,4},{8,11},{9,10},{10,... | collective-permute-start | bytes 442376 | tf_op jit(solution)/shard_map/ppermute | solution.py:388
  6.7 7.2 %collective-permute-start.2 = (bf16[64,1152]{1,0:T(8,128)(2,1)S(1)}, bf16[64,1152]{1,0:T(8,128)(2,1)S(1)}, u32[]{:S(2)}, u32[]{:S(2)}) collective-permute-start(bf16[64,1152]{1,0:T(8,128)(2,1)S(1)} %get-tuple-element.23), channel_id=1, source_target_pairs={{0,1},{1,0},{2,3},{3,2},{4,5},{5,4},{6,7},{7,6},{8,9},{9,8},{10,11... | collective-permute-start | bytes 442376 | tf_op jit(solution)/shard_map/ppermute | solution.py:388
  6.7 12.6 %slice-start = ((s8[9437184]{0:T(1024)(128)(4,1)}), s8[4194304]{0:T(1024)(128)(4,1)S(1)}, s32[]{:S(2)}) async-start(s8[9437184]{0:T(1024)(128)(4,1)} %bitcast.7), calls=%async_computation | async-start | bytes 8388608
  6.7 12.6 %slice-start.1 = ((s8[9437184]{0:T(1024)(128)(4,1)}), s8[4194304]{0:T(1024)(128)(4,1)S(1)}, s32[]{:S(2)}) async-start(s8[9437184]{0:T(1024)(128)(4,1)} %bitcast.7), calls=%async_computation.1 | async-start | bytes 8388608
  9.3 5.0 %collective-permute-start.3 = (bf16[64,1152]{1,0:T(8,128)(2,1)S(1)}, bf16[64,1152]{1,0:T(8,128)(2,1)S(1)}, u32[]{:S(2)}, u32[]{:S(2)}) collective-permute-start(bf16[64,1152]{1,0:T(8,128)(2,1)S(1)} %collective-permute-done.q1_ref), channel_id=1, source_target_pairs={{0,4},{4,0},{1,5},{5,1},{2,6},{6,2},{3,7},{7,3},{8,12},{12,8},{9,1... | collective-permute-start | bytes 442376 | tf_op jit(solution)/shard_map/ppermute | solution.py:416
  12.8 2.1 %collective-permute-start.4 = (bf16[64,1152]{1,0:T(8,128)(2,1)S(1)}, bf16[64,1152]{1,0:T(8,128)(2,1)S(1)}, u32[]{:S(2)}, u32[]{:S(2)}) collective-permute-start(bf16[64,1152]{1,0:T(8,128)(2,1)S(1)} %collective-permute-done.1.q2_ref), channel_id=1, source_target_pairs={{0,4},{4,0},{1,5},{5,1},{2,6},{6,2},{3,7},{7,3},{8,12},{12,8},{9,1... | collective-permute-start | bytes 442376 | tf_op jit(solution)/shard_map/ppermute | solution.py:416
  13.9 1.4 %collective-permute-start.5 = (bf16[64,1152]{1,0:T(8,128)(2,1)S(1)}, bf16[64,1152]{1,0:T(8,128)(2,1)S(1)}, u32[]{:S(2)}, u32[]{:S(2)}) collective-permute-start(bf16[64,1152]{1,0:T(8,128)(2,1)S(1)} %collective-permute-done.2.q3_ref), channel_id=1, source_target_pairs={{0,4},{4,0},{1,5},{5,1},{2,6},{6,2},{3,7},{7,3},{8,12},{12,8},{9,1... | collective-permute-start | bytes 442376 | tf_op jit(solution)/shard_map/ppermute | solution.py:416
  15.3 4.0 %slice-start.2 = ((s8[9437184]{0:T(1024)(128)(4,1)}), s8[1048576]{0:T(1024)(128)(4,1)S(1)}, s32[]{:S(2)}) async-start(s8[9437184]{0:T(1024)(128)(4,1)} %bitcast.7), calls=%async_computation.2 | async-start | bytes 2097152
  18.8 4.0 %collective-permute-start.6 = (bf16[4,128,640]{2,1,0:T(8,128)(2,1)S(1)}, bf16[4,128,640]{2,1,0:T(8,128)(2,1)S(1)}, u32[]{:S(2)}, u32[]{:S(2)}) collective-permute-start(bf16[4,128,640]{2,1,0:T(8,128)(2,1)S(1)} %attention.2), channel_id=1, source_target_pairs={{0,4},{4,0},{1,5},{5,1},{2,6},{6,2},{3,7},{7,3},{8,12},{12,8},{9,1... | collective-permute-start | bytes 1966088 | tf_op jit(solution)/shard_map/ppermute | solution.py:438
  22.8 11.5 %copy-start = (bf16[16,512,128]{2,1,0:T(8,128)(2,1)S(1)}, bf16[16,512,128]{2,1,0:T(8,128)(2,1)}, u32[]{:S(2)}) copy-start(bf16[16,512,128]{2,1,0:T(8,128)(2,1)} %refs_5_.1) | copy-start | bytes 6291460
  23.8 6.9 %collective-permute-start.7 = (bf16[144,512]{1,0:T(8,128)(2,1)S(1)}, bf16[144,512]{1,0:T(8,128)(2,1)S(1)}, u32[]{:S(2)}, u32[]{:S(2)}) collective-permute-start(bf16[144,512]{1,0:T(8,128)(2,1)S(1)} %get-tuple-element.33), channel_id=1, source_target_pairs={{0,2},{1,3},{2,0},{3,1},{4,6},{5,7},{6,4},{7,5},{8,10},{9,11},{10,... | collective-permute-start | bytes 442376 | tf_op jit(solution)/shard_map/ppermute | solution.py:388
  25.9 8.4 %collective-permute-start.8 = (bf16[144,512]{1,0:T(8,128)(2,1)S(1)}, bf16[144,512]{1,0:T(8,128)(2,1)S(1)}, u32[]{:S(2)}, u32[]{:S(2)}) collective-permute-start(bf16[144,512]{1,0:T(8,128)(2,1)S(1)} %get-tuple-element.34), channel_id=1, source_target_pairs={{0,3},{1,2},{2,1},{3,0},{4,7},{5,6},{6,5},{7,4},{8,11},{9,10},{10,... | collective-permute-start | bytes 442376 | tf_op jit(solution)/shard_map/ppermute | solution.py:388
  27.4 6.9 %collective-permute-start.9 = (bf16[144,512]{1,0:T(8,128)(2,1)S(1)}, bf16[144,512]{1,0:T(8,128)(2,1)S(1)}, u32[]{:S(2)}, u32[]{:S(2)}) collective-permute-start(bf16[144,512]{1,0:T(8,128)(2,1)S(1)} %get-tuple-element.35), channel_id=1, source_target_pairs={{0,1},{1,0},{2,3},{3,2},{4,5},{5,4},{6,7},{7,6},{8,9},{9,8},{10,11... | collective-permute-start | bytes 442376 | tf_op jit(solution)/shard_map/ppermute | solution.py:388
  35.3 4.4 %collective-permute-start.10 = (bf16[144,128]{1,0:T(8,128)(2,1)S(1)}, bf16[144,128]{1,0:T(8,128)(2,1)S(1)}, u32[]{:S(2)}, u32[]{:S(2)}) collective-permute-start(bf16[144,128]{1,0:T(8,128)(2,1)S(1)} %project.1.refs_0_), channel_id=1, source_target_pairs={{0,16},{8,24},{16,0},{24,8},{32,48},{40,56},{48,32},{56,40},{64,80... | collective-permute-start | bytes 110600 | tf_op jit(solution)/shard_map/ppermute | solution.py:459
  38.1 4.0 %collective-permute-start.11 = (bf16[144,128]{1,0:T(8,128)(2,1)S(1)}, bf16[144,128]{1,0:T(8,128)(2,1)S(1)}, u32[]{:S(2)}, u32[]{:S(2)}) collective-permute-start(bf16[144,128]{1,0:T(8,128)(2,1)S(1)} %project.1.refs_0_), channel_id=1, source_target_pairs={{0,24},{8,16},{16,8},{24,0},{32,56},{40,48},{48,40},{56,32},{64,88... | collective-permute-start | bytes 110600 | tf_op jit(solution)/shard_map/ppermute | solution.py:459
  39.0 3.2 %collective-permute-start.12 = (bf16[144,128]{1,0:T(8,128)(2,1)S(1)}, bf16[144,128]{1,0:T(8,128)(2,1)S(1)}, u32[]{:S(2)}, u32[]{:S(2)}) collective-permute-start(bf16[144,128]{1,0:T(8,128)(2,1)S(1)} %project.1.refs_0_), channel_id=1, source_target_pairs={{0,8},{8,0},{16,24},{24,16},{32,40},{40,32},{48,56},{56,48},{64,72... | collective-permute-start | bytes 110600 | tf_op jit(solution)/shard_map/ppermute | solution.py:459
  42.4 5.0 %collective-permute-start.13 = (bf16[144,128]{1,0:T(8,128)(2,1)S(1)}, bf16[144,128]{1,0:T(8,128)(2,1)S(1)}, u32[]{:S(2)}, u32[]{:S(2)}) collective-permute-start(bf16[144,128]{1,0:T(8,128)(2,1)S(1)} %middle_merge.1.refs_0_), channel_id=1, source_target_pairs={{0,64},{8,72},{16,80},{24,88},{32,96},{40,104},{48,112},{56,120},{... | collective-permute-start | bytes 110600 | tf_op jit(solution)/shard_map/ppermute | solution.py:459
  46.1 4.1 %collective-permute-start.14 = (bf16[144,128]{1,0:T(8,128)(2,1)S(1)}, bf16[144,128]{1,0:T(8,128)(2,1)S(1)}, u32[]{:S(2)}, u32[]{:S(2)}) collective-permute-start(bf16[144,128]{1,0:T(8,128)(2,1)S(1)} %middle_merge.1.refs_0_), channel_id=1, source_target_pairs={{0,96},{8,104},{16,112},{24,120},{32,64},{40,72},{48,80},{56,88},{... | collective-permute-start | bytes 110600 | tf_op jit(solution)/shard_map/ppermute | solution.py:459
  46.5 3.6 %collective-permute-start.15 = (bf16[144,128]{1,0:T(8,128)(2,1)S(1)}, bf16[144,128]{1,0:T(8,128)(2,1)S(1)}, u32[]{:S(2)}, u32[]{:S(2)}) collective-permute-start(bf16[144,128]{1,0:T(8,128)(2,1)S(1)} %middle_merge.1.refs_0_), channel_id=1, source_target_pairs={{0,32},{8,40},{16,48},{24,56},{32,0},{40,8},{48,16},{56,24},{64,96... | collective-permute-start | bytes 110600 | tf_op jit(solution)/shard_map/ppermute | solution.py:459
  50.5 4.5 %collective-permute-start.16 = (bf16[4,2,16,128]{3,2,1,0:T(8,128)(2,1)S(1)}, bf16[4,2,16,128]{3,2,1,0:T(8,128)(2,1)S(1)}, u32[]{:S(2)}, u32[]{:S(2)}) collective-permute-start(bf16[4,2,16,128]{3,2,1,0:T(8,128)(2,1)S(1)} %finish.1.own_ref), channel_id=1, source_target_pairs={{0,4},{4,0},{1,5},{5,1},{2,6},{6,2},{3,7},{7,3},{8,12},{12,8},{9,1... | collective-permute-start | bytes 98312 | tf_op jit(solution)/shard_map/ppermute | solution.py:477

commit v11 on v10

--- a/solution.py
+++ b/solution.py
@@ -414,7 +414,6 @@
     )(other_first, in_hbm(cache))
     got[0], staged = lax.optimization_barrier((got[0], staged))
     passed = [lax.ppermute(g, "core", swap) for g in got]
-    got, passed = lax.optimization_barrier((got, passed))
 
     rows = owners * steps * heads
 
@@ -428,7 +427,7 @@
             out_shape=jax.ShapeDtypeStruct((owners, chunk, width + 128), bf16),
             compiler_params=pltpu.CompilerParams(vmem_limit_bytes=18 * 2**20),
             cost_estimate=pl.CostEstimate(
-                flops=2 * half * rows * cached * (key_width + width),
+                flops=20 * half * rows * cached * (key_width + width),
                 bytes_accessed=half * cached * key_width * 2,
                 transcendentals=half * rows * cached,
             ),

time: 55.7 us -> 54.7 us (0.982)
  waiting for transfers between devices: 16.3 us -> 15.3 us
    ppermute x3, waiting for transfers between devices: 1.01 us -> 0.01 us  [on_device(): passed = [lax.ppermute(g, 'core', swap) for g in got]]
  transfers between devices with their start and end apart: 17 -> 17, of which waited for: 10 -> 9; matrix products, arithmetic and copies ran while one was open for 0% -> 0% of each run, Pallas kernels for 12% -> 19%
where the time goes in v11:
time: 54.7 us; the launch traced here: 54.6 us
  starting transfers between devices  23.7 us (43%)
  Pallas kernels  15.4 us (28%)
  waiting for transfers between devices  15.3 us (28%)
    ppermute x6, starting transfers between devices, over_head(): return lax.ppermute(array, 'head', [(i, i ^ k) for i in range(owners)])  8.4 us
    ppermute x6, starting transfers between devices, over_plane(): return lax.ppermute(array, ('z', 'x'), [(i, i ^ k) for i in range(plane)])  8.1 us
    ppermute x6, waiting for transfers between devices, over_head(): return lax.ppermute(array, 'head', [(i, i ^ k) for i in range(owners)])  7.84 us
    pallas_call x2, Pallas kernels, attend(): pl.pallas_call(functools.partial(attention_kernel, scale), in_specs=[smem...  7.03 us
    ppermute x6, waiting for transfers between devices, over_plane(): return lax.ppermute(array, ('z', 'x'), [(i, i ^ k) for i in range(plane)])  6.6 us
    ppermute x1, starting transfers between devices, on_device(): theirs = lax.ppermute(own, 'core', swap)  3.61 us
    ppermute x3, starting transfers between devices, on_device(): passed = [lax.ppermute(g, 'core', swap) for g in got]  3.38 us
    pallas_call x1, Pallas kernels, on_device(): pl.pallas_call(stage_kernel, in_specs=[smem, anywhere], out_specs=vmem, o...  2.54 us
  transfers between devices with their start and end apart: 17, of which 9 were waited for; matrix products, arithmetic and copies ran while one was open for 0% of the time, Pallas kernels for 19%

profile of v11, /device:TPU:1, one launch (start us, length us, event | category | flops | bytes accessed | tf_op | source)
XLA Modules:
  0.0 54.6 jit_solution(4199650557485074114)
XLA Ops:
  0.0 2.1 %queries.1 = (bf16[4,64,640]{2,1,0:T(8,128)(2,1)S(1)}, bf16[64,1152]{1,0:T(8,128)(2,1)S(1)}, bf16[16,576]{1,0:T(8,128)(2,1)S(1)}, s32[8,128]{1,0:T(8,128)S(1)}) custom-call(s32[1]{0:T(128)} %bitcast.1.info_ref, s32[1]{0:T(128)} %bitcast.own_first_ref.info_ref, s32[1]{0:T(128)} %bitcast.2.row_ref, s32[1]{0:T(128)} %bitcast.3.place_ref, s32[4]{0:T(128)} %positions_hbm.1, ...), custom_call_target="tpu_custom_call" | custom-call | tf_op jit(solution)/shard_map/queries/pallas_call | solution.py:354
  2.1 3.8 %collective-permute-start = (bf16[64,1152]{1,0:T(8,128)(2,1)S(1)}, bf16[64,1152]{1,0:T(8,128)(2,1)S(1)}, u32[]{:S(2)}, u32[]{:S(2)}) collective-permute-start(bf16[64,1152]{1,0:T(8,128)(2,1)S(1)} %get-tuple-element.17), channel_id=1, source_target_pairs={{0,2},{1,3},{2,0},{3,1},{4,6},{5,7},{6,4},{7,5},{8,10},{9,11},{10,... | collective-permute-start | bytes 442376 | tf_op jit(solution)/shard_map/ppermute | solution.py:388
  5.9 0.8 %collective-permute-start.1 = (bf16[64,1152]{1,0:T(8,128)(2,1)S(1)}, bf16[64,1152]{1,0:T(8,128)(2,1)S(1)}, u32[]{:S(2)}, u32[]{:S(2)}) collective-permute-start(bf16[64,1152]{1,0:T(8,128)(2,1)S(1)} %get-tuple-element.17), channel_id=1, source_target_pairs={{0,3},{1,2},{2,1},{3,0},{4,7},{5,6},{6,5},{7,4},{8,11},{9,10},{10,... | collective-permute-start | bytes 442376 | tf_op jit(solution)/shard_map/ppermute | solution.py:388
  6.7 2.5 %stage.1.k_ref = bf16[2,576,2048]{2,1,0:T(8,128)(2,1)S(1)} custom-call(s32[1]{0:T(128)} %bitcast.1.info_ref, bf16[4,576,2048]{2,1,0:T(8,128)(2,1)} %bitcast.6), custom_call_target="tpu_custom_call" | custom-call | bytes 4718592 | tf_op jit(solution)/shard_map/stage/pallas_call | solution.py:405
  9.2 1.9 %collective-permute-start.4 = (bf16[64,1152]{1,0:T(8,128)(2,1)S(1)}, bf16[64,1152]{1,0:T(8,128)(2,1)S(1)}, u32[]{:S(2)}, u32[]{:S(2)}) collective-permute-start(bf16[64,1152]{1,0:T(8,128)(2,1)S(1)} %collective-permute-done.q1_ref), channel_id=1, source_target_pairs={{0,4},{4,0},{1,5},{5,1},{2,6},{6,2},{3,7},{7,3},{8,12},{12,8},{9,1... | collective-permute-start | bytes 442376 | tf_op jit(solution)/shard_map/ppermute | solution.py:416
  11.1 1.6 %collective-permute-done.1.q2_ref = bf16[64,1152]{1,0:T(8,128)(2,1)S(1)} collective-permute-done((bf16[64,1152]{1,0:T(8,128)(2,1)S(1)}, bf16[64,1152]{1,0:T(8,128)(2,1)S(1)}, u32[]{:S(2)}, u32[]{:S(2)}) %collective-permute-start.1) | collective-permute-done | bytes 147488 | tf_op jit(solution)/shard_map/ppermute | solution.py:388
  12.8 1.1 %collective-permute-start.5 = (bf16[64,1152]{1,0:T(8,128)(2,1)S(1)}, bf16[64,1152]{1,0:T(8,128)(2,1)S(1)}, u32[]{:S(2)}, u32[]{:S(2)}) collective-permute-start(bf16[64,1152]{1,0:T(8,128)(2,1)S(1)} %collective-permute-done.1.q2_ref), channel_id=1, source_target_pairs={{0,4},{4,0},{1,5},{5,1},{2,6},{6,2},{3,7},{7,3},{8,12},{12,8},{9,1... | collective-permute-start | bytes 442376 | tf_op jit(solution)/shard_map/ppermute | solution.py:416
  14.3 3.5 %attention.2 = bf16[4,128,640]{2,1,0:T(8,128)(2,1)S(1)} custom-call(s32[1]{0:T(128)} %bitcast.1.info_ref, s32[8,128]{1,0:T(8,128)S(1)} %get-tuple-element.15.limits_ref, bf16[4,64,640]{2,1,0:T(8,128)(2,1)S(1)} %get-tuple-element.16.own_ref, bf16[64,1152]{1,0:T(8,128)(2,1)S(1)} %collective-permute-done.q1_ref, ...), custom_call_target="tpu_custom_call" | custom-call | flops 22817013760 | bytes 4718592 | tf_op jit(solution)/shard_map/attention/pallas_call | solution.py:421
  18.0 3.5 %attention.3.b_ref = bf16[4,128,640]{2,1,0:T(8,128)(2,1)S(1)} custom-call(s32[1]{0:T(128)} %bitcast.own_first_ref.info_ref, s32[8,128]{1,0:T(8,128)S(1)} %get-tuple-element.15.limits_ref, bf16[4,64,640]{2,1,0:T(8,128)(2,1)S(1)} %get-tuple-element.16.own_ref, bf16[64,1152]{1,0:T(8,128)(2,1)S(1)} %collective-permute-done.4.q1_ref, ...), custom_call_target="tpu_custom_call" | custom-call | flops 22817013760 | bytes 4718592 | tf_op jit(solution)/shard_map/attention/pallas_call | solution.py:421
  21.6 1.0 %pair_merge.1 = (bf16[144,512]{1,0:T(8,128)(2,1)S(1)}, bf16[144,512]{1,0:T(8,128)(2,1)S(1)}, bf16[144,512]{1,0:T(8,128)(2,1)S(1)}, bf16[144,512]{1,0:T(8,128)(2,1)S(1)}) custom-call(bf16[4,128,640]{2,1,0:T(8,128)(2,1)S(1)} %collective-permute-done.3.a_ref, bf16[4,128,640]{2,1,0:T(8,128)(2,1)S(1)} %attention.3.b_ref), custom_call_target="tpu_custom_call" | custom-call | tf_op jit(solution)/shard_map/pair_merge/pallas_call | solution.py:439
  22.6 2.2 %collective-permute-start.7 = (bf16[144,512]{1,0:T(8,128)(2,1)S(1)}, bf16[144,512]{1,0:T(8,128)(2,1)S(1)}, u32[]{:S(2)}, u32[]{:S(2)}) collective-permute-start(bf16[144,512]{1,0:T(8,128)(2,1)S(1)} %get-tuple-element.21), channel_id=1, source_target_pairs={{0,2},{1,3},{2,0},{3,1},{4,6},{5,7},{6,4},{7,5},{8,10},{9,11},{10,... | collective-permute-start | bytes 442376 | tf_op jit(solution)/shard_map/ppermute | solution.py:388
  24.9 1.6 %collective-permute-start.8 = (bf16[144,512]{1,0:T(8,128)(2,1)S(1)}, bf16[144,512]{1,0:T(8,128)(2,1)S(1)}, u32[]{:S(2)}, u32[]{:S(2)}) collective-permute-start(bf16[144,512]{1,0:T(8,128)(2,1)S(1)} %get-tuple-element.22), channel_id=1, source_target_pairs={{0,3},{1,2},{2,1},{3,0},{4,7},{5,6},{6,5},{7,4},{8,11},{9,10},{10,... | collective-permute-start | bytes 442376 | tf_op jit(solution)/shard_map/ppermute | solution.py:388
  27.0 2.2 %collective-permute-done.7.refs_1_ = bf16[144,512]{1,0:T(8,128)(2,1)S(1)} collective-permute-done((bf16[144,512]{1,0:T(8,128)(2,1)S(1)}, bf16[144,512]{1,0:T(8,128)(2,1)S(1)}, u32[]{:S(2)}, u32[]{:S(2)}) %collective-permute-start.7) | collective-permute-done | bytes 147488 | tf_op jit(solution)/shard_map/ppermute | solution.py:388
  29.2 3.9 %collective-permute-done.8.refs_2_ = bf16[144,512]{1,0:T(8,128)(2,1)S(1)} collective-permute-done((bf16[144,512]{1,0:T(8,128)(2,1)S(1)}, bf16[144,512]{1,0:T(8,128)(2,1)S(1)}, u32[]{:S(2)}, u32[]{:S(2)}) %collective-permute-start.8) | collective-permute-done | bytes 147488 | tf_op jit(solution)/shard_map/ppermute | solution.py:388
  33.2 1.0 %project.1.refs_0_ = bf16[144,128]{1,0:T(8,128)(2,1)S(1)} custom-call(bf16[144,512]{1,0:T(8,128)(2,1)S(1)} %get-tuple-element.20.refs_0_, bf16[144,512]{1,0:T(8,128)(2,1)S(1)} %collective-permute-done.7.refs_1_, bf16[144,512]{1,0:T(8,128)(2,1)S(1)} %collective-permute-done.8.refs_2_, bf16[144,512]{1,0:T(8,128)(2,1)S(1)} %collective-permute-done.9.refs_3_, ...), custom_call_target="tpu_custom_call" | custom-call | tf_op jit(solution)/shard_map/project/pallas_call | solution.py:448
  34.2 2.8 %collective-permute-start.10 = (bf16[144,128]{1,0:T(8,128)(2,1)S(1)}, bf16[144,128]{1,0:T(8,128)(2,1)S(1)}, u32[]{:S(2)}, u32[]{:S(2)}) collective-permute-start(bf16[144,128]{1,0:T(8,128)(2,1)S(1)} %project.1.refs_0_), channel_id=1, source_target_pairs={{0,16},{8,24},{16,0},{24,8},{32,48},{40,56},{48,32},{56,40},{64,80... | collective-permute-start | bytes 110600 | tf_op jit(solution)/shard_map/ppermute | solution.py:458
  37.0 0.9 %collective-permute-start.11 = (bf16[144,128]{1,0:T(8,128)(2,1)S(1)}, bf16[144,128]{1,0:T(8,128)(2,1)S(1)}, u32[]{:S(2)}, u32[]{:S(2)}) collective-permute-start(bf16[144,128]{1,0:T(8,128)(2,1)S(1)} %project.1.refs_0_), channel_id=1, source_target_pairs={{0,24},{8,16},{16,8},{24,0},{32,56},{40,48},{48,40},{56,32},{64,88... | collective-permute-start | bytes 110600 | tf_op jit(solution)/shard_map/ppermute | solution.py:458
  37.9 0.7 %collective-permute-done.10.refs_1_ = bf16[144,128]{1,0:T(8,128)(2,1)S(1)} collective-permute-done((bf16[144,128]{1,0:T(8,128)(2,1)S(1)}, bf16[144,128]{1,0:T(8,128)(2,1)S(1)}, u32[]{:S(2)}, u32[]{:S(2)}) %collective-permute-start.10) | collective-permute-done | bytes 36896 | tf_op jit(solution)/shard_map/ppermute | solution.py:458
  38.6 2.5 %collective-permute-done.11.refs_2_ = bf16[144,128]{1,0:T(8,128)(2,1)S(1)} collective-permute-done((bf16[144,128]{1,0:T(8,128)(2,1)S(1)}, bf16[144,128]{1,0:T(8,128)(2,1)S(1)}, u32[]{:S(2)}, u32[]{:S(2)}) %collective-permute-start.11) | collective-permute-done | bytes 36896 | tf_op jit(solution)/shard_map/ppermute | solution.py:458
  41.3 3.7 %collective-permute-start.13 = (bf16[144,128]{1,0:T(8,128)(2,1)S(1)}, bf16[144,128]{1,0:T(8,128)(2,1)S(1)}, u32[]{:S(2)}, u32[]{:S(2)}) collective-permute-start(bf16[144,128]{1,0:T(8,128)(2,1)S(1)} %middle_merge.1.refs_0_), channel_id=1, source_target_pairs={{0,64},{8,72},{16,80},{24,88},{32,96},{40,104},{48,112},{56,120},{... | collective-permute-start | bytes 110600 | tf_op jit(solution)/shard_map/ppermute | solution.py:458
  46.4 2.8 %collective-permute-done.14.refs_2_ = bf16[144,128]{1,0:T(8,128)(2,1)S(1)} collective-permute-done((bf16[144,128]{1,0:T(8,128)(2,1)S(1)}, bf16[144,128]{1,0:T(8,128)(2,1)S(1)}, u32[]{:S(2)}, u32[]{:S(2)}) %collective-permute-start.14) | collective-permute-done | bytes 36896 | tf_op jit(solution)/shard_map/ppermute | solution.py:458
  49.5 3.6 %collective-permute-start.16 = (bf16[4,2,16,128]{3,2,1,0:T(8,128)(2,1)S(1)}, bf16[4,2,16,128]{3,2,1,0:T(8,128)(2,1)S(1)}, u32[]{:S(2)}, u32[]{:S(2)}) collective-permute-start(bf16[4,2,16,128]{3,2,1,0:T(8,128)(2,1)S(1)} %finish.1.own_ref), channel_id=1, source_target_pairs={{0,4},{4,0},{1,5},{5,1},{2,6},{6,2},{3,7},{7,3},{8,12},{12,8},{9,1... | collective-permute-start | bytes 98312 | tf_op jit(solution)/shard_map/ppermute | solution.py:476
  53.1 0.9 %collective-permute-done.16.other_ref = bf16[4,2,16,128]{3,2,1,0:T(8,128)(2,1)S(1)} collective-permute-done((bf16[4,2,16,128]{3,2,1,0:T(8,128)(2,1)S(1)}, bf16[4,2,16,128]{3,2,1,0:T(8,128)(2,1)S(1)}, u32[]{:S(2)}, u32[]{:S(2)}) %collective-permute-start.16) | collective-permute-done | bytes 32800 | tf_op jit(solution)/shard_map/ppermute | solution.py:476
  53.9 0.6 %place.1 = bf16[4,4,16,128]{3,2,1,0:T(8,128)(2,1)} custom-call(s32[1]{0:T(128)} %bitcast.own_first_ref.info_ref, bf16[4,2,16,128]{3,2,1,0:T(8,128)(2,1)S(1)} %finish.1.own_ref, bf16[4,2,16,128]{3,2,1,0:T(8,128)(2,1)S(1)} %collective-permute-done.16.other_ref), custom_call_target="tpu_custom_call" | custom-call | tf_op jit(solution)/shard_map/place/pallas_call | solution.py:477
  (29 shorter events, 3.2 us)
Async XLA Ops:
  2.1 7.2 %collective-permute-start = (bf16[64,1152]{1,0:T(8,128)(2,1)S(1)}, bf16[64,1152]{1,0:T(8,128)(2,1)S(1)}, u32[]{:S(2)}, u32[]{:S(2)}) collective-permute-start(bf16[64,1152]{1,0:T(8,128)(2,1)S(1)} %get-tuple-element.17), channel_id=1, source_target_pairs={{0,2},{1,3},{2,0},{3,1},{4,6},{5,7},{6,4},{7,5},{8,10},{9,11},{10,... | collective-permute-start | bytes 442376 | tf_op jit(solution)/shard_map/ppermute | solution.py:388
  5.9 6.8 %collective-permute-start.1 = (bf16[64,1152]{1,0:T(8,128)(2,1)S(1)}, bf16[64,1152]{1,0:T(8,128)(2,1)S(1)}, u32[]{:S(2)}, u32[]{:S(2)}) collective-permute-start(bf16[64,1152]{1,0:T(8,128)(2,1)S(1)} %get-tuple-element.17), channel_id=1, source_target_pairs={{0,3},{1,2},{2,1},{3,0},{4,7},{5,6},{6,5},{7,4},{8,11},{9,10},{10,... | collective-permute-start | bytes 442376 | tf_op jit(solution)/shard_map/ppermute | solution.py:388
  6.7 7.2 %collective-permute-start.2 = (bf16[64,1152]{1,0:T(8,128)(2,1)S(1)}, bf16[64,1152]{1,0:T(8,128)(2,1)S(1)}, u32[]{:S(2)}, u32[]{:S(2)}) collective-permute-start(bf16[64,1152]{1,0:T(8,128)(2,1)S(1)} %get-tuple-element.17), channel_id=1, source_target_pairs={{0,1},{1,0},{2,3},{3,2},{4,5},{5,4},{6,7},{7,6},{8,9},{9,8},{10,11... | collective-permute-start | bytes 442376 | tf_op jit(solution)/shard_map/ppermute | solution.py:388
  6.7 11.3 %slice-start = ((s8[9437184]{0:T(1024)(128)(4,1)}), s8[4194304]{0:T(1024)(128)(4,1)S(1)}, s32[]{:S(2)}) async-start(s8[9437184]{0:T(1024)(128)(4,1)} %bitcast.7), calls=%async_computation | async-start | bytes 8388608
  9.2 8.7 %collective-permute-start.4 = (bf16[64,1152]{1,0:T(8,128)(2,1)S(1)}, bf16[64,1152]{1,0:T(8,128)(2,1)S(1)}, u32[]{:S(2)}, u32[]{:S(2)}) collective-permute-start(bf16[64,1152]{1,0:T(8,128)(2,1)S(1)} %collective-permute-done.q1_ref), channel_id=1, source_target_pairs={{0,4},{4,0},{1,5},{5,1},{2,6},{6,2},{3,7},{7,3},{8,12},{12,8},{9,1... | collective-permute-start | bytes 442376 | tf_op jit(solution)/shard_map/ppermute | solution.py:416
  12.8 5.2 %collective-permute-start.5 = (bf16[64,1152]{1,0:T(8,128)(2,1)S(1)}, bf16[64,1152]{1,0:T(8,128)(2,1)S(1)}, u32[]{:S(2)}, u32[]{:S(2)}) collective-permute-start(bf16[64,1152]{1,0:T(8,128)(2,1)S(1)} %collective-permute-done.1.q2_ref), channel_id=1, source_target_pairs={{0,4},{4,0},{1,5},{5,1},{2,6},{6,2},{3,7},{7,3},{8,12},{12,8},{9,1... | collective-permute-start | bytes 442376 | tf_op jit(solution)/shard_map/ppermute | solution.py:416
  13.9 4.1 %collective-permute-start.6 = (bf16[64,1152]{1,0:T(8,128)(2,1)S(1)}, bf16[64,1152]{1,0:T(8,128)(2,1)S(1)}, u32[]{:S(2)}, u32[]{:S(2)}) collective-permute-start(bf16[64,1152]{1,0:T(8,128)(2,1)S(1)} %collective-permute-done.2.q3_ref), channel_id=1, source_target_pairs={{0,4},{4,0},{1,5},{5,1},{2,6},{6,2},{3,7},{7,3},{8,12},{12,8},{9,1... | collective-permute-start | bytes 442376 | tf_op jit(solution)/shard_map/ppermute | solution.py:416
  14.3 3.8 %slice-start.1 = ((s8[9437184]{0:T(1024)(128)(4,1)}), s8[4194304]{0:T(1024)(128)(4,1)S(1)}, s32[]{:S(2)}) async-start(s8[9437184]{0:T(1024)(128)(4,1)} %bitcast.7), calls=%async_computation.1 | async-start | bytes 8388608
  14.3 3.8 %slice-start.2 = ((s8[9437184]{0:T(1024)(128)(4,1)}), s8[1048576]{0:T(1024)(128)(4,1)S(1)}, s32[]{:S(2)}) async-start(s8[9437184]{0:T(1024)(128)(4,1)} %bitcast.7), calls=%async_computation.2 | async-start | bytes 2097152
  17.8 3.8 %collective-permute-start.3 = (bf16[4,128,640]{2,1,0:T(8,128)(2,1)S(1)}, bf16[4,128,640]{2,1,0:T(8,128)(2,1)S(1)}, u32[]{:S(2)}, u32[]{:S(2)}) collective-permute-start(bf16[4,128,640]{2,1,0:T(8,128)(2,1)S(1)} %attention.2), channel_id=1, source_target_pairs={{0,4},{4,0},{1,5},{5,1},{2,6},{6,2},{3,7},{7,3},{8,12},{12,8},{9,1... | collective-permute-start | bytes 1966088 | tf_op jit(solution)/shard_map/ppermute | solution.py:437
  21.6 11.7 %copy-start = (bf16[16,512,128]{2,1,0:T(8,128)(2,1)S(1)}, bf16[16,512,128]{2,1,0:T(8,128)(2,1)}, u32[]{:S(2)}) copy-start(bf16[16,512,128]{2,1,0:T(8,128)(2,1)} %refs_5_.1) | copy-start | bytes 6291460
  22.6 6.6 %collective-permute-start.7 = (bf16[144,512]{1,0:T(8,128)(2,1)S(1)}, bf16[144,512]{1,0:T(8,128)(2,1)S(1)}, u32[]{:S(2)}, u32[]{:S(2)}) collective-permute-start(bf16[144,512]{1,0:T(8,128)(2,1)S(1)} %get-tuple-element.21), channel_id=1, source_target_pairs={{0,2},{1,3},{2,0},{3,1},{4,6},{5,7},{6,4},{7,5},{8,10},{9,11},{10,... | collective-permute-start | bytes 442376 | tf_op jit(solution)/shard_map/ppermute | solution.py:388
  24.9 8.3 %collective-permute-start.8 = (bf16[144,512]{1,0:T(8,128)(2,1)S(1)}, bf16[144,512]{1,0:T(8,128)(2,1)S(1)}, u32[]{:S(2)}, u32[]{:S(2)}) collective-permute-start(bf16[144,512]{1,0:T(8,128)(2,1)S(1)} %get-tuple-element.22), channel_id=1, source_target_pairs={{0,3},{1,2},{2,1},{3,0},{4,7},{5,6},{6,5},{7,4},{8,11},{9,10},{10,... | collective-permute-start | bytes 442376 | tf_op jit(solution)/shard_map/ppermute | solution.py:388
  26.4 6.8 %collective-permute-start.9 = (bf16[144,512]{1,0:T(8,128)(2,1)S(1)}, bf16[144,512]{1,0:T(8,128)(2,1)S(1)}, u32[]{:S(2)}, u32[]{:S(2)}) collective-permute-start(bf16[144,512]{1,0:T(8,128)(2,1)S(1)} %get-tuple-element.23), channel_id=1, source_target_pairs={{0,1},{1,0},{2,3},{3,2},{4,5},{5,4},{6,7},{7,6},{8,9},{9,8},{10,11... | collective-permute-start | bytes 442376 | tf_op jit(solution)/shard_map/ppermute | solution.py:388
  34.2 4.4 %collective-permute-start.10 = (bf16[144,128]{1,0:T(8,128)(2,1)S(1)}, bf16[144,128]{1,0:T(8,128)(2,1)S(1)}, u32[]{:S(2)}, u32[]{:S(2)}) collective-permute-start(bf16[144,128]{1,0:T(8,128)(2,1)S(1)} %project.1.refs_0_), channel_id=1, source_target_pairs={{0,16},{8,24},{16,0},{24,8},{32,48},{40,56},{48,32},{56,40},{64,80... | collective-permute-start | bytes 110600 | tf_op jit(solution)/shard_map/ppermute | solution.py:458
  37.0 4.0 %collective-permute-start.11 = (bf16[144,128]{1,0:T(8,128)(2,1)S(1)}, bf16[144,128]{1,0:T(8,128)(2,1)S(1)}, u32[]{:S(2)}, u32[]{:S(2)}) collective-permute-start(bf16[144,128]{1,0:T(8,128)(2,1)S(1)} %project.1.refs_0_), channel_id=1, source_target_pairs={{0,24},{8,16},{16,8},{24,0},{32,56},{40,48},{48,40},{56,32},{64,88... | collective-permute-start | bytes 110600 | tf_op jit(solution)/shard_map/ppermute | solution.py:458
  37.9 3.2 %collective-permute-start.12 = (bf16[144,128]{1,0:T(8,128)(2,1)S(1)}, bf16[144,128]{1,0:T(8,128)(2,1)S(1)}, u32[]{:S(2)}, u32[]{:S(2)}) collective-permute-start(bf16[144,128]{1,0:T(8,128)(2,1)S(1)} %project.1.refs_0_), channel_id=1, source_target_pairs={{0,8},{8,0},{16,24},{24,16},{32,40},{40,32},{48,56},{56,48},{64,72... | collective-permute-start | bytes 110600 | tf_op jit(solution)/shard_map/ppermute | solution.py:458
  41.3 5.0 %collective-permute-start.13 = (bf16[144,128]{1,0:T(8,128)(2,1)S(1)}, bf16[144,128]{1,0:T(8,128)(2,1)S(1)}, u32[]{:S(2)}, u32[]{:S(2)}) collective-permute-start(bf16[144,128]{1,0:T(8,128)(2,1)S(1)} %middle_merge.1.refs_0_), channel_id=1, source_target_pairs={{0,64},{8,72},{16,80},{24,88},{32,96},{40,104},{48,112},{56,120},{... | collective-permute-start | bytes 110600 | tf_op jit(solution)/shard_map/ppermute | solution.py:458
  45.0 4.2 %collective-permute-start.14 = (bf16[144,128]{1,0:T(8,128)(2,1)S(1)}, bf16[144,128]{1,0:T(8,128)(2,1)S(1)}, u32[]{:S(2)}, u32[]{:S(2)}) collective-permute-start(bf16[144,128]{1,0:T(8,128)(2,1)S(1)} %middle_merge.1.refs_0_), channel_id=1, source_target_pairs={{0,96},{8,104},{16,112},{24,120},{32,64},{40,72},{48,80},{56,88},{... | collective-permute-start | bytes 110600 | tf_op jit(solution)/shard_map/ppermute | solution.py:458
  45.4 3.7 %collective-permute-start.15 = (bf16[144,128]{1,0:T(8,128)(2,1)S(1)}, bf16[144,128]{1,0:T(8,128)(2,1)S(1)}, u32[]{:S(2)}, u32[]{:S(2)}) collective-permute-start(bf16[144,128]{1,0:T(8,128)(2,1)S(1)} %middle_merge.1.refs_0_), channel_id=1, source_target_pairs={{0,32},{8,40},{16,48},{24,56},{32,0},{40,8},{48,16},{56,24},{64,96... | collective-permute-start | bytes 110600 | tf_op jit(solution)/shard_map/ppermute | solution.py:458
  49.5 4.5 %collective-permute-start.16 = (bf16[4,2,16,128]{3,2,1,0:T(8,128)(2,1)S(1)}, bf16[4,2,16,128]{3,2,1,0:T(8,128)(2,1)S(1)}, u32[]{:S(2)}, u32[]{:S(2)}) collective-permute-start(bf16[4,2,16,128]{3,2,1,0:T(8,128)(2,1)S(1)} %finish.1.own_ref), channel_id=1, source_target_pairs={{0,4},{4,0},{1,5},{5,1},{2,6},{6,2},{3,7},{7,3},{8,12},{12,8},{9,1... | collective-permute-start | bytes 98312 | tf_op jit(solution)/shard_map/ppermute | solution.py:476

commit v12 on v11

--- a/solution.py
+++ b/solution.py
@@ -242,10 +242,10 @@
     return merged, peak, weight_sum
 
 
-def pair_kernel(a_ref, b_ref, *sent_refs):
+def pair_kernel(first, a_ref, b_ref, *sent_refs):
     width = sent_refs[0].shape[1]
     rows = sent_refs[0].shape[0] - 16
-    for owner, sent_ref in enumerate(sent_refs):
+    for owner, sent_ref in enumerate(sent_refs, first):
         merged, peak, weight_sum = merge_parts((a_ref[owner], b_ref[owner]), width)
         sent_ref[:rows, :] = merged.astype(bf16)
         sent_ref[rows:, :] = jnp.zeros((16, width), bf16)
@@ -436,15 +436,19 @@
 
     other_part = lax.ppermute(attend(other_first, got, in_vmem(staged)), "core", swap)
     own_part = attend(own_first, passed, cache)
-    sent = pl.pallas_call(
-        pair_kernel,
-        in_specs=[vmem] * 2,
-        out_specs=[vmem] * owners,
-        out_shape=[jax.ShapeDtypeStruct((chunk + 16, width), bf16)] * owners,
-        compiler_params=small,
-        name="pair_merge",
-    )(other_part, own_part)
-    arrived = [over_head(array, k) for array, k in zip(sent[1:], partners)]
+    def pair(first, count):
+        return pl.pallas_call(
+            functools.partial(pair_kernel, first),
+            in_specs=[vmem] * 2,
+            out_specs=[vmem] * count,
+            out_shape=[pltpu.VMEM((chunk + 16, width), bf16)] * count,
+            compiler_params=small,
+            name="pair_merge",
+        )(other_part, own_part)
+
+    sent = dict(zip(partners, pair(1, owners - 1)))
+    arrived = [over_head(sent[k], k) for k in (1, 3, 2)]
+    (kept,) = pair(0, 1)
     part = pl.pallas_call(
         functools.partial(project_kernel, heads),
         in_specs=[vmem] * 6,
@@ -452,7 +456,7 @@
         out_shape=jax.ShapeDtypeStruct((chunk + 16, value_width), bf16),
         compiler_params=small,
         name="project",
-    )(sent[0], *arrived, fresh, up_values)
+    )(kept, *arrived, fresh, up_values)
 
     def over_plane(array, k):
         return lax.ppermute(array, ("z", "x"), [(i, i ^ k) for i in range(plane)])

time: 54.7 us -> 55.1 us (level)
    pallas_call x1 -> x2, Pallas kernels: 1.02 us -> 1.13 us  [pair(): pl.pallas_call(functools.partial(pair_kernel, first), in_specs=[vmem] * 2...]
where the time goes in v12:
time: 55.1 us; the launch traced here: 55 us
  starting transfers between devices  23.9 us (43%)
  Pallas kernels  15.5 us (28%)
  waiting for transfers between devices  15.4 us (28%)
    ppermute x6, starting transfers between devices, over_head(): return lax.ppermute(array, 'head', [(i, i ^ k) for i in range(owners)])  8.63 us
    ppermute x6, starting transfers between devices, over_plane(): return lax.ppermute(array, ('z', 'x'), [(i, i ^ k) for i in range(plane)])  8.09 us
    ppermute x6, waiting for transfers between devices, over_head(): return lax.ppermute(array, 'head', [(i, i ^ k) for i in range(owners)])  7.85 us
    pallas_call x2, Pallas kernels, attend(): pl.pallas_call(functools.partial(attention_kernel, scale), in_specs=[smem...  7.03 us
    ppermute x6, waiting for transfers between devices, over_plane(): return lax.ppermute(array, ('z', 'x'), [(i, i ^ k) for i in range(plane)])  6.66 us
    ppermute x1, starting transfers between devices, on_device(): theirs = lax.ppermute(own, 'core', swap)  3.61 us
    ppermute x3, starting transfers between devices, on_device(): passed = [lax.ppermute(g, 'core', swap) for g in got]  3.38 us
    pallas_call x1, Pallas kernels, on_device(): pl.pallas_call(stage_kernel, in_specs=[smem, anywhere], out_specs=vmem, o...  2.54 us
  transfers between devices with their start and end apart: 17, of which 9 were waited for; matrix products, arithmetic and copies ran while one was open for 0% of the time, Pallas kernels for 19%

profile of v12, /device:TPU:1, one launch (start us, length us, event | category | flops | bytes accessed | tf_op | source)
XLA Modules:
  0.0 55.0 jit_solution(712830149575328948)
XLA Ops:
  0.0 2.1 %queries.1 = (bf16[4,64,640]{2,1,0:T(8,128)(2,1)S(1)}, bf16[64,1152]{1,0:T(8,128)(2,1)S(1)}, bf16[16,576]{1,0:T(8,128)(2,1)S(1)}, s32[8,128]{1,0:T(8,128)S(1)}) custom-call(s32[1]{0:T(128)} %bitcast.1.info_ref, s32[1]{0:T(128)} %bitcast.own_first_ref.info_ref, s32[1]{0:T(128)} %bitcast.2.row_ref, s32[1]{0:T(128)} %bitcast.3.place_ref, s32[4]{0:T(128)} %positions_hbm.1, ...), custom_call_target="tpu_custom_call" | custom-call | tf_op jit(solution)/shard_map/queries/pallas_call | solution.py:354
  2.1 3.8 %collective-permute-start = (bf16[64,1152]{1,0:T(8,128)(2,1)S(1)}, bf16[64,1152]{1,0:T(8,128)(2,1)S(1)}, u32[]{:S(2)}, u32[]{:S(2)}) collective-permute-start(bf16[64,1152]{1,0:T(8,128)(2,1)S(1)} %get-tuple-element.16), channel_id=1, source_target_pairs={{0,2},{1,3},{2,0},{3,1},{4,6},{5,7},{6,4},{7,5},{8,10},{9,11},{10,... | collective-permute-start | bytes 442376 | tf_op jit(solution)/shard_map/ppermute | solution.py:388
  5.9 0.8 %collective-permute-start.1 = (bf16[64,1152]{1,0:T(8,128)(2,1)S(1)}, bf16[64,1152]{1,0:T(8,128)(2,1)S(1)}, u32[]{:S(2)}, u32[]{:S(2)}) collective-permute-start(bf16[64,1152]{1,0:T(8,128)(2,1)S(1)} %get-tuple-element.16), channel_id=1, source_target_pairs={{0,3},{1,2},{2,1},{3,0},{4,7},{5,6},{6,5},{7,4},{8,11},{9,10},{10,... | collective-permute-start | bytes 442376 | tf_op jit(solution)/shard_map/ppermute | solution.py:388
  6.7 2.5 %stage.1.k_ref = bf16[2,576,2048]{2,1,0:T(8,128)(2,1)S(1)} custom-call(s32[1]{0:T(128)} %bitcast.1.info_ref, bf16[4,576,2048]{2,1,0:T(8,128)(2,1)} %bitcast.6), custom_call_target="tpu_custom_call" | custom-call | bytes 4718592 | tf_op jit(solution)/shard_map/stage/pallas_call | solution.py:405
  9.2 1.9 %collective-permute-start.4 = (bf16[64,1152]{1,0:T(8,128)(2,1)S(1)}, bf16[64,1152]{1,0:T(8,128)(2,1)S(1)}, u32[]{:S(2)}, u32[]{:S(2)}) collective-permute-start(bf16[64,1152]{1,0:T(8,128)(2,1)S(1)} %collective-permute-done.q1_ref), channel_id=1, source_target_pairs={{0,4},{4,0},{1,5},{5,1},{2,6},{6,2},{3,7},{7,3},{8,12},{12,8},{9,1... | collective-permute-start | bytes 442376 | tf_op jit(solution)/shard_map/ppermute | solution.py:416
  11.1 1.6 %collective-permute-done.1.q2_ref = bf16[64,1152]{1,0:T(8,128)(2,1)S(1)} collective-permute-done((bf16[64,1152]{1,0:T(8,128)(2,1)S(1)}, bf16[64,1152]{1,0:T(8,128)(2,1)S(1)}, u32[]{:S(2)}, u32[]{:S(2)}) %collective-permute-start.1) | collective-permute-done | bytes 147488 | tf_op jit(solution)/shard_map/ppermute | solution.py:388
  12.8 1.1 %collective-permute-start.5 = (bf16[64,1152]{1,0:T(8,128)(2,1)S(1)}, bf16[64,1152]{1,0:T(8,128)(2,1)S(1)}, u32[]{:S(2)}, u32[]{:S(2)}) collective-permute-start(bf16[64,1152]{1,0:T(8,128)(2,1)S(1)} %collective-permute-done.1.q2_ref), channel_id=1, source_target_pairs={{0,4},{4,0},{1,5},{5,1},{2,6},{6,2},{3,7},{7,3},{8,12},{12,8},{9,1... | collective-permute-start | bytes 442376 | tf_op jit(solution)/shard_map/ppermute | solution.py:416
  14.3 3.5 %attention.2 = bf16[4,128,640]{2,1,0:T(8,128)(2,1)S(1)} custom-call(s32[1]{0:T(128)} %bitcast.1.info_ref, s32[8,128]{1,0:T(8,128)S(1)} %get-tuple-element.14.limits_ref, bf16[4,64,640]{2,1,0:T(8,128)(2,1)S(1)} %get-tuple-element.15.own_ref, bf16[64,1152]{1,0:T(8,128)(2,1)S(1)} %collective-permute-done.q1_ref, ...), custom_call_target="tpu_custom_call" | custom-call | flops 22817013760 | bytes 4718592 | tf_op jit(solution)/shard_map/attention/pallas_call | solution.py:421
  18.0 3.5 %attention.3.b_ref = bf16[4,128,640]{2,1,0:T(8,128)(2,1)S(1)} custom-call(s32[1]{0:T(128)} %bitcast.own_first_ref.info_ref, s32[8,128]{1,0:T(8,128)S(1)} %get-tuple-element.14.limits_ref, bf16[4,64,640]{2,1,0:T(8,128)(2,1)S(1)} %get-tuple-element.15.own_ref, bf16[64,1152]{1,0:T(8,128)(2,1)S(1)} %collective-permute-done.4.q1_ref, ...), custom_call_target="tpu_custom_call" | custom-call | flops 22817013760 | bytes 4718592 | tf_op jit(solution)/shard_map/attention/pallas_call | solution.py:421
  21.6 0.8 %pair_merge.3 = (bf16[144,512]{1,0:T(8,128)(2,1)S(1)}, bf16[144,512]{1,0:T(8,128)(2,1)S(1)}, bf16[144,512]{1,0:T(8,128)(2,1)S(1)}) custom-call(bf16[4,128,640]{2,1,0:T(8,128)(2,1)S(1)} %collective-permute-done.3.a_ref, bf16[4,128,640]{2,1,0:T(8,128)(2,1)S(1)} %attention.3.b_ref), custom_call_target="tpu_custom_call" | custom-call | tf_op jit(solution)/shard_map/pair_merge/pallas_call | solution.py:440
  22.4 1.4 %collective-permute-start.7 = (bf16[144,512]{1,0:T(8,128)(2,1)S(1)}, bf16[144,512]{1,0:T(8,128)(2,1)S(1)}, u32[]{:S(2)}, u32[]{:S(2)}) collective-permute-start(bf16[144,512]{1,0:T(8,128)(2,1)S(1)} %get-tuple-element.19), channel_id=1, source_target_pairs={{0,1},{1,0},{2,3},{3,2},{4,5},{5,4},{6,7},{7,6},{8,9},{9,8},{10,11... | collective-permute-start | bytes 442376 | tf_op jit(solution)/shard_map/ppermute | solution.py:388
  23.8 1.5 %collective-permute-start.8 = (bf16[144,512]{1,0:T(8,128)(2,1)S(1)}, bf16[144,512]{1,0:T(8,128)(2,1)S(1)}, u32[]{:S(2)}, u32[]{:S(2)}) collective-permute-start(bf16[144,512]{1,0:T(8,128)(2,1)S(1)} %get-tuple-element.20), channel_id=1, source_target_pairs={{0,3},{1,2},{2,1},{3,0},{4,7},{5,6},{6,5},{7,4},{8,11},{9,10},{10,... | collective-permute-start | bytes 442376 | tf_op jit(solution)/shard_map/ppermute | solution.py:388
  25.3 1.1 %collective-permute-start.9 = (bf16[144,512]{1,0:T(8,128)(2,1)S(1)}, bf16[144,512]{1,0:T(8,128)(2,1)S(1)}, u32[]{:S(2)}, u32[]{:S(2)}) collective-permute-start(bf16[144,512]{1,0:T(8,128)(2,1)S(1)} %get-tuple-element.21), channel_id=1, source_target_pairs={{0,2},{1,3},{2,0},{3,1},{4,6},{5,7},{6,4},{7,5},{8,10},{9,11},{10,... | collective-permute-start | bytes 442376 | tf_op jit(solution)/shard_map/ppermute | solution.py:388
  27.5 4.1 %collective-permute-done.8.refs_2_ = bf16[144,512]{1,0:T(8,128)(2,1)S(1)} collective-permute-done((bf16[144,512]{1,0:T(8,128)(2,1)S(1)}, bf16[144,512]{1,0:T(8,128)(2,1)S(1)}, u32[]{:S(2)}, u32[]{:S(2)}) %collective-permute-start.8) | collective-permute-done | bytes 147488 | tf_op jit(solution)/shard_map/ppermute | solution.py:388
  31.6 2.0 %collective-permute-done.9.refs_3_ = bf16[144,512]{1,0:T(8,128)(2,1)S(1)} collective-permute-done((bf16[144,512]{1,0:T(8,128)(2,1)S(1)}, bf16[144,512]{1,0:T(8,128)(2,1)S(1)}, u32[]{:S(2)}, u32[]{:S(2)}) %collective-permute-start.9) | collective-permute-done | bytes 147488 | tf_op jit(solution)/shard_map/ppermute | solution.py:388
  33.6 1.0 %project.1.refs_0_ = bf16[144,128]{1,0:T(8,128)(2,1)S(1)} custom-call(bf16[144,512]{1,0:T(8,128)(2,1)S(1)} %pair_merge.2.refs_0_, bf16[144,512]{1,0:T(8,128)(2,1)S(1)} %collective-permute-done.7.refs_1_, bf16[144,512]{1,0:T(8,128)(2,1)S(1)} %collective-permute-done.8.refs_2_, bf16[144,512]{1,0:T(8,128)(2,1)S(1)} %collective-permute-done.9.refs_3_, ...), custom_call_target="tpu_custom_call" | custom-call | tf_op jit(solution)/shard_map/project/pallas_call | solution.py:452
  34.6 2.8 %collective-permute-start.10 = (bf16[144,128]{1,0:T(8,128)(2,1)S(1)}, bf16[144,128]{1,0:T(8,128)(2,1)S(1)}, u32[]{:S(2)}, u32[]{:S(2)}) collective-permute-start(bf16[144,128]{1,0:T(8,128)(2,1)S(1)} %project.1.refs_0_), channel_id=1, source_target_pairs={{0,16},{8,24},{16,0},{24,8},{32,48},{40,56},{48,32},{56,40},{64,80... | collective-permute-start | bytes 110600 | tf_op jit(solution)/shard_map/ppermute | solution.py:462
  37.4 0.8 %collective-permute-start.11 = (bf16[144,128]{1,0:T(8,128)(2,1)S(1)}, bf16[144,128]{1,0:T(8,128)(2,1)S(1)}, u32[]{:S(2)}, u32[]{:S(2)}) collective-permute-start(bf16[144,128]{1,0:T(8,128)(2,1)S(1)} %project.1.refs_0_), channel_id=1, source_target_pairs={{0,24},{8,16},{16,8},{24,0},{32,56},{40,48},{48,40},{56,32},{64,88... | collective-permute-start | bytes 110600 | tf_op jit(solution)/shard_map/ppermute | solution.py:462
  38.2 0.7 %collective-permute-done.10.refs_1_ = bf16[144,128]{1,0:T(8,128)(2,1)S(1)} collective-permute-done((bf16[144,128]{1,0:T(8,128)(2,1)S(1)}, bf16[144,128]{1,0:T(8,128)(2,1)S(1)}, u32[]{:S(2)}, u32[]{:S(2)}) %collective-permute-start.10) | collective-permute-done | bytes 36896 | tf_op jit(solution)/shard_map/ppermute | solution.py:462
  38.9 2.5 %collective-permute-done.11.refs_2_ = bf16[144,128]{1,0:T(8,128)(2,1)S(1)} collective-permute-done((bf16[144,128]{1,0:T(8,128)(2,1)S(1)}, bf16[144,128]{1,0:T(8,128)(2,1)S(1)}, u32[]{:S(2)}, u32[]{:S(2)}) %collective-permute-start.11) | collective-permute-done | bytes 36896 | tf_op jit(solution)/shard_map/ppermute | solution.py:462
  41.7 3.7 %collective-permute-start.13 = (bf16[144,128]{1,0:T(8,128)(2,1)S(1)}, bf16[144,128]{1,0:T(8,128)(2,1)S(1)}, u32[]{:S(2)}, u32[]{:S(2)}) collective-permute-start(bf16[144,128]{1,0:T(8,128)(2,1)S(1)} %middle_merge.1.refs_0_), channel_id=1, source_target_pairs={{0,64},{8,72},{16,80},{24,88},{32,96},{40,104},{48,112},{56,120},{... | collective-permute-start | bytes 110600 | tf_op jit(solution)/shard_map/ppermute | solution.py:462
  46.7 2.9 %collective-permute-done.14.refs_2_ = bf16[144,128]{1,0:T(8,128)(2,1)S(1)} collective-permute-done((bf16[144,128]{1,0:T(8,128)(2,1)S(1)}, bf16[144,128]{1,0:T(8,128)(2,1)S(1)}, u32[]{:S(2)}, u32[]{:S(2)}) %collective-permute-start.14) | collective-permute-done | bytes 36896 | tf_op jit(solution)/shard_map/ppermute | solution.py:462
  49.9 3.6 %collective-permute-start.16 = (bf16[4,2,16,128]{3,2,1,0:T(8,128)(2,1)S(1)}, bf16[4,2,16,128]{3,2,1,0:T(8,128)(2,1)S(1)}, u32[]{:S(2)}, u32[]{:S(2)}) collective-permute-start(bf16[4,2,16,128]{3,2,1,0:T(8,128)(2,1)S(1)} %finish.1.own_ref), channel_id=1, source_target_pairs={{0,4},{4,0},{1,5},{5,1},{2,6},{6,2},{3,7},{7,3},{8,12},{12,8},{9,1... | collective-permute-start | bytes 98312 | tf_op jit(solution)/shard_map/ppermute | solution.py:480
  53.5 0.9 %collective-permute-done.16.other_ref = bf16[4,2,16,128]{3,2,1,0:T(8,128)(2,1)S(1)} collective-permute-done((bf16[4,2,16,128]{3,2,1,0:T(8,128)(2,1)S(1)}, bf16[4,2,16,128]{3,2,1,0:T(8,128)(2,1)S(1)}, u32[]{:S(2)}, u32[]{:S(2)}) %collective-permute-start.16) | collective-permute-done | bytes 32800 | tf_op jit(solution)/shard_map/ppermute | solution.py:480
  (30 shorter events, 4.2 us)
Async XLA Ops:
  2.1 7.2 %collective-permute-start = (bf16[64,1152]{1,0:T(8,128)(2,1)S(1)}, bf16[64,1152]{1,0:T(8,128)(2,1)S(1)}, u32[]{:S(2)}, u32[]{:S(2)}) collective-permute-start(bf16[64,1152]{1,0:T(8,128)(2,1)S(1)} %get-tuple-element.16), channel_id=1, source_target_pairs={{0,2},{1,3},{2,0},{3,1},{4,6},{5,7},{6,4},{7,5},{8,10},{9,11},{10,... | collective-permute-start | bytes 442376 | tf_op jit(solution)/shard_map/ppermute | solution.py:388
  5.9 6.8 %collective-permute-start.1 = (bf16[64,1152]{1,0:T(8,128)(2,1)S(1)}, bf16[64,1152]{1,0:T(8,128)(2,1)S(1)}, u32[]{:S(2)}, u32[]{:S(2)}) collective-permute-start(bf16[64,1152]{1,0:T(8,128)(2,1)S(1)} %get-tuple-element.16), channel_id=1, source_target_pairs={{0,3},{1,2},{2,1},{3,0},{4,7},{5,6},{6,5},{7,4},{8,11},{9,10},{10,... | collective-permute-start | bytes 442376 | tf_op jit(solution)/shard_map/ppermute | solution.py:388
  6.7 7.2 %collective-permute-start.2 = (bf16[64,1152]{1,0:T(8,128)(2,1)S(1)}, bf16[64,1152]{1,0:T(8,128)(2,1)S(1)}, u32[]{:S(2)}, u32[]{:S(2)}) collective-permute-start(bf16[64,1152]{1,0:T(8,128)(2,1)S(1)} %get-tuple-element.16), channel_id=1, source_target_pairs={{0,1},{1,0},{2,3},{3,2},{4,5},{5,4},{6,7},{7,6},{8,9},{9,8},{10,11... | collective-permute-start | bytes 442376 | tf_op jit(solution)/shard_map/ppermute | solution.py:388
  6.7 11.3 %slice-start = ((s8[9437184]{0:T(1024)(128)(4,1)}), s8[4194304]{0:T(1024)(128)(4,1)S(1)}, s32[]{:S(2)}) async-start(s8[9437184]{0:T(1024)(128)(4,1)} %bitcast.7), calls=%async_computation | async-start | bytes 8388608
  9.2 8.7 %collective-permute-start.4 = (bf16[64,1152]{1,0:T(8,128)(2,1)S(1)}, bf16[64,1152]{1,0:T(8,128)(2,1)S(1)}, u32[]{:S(2)}, u32[]{:S(2)}) collective-permute-start(bf16[64,1152]{1,0:T(8,128)(2,1)S(1)} %collective-permute-done.q1_ref), channel_id=1, source_target_pairs={{0,4},{4,0},{1,5},{5,1},{2,6},{6,2},{3,7},{7,3},{8,12},{12,8},{9,1... | collective-permute-start | bytes 442376 | tf_op jit(solution)/shard_map/ppermute | solution.py:416
  12.8 5.2 %collective-permute-start.5 = (bf16[64,1152]{1,0:T(8,128)(2,1)S(1)}, bf16[64,1152]{1,0:T(8,128)(2,1)S(1)}, u32[]{:S(2)}, u32[]{:S(2)}) collective-permute-start(bf16[64,1152]{1,0:T(8,128)(2,1)S(1)} %collective-permute-done.1.q2_ref), channel_id=1, source_target_pairs={{0,4},{4,0},{1,5},{5,1},{2,6},{6,2},{3,7},{7,3},{8,12},{12,8},{9,1... | collective-permute-start | bytes 442376 | tf_op jit(solution)/shard_map/ppermute | solution.py:416
  13.9 4.1 %collective-permute-start.6 = (bf16[64,1152]{1,0:T(8,128)(2,1)S(1)}, bf16[64,1152]{1,0:T(8,128)(2,1)S(1)}, u32[]{:S(2)}, u32[]{:S(2)}) collective-permute-start(bf16[64,1152]{1,0:T(8,128)(2,1)S(1)} %collective-permute-done.2.q3_ref), channel_id=1, source_target_pairs={{0,4},{4,0},{1,5},{5,1},{2,6},{6,2},{3,7},{7,3},{8,12},{12,8},{9,1... | collective-permute-start | bytes 442376 | tf_op jit(solution)/shard_map/ppermute | solution.py:416
  14.3 3.8 %slice-start.1 = ((s8[9437184]{0:T(1024)(128)(4,1)}), s8[4194304]{0:T(1024)(128)(4,1)S(1)}, s32[]{:S(2)}) async-start(s8[9437184]{0:T(1024)(128)(4,1)} %bitcast.7), calls=%async_computation.1 | async-start | bytes 8388608
  14.3 3.8 %slice-start.2 = ((s8[9437184]{0:T(1024)(128)(4,1)}), s8[1048576]{0:T(1024)(128)(4,1)S(1)}, s32[]{:S(2)}) async-start(s8[9437184]{0:T(1024)(128)(4,1)} %bitcast.7), calls=%async_computation.2 | async-start | bytes 2097152
  17.8 3.8 %collective-permute-start.3 = (bf16[4,128,640]{2,1,0:T(8,128)(2,1)S(1)}, bf16[4,128,640]{2,1,0:T(8,128)(2,1)S(1)}, u32[]{:S(2)}, u32[]{:S(2)}) collective-permute-start(bf16[4,128,640]{2,1,0:T(8,128)(2,1)S(1)} %attention.2), channel_id=1, source_target_pairs={{0,4},{4,0},{1,5},{5,1},{2,6},{6,2},{3,7},{7,3},{8,12},{12,8},{9,1... | collective-permute-start | bytes 1966088 | tf_op jit(solution)/shard_map/ppermute | solution.py:437
  21.6 12.0 %copy-start = (bf16[16,512,128]{2,1,0:T(8,128)(2,1)S(1)}, bf16[16,512,128]{2,1,0:T(8,128)(2,1)}, u32[]{:S(2)}) copy-start(bf16[16,512,128]{2,1,0:T(8,128)(2,1)} %refs_5_.1) | copy-start | bytes 6291460
  22.4 5.1 %collective-permute-start.7 = (bf16[144,512]{1,0:T(8,128)(2,1)S(1)}, bf16[144,512]{1,0:T(8,128)(2,1)S(1)}, u32[]{:S(2)}, u32[]{:S(2)}) collective-permute-start(bf16[144,512]{1,0:T(8,128)(2,1)S(1)} %get-tuple-element.19), channel_id=1, source_target_pairs={{0,1},{1,0},{2,3},{3,2},{4,5},{5,4},{6,7},{7,6},{8,9},{9,8},{10,11... | collective-permute-start | bytes 442376 | tf_op jit(solution)/shard_map/ppermute | solution.py:388
  23.8 7.8 %collective-permute-start.8 = (bf16[144,512]{1,0:T(8,128)(2,1)S(1)}, bf16[144,512]{1,0:T(8,128)(2,1)S(1)}, u32[]{:S(2)}, u32[]{:S(2)}) collective-permute-start(bf16[144,512]{1,0:T(8,128)(2,1)S(1)} %get-tuple-element.20), channel_id=1, source_target_pairs={{0,3},{1,2},{2,1},{3,0},{4,7},{5,6},{6,5},{7,4},{8,11},{9,10},{10,... | collective-permute-start | bytes 442376 | tf_op jit(solution)/shard_map/ppermute | solution.py:388
  25.3 8.2 %collective-permute-start.9 = (bf16[144,512]{1,0:T(8,128)(2,1)S(1)}, bf16[144,512]{1,0:T(8,128)(2,1)S(1)}, u32[]{:S(2)}, u32[]{:S(2)}) collective-permute-start(bf16[144,512]{1,0:T(8,128)(2,1)S(1)} %get-tuple-element.21), channel_id=1, source_target_pairs={{0,2},{1,3},{2,0},{3,1},{4,6},{5,7},{6,4},{7,5},{8,10},{9,11},{10,... | collective-permute-start | bytes 442376 | tf_op jit(solution)/shard_map/ppermute | solution.py:388
  34.6 4.4 %collective-permute-start.10 = (bf16[144,128]{1,0:T(8,128)(2,1)S(1)}, bf16[144,128]{1,0:T(8,128)(2,1)S(1)}, u32[]{:S(2)}, u32[]{:S(2)}) collective-permute-start(bf16[144,128]{1,0:T(8,128)(2,1)S(1)} %project.1.refs_0_), channel_id=1, source_target_pairs={{0,16},{8,24},{16,0},{24,8},{32,48},{40,56},{48,32},{56,40},{64,80... | collective-permute-start | bytes 110600 | tf_op jit(solution)/shard_map/ppermute | solution.py:462
  37.4 4.0 %collective-permute-start.11 = (bf16[144,128]{1,0:T(8,128)(2,1)S(1)}, bf16[144,128]{1,0:T(8,128)(2,1)S(1)}, u32[]{:S(2)}, u32[]{:S(2)}) collective-permute-start(bf16[144,128]{1,0:T(8,128)(2,1)S(1)} %project.1.refs_0_), channel_id=1, source_target_pairs={{0,24},{8,16},{16,8},{24,0},{32,56},{40,48},{48,40},{56,32},{64,88... | collective-permute-start | bytes 110600 | tf_op jit(solution)/shard_map/ppermute | solution.py:462
  38.2 3.2 %collective-permute-start.12 = (bf16[144,128]{1,0:T(8,128)(2,1)S(1)}, bf16[144,128]{1,0:T(8,128)(2,1)S(1)}, u32[]{:S(2)}, u32[]{:S(2)}) collective-permute-start(bf16[144,128]{1,0:T(8,128)(2,1)S(1)} %project.1.refs_0_), channel_id=1, source_target_pairs={{0,8},{8,0},{16,24},{24,16},{32,40},{40,32},{48,56},{56,48},{64,72... | collective-permute-start | bytes 110600 | tf_op jit(solution)/shard_map/ppermute | solution.py:462
  41.7 5.0 %collective-permute-start.13 = (bf16[144,128]{1,0:T(8,128)(2,1)S(1)}, bf16[144,128]{1,0:T(8,128)(2,1)S(1)}, u32[]{:S(2)}, u32[]{:S(2)}) collective-permute-start(bf16[144,128]{1,0:T(8,128)(2,1)S(1)} %middle_merge.1.refs_0_), channel_id=1, source_target_pairs={{0,64},{8,72},{16,80},{24,88},{32,96},{40,104},{48,112},{56,120},{... | collective-permute-start | bytes 110600 | tf_op jit(solution)/shard_map/ppermute | solution.py:462
  45.4 4.2 %collective-permute-start.14 = (bf16[144,128]{1,0:T(8,128)(2,1)S(1)}, bf16[144,128]{1,0:T(8,128)(2,1)S(1)}, u32[]{:S(2)}, u32[]{:S(2)}) collective-permute-start(bf16[144,128]{1,0:T(8,128)(2,1)S(1)} %middle_merge.1.refs_0_), channel_id=1, source_target_pairs={{0,96},{8,104},{16,112},{24,120},{32,64},{40,72},{48,80},{56,88},{... | collective-permute-start | bytes 110600 | tf_op jit(solution)/shard_map/ppermute | solution.py:462
  45.8 3.8 %collective-permute-start.15 = (bf16[144,128]{1,0:T(8,128)(2,1)S(1)}, bf16[144,128]{1,0:T(8,128)(2,1)S(1)}, u32[]{:S(2)}, u32[]{:S(2)}) collective-permute-start(bf16[144,128]{1,0:T(8,128)(2,1)S(1)} %middle_merge.1.refs_0_), channel_id=1, source_target_pairs={{0,32},{8,40},{16,48},{24,56},{32,0},{40,8},{48,16},{56,24},{64,96... | collective-permute-start | bytes 110600 | tf_op jit(solution)/shard_map/ppermute | solution.py:462
  49.9 4.5 %collective-permute-start.16 = (bf16[4,2,16,128]{3,2,1,0:T(8,128)(2,1)S(1)}, bf16[4,2,16,128]{3,2,1,0:T(8,128)(2,1)S(1)}, u32[]{:S(2)}, u32[]{:S(2)}) collective-permute-start(bf16[4,2,16,128]{3,2,1,0:T(8,128)(2,1)S(1)} %finish.1.own_ref), channel_id=1, source_target_pairs={{0,4},{4,0},{1,5},{5,1},{2,6},{6,2},{3,7},{7,3},{8,12},{12,8},{9,1... | collective-permute-start | bytes 98312 | tf_op jit(solution)/shard_map/ppermute | solution.py:480

commit v13 on v12

--- a/solution.py
+++ b/solution.py
@@ -468,7 +468,7 @@
         out_shape=jax.ShapeDtypeStruct(part.shape, bf16),
         compiler_params=small,
         name="middle_merge",
-    )(part, *[over_plane(part, k) for k in (2, 3, 1)])
+    )(part, *[over_plane(part, k) for k in (8, 12, 4)])
     own = pl.pallas_call(
         finish_kernel,
         in_specs=[vmem] * 4,
@@ -476,7 +476,7 @@
         out_shape=jax.ShapeDtypeStruct((steps, half, heads, value_width), bf16),
         compiler_params=small,
         name="finish",
-    )(part, *[over_plane(part, k) for k in (8, 12, 4)])
+    )(part, *[over_plane(part, k) for k in (2, 3, 1)])
     theirs = lax.ppermute(own, "core", swap)
     return pl.pallas_call(
         place_kernel,

time: 55.1 us -> 55.1 us (level)
  no operation moved by 1% of the time
where the time goes in v13:
time: 55.1 us; the launch traced here: 55 us
  starting transfers between devices  23.8 us (43%)
  Pallas kernels  15.5 us (28%)
  waiting for transfers between devices  15.5 us (28%)
    ppermute x6, starting transfers between devices, over_head(): return lax.ppermute(array, 'head', [(i, i ^ k) for i in range(owners)])  8.63 us
    ppermute x6, starting transfers between devices, over_plane(): return lax.ppermute(array, ('z', 'x'), [(i, i ^ k) for i in range(plane)])  8.09 us
    ppermute x6, waiting for transfers between devices, over_head(): return lax.ppermute(array, 'head', [(i, i ^ k) for i in range(owners)])  7.85 us
    pallas_call x2, Pallas kernels, attend(): pl.pallas_call(functools.partial(attention_kernel, scale), in_specs=[smem...  7.03 us
    ppermute x6, waiting for transfers between devices, over_plane(): return lax.ppermute(array, ('z', 'x'), [(i, i ^ k) for i in range(plane)])  6.77 us
    ppermute x1, starting transfers between devices, on_device(): theirs = lax.ppermute(own, 'core', swap)  3.49 us
    ppermute x3, starting transfers between devices, on_device(): passed = [lax.ppermute(g, 'core', swap) for g in got]  3.38 us
    pallas_call x1, Pallas kernels, on_device(): pl.pallas_call(stage_kernel, in_specs=[smem, anywhere], out_specs=vmem, o...  2.54 us
  transfers between devices with their start and end apart: 17, of which 9 were waited for; matrix products, arithmetic and copies ran while one was open for 0% of the time, Pallas kernels for 19%

profile of v13, /device:TPU:1, one launch (start us, length us, event | category | flops | bytes accessed | tf_op | source)
XLA Modules:
  0.0 55.0 jit_solution(7445257003973940839)
XLA Ops:
  0.0 2.1 %queries.1 = (bf16[4,64,640]{2,1,0:T(8,128)(2,1)S(1)}, bf16[64,1152]{1,0:T(8,128)(2,1)S(1)}, bf16[16,576]{1,0:T(8,128)(2,1)S(1)}, s32[8,128]{1,0:T(8,128)S(1)}) custom-call(s32[1]{0:T(128)} %bitcast.1.info_ref, s32[1]{0:T(128)} %bitcast.own_first_ref.info_ref, s32[1]{0:T(128)} %bitcast.2.row_ref, s32[1]{0:T(128)} %bitcast.3.place_ref, s32[4]{0:T(128)} %positions_hbm.1, ...), custom_call_target="tpu_custom_call" | custom-call | tf_op jit(solution)/shard_map/queries/pallas_call | solution.py:354
  2.1 3.8 %collective-permute-start = (bf16[64,1152]{1,0:T(8,128)(2,1)S(1)}, bf16[64,1152]{1,0:T(8,128)(2,1)S(1)}, u32[]{:S(2)}, u32[]{:S(2)}) collective-permute-start(bf16[64,1152]{1,0:T(8,128)(2,1)S(1)} %get-tuple-element.16), channel_id=1, source_target_pairs={{0,2},{1,3},{2,0},{3,1},{4,6},{5,7},{6,4},{7,5},{8,10},{9,11},{10,... | collective-permute-start | bytes 442376 | tf_op jit(solution)/shard_map/ppermute | solution.py:388
  5.9 0.8 %collective-permute-start.1 = (bf16[64,1152]{1,0:T(8,128)(2,1)S(1)}, bf16[64,1152]{1,0:T(8,128)(2,1)S(1)}, u32[]{:S(2)}, u32[]{:S(2)}) collective-permute-start(bf16[64,1152]{1,0:T(8,128)(2,1)S(1)} %get-tuple-element.16), channel_id=1, source_target_pairs={{0,3},{1,2},{2,1},{3,0},{4,7},{5,6},{6,5},{7,4},{8,11},{9,10},{10,... | collective-permute-start | bytes 442376 | tf_op jit(solution)/shard_map/ppermute | solution.py:388
  6.7 2.5 %stage.1.k_ref = bf16[2,576,2048]{2,1,0:T(8,128)(2,1)S(1)} custom-call(s32[1]{0:T(128)} %bitcast.1.info_ref, bf16[4,576,2048]{2,1,0:T(8,128)(2,1)} %bitcast.6), custom_call_target="tpu_custom_call" | custom-call | bytes 4718592 | tf_op jit(solution)/shard_map/stage/pallas_call | solution.py:405
  9.2 1.9 %collective-permute-start.4 = (bf16[64,1152]{1,0:T(8,128)(2,1)S(1)}, bf16[64,1152]{1,0:T(8,128)(2,1)S(1)}, u32[]{:S(2)}, u32[]{:S(2)}) collective-permute-start(bf16[64,1152]{1,0:T(8,128)(2,1)S(1)} %collective-permute-done.q1_ref), channel_id=1, source_target_pairs={{0,4},{4,0},{1,5},{5,1},{2,6},{6,2},{3,7},{7,3},{8,12},{12,8},{9,1... | collective-permute-start | bytes 442376 | tf_op jit(solution)/shard_map/ppermute | solution.py:416
  11.1 1.6 %collective-permute-done.1.q2_ref = bf16[64,1152]{1,0:T(8,128)(2,1)S(1)} collective-permute-done((bf16[64,1152]{1,0:T(8,128)(2,1)S(1)}, bf16[64,1152]{1,0:T(8,128)(2,1)S(1)}, u32[]{:S(2)}, u32[]{:S(2)}) %collective-permute-start.1) | collective-permute-done | bytes 147488 | tf_op jit(solution)/shard_map/ppermute | solution.py:388
  12.8 1.1 %collective-permute-start.5 = (bf16[64,1152]{1,0:T(8,128)(2,1)S(1)}, bf16[64,1152]{1,0:T(8,128)(2,1)S(1)}, u32[]{:S(2)}, u32[]{:S(2)}) collective-permute-start(bf16[64,1152]{1,0:T(8,128)(2,1)S(1)} %collective-permute-done.1.q2_ref), channel_id=1, source_target_pairs={{0,4},{4,0},{1,5},{5,1},{2,6},{6,2},{3,7},{7,3},{8,12},{12,8},{9,1... | collective-permute-start | bytes 442376 | tf_op jit(solution)/shard_map/ppermute | solution.py:416
  14.3 3.5 %attention.2 = bf16[4,128,640]{2,1,0:T(8,128)(2,1)S(1)} custom-call(s32[1]{0:T(128)} %bitcast.1.info_ref, s32[8,128]{1,0:T(8,128)S(1)} %get-tuple-element.14.limits_ref, bf16[4,64,640]{2,1,0:T(8,128)(2,1)S(1)} %get-tuple-element.15.own_ref, bf16[64,1152]{1,0:T(8,128)(2,1)S(1)} %collective-permute-done.q1_ref, ...), custom_call_target="tpu_custom_call" | custom-call | flops 22817013760 | bytes 4718592 | tf_op jit(solution)/shard_map/attention/pallas_call | solution.py:421
  18.0 3.5 %attention.3.b_ref = bf16[4,128,640]{2,1,0:T(8,128)(2,1)S(1)} custom-call(s32[1]{0:T(128)} %bitcast.own_first_ref.info_ref, s32[8,128]{1,0:T(8,128)S(1)} %get-tuple-element.14.limits_ref, bf16[4,64,640]{2,1,0:T(8,128)(2,1)S(1)} %get-tuple-element.15.own_ref, bf16[64,1152]{1,0:T(8,128)(2,1)S(1)} %collective-permute-done.4.q1_ref, ...), custom_call_target="tpu_custom_call" | custom-call | flops 22817013760 | bytes 4718592 | tf_op jit(solution)/shard_map/attention/pallas_call | solution.py:421
  21.6 0.8 %pair_merge.3 = (bf16[144,512]{1,0:T(8,128)(2,1)S(1)}, bf16[144,512]{1,0:T(8,128)(2,1)S(1)}, bf16[144,512]{1,0:T(8,128)(2,1)S(1)}) custom-call(bf16[4,128,640]{2,1,0:T(8,128)(2,1)S(1)} %collective-permute-done.3.a_ref, bf16[4,128,640]{2,1,0:T(8,128)(2,1)S(1)} %attention.3.b_ref), custom_call_target="tpu_custom_call" | custom-call | tf_op jit(solution)/shard_map/pair_merge/pallas_call | solution.py:440
  22.4 1.4 %collective-permute-start.7 = (bf16[144,512]{1,0:T(8,128)(2,1)S(1)}, bf16[144,512]{1,0:T(8,128)(2,1)S(1)}, u32[]{:S(2)}, u32[]{:S(2)}) collective-permute-start(bf16[144,512]{1,0:T(8,128)(2,1)S(1)} %get-tuple-element.19), channel_id=1, source_target_pairs={{0,1},{1,0},{2,3},{3,2},{4,5},{5,4},{6,7},{7,6},{8,9},{9,8},{10,11... | collective-permute-start | bytes 442376 | tf_op jit(solution)/shard_map/ppermute | solution.py:388
  23.8 1.5 %collective-permute-start.8 = (bf16[144,512]{1,0:T(8,128)(2,1)S(1)}, bf16[144,512]{1,0:T(8,128)(2,1)S(1)}, u32[]{:S(2)}, u32[]{:S(2)}) collective-permute-start(bf16[144,512]{1,0:T(8,128)(2,1)S(1)} %get-tuple-element.20), channel_id=1, source_target_pairs={{0,3},{1,2},{2,1},{3,0},{4,7},{5,6},{6,5},{7,4},{8,11},{9,10},{10,... | collective-permute-start | bytes 442376 | tf_op jit(solution)/shard_map/ppermute | solution.py:388
  25.3 1.1 %collective-permute-start.9 = (bf16[144,512]{1,0:T(8,128)(2,1)S(1)}, bf16[144,512]{1,0:T(8,128)(2,1)S(1)}, u32[]{:S(2)}, u32[]{:S(2)}) collective-permute-start(bf16[144,512]{1,0:T(8,128)(2,1)S(1)} %get-tuple-element.21), channel_id=1, source_target_pairs={{0,2},{1,3},{2,0},{3,1},{4,6},{5,7},{6,4},{7,5},{8,10},{9,11},{10,... | collective-permute-start | bytes 442376 | tf_op jit(solution)/shard_map/ppermute | solution.py:388
  27.5 4.1 %collective-permute-done.8.refs_2_ = bf16[144,512]{1,0:T(8,128)(2,1)S(1)} collective-permute-done((bf16[144,512]{1,0:T(8,128)(2,1)S(1)}, bf16[144,512]{1,0:T(8,128)(2,1)S(1)}, u32[]{:S(2)}, u32[]{:S(2)}) %collective-permute-start.8) | collective-permute-done | bytes 147488 | tf_op jit(solution)/shard_map/ppermute | solution.py:388
  31.6 2.0 %collective-permute-done.9.refs_3_ = bf16[144,512]{1,0:T(8,128)(2,1)S(1)} collective-permute-done((bf16[144,512]{1,0:T(8,128)(2,1)S(1)}, bf16[144,512]{1,0:T(8,128)(2,1)S(1)}, u32[]{:S(2)}, u32[]{:S(2)}) %collective-permute-start.9) | collective-permute-done | bytes 147488 | tf_op jit(solution)/shard_map/ppermute | solution.py:388
  33.6 1.0 %project.1.refs_0_ = bf16[144,128]{1,0:T(8,128)(2,1)S(1)} custom-call(bf16[144,512]{1,0:T(8,128)(2,1)S(1)} %pair_merge.2.refs_0_, bf16[144,512]{1,0:T(8,128)(2,1)S(1)} %collective-permute-done.7.refs_1_, bf16[144,512]{1,0:T(8,128)(2,1)S(1)} %collective-permute-done.8.refs_2_, bf16[144,512]{1,0:T(8,128)(2,1)S(1)} %collective-permute-done.9.refs_3_, ...), custom_call_target="tpu_custom_call" | custom-call | tf_op jit(solution)/shard_map/project/pallas_call | solution.py:452
  34.6 3.7 %collective-permute-start.10 = (bf16[144,128]{1,0:T(8,128)(2,1)S(1)}, bf16[144,128]{1,0:T(8,128)(2,1)S(1)}, u32[]{:S(2)}, u32[]{:S(2)}) collective-permute-start(bf16[144,128]{1,0:T(8,128)(2,1)S(1)} %project.1.refs_0_), channel_id=1, source_target_pairs={{0,64},{8,72},{16,80},{24,88},{32,96},{40,104},{48,112},{56,120},{... | collective-permute-start | bytes 110600 | tf_op jit(solution)/shard_map/ppermute | solution.py:462
  39.6 2.7 %collective-permute-done.11.refs_2_ = bf16[144,128]{1,0:T(8,128)(2,1)S(1)} collective-permute-done((bf16[144,128]{1,0:T(8,128)(2,1)S(1)}, bf16[144,128]{1,0:T(8,128)(2,1)S(1)}, u32[]{:S(2)}, u32[]{:S(2)}) %collective-permute-start.11) | collective-permute-done | bytes 36896 | tf_op jit(solution)/shard_map/ppermute | solution.py:462
  42.6 2.8 %collective-permute-start.13 = (bf16[144,128]{1,0:T(8,128)(2,1)S(1)}, bf16[144,128]{1,0:T(8,128)(2,1)S(1)}, u32[]{:S(2)}, u32[]{:S(2)}) collective-permute-start(bf16[144,128]{1,0:T(8,128)(2,1)S(1)} %middle_merge.1.refs_0_), channel_id=1, source_target_pairs={{0,16},{8,24},{16,0},{24,8},{32,48},{40,56},{48,32},{56,40},{64,80... | collective-permute-start | bytes 110600 | tf_op jit(solution)/shard_map/ppermute | solution.py:462
  45.4 0.8 %collective-permute-start.14 = (bf16[144,128]{1,0:T(8,128)(2,1)S(1)}, bf16[144,128]{1,0:T(8,128)(2,1)S(1)}, u32[]{:S(2)}, u32[]{:S(2)}) collective-permute-start(bf16[144,128]{1,0:T(8,128)(2,1)S(1)} %middle_merge.1.refs_0_), channel_id=1, source_target_pairs={{0,24},{8,16},{16,8},{24,0},{32,56},{40,48},{48,40},{56,32},{64,88... | collective-permute-start | bytes 110600 | tf_op jit(solution)/shard_map/ppermute | solution.py:462
  46.2 0.7 %collective-permute-done.13.refs_1_ = bf16[144,128]{1,0:T(8,128)(2,1)S(1)} collective-permute-done((bf16[144,128]{1,0:T(8,128)(2,1)S(1)}, bf16[144,128]{1,0:T(8,128)(2,1)S(1)}, u32[]{:S(2)}, u32[]{:S(2)}) %collective-permute-start.13) | collective-permute-done | bytes 36896 | tf_op jit(solution)/shard_map/ppermute | solution.py:462
  46.9 2.8 %collective-permute-done.14.refs_2_ = bf16[144,128]{1,0:T(8,128)(2,1)S(1)} collective-permute-done((bf16[144,128]{1,0:T(8,128)(2,1)S(1)}, bf16[144,128]{1,0:T(8,128)(2,1)S(1)}, u32[]{:S(2)}, u32[]{:S(2)}) %collective-permute-start.14) | collective-permute-done | bytes 36896 | tf_op jit(solution)/shard_map/ppermute | solution.py:462
  50.0 3.5 %collective-permute-start.16 = (bf16[4,2,16,128]{3,2,1,0:T(8,128)(2,1)S(1)}, bf16[4,2,16,128]{3,2,1,0:T(8,128)(2,1)S(1)}, u32[]{:S(2)}, u32[]{:S(2)}) collective-permute-start(bf16[4,2,16,128]{3,2,1,0:T(8,128)(2,1)S(1)} %finish.1.own_ref), channel_id=1, source_target_pairs={{0,4},{4,0},{1,5},{5,1},{2,6},{6,2},{3,7},{7,3},{8,12},{12,8},{9,1... | collective-permute-start | bytes 98312 | tf_op jit(solution)/shard_map/ppermute | solution.py:480
  53.5 0.9 %collective-permute-done.16.other_ref = bf16[4,2,16,128]{3,2,1,0:T(8,128)(2,1)S(1)} collective-permute-done((bf16[4,2,16,128]{3,2,1,0:T(8,128)(2,1)S(1)}, bf16[4,2,16,128]{3,2,1,0:T(8,128)(2,1)S(1)}, u32[]{:S(2)}, u32[]{:S(2)}) %collective-permute-start.16) | collective-permute-done | bytes 32800 | tf_op jit(solution)/shard_map/ppermute | solution.py:480
  (30 shorter events, 4.2 us)
Async XLA Ops:
  2.1 7.2 %collective-permute-start = (bf16[64,1152]{1,0:T(8,128)(2,1)S(1)}, bf16[64,1152]{1,0:T(8,128)(2,1)S(1)}, u32[]{:S(2)}, u32[]{:S(2)}) collective-permute-start(bf16[64,1152]{1,0:T(8,128)(2,1)S(1)} %get-tuple-element.16), channel_id=1, source_target_pairs={{0,2},{1,3},{2,0},{3,1},{4,6},{5,7},{6,4},{7,5},{8,10},{9,11},{10,... | collective-permute-start | bytes 442376 | tf_op jit(solution)/shard_map/ppermute | solution.py:388
  5.9 6.8 %collective-permute-start.1 = (bf16[64,1152]{1,0:T(8,128)(2,1)S(1)}, bf16[64,1152]{1,0:T(8,128)(2,1)S(1)}, u32[]{:S(2)}, u32[]{:S(2)}) collective-permute-start(bf16[64,1152]{1,0:T(8,128)(2,1)S(1)} %get-tuple-element.16), channel_id=1, source_target_pairs={{0,3},{1,2},{2,1},{3,0},{4,7},{5,6},{6,5},{7,4},{8,11},{9,10},{10,... | collective-permute-start | bytes 442376 | tf_op jit(solution)/shard_map/ppermute | solution.py:388
  6.7 7.2 %collective-permute-start.2 = (bf16[64,1152]{1,0:T(8,128)(2,1)S(1)}, bf16[64,1152]{1,0:T(8,128)(2,1)S(1)}, u32[]{:S(2)}, u32[]{:S(2)}) collective-permute-start(bf16[64,1152]{1,0:T(8,128)(2,1)S(1)} %get-tuple-element.16), channel_id=1, source_target_pairs={{0,1},{1,0},{2,3},{3,2},{4,5},{5,4},{6,7},{7,6},{8,9},{9,8},{10,11... | collective-permute-start | bytes 442376 | tf_op jit(solution)/shard_map/ppermute | solution.py:388
  6.7 11.3 %slice-start = ((s8[9437184]{0:T(1024)(128)(4,1)}), s8[4194304]{0:T(1024)(128)(4,1)S(1)}, s32[]{:S(2)}) async-start(s8[9437184]{0:T(1024)(128)(4,1)} %bitcast.7), calls=%async_computation | async-start | bytes 8388608
  9.2 8.7 %collective-permute-start.4 = (bf16[64,1152]{1,0:T(8,128)(2,1)S(1)}, bf16[64,1152]{1,0:T(8,128)(2,1)S(1)}, u32[]{:S(2)}, u32[]{:S(2)}) collective-permute-start(bf16[64,1152]{1,0:T(8,128)(2,1)S(1)} %collective-permute-done.q1_ref), channel_id=1, source_target_pairs={{0,4},{4,0},{1,5},{5,1},{2,6},{6,2},{3,7},{7,3},{8,12},{12,8},{9,1... | collective-permute-start | bytes 442376 | tf_op jit(solution)/shard_map/ppermute | solution.py:416
  12.8 5.2 %collective-permute-start.5 = (bf16[64,1152]{1,0:T(8,128)(2,1)S(1)}, bf16[64,1152]{1,0:T(8,128)(2,1)S(1)}, u32[]{:S(2)}, u32[]{:S(2)}) collective-permute-start(bf16[64,1152]{1,0:T(8,128)(2,1)S(1)} %collective-permute-done.1.q2_ref), channel_id=1, source_target_pairs={{0,4},{4,0},{1,5},{5,1},{2,6},{6,2},{3,7},{7,3},{8,12},{12,8},{9,1... | collective-permute-start | bytes 442376 | tf_op jit(solution)/shard_map/ppermute | solution.py:416
  13.9 4.1 %collective-permute-start.6 = (bf16[64,1152]{1,0:T(8,128)(2,1)S(1)}, bf16[64,1152]{1,0:T(8,128)(2,1)S(1)}, u32[]{:S(2)}, u32[]{:S(2)}) collective-permute-start(bf16[64,1152]{1,0:T(8,128)(2,1)S(1)} %collective-permute-done.2.q3_ref), channel_id=1, source_target_pairs={{0,4},{4,0},{1,5},{5,1},{2,6},{6,2},{3,7},{7,3},{8,12},{12,8},{9,1... | collective-permute-start | bytes 442376 | tf_op jit(solution)/shard_map/ppermute | solution.py:416
  14.3 3.8 %slice-start.1 = ((s8[9437184]{0:T(1024)(128)(4,1)}), s8[4194304]{0:T(1024)(128)(4,1)S(1)}, s32[]{:S(2)}) async-start(s8[9437184]{0:T(1024)(128)(4,1)} %bitcast.7), calls=%async_computation.1 | async-start | bytes 8388608
  14.3 3.8 %slice-start.2 = ((s8[9437184]{0:T(1024)(128)(4,1)}), s8[1048576]{0:T(1024)(128)(4,1)S(1)}, s32[]{:S(2)}) async-start(s8[9437184]{0:T(1024)(128)(4,1)} %bitcast.7), calls=%async_computation.2 | async-start | bytes 2097152
  17.8 3.8 %collective-permute-start.3 = (bf16[4,128,640]{2,1,0:T(8,128)(2,1)S(1)}, bf16[4,128,640]{2,1,0:T(8,128)(2,1)S(1)}, u32[]{:S(2)}, u32[]{:S(2)}) collective-permute-start(bf16[4,128,640]{2,1,0:T(8,128)(2,1)S(1)} %attention.2), channel_id=1, source_target_pairs={{0,4},{4,0},{1,5},{5,1},{2,6},{6,2},{3,7},{7,3},{8,12},{12,8},{9,1... | collective-permute-start | bytes 1966088 | tf_op jit(solution)/shard_map/ppermute | solution.py:437
  21.6 12.0 %copy-start = (bf16[16,512,128]{2,1,0:T(8,128)(2,1)S(1)}, bf16[16,512,128]{2,1,0:T(8,128)(2,1)}, u32[]{:S(2)}) copy-start(bf16[16,512,128]{2,1,0:T(8,128)(2,1)} %refs_5_.1) | copy-start | bytes 6291460
  22.4 5.1 %collective-permute-start.7 = (bf16[144,512]{1,0:T(8,128)(2,1)S(1)}, bf16[144,512]{1,0:T(8,128)(2,1)S(1)}, u32[]{:S(2)}, u32[]{:S(2)}) collective-permute-start(bf16[144,512]{1,0:T(8,128)(2,1)S(1)} %get-tuple-element.19), channel_id=1, source_target_pairs={{0,1},{1,0},{2,3},{3,2},{4,5},{5,4},{6,7},{7,6},{8,9},{9,8},{10,11... | collective-permute-start | bytes 442376 | tf_op jit(solution)/shard_map/ppermute | solution.py:388
  23.8 7.8 %collective-permute-start.8 = (bf16[144,512]{1,0:T(8,128)(2,1)S(1)}, bf16[144,512]{1,0:T(8,128)(2,1)S(1)}, u32[]{:S(2)}, u32[]{:S(2)}) collective-permute-start(bf16[144,512]{1,0:T(8,128)(2,1)S(1)} %get-tuple-element.20), channel_id=1, source_target_pairs={{0,3},{1,2},{2,1},{3,0},{4,7},{5,6},{6,5},{7,4},{8,11},{9,10},{10,... | collective-permute-start | bytes 442376 | tf_op jit(solution)/shard_map/ppermute | solution.py:388
  25.3 8.2 %collective-permute-start.9 = (bf16[144,512]{1,0:T(8,128)(2,1)S(1)}, bf16[144,512]{1,0:T(8,128)(2,1)S(1)}, u32[]{:S(2)}, u32[]{:S(2)}) collective-permute-start(bf16[144,512]{1,0:T(8,128)(2,1)S(1)} %get-tuple-element.21), channel_id=1, source_target_pairs={{0,2},{1,3},{2,0},{3,1},{4,6},{5,7},{6,4},{7,5},{8,10},{9,11},{10,... | collective-permute-start | bytes 442376 | tf_op jit(solution)/shard_map/ppermute | solution.py:388
  34.6 5.0 %collective-permute-start.10 = (bf16[144,128]{1,0:T(8,128)(2,1)S(1)}, bf16[144,128]{1,0:T(8,128)(2,1)S(1)}, u32[]{:S(2)}, u32[]{:S(2)}) collective-permute-start(bf16[144,128]{1,0:T(8,128)(2,1)S(1)} %project.1.refs_0_), channel_id=1, source_target_pairs={{0,64},{8,72},{16,80},{24,88},{32,96},{40,104},{48,112},{56,120},{... | collective-permute-start | bytes 110600 | tf_op jit(solution)/shard_map/ppermute | solution.py:462
  38.3 4.0 %collective-permute-start.11 = (bf16[144,128]{1,0:T(8,128)(2,1)S(1)}, bf16[144,128]{1,0:T(8,128)(2,1)S(1)}, u32[]{:S(2)}, u32[]{:S(2)}) collective-permute-start(bf16[144,128]{1,0:T(8,128)(2,1)S(1)} %project.1.refs_0_), channel_id=1, source_target_pairs={{0,96},{8,104},{16,112},{24,120},{32,64},{40,72},{48,80},{56,88},{... | collective-permute-start | bytes 110600 | tf_op jit(solution)/shard_map/ppermute | solution.py:462
  38.7 3.6 %collective-permute-start.12 = (bf16[144,128]{1,0:T(8,128)(2,1)S(1)}, bf16[144,128]{1,0:T(8,128)(2,1)S(1)}, u32[]{:S(2)}, u32[]{:S(2)}) collective-permute-start(bf16[144,128]{1,0:T(8,128)(2,1)S(1)} %project.1.refs_0_), channel_id=1, source_target_pairs={{0,32},{8,40},{16,48},{24,56},{32,0},{40,8},{48,16},{56,24},{64,96... | collective-permute-start | bytes 110600 | tf_op jit(solution)/shard_map/ppermute | solution.py:462
  42.6 4.4 %collective-permute-start.13 = (bf16[144,128]{1,0:T(8,128)(2,1)S(1)}, bf16[144,128]{1,0:T(8,128)(2,1)S(1)}, u32[]{:S(2)}, u32[]{:S(2)}) collective-permute-start(bf16[144,128]{1,0:T(8,128)(2,1)S(1)} %middle_merge.1.refs_0_), channel_id=1, source_target_pairs={{0,16},{8,24},{16,0},{24,8},{32,48},{40,56},{48,32},{56,40},{64,80... | collective-permute-start | bytes 110600 | tf_op jit(solution)/shard_map/ppermute | solution.py:462
  45.4 4.3 %collective-permute-start.14 = (bf16[144,128]{1,0:T(8,128)(2,1)S(1)}, bf16[144,128]{1,0:T(8,128)(2,1)S(1)}, u32[]{:S(2)}, u32[]{:S(2)}) collective-permute-start(bf16[144,128]{1,0:T(8,128)(2,1)S(1)} %middle_merge.1.refs_0_), channel_id=1, source_target_pairs={{0,24},{8,16},{16,8},{24,0},{32,56},{40,48},{48,40},{56,32},{64,88... | collective-permute-start | bytes 110600 | tf_op jit(solution)/shard_map/ppermute | solution.py:462
  46.2 3.5 %collective-permute-start.15 = (bf16[144,128]{1,0:T(8,128)(2,1)S(1)}, bf16[144,128]{1,0:T(8,128)(2,1)S(1)}, u32[]{:S(2)}, u32[]{:S(2)}) collective-permute-start(bf16[144,128]{1,0:T(8,128)(2,1)S(1)} %middle_merge.1.refs_0_), channel_id=1, source_target_pairs={{0,8},{8,0},{16,24},{24,16},{32,40},{40,32},{48,56},{56,48},{64,72... | collective-permute-start | bytes 110600 | tf_op jit(solution)/shard_map/ppermute | solution.py:462
  50.0 4.4 %collective-permute-start.16 = (bf16[4,2,16,128]{3,2,1,0:T(8,128)(2,1)S(1)}, bf16[4,2,16,128]{3,2,1,0:T(8,128)(2,1)S(1)}, u32[]{:S(2)}, u32[]{:S(2)}) collective-permute-start(bf16[4,2,16,128]{3,2,1,0:T(8,128)(2,1)S(1)} %finish.1.own_ref), channel_id=1, source_target_pairs={{0,4},{4,0},{1,5},{5,1},{2,6},{6,2},{3,7},{7,3},{8,12},{12,8},{9,1... | collective-permute-start | bytes 98312 | tf_op jit(solution)/shard_map/ppermute | solution.py:480

commit v14 on v13

--- a/solution.py
+++ b/solution.py
@@ -458,8 +458,14 @@
         name="project",
     )(kept, *arrived, fresh, up_values)
 
-    def over_plane(array, k):
-        return lax.ppermute(array, ("z", "x"), [(i, i ^ k) for i in range(plane)])
+    def crossing(array, axis):
+        size = lax.axis_size(axis)
+        sides = [(i, c) for i in range(size) for c in range(2)]
+        got = [
+            lax.ppermute(array, (axis, "core"), [(2 * i + c, 2 * (i ^ k) + 1 - c) for i, c in sides])
+            for k in (2, 3, 1)
+        ]
+        return got + [lax.ppermute(array, "core", swap)]
 
     part = pl.pallas_call(
         middle_kernel,
@@ -468,7 +474,7 @@
         out_shape=jax.ShapeDtypeStruct(part.shape, bf16),
         compiler_params=small,
         name="middle_merge",
-    )(part, *[over_plane(part, k) for k in (8, 12, 4)])
+    )(*crossing(part, "z"))
     own = pl.pallas_call(
         finish_kernel,
         in_specs=[vmem] * 4,
@@ -476,7 +482,7 @@
         out_shape=jax.ShapeDtypeStruct((steps, half, heads, value_width), bf16),
         compiler_params=small,
         name="finish",
-    )(part, *[over_plane(part, k) for k in (2, 3, 1)])
+    )(*crossing(part, "x"))
     theirs = lax.ppermute(own, "core", swap)
     return pl.pallas_call(
         place_kernel,

time: 55.1 us -> 54 us (0.980)
  starting transfers between devices: 23.8 us -> 22.2 us
    ppermute x1, starting transfers between devices: 3.49 us -> 0.47 us  [on_device(): theirs = lax.ppermute(own, 'core', swap)]
    ppermute x6 -> x8, starting transfers between devices: 8.09 us -> 9.54 us  [the longest x6 8.67 us: crossing(): lax.ppermute(array, (axis, 'core'), [(2 * i + c, 2 * (i ^ k) + 1 - c) for...]
    ppermute x6 -> x8, waiting for transfers between devices: 6.77 us -> 7.25 us  [the longest x6 7.24 us: crossing(): lax.ppermute(array, (axis, 'core'), [(2 * i + c, 2 * (i ^ k) + 1 - c) for...]
  transfers between devices with their start and end apart: 17 -> 19, of which waited for: 9 -> 9; matrix products, arithmetic and copies ran while one was open for 0% -> 0% of each run, Pallas kernels for 19% -> 19%
where the time goes in v14:
time: 54 us; the launch traced here: 53.9 us
  starting transfers between devices  22.2 us (41%)
  waiting for transfers between devices  16 us (30%)
  Pallas kernels  15.6 us (29%)
    ppermute x6, starting transfers between devices, crossing(): lax.ppermute(array, (axis, 'core'), [(2 * i + c, 2 * (i ^ k) + 1 - c) for...  8.67 us
    ppermute x6, starting transfers between devices, over_head(): return lax.ppermute(array, 'head', [(i, i ^ k) for i in range(owners)])  8.63 us
    ppermute x6, waiting for transfers between devices, over_head(): return lax.ppermute(array, 'head', [(i, i ^ k) for i in range(owners)])  7.85 us
    ppermute x6, waiting for transfers between devices, crossing(): lax.ppermute(array, (axis, 'core'), [(2 * i + c, 2 * (i ^ k) + 1 - c) for...  7.24 us
    pallas_call x2, Pallas kernels, attend(): pl.pallas_call(functools.partial(attention_kernel, scale), in_specs=[smem...  7.03 us
    ppermute x3, starting transfers between devices, on_device(): passed = [lax.ppermute(g, 'core', swap) for g in got]  3.38 us
    pallas_call x1, Pallas kernels, on_device(): pl.pallas_call(stage_kernel, in_specs=[smem, anywhere], out_specs=vmem, o...  2.54 us
    pallas_call x1, Pallas kernels, on_device(): pl.pallas_call(functools.partial(queries_kernel, steps), in_specs=[smem]...  2.08 us
  transfers between devices with their start and end apart: 19, of which 9 were waited for; matrix products, arithmetic and copies ran while one was open for 0% of the time, Pallas kernels for 19%

profile of v14, /device:TPU:1, one launch (start us, length us, event | category | flops | bytes accessed | tf_op | source)
XLA Modules:
  0.0 53.9 jit_solution(2448459936942301145)
XLA Ops:
  0.0 2.1 %queries.1 = (bf16[4,64,640]{2,1,0:T(8,128)(2,1)S(1)}, bf16[64,1152]{1,0:T(8,128)(2,1)S(1)}, bf16[16,576]{1,0:T(8,128)(2,1)S(1)}, s32[8,128]{1,0:T(8,128)S(1)}) custom-call(s32[1]{0:T(128)} %bitcast.1.info_ref, s32[1]{0:T(128)} %bitcast.own_first_ref.info_ref, s32[1]{0:T(128)} %bitcast.2.row_ref, s32[1]{0:T(128)} %bitcast.3.place_ref, s32[4]{0:T(128)} %positions_hbm.1, ...), custom_call_target="tpu_custom_call" | custom-call | tf_op jit(solution)/shard_map/queries/pallas_call | solution.py:354
  2.1 3.8 %collective-permute-start = (bf16[64,1152]{1,0:T(8,128)(2,1)S(1)}, bf16[64,1152]{1,0:T(8,128)(2,1)S(1)}, u32[]{:S(2)}, u32[]{:S(2)}) collective-permute-start(bf16[64,1152]{1,0:T(8,128)(2,1)S(1)} %get-tuple-element.16), channel_id=1, source_target_pairs={{0,2},{1,3},{2,0},{3,1},{4,6},{5,7},{6,4},{7,5},{8,10},{9,11},{10,... | collective-permute-start | bytes 442376 | tf_op jit(solution)/shard_map/ppermute | solution.py:388
  5.9 0.8 %collective-permute-start.1 = (bf16[64,1152]{1,0:T(8,128)(2,1)S(1)}, bf16[64,1152]{1,0:T(8,128)(2,1)S(1)}, u32[]{:S(2)}, u32[]{:S(2)}) collective-permute-start(bf16[64,1152]{1,0:T(8,128)(2,1)S(1)} %get-tuple-element.16), channel_id=1, source_target_pairs={{0,3},{1,2},{2,1},{3,0},{4,7},{5,6},{6,5},{7,4},{8,11},{9,10},{10,... | collective-permute-start | bytes 442376 | tf_op jit(solution)/shard_map/ppermute | solution.py:388
  6.7 2.5 %stage.1.k_ref = bf16[2,576,2048]{2,1,0:T(8,128)(2,1)S(1)} custom-call(s32[1]{0:T(128)} %bitcast.1.info_ref, bf16[4,576,2048]{2,1,0:T(8,128)(2,1)} %bitcast.6), custom_call_target="tpu_custom_call" | custom-call | bytes 4718592 | tf_op jit(solution)/shard_map/stage/pallas_call | solution.py:405
  9.2 1.9 %collective-permute-start.4 = (bf16[64,1152]{1,0:T(8,128)(2,1)S(1)}, bf16[64,1152]{1,0:T(8,128)(2,1)S(1)}, u32[]{:S(2)}, u32[]{:S(2)}) collective-permute-start(bf16[64,1152]{1,0:T(8,128)(2,1)S(1)} %collective-permute-done.q1_ref), channel_id=1, source_target_pairs={{0,4},{4,0},{1,5},{5,1},{2,6},{6,2},{3,7},{7,3},{8,12},{12,8},{9,1... | collective-permute-start | bytes 442376 | tf_op jit(solution)/shard_map/ppermute | solution.py:416
  11.1 1.6 %collective-permute-done.1.q2_ref = bf16[64,1152]{1,0:T(8,128)(2,1)S(1)} collective-permute-done((bf16[64,1152]{1,0:T(8,128)(2,1)S(1)}, bf16[64,1152]{1,0:T(8,128)(2,1)S(1)}, u32[]{:S(2)}, u32[]{:S(2)}) %collective-permute-start.1) | collective-permute-done | bytes 147488 | tf_op jit(solution)/shard_map/ppermute | solution.py:388
  12.8 1.1 %collective-permute-start.5 = (bf16[64,1152]{1,0:T(8,128)(2,1)S(1)}, bf16[64,1152]{1,0:T(8,128)(2,1)S(1)}, u32[]{:S(2)}, u32[]{:S(2)}) collective-permute-start(bf16[64,1152]{1,0:T(8,128)(2,1)S(1)} %collective-permute-done.1.q2_ref), channel_id=1, source_target_pairs={{0,4},{4,0},{1,5},{5,1},{2,6},{6,2},{3,7},{7,3},{8,12},{12,8},{9,1... | collective-permute-start | bytes 442376 | tf_op jit(solution)/shard_map/ppermute | solution.py:416
  14.3 3.5 %attention.2 = bf16[4,128,640]{2,1,0:T(8,128)(2,1)S(1)} custom-call(s32[1]{0:T(128)} %bitcast.1.info_ref, s32[8,128]{1,0:T(8,128)S(1)} %get-tuple-element.14.limits_ref, bf16[4,64,640]{2,1,0:T(8,128)(2,1)S(1)} %get-tuple-element.15.own_ref, bf16[64,1152]{1,0:T(8,128)(2,1)S(1)} %collective-permute-done.q1_ref, ...), custom_call_target="tpu_custom_call" | custom-call | flops 22817013760 | bytes 4718592 | tf_op jit(solution)/shard_map/attention/pallas_call | solution.py:421
  18.0 3.5 %attention.3.b_ref = bf16[4,128,640]{2,1,0:T(8,128)(2,1)S(1)} custom-call(s32[1]{0:T(128)} %bitcast.own_first_ref.info_ref, s32[8,128]{1,0:T(8,128)S(1)} %get-tuple-element.14.limits_ref, bf16[4,64,640]{2,1,0:T(8,128)(2,1)S(1)} %get-tuple-element.15.own_ref, bf16[64,1152]{1,0:T(8,128)(2,1)S(1)} %collective-permute-done.4.q1_ref, ...), custom_call_target="tpu_custom_call" | custom-call | flops 22817013760 | bytes 4718592 | tf_op jit(solution)/shard_map/attention/pallas_call | solution.py:421
  21.6 0.8 %pair_merge.3 = (bf16[144,512]{1,0:T(8,128)(2,1)S(1)}, bf16[144,512]{1,0:T(8,128)(2,1)S(1)}, bf16[144,512]{1,0:T(8,128)(2,1)S(1)}) custom-call(bf16[4,128,640]{2,1,0:T(8,128)(2,1)S(1)} %collective-permute-done.3.a_ref, bf16[4,128,640]{2,1,0:T(8,128)(2,1)S(1)} %attention.3.b_ref), custom_call_target="tpu_custom_call" | custom-call | tf_op jit(solution)/shard_map/pair_merge/pallas_call | solution.py:440
  22.4 1.4 %collective-permute-start.7 = (bf16[144,512]{1,0:T(8,128)(2,1)S(1)}, bf16[144,512]{1,0:T(8,128)(2,1)S(1)}, u32[]{:S(2)}, u32[]{:S(2)}) collective-permute-start(bf16[144,512]{1,0:T(8,128)(2,1)S(1)} %get-tuple-element.19), channel_id=1, source_target_pairs={{0,1},{1,0},{2,3},{3,2},{4,5},{5,4},{6,7},{7,6},{8,9},{9,8},{10,11... | collective-permute-start | bytes 442376 | tf_op jit(solution)/shard_map/ppermute | solution.py:388
  23.8 1.5 %collective-permute-start.8 = (bf16[144,512]{1,0:T(8,128)(2,1)S(1)}, bf16[144,512]{1,0:T(8,128)(2,1)S(1)}, u32[]{:S(2)}, u32[]{:S(2)}) collective-permute-start(bf16[144,512]{1,0:T(8,128)(2,1)S(1)} %get-tuple-element.20), channel_id=1, source_target_pairs={{0,3},{1,2},{2,1},{3,0},{4,7},{5,6},{6,5},{7,4},{8,11},{9,10},{10,... | collective-permute-start | bytes 442376 | tf_op jit(solution)/shard_map/ppermute | solution.py:388
  25.3 1.1 %collective-permute-start.9 = (bf16[144,512]{1,0:T(8,128)(2,1)S(1)}, bf16[144,512]{1,0:T(8,128)(2,1)S(1)}, u32[]{:S(2)}, u32[]{:S(2)}) collective-permute-start(bf16[144,512]{1,0:T(8,128)(2,1)S(1)} %get-tuple-element.21), channel_id=1, source_target_pairs={{0,2},{1,3},{2,0},{3,1},{4,6},{5,7},{6,4},{7,5},{8,10},{9,11},{10,... | collective-permute-start | bytes 442376 | tf_op jit(solution)/shard_map/ppermute | solution.py:388
  27.5 4.1 %collective-permute-done.8.refs_2_ = bf16[144,512]{1,0:T(8,128)(2,1)S(1)} collective-permute-done((bf16[144,512]{1,0:T(8,128)(2,1)S(1)}, bf16[144,512]{1,0:T(8,128)(2,1)S(1)}, u32[]{:S(2)}, u32[]{:S(2)}) %collective-permute-start.8) | collective-permute-done | bytes 147488 | tf_op jit(solution)/shard_map/ppermute | solution.py:388
  31.6 2.0 %collective-permute-done.9.refs_3_ = bf16[144,512]{1,0:T(8,128)(2,1)S(1)} collective-permute-done((bf16[144,512]{1,0:T(8,128)(2,1)S(1)}, bf16[144,512]{1,0:T(8,128)(2,1)S(1)}, u32[]{:S(2)}, u32[]{:S(2)}) %collective-permute-start.9) | collective-permute-done | bytes 147488 | tf_op jit(solution)/shard_map/ppermute | solution.py:388
  33.6 1.0 %project.1 = bf16[144,128]{1,0:T(8,128)(2,1)S(1)} custom-call(bf16[144,512]{1,0:T(8,128)(2,1)S(1)} %pair_merge.2.refs_0_, bf16[144,512]{1,0:T(8,128)(2,1)S(1)} %collective-permute-done.7.refs_1_, bf16[144,512]{1,0:T(8,128)(2,1)S(1)} %collective-permute-done.8.refs_2_, bf16[144,512]{1,0:T(8,128)(2,1)S(1)} %collective-permute-done.9.refs_3_, ...), custom_call_target="tpu_custom_call" | custom-call | tf_op jit(solution)/shard_map/project/pallas_call | solution.py:452
  34.6 4.4 %collective-permute-start.10 = (bf16[144,128]{1,0:T(8,128)(2,1)S(1)}, bf16[144,128]{1,0:T(8,128)(2,1)S(1)}, u32[]{:S(2)}, u32[]{:S(2)}) collective-permute-start(bf16[144,128]{1,0:T(8,128)(2,1)S(1)} %project.1), channel_id=1, source_target_pairs={{0,68},{4,64},{32,100},{36,96},{64,4},{68,0},{96,36},{100,32},{1,6... | collective-permute-start | bytes 110600 | tf_op jit(solution)/shard_map/ppermute | solution.py:465
  39.3 0.9 %collective-permute-start.13 = (bf16[144,128]{1,0:T(8,128)(2,1)S(1)}, bf16[144,128]{1,0:T(8,128)(2,1)S(1)}, u32[]{:S(2)}, u32[]{:S(2)}) collective-permute-start(bf16[144,128]{1,0:T(8,128)(2,1)S(1)} %project.1), channel_id=1, source_target_pairs={{0,4},{4,0},{1,5},{5,1},{2,6},{6,2},{3,7},{7,3},{8,12},{12,8},{9,1... | collective-permute-start | bytes 110600 | tf_op jit(solution)/shard_map/ppermute | solution.py:468
  40.6 3.0 %collective-permute-done.11.refs_1_ = bf16[144,128]{1,0:T(8,128)(2,1)S(1)} collective-permute-done((bf16[144,128]{1,0:T(8,128)(2,1)S(1)}, bf16[144,128]{1,0:T(8,128)(2,1)S(1)}, u32[]{:S(2)}, u32[]{:S(2)}) %collective-permute-start.11) | collective-permute-done | bytes 36896 | tf_op jit(solution)/shard_map/ppermute | solution.py:465
  43.9 2.6 %collective-permute-start.14 = (bf16[144,128]{1,0:T(8,128)(2,1)S(1)}, bf16[144,128]{1,0:T(8,128)(2,1)S(1)}, u32[]{:S(2)}, u32[]{:S(2)}) collective-permute-start(bf16[144,128]{1,0:T(8,128)(2,1)S(1)} %middle_merge.1), channel_id=1, source_target_pairs={{0,20},{4,16},{8,28},{12,24},{16,4},{20,0},{24,12},{28,8},{1,21},{... | collective-permute-start | bytes 110600 | tf_op jit(solution)/shard_map/ppermute | solution.py:465
  46.5 1.4 %collective-permute-start.15 = (bf16[144,128]{1,0:T(8,128)(2,1)S(1)}, bf16[144,128]{1,0:T(8,128)(2,1)S(1)}, u32[]{:S(2)}, u32[]{:S(2)}) collective-permute-start(bf16[144,128]{1,0:T(8,128)(2,1)S(1)} %middle_merge.1), channel_id=1, source_target_pairs={{0,28},{4,24},{8,20},{12,16},{16,12},{20,8},{24,4},{28,0},{1,29},{... | collective-permute-start | bytes 110600 | tf_op jit(solution)/shard_map/ppermute | solution.py:465
  47.8 1.0 %collective-permute-done.14.refs_0_ = bf16[144,128]{1,0:T(8,128)(2,1)S(1)} collective-permute-done((bf16[144,128]{1,0:T(8,128)(2,1)S(1)}, bf16[144,128]{1,0:T(8,128)(2,1)S(1)}, u32[]{:S(2)}, u32[]{:S(2)}) %collective-permute-start.14) | collective-permute-done | bytes 36896 | tf_op jit(solution)/shard_map/ppermute | solution.py:465
  48.8 2.8 %collective-permute-done.15.refs_1_ = bf16[144,128]{1,0:T(8,128)(2,1)S(1)} collective-permute-done((bf16[144,128]{1,0:T(8,128)(2,1)S(1)}, bf16[144,128]{1,0:T(8,128)(2,1)S(1)}, u32[]{:S(2)}, u32[]{:S(2)}) %collective-permute-start.15) | collective-permute-done | bytes 36896 | tf_op jit(solution)/shard_map/ppermute | solution.py:465
  52.4 0.9 %collective-permute-done.18.other_ref = bf16[4,2,16,128]{3,2,1,0:T(8,128)(2,1)S(1)} collective-permute-done((bf16[4,2,16,128]{3,2,1,0:T(8,128)(2,1)S(1)}, bf16[4,2,16,128]{3,2,1,0:T(8,128)(2,1)S(1)}, u32[]{:S(2)}, u32[]{:S(2)}) %collective-permute-start.18) | collective-permute-done | bytes 32800 | tf_op jit(solution)/shard_map/ppermute | solution.py:486
  (34 shorter events, 4.2 us)
Async XLA Ops:
  2.1 7.2 %collective-permute-start = (bf16[64,1152]{1,0:T(8,128)(2,1)S(1)}, bf16[64,1152]{1,0:T(8,128)(2,1)S(1)}, u32[]{:S(2)}, u32[]{:S(2)}) collective-permute-start(bf16[64,1152]{1,0:T(8,128)(2,1)S(1)} %get-tuple-element.16), channel_id=1, source_target_pairs={{0,2},{1,3},{2,0},{3,1},{4,6},{5,7},{6,4},{7,5},{8,10},{9,11},{10,... | collective-permute-start | bytes 442376 | tf_op jit(solution)/shard_map/ppermute | solution.py:388
  5.9 6.8 %collective-permute-start.1 = (bf16[64,1152]{1,0:T(8,128)(2,1)S(1)}, bf16[64,1152]{1,0:T(8,128)(2,1)S(1)}, u32[]{:S(2)}, u32[]{:S(2)}) collective-permute-start(bf16[64,1152]{1,0:T(8,128)(2,1)S(1)} %get-tuple-element.16), channel_id=1, source_target_pairs={{0,3},{1,2},{2,1},{3,0},{4,7},{5,6},{6,5},{7,4},{8,11},{9,10},{10,... | collective-permute-start | bytes 442376 | tf_op jit(solution)/shard_map/ppermute | solution.py:388
  6.7 7.2 %collective-permute-start.2 = (bf16[64,1152]{1,0:T(8,128)(2,1)S(1)}, bf16[64,1152]{1,0:T(8,128)(2,1)S(1)}, u32[]{:S(2)}, u32[]{:S(2)}) collective-permute-start(bf16[64,1152]{1,0:T(8,128)(2,1)S(1)} %get-tuple-element.16), channel_id=1, source_target_pairs={{0,1},{1,0},{2,3},{3,2},{4,5},{5,4},{6,7},{7,6},{8,9},{9,8},{10,11... | collective-permute-start | bytes 442376 | tf_op jit(solution)/shard_map/ppermute | solution.py:388
  6.7 11.3 %slice-start = ((s8[9437184]{0:T(1024)(128)(4,1)}), s8[4194304]{0:T(1024)(128)(4,1)S(1)}, s32[]{:S(2)}) async-start(s8[9437184]{0:T(1024)(128)(4,1)} %bitcast.7), calls=%async_computation | async-start | bytes 8388608
  9.2 8.7 %collective-permute-start.4 = (bf16[64,1152]{1,0:T(8,128)(2,1)S(1)}, bf16[64,1152]{1,0:T(8,128)(2,1)S(1)}, u32[]{:S(2)}, u32[]{:S(2)}) collective-permute-start(bf16[64,1152]{1,0:T(8,128)(2,1)S(1)} %collective-permute-done.q1_ref), channel_id=1, source_target_pairs={{0,4},{4,0},{1,5},{5,1},{2,6},{6,2},{3,7},{7,3},{8,12},{12,8},{9,1... | collective-permute-start | bytes 442376 | tf_op jit(solution)/shard_map/ppermute | solution.py:416
  12.8 5.2 %collective-permute-start.5 = (bf16[64,1152]{1,0:T(8,128)(2,1)S(1)}, bf16[64,1152]{1,0:T(8,128)(2,1)S(1)}, u32[]{:S(2)}, u32[]{:S(2)}) collective-permute-start(bf16[64,1152]{1,0:T(8,128)(2,1)S(1)} %collective-permute-done.1.q2_ref), channel_id=1, source_target_pairs={{0,4},{4,0},{1,5},{5,1},{2,6},{6,2},{3,7},{7,3},{8,12},{12,8},{9,1... | collective-permute-start | bytes 442376 | tf_op jit(solution)/shard_map/ppermute | solution.py:416
  13.9 4.1 %collective-permute-start.6 = (bf16[64,1152]{1,0:T(8,128)(2,1)S(1)}, bf16[64,1152]{1,0:T(8,128)(2,1)S(1)}, u32[]{:S(2)}, u32[]{:S(2)}) collective-permute-start(bf16[64,1152]{1,0:T(8,128)(2,1)S(1)} %collective-permute-done.2.q3_ref), channel_id=1, source_target_pairs={{0,4},{4,0},{1,5},{5,1},{2,6},{6,2},{3,7},{7,3},{8,12},{12,8},{9,1... | collective-permute-start | bytes 442376 | tf_op jit(solution)/shard_map/ppermute | solution.py:416
  14.3 3.8 %slice-start.1 = ((s8[9437184]{0:T(1024)(128)(4,1)}), s8[4194304]{0:T(1024)(128)(4,1)S(1)}, s32[]{:S(2)}) async-start(s8[9437184]{0:T(1024)(128)(4,1)} %bitcast.7), calls=%async_computation.1 | async-start | bytes 8388608
  14.3 3.8 %slice-start.2 = ((s8[9437184]{0:T(1024)(128)(4,1)}), s8[1048576]{0:T(1024)(128)(4,1)S(1)}, s32[]{:S(2)}) async-start(s8[9437184]{0:T(1024)(128)(4,1)} %bitcast.7), calls=%async_computation.2 | async-start | bytes 2097152
  17.8 3.8 %collective-permute-start.3 = (bf16[4,128,640]{2,1,0:T(8,128)(2,1)S(1)}, bf16[4,128,640]{2,1,0:T(8,128)(2,1)S(1)}, u32[]{:S(2)}, u32[]{:S(2)}) collective-permute-start(bf16[4,128,640]{2,1,0:T(8,128)(2,1)S(1)} %attention.2), channel_id=1, source_target_pairs={{0,4},{4,0},{1,5},{5,1},{2,6},{6,2},{3,7},{7,3},{8,12},{12,8},{9,1... | collective-permute-start | bytes 1966088 | tf_op jit(solution)/shard_map/ppermute | solution.py:437
  21.6 12.0 %copy-start = (bf16[16,512,128]{2,1,0:T(8,128)(2,1)S(1)}, bf16[16,512,128]{2,1,0:T(8,128)(2,1)}, u32[]{:S(2)}) copy-start(bf16[16,512,128]{2,1,0:T(8,128)(2,1)} %refs_5_.1) | copy-start | bytes 6291460
  22.4 5.1 %collective-permute-start.7 = (bf16[144,512]{1,0:T(8,128)(2,1)S(1)}, bf16[144,512]{1,0:T(8,128)(2,1)S(1)}, u32[]{:S(2)}, u32[]{:S(2)}) collective-permute-start(bf16[144,512]{1,0:T(8,128)(2,1)S(1)} %get-tuple-element.19), channel_id=1, source_target_pairs={{0,1},{1,0},{2,3},{3,2},{4,5},{5,4},{6,7},{7,6},{8,9},{9,8},{10,11... | collective-permute-start | bytes 442376 | tf_op jit(solution)/shard_map/ppermute | solution.py:388
  23.8 7.8 %collective-permute-start.8 = (bf16[144,512]{1,0:T(8,128)(2,1)S(1)}, bf16[144,512]{1,0:T(8,128)(2,1)S(1)}, u32[]{:S(2)}, u32[]{:S(2)}) collective-permute-start(bf16[144,512]{1,0:T(8,128)(2,1)S(1)} %get-tuple-element.20), channel_id=1, source_target_pairs={{0,3},{1,2},{2,1},{3,0},{4,7},{5,6},{6,5},{7,4},{8,11},{9,10},{10,... | collective-permute-start | bytes 442376 | tf_op jit(solution)/shard_map/ppermute | solution.py:388
  25.3 8.2 %collective-permute-start.9 = (bf16[144,512]{1,0:T(8,128)(2,1)S(1)}, bf16[144,512]{1,0:T(8,128)(2,1)S(1)}, u32[]{:S(2)}, u32[]{:S(2)}) collective-permute-start(bf16[144,512]{1,0:T(8,128)(2,1)S(1)} %get-tuple-element.21), channel_id=1, source_target_pairs={{0,2},{1,3},{2,0},{3,1},{4,6},{5,7},{6,4},{7,5},{8,10},{9,11},{10,... | collective-permute-start | bytes 442376 | tf_op jit(solution)/shard_map/ppermute | solution.py:388
  34.6 6.1 %collective-permute-start.10 = (bf16[144,128]{1,0:T(8,128)(2,1)S(1)}, bf16[144,128]{1,0:T(8,128)(2,1)S(1)}, u32[]{:S(2)}, u32[]{:S(2)}) collective-permute-start(bf16[144,128]{1,0:T(8,128)(2,1)S(1)} %project.1), channel_id=1, source_target_pairs={{0,68},{4,64},{32,100},{36,96},{64,4},{68,0},{96,36},{100,32},{1,6... | collective-permute-start | bytes 110600 | tf_op jit(solution)/shard_map/ppermute | solution.py:465
  39.0 4.6 %collective-permute-start.11 = (bf16[144,128]{1,0:T(8,128)(2,1)S(1)}, bf16[144,128]{1,0:T(8,128)(2,1)S(1)}, u32[]{:S(2)}, u32[]{:S(2)}) collective-permute-start(bf16[144,128]{1,0:T(8,128)(2,1)S(1)} %project.1), channel_id=1, source_target_pairs={{0,100},{4,96},{32,68},{36,64},{64,36},{68,32},{96,4},{100,0},{1,1... | collective-permute-start | bytes 110600 | tf_op jit(solution)/shard_map/ppermute | solution.py:465
  39.2 4.4 %collective-permute-start.12 = (bf16[144,128]{1,0:T(8,128)(2,1)S(1)}, bf16[144,128]{1,0:T(8,128)(2,1)S(1)}, u32[]{:S(2)}, u32[]{:S(2)}) collective-permute-start(bf16[144,128]{1,0:T(8,128)(2,1)S(1)} %project.1), channel_id=1, source_target_pairs={{0,36},{4,32},{32,4},{36,0},{64,100},{68,96},{96,68},{100,64},{1,3... | collective-permute-start | bytes 110600 | tf_op jit(solution)/shard_map/ppermute | solution.py:465
  39.3 4.3 %collective-permute-start.13 = (bf16[144,128]{1,0:T(8,128)(2,1)S(1)}, bf16[144,128]{1,0:T(8,128)(2,1)S(1)}, u32[]{:S(2)}, u32[]{:S(2)}) collective-permute-start(bf16[144,128]{1,0:T(8,128)(2,1)S(1)} %project.1), channel_id=1, source_target_pairs={{0,4},{4,0},{1,5},{5,1},{2,6},{6,2},{3,7},{7,3},{8,12},{12,8},{9,1... | collective-permute-start | bytes 110600 | tf_op jit(solution)/shard_map/ppermute | solution.py:468
  43.9 5.0 %collective-permute-start.14 = (bf16[144,128]{1,0:T(8,128)(2,1)S(1)}, bf16[144,128]{1,0:T(8,128)(2,1)S(1)}, u32[]{:S(2)}, u32[]{:S(2)}) collective-permute-start(bf16[144,128]{1,0:T(8,128)(2,1)S(1)} %middle_merge.1), channel_id=1, source_target_pairs={{0,20},{4,16},{8,28},{12,24},{16,4},{20,0},{24,12},{28,8},{1,21},{... | collective-permute-start | bytes 110600 | tf_op jit(solution)/shard_map/ppermute | solution.py:465
  46.5 5.2 %collective-permute-start.15 = (bf16[144,128]{1,0:T(8,128)(2,1)S(1)}, bf16[144,128]{1,0:T(8,128)(2,1)S(1)}, u32[]{:S(2)}, u32[]{:S(2)}) collective-permute-start(bf16[144,128]{1,0:T(8,128)(2,1)S(1)} %middle_merge.1), channel_id=1, source_target_pairs={{0,28},{4,24},{8,20},{12,16},{16,12},{20,8},{24,4},{28,0},{1,29},{... | collective-permute-start | bytes 110600 | tf_op jit(solution)/shard_map/ppermute | solution.py:465
  47.8 3.8 %collective-permute-start.16 = (bf16[144,128]{1,0:T(8,128)(2,1)S(1)}, bf16[144,128]{1,0:T(8,128)(2,1)S(1)}, u32[]{:S(2)}, u32[]{:S(2)}) collective-permute-start(bf16[144,128]{1,0:T(8,128)(2,1)S(1)} %middle_merge.1), channel_id=1, source_target_pairs={{0,12},{4,8},{8,4},{12,0},{16,28},{20,24},{24,20},{28,16},{1,13},{... | collective-permute-start | bytes 110600 | tf_op jit(solution)/shard_map/ppermute | solution.py:465
  47.8 3.8 %collective-permute-start.17 = (bf16[144,128]{1,0:T(8,128)(2,1)S(1)}, bf16[144,128]{1,0:T(8,128)(2,1)S(1)}, u32[]{:S(2)}, u32[]{:S(2)}) collective-permute-start(bf16[144,128]{1,0:T(8,128)(2,1)S(1)} %middle_merge.1), channel_id=1, source_target_pairs={{0,4},{4,0},{1,5},{5,1},{2,6},{6,2},{3,7},{7,3},{8,12},{12,8},{9,1... | collective-permute-start | bytes 110600 | tf_op jit(solution)/shard_map/ppermute | solution.py:468
  51.9 1.3 %collective-permute-start.18 = (bf16[4,2,16,128]{3,2,1,0:T(8,128)(2,1)S(1)}, bf16[4,2,16,128]{3,2,1,0:T(8,128)(2,1)S(1)}, u32[]{:S(2)}, u32[]{:S(2)}) collective-permute-start(bf16[4,2,16,128]{3,2,1,0:T(8,128)(2,1)S(1)} %finish.1.own_ref), channel_id=1, source_target_pairs={{0,4},{4,0},{1,5},{5,1},{2,6},{6,2},{3,7},{7,3},{8,12},{12,8},{9,1... | collective-permute-start | bytes 98312 | tf_op jit(solution)/shard_map/ppermute | solution.py:486

commit v15 on v14

--- a/solution.py
+++ b/solution.py
@@ -447,7 +447,7 @@
         )(other_part, own_part)
 
     sent = dict(zip(partners, pair(1, owners - 1)))
-    arrived = [over_head(sent[k], k) for k in (1, 3, 2)]
+    arrived = [over_head(sent[k], k) for k in (2, 3, 1)]
     (kept,) = pair(0, 1)
     part = pl.pallas_call(
         functools.partial(project_kernel, heads),

time: 54 us -> 53.4 us (0.989)
  transfers between devices with their start and end apart: 19 -> 19, of which waited for: 9 -> 9; matrix products, arithmetic and copies ran while one was open for 0% -> 0% of each run, Pallas kernels for 19% -> 20%
where the time goes in v15:
time: 53.4 us; the launch traced here: 53.3 us
  starting transfers between devices  21.9 us (41%)
  Pallas kernels  15.6 us (29%)
  waiting for transfers between devices  15.6 us (29%)
    ppermute x6, starting transfers between devices, crossing(): lax.ppermute(array, (axis, 'core'), [(2 * i + c, 2 * (i ^ k) + 1 - c) for...  8.65 us
    ppermute x6, starting transfers between devices, over_head(): return lax.ppermute(array, 'head', [(i, i ^ k) for i in range(owners)])  8.4 us
    ppermute x6, waiting for transfers between devices, over_head(): return lax.ppermute(array, 'head', [(i, i ^ k) for i in range(owners)])  7.52 us
    ppermute x6, waiting for transfers between devices, crossing(): lax.ppermute(array, (axis, 'core'), [(2 * i + c, 2 * (i ^ k) + 1 - c) for...  7.25 us
    pallas_call x2, Pallas kernels, attend(): pl.pallas_call(functools.partial(attention_kernel, scale), in_specs=[smem...  7.03 us
    ppermute x3, starting transfers between devices, on_device(): passed = [lax.ppermute(g, 'core', swap) for g in got]  3.38 us
    pallas_call x1, Pallas kernels, on_device(): pl.pallas_call(stage_kernel, in_specs=[smem, anywhere], out_specs=vmem, o...  2.54 us
    pallas_call x1, Pallas kernels, on_device(): pl.pallas_call(functools.partial(queries_kernel, steps), in_specs=[smem]...  2.08 us
  transfers between devices with their start and end apart: 19, of which 9 were waited for; matrix products, arithmetic and copies ran while one was open for 0% of the time, Pallas kernels for 20%

profile of v15, /device:TPU:1, one launch (start us, length us, event | category | flops | bytes accessed | tf_op | source)
XLA Modules:
  0.0 53.3 jit_solution(17662948875960052542)
XLA Ops:
  0.0 2.1 %queries.1 = (bf16[4,64,640]{2,1,0:T(8,128)(2,1)S(1)}, bf16[64,1152]{1,0:T(8,128)(2,1)S(1)}, bf16[16,576]{1,0:T(8,128)(2,1)S(1)}, s32[8,128]{1,0:T(8,128)S(1)}) custom-call(s32[1]{0:T(128)} %bitcast.1.info_ref, s32[1]{0:T(128)} %bitcast.own_first_ref.info_ref, s32[1]{0:T(128)} %bitcast.2.row_ref, s32[1]{0:T(128)} %bitcast.3.place_ref, s32[4]{0:T(128)} %positions_hbm.1, ...), custom_call_target="tpu_custom_call" | custom-call | tf_op jit(solution)/shard_map/queries/pallas_call | solution.py:354
  2.1 3.8 %collective-permute-start = (bf16[64,1152]{1,0:T(8,128)(2,1)S(1)}, bf16[64,1152]{1,0:T(8,128)(2,1)S(1)}, u32[]{:S(2)}, u32[]{:S(2)}) collective-permute-start(bf16[64,1152]{1,0:T(8,128)(2,1)S(1)} %get-tuple-element.16), channel_id=1, source_target_pairs={{0,2},{1,3},{2,0},{3,1},{4,6},{5,7},{6,4},{7,5},{8,10},{9,11},{10,... | collective-permute-start | bytes 442376 | tf_op jit(solution)/shard_map/ppermute | solution.py:388
  5.9 0.8 %collective-permute-start.1 = (bf16[64,1152]{1,0:T(8,128)(2,1)S(1)}, bf16[64,1152]{1,0:T(8,128)(2,1)S(1)}, u32[]{:S(2)}, u32[]{:S(2)}) collective-permute-start(bf16[64,1152]{1,0:T(8,128)(2,1)S(1)} %get-tuple-element.16), channel_id=1, source_target_pairs={{0,3},{1,2},{2,1},{3,0},{4,7},{5,6},{6,5},{7,4},{8,11},{9,10},{10,... | collective-permute-start | bytes 442376 | tf_op jit(solution)/shard_map/ppermute | solution.py:388
  6.7 2.5 %stage.1.k_ref = bf16[2,576,2048]{2,1,0:T(8,128)(2,1)S(1)} custom-call(s32[1]{0:T(128)} %bitcast.1.info_ref, bf16[4,576,2048]{2,1,0:T(8,128)(2,1)} %bitcast.6), custom_call_target="tpu_custom_call" | custom-call | bytes 4718592 | tf_op jit(solution)/shard_map/stage/pallas_call | solution.py:405
  9.2 1.9 %collective-permute-start.4 = (bf16[64,1152]{1,0:T(8,128)(2,1)S(1)}, bf16[64,1152]{1,0:T(8,128)(2,1)S(1)}, u32[]{:S(2)}, u32[]{:S(2)}) collective-permute-start(bf16[64,1152]{1,0:T(8,128)(2,1)S(1)} %collective-permute-done.q1_ref), channel_id=1, source_target_pairs={{0,4},{4,0},{1,5},{5,1},{2,6},{6,2},{3,7},{7,3},{8,12},{12,8},{9,1... | collective-permute-start | bytes 442376 | tf_op jit(solution)/shard_map/ppermute | solution.py:416
  11.1 1.6 %collective-permute-done.1.q2_ref = bf16[64,1152]{1,0:T(8,128)(2,1)S(1)} collective-permute-done((bf16[64,1152]{1,0:T(8,128)(2,1)S(1)}, bf16[64,1152]{1,0:T(8,128)(2,1)S(1)}, u32[]{:S(2)}, u32[]{:S(2)}) %collective-permute-start.1) | collective-permute-done | bytes 147488 | tf_op jit(solution)/shard_map/ppermute | solution.py:388
  12.8 1.1 %collective-permute-start.5 = (bf16[64,1152]{1,0:T(8,128)(2,1)S(1)}, bf16[64,1152]{1,0:T(8,128)(2,1)S(1)}, u32[]{:S(2)}, u32[]{:S(2)}) collective-permute-start(bf16[64,1152]{1,0:T(8,128)(2,1)S(1)} %collective-permute-done.1.q2_ref), channel_id=1, source_target_pairs={{0,4},{4,0},{1,5},{5,1},{2,6},{6,2},{3,7},{7,3},{8,12},{12,8},{9,1... | collective-permute-start | bytes 442376 | tf_op jit(solution)/shard_map/ppermute | solution.py:416
  14.3 3.5 %attention.2 = bf16[4,128,640]{2,1,0:T(8,128)(2,1)S(1)} custom-call(s32[1]{0:T(128)} %bitcast.1.info_ref, s32[8,128]{1,0:T(8,128)S(1)} %get-tuple-element.14.limits_ref, bf16[4,64,640]{2,1,0:T(8,128)(2,1)S(1)} %get-tuple-element.15.own_ref, bf16[64,1152]{1,0:T(8,128)(2,1)S(1)} %collective-permute-done.q1_ref, ...), custom_call_target="tpu_custom_call" | custom-call | flops 22817013760 | bytes 4718592 | tf_op jit(solution)/shard_map/attention/pallas_call | solution.py:421
  18.0 3.5 %attention.3.b_ref = bf16[4,128,640]{2,1,0:T(8,128)(2,1)S(1)} custom-call(s32[1]{0:T(128)} %bitcast.own_first_ref.info_ref, s32[8,128]{1,0:T(8,128)S(1)} %get-tuple-element.14.limits_ref, bf16[4,64,640]{2,1,0:T(8,128)(2,1)S(1)} %get-tuple-element.15.own_ref, bf16[64,1152]{1,0:T(8,128)(2,1)S(1)} %collective-permute-done.4.q1_ref, ...), custom_call_target="tpu_custom_call" | custom-call | flops 22817013760 | bytes 4718592 | tf_op jit(solution)/shard_map/attention/pallas_call | solution.py:421
  21.6 0.8 %pair_merge.3 = (bf16[144,512]{1,0:T(8,128)(2,1)S(1)}, bf16[144,512]{1,0:T(8,128)(2,1)S(1)}, bf16[144,512]{1,0:T(8,128)(2,1)S(1)}) custom-call(bf16[4,128,640]{2,1,0:T(8,128)(2,1)S(1)} %collective-permute-done.3.a_ref, bf16[4,128,640]{2,1,0:T(8,128)(2,1)S(1)} %attention.3.b_ref), custom_call_target="tpu_custom_call" | custom-call | tf_op jit(solution)/shard_map/pair_merge/pallas_call | solution.py:440
  22.4 2.2 %collective-permute-start.7 = (bf16[144,512]{1,0:T(8,128)(2,1)S(1)}, bf16[144,512]{1,0:T(8,128)(2,1)S(1)}, u32[]{:S(2)}, u32[]{:S(2)}) collective-permute-start(bf16[144,512]{1,0:T(8,128)(2,1)S(1)} %get-tuple-element.19), channel_id=1, source_target_pairs={{0,2},{1,3},{2,0},{3,1},{4,6},{5,7},{6,4},{7,5},{8,10},{9,11},{10,... | collective-permute-start | bytes 442376 | tf_op jit(solution)/shard_map/ppermute | solution.py:388
  24.6 1.6 %collective-permute-start.8 = (bf16[144,512]{1,0:T(8,128)(2,1)S(1)}, bf16[144,512]{1,0:T(8,128)(2,1)S(1)}, u32[]{:S(2)}, u32[]{:S(2)}) collective-permute-start(bf16[144,512]{1,0:T(8,128)(2,1)S(1)} %get-tuple-element.20), channel_id=1, source_target_pairs={{0,3},{1,2},{2,1},{3,0},{4,7},{5,6},{6,5},{7,4},{8,11},{9,10},{10,... | collective-permute-start | bytes 442376 | tf_op jit(solution)/shard_map/ppermute | solution.py:388
  27.1 1.9 %collective-permute-done.7.refs_1_ = bf16[144,512]{1,0:T(8,128)(2,1)S(1)} collective-permute-done((bf16[144,512]{1,0:T(8,128)(2,1)S(1)}, bf16[144,512]{1,0:T(8,128)(2,1)S(1)}, u32[]{:S(2)}, u32[]{:S(2)}) %collective-permute-start.7) | collective-permute-done | bytes 147488 | tf_op jit(solution)/shard_map/ppermute | solution.py:388
  29.0 3.9 %collective-permute-done.8.refs_2_ = bf16[144,512]{1,0:T(8,128)(2,1)S(1)} collective-permute-done((bf16[144,512]{1,0:T(8,128)(2,1)S(1)}, bf16[144,512]{1,0:T(8,128)(2,1)S(1)}, u32[]{:S(2)}, u32[]{:S(2)}) %collective-permute-start.8) | collective-permute-done | bytes 147488 | tf_op jit(solution)/shard_map/ppermute | solution.py:388
  33.0 1.0 %project.1 = bf16[144,128]{1,0:T(8,128)(2,1)S(1)} custom-call(bf16[144,512]{1,0:T(8,128)(2,1)S(1)} %pair_merge.2.refs_0_, bf16[144,512]{1,0:T(8,128)(2,1)S(1)} %collective-permute-done.7.refs_1_, bf16[144,512]{1,0:T(8,128)(2,1)S(1)} %collective-permute-done.8.refs_2_, bf16[144,512]{1,0:T(8,128)(2,1)S(1)} %collective-permute-done.9.refs_3_, ...), custom_call_target="tpu_custom_call" | custom-call | tf_op jit(solution)/shard_map/project/pallas_call | solution.py:452
  34.0 4.4 %collective-permute-start.10 = (bf16[144,128]{1,0:T(8,128)(2,1)S(1)}, bf16[144,128]{1,0:T(8,128)(2,1)S(1)}, u32[]{:S(2)}, u32[]{:S(2)}) collective-permute-start(bf16[144,128]{1,0:T(8,128)(2,1)S(1)} %project.1), channel_id=1, source_target_pairs={{0,68},{4,64},{32,100},{36,96},{64,4},{68,0},{96,36},{100,32},{1,6... | collective-permute-start | bytes 110600 | tf_op jit(solution)/shard_map/ppermute | solution.py:465
  38.7 0.8 %collective-permute-start.13 = (bf16[144,128]{1,0:T(8,128)(2,1)S(1)}, bf16[144,128]{1,0:T(8,128)(2,1)S(1)}, u32[]{:S(2)}, u32[]{:S(2)}) collective-permute-start(bf16[144,128]{1,0:T(8,128)(2,1)S(1)} %project.1), channel_id=1, source_target_pairs={{0,4},{4,0},{1,5},{5,1},{2,6},{6,2},{3,7},{7,3},{8,12},{12,8},{9,1... | collective-permute-start | bytes 110600 | tf_op jit(solution)/shard_map/ppermute | solution.py:468
  40.0 3.0 %collective-permute-done.11.refs_1_ = bf16[144,128]{1,0:T(8,128)(2,1)S(1)} collective-permute-done((bf16[144,128]{1,0:T(8,128)(2,1)S(1)}, bf16[144,128]{1,0:T(8,128)(2,1)S(1)}, u32[]{:S(2)}, u32[]{:S(2)}) %collective-permute-start.11) | collective-permute-done | bytes 36896 | tf_op jit(solution)/shard_map/ppermute | solution.py:465
  43.3 2.6 %collective-permute-start.14 = (bf16[144,128]{1,0:T(8,128)(2,1)S(1)}, bf16[144,128]{1,0:T(8,128)(2,1)S(1)}, u32[]{:S(2)}, u32[]{:S(2)}) collective-permute-start(bf16[144,128]{1,0:T(8,128)(2,1)S(1)} %middle_merge.1), channel_id=1, source_target_pairs={{0,20},{4,16},{8,28},{12,24},{16,4},{20,0},{24,12},{28,8},{1,21},{... | collective-permute-start | bytes 110600 | tf_op jit(solution)/shard_map/ppermute | solution.py:465
  45.9 1.4 %collective-permute-start.15 = (bf16[144,128]{1,0:T(8,128)(2,1)S(1)}, bf16[144,128]{1,0:T(8,128)(2,1)S(1)}, u32[]{:S(2)}, u32[]{:S(2)}) collective-permute-start(bf16[144,128]{1,0:T(8,128)(2,1)S(1)} %middle_merge.1), channel_id=1, source_target_pairs={{0,28},{4,24},{8,20},{12,16},{16,12},{20,8},{24,4},{28,0},{1,29},{... | collective-permute-start | bytes 110600 | tf_op jit(solution)/shard_map/ppermute | solution.py:465
  47.2 1.0 %collective-permute-done.14.refs_0_ = bf16[144,128]{1,0:T(8,128)(2,1)S(1)} collective-permute-done((bf16[144,128]{1,0:T(8,128)(2,1)S(1)}, bf16[144,128]{1,0:T(8,128)(2,1)S(1)}, u32[]{:S(2)}, u32[]{:S(2)}) %collective-permute-start.14) | collective-permute-done | bytes 36896 | tf_op jit(solution)/shard_map/ppermute | solution.py:465
  48.2 2.8 %collective-permute-done.15.refs_1_ = bf16[144,128]{1,0:T(8,128)(2,1)S(1)} collective-permute-done((bf16[144,128]{1,0:T(8,128)(2,1)S(1)}, bf16[144,128]{1,0:T(8,128)(2,1)S(1)}, u32[]{:S(2)}, u32[]{:S(2)}) %collective-permute-start.15) | collective-permute-done | bytes 36896 | tf_op jit(solution)/shard_map/ppermute | solution.py:465
  51.8 0.9 %collective-permute-done.18.other_ref = bf16[4,2,16,128]{3,2,1,0:T(8,128)(2,1)S(1)} collective-permute-done((bf16[4,2,16,128]{3,2,1,0:T(8,128)(2,1)S(1)}, bf16[4,2,16,128]{3,2,1,0:T(8,128)(2,1)S(1)}, u32[]{:S(2)}, u32[]{:S(2)}) %collective-permute-start.18) | collective-permute-done | bytes 32800 | tf_op jit(solution)/shard_map/ppermute | solution.py:486
  52.6 0.6 %place.1 = bf16[4,4,16,128]{3,2,1,0:T(8,128)(2,1)} custom-call(s32[1]{0:T(128)} %bitcast.own_first_ref.info_ref, bf16[4,2,16,128]{3,2,1,0:T(8,128)(2,1)S(1)} %finish.1.own_ref, bf16[4,2,16,128]{3,2,1,0:T(8,128)(2,1)S(1)} %collective-permute-done.18.other_ref), custom_call_target="tpu_custom_call" | custom-call | tf_op jit(solution)/shard_map/place/pallas_call | solution.py:487
  (34 shorter events, 3.5 us)
Async XLA Ops:
  2.1 7.2 %collective-permute-start = (bf16[64,1152]{1,0:T(8,128)(2,1)S(1)}, bf16[64,1152]{1,0:T(8,128)(2,1)S(1)}, u32[]{:S(2)}, u32[]{:S(2)}) collective-permute-start(bf16[64,1152]{1,0:T(8,128)(2,1)S(1)} %get-tuple-element.16), channel_id=1, source_target_pairs={{0,2},{1,3},{2,0},{3,1},{4,6},{5,7},{6,4},{7,5},{8,10},{9,11},{10,... | collective-permute-start | bytes 442376 | tf_op jit(solution)/shard_map/ppermute | solution.py:388
  5.9 6.8 %collective-permute-start.1 = (bf16[64,1152]{1,0:T(8,128)(2,1)S(1)}, bf16[64,1152]{1,0:T(8,128)(2,1)S(1)}, u32[]{:S(2)}, u32[]{:S(2)}) collective-permute-start(bf16[64,1152]{1,0:T(8,128)(2,1)S(1)} %get-tuple-element.16), channel_id=1, source_target_pairs={{0,3},{1,2},{2,1},{3,0},{4,7},{5,6},{6,5},{7,4},{8,11},{9,10},{10,... | collective-permute-start | bytes 442376 | tf_op jit(solution)/shard_map/ppermute | solution.py:388
  6.7 7.2 %collective-permute-start.2 = (bf16[64,1152]{1,0:T(8,128)(2,1)S(1)}, bf16[64,1152]{1,0:T(8,128)(2,1)S(1)}, u32[]{:S(2)}, u32[]{:S(2)}) collective-permute-start(bf16[64,1152]{1,0:T(8,128)(2,1)S(1)} %get-tuple-element.16), channel_id=1, source_target_pairs={{0,1},{1,0},{2,3},{3,2},{4,5},{5,4},{6,7},{7,6},{8,9},{9,8},{10,11... | collective-permute-start | bytes 442376 | tf_op jit(solution)/shard_map/ppermute | solution.py:388
  6.7 11.3 %slice-start = ((s8[9437184]{0:T(1024)(128)(4,1)}), s8[4194304]{0:T(1024)(128)(4,1)S(1)}, s32[]{:S(2)}) async-start(s8[9437184]{0:T(1024)(128)(4,1)} %bitcast.7), calls=%async_computation | async-start | bytes 8388608
  9.2 8.7 %collective-permute-start.4 = (bf16[64,1152]{1,0:T(8,128)(2,1)S(1)}, bf16[64,1152]{1,0:T(8,128)(2,1)S(1)}, u32[]{:S(2)}, u32[]{:S(2)}) collective-permute-start(bf16[64,1152]{1,0:T(8,128)(2,1)S(1)} %collective-permute-done.q1_ref), channel_id=1, source_target_pairs={{0,4},{4,0},{1,5},{5,1},{2,6},{6,2},{3,7},{7,3},{8,12},{12,8},{9,1... | collective-permute-start | bytes 442376 | tf_op jit(solution)/shard_map/ppermute | solution.py:416
  12.8 5.2 %collective-permute-start.5 = (bf16[64,1152]{1,0:T(8,128)(2,1)S(1)}, bf16[64,1152]{1,0:T(8,128)(2,1)S(1)}, u32[]{:S(2)}, u32[]{:S(2)}) collective-permute-start(bf16[64,1152]{1,0:T(8,128)(2,1)S(1)} %collective-permute-done.1.q2_ref), channel_id=1, source_target_pairs={{0,4},{4,0},{1,5},{5,1},{2,6},{6,2},{3,7},{7,3},{8,12},{12,8},{9,1... | collective-permute-start | bytes 442376 | tf_op jit(solution)/shard_map/ppermute | solution.py:416
  13.9 4.1 %collective-permute-start.6 = (bf16[64,1152]{1,0:T(8,128)(2,1)S(1)}, bf16[64,1152]{1,0:T(8,128)(2,1)S(1)}, u32[]{:S(2)}, u32[]{:S(2)}) collective-permute-start(bf16[64,1152]{1,0:T(8,128)(2,1)S(1)} %collective-permute-done.2.q3_ref), channel_id=1, source_target_pairs={{0,4},{4,0},{1,5},{5,1},{2,6},{6,2},{3,7},{7,3},{8,12},{12,8},{9,1... | collective-permute-start | bytes 442376 | tf_op jit(solution)/shard_map/ppermute | solution.py:416
  14.3 3.8 %slice-start.1 = ((s8[9437184]{0:T(1024)(128)(4,1)}), s8[4194304]{0:T(1024)(128)(4,1)S(1)}, s32[]{:S(2)}) async-start(s8[9437184]{0:T(1024)(128)(4,1)} %bitcast.7), calls=%async_computation.1 | async-start | bytes 8388608
  14.3 3.8 %slice-start.2 = ((s8[9437184]{0:T(1024)(128)(4,1)}), s8[1048576]{0:T(1024)(128)(4,1)S(1)}, s32[]{:S(2)}) async-start(s8[9437184]{0:T(1024)(128)(4,1)} %bitcast.7), calls=%async_computation.2 | async-start | bytes 2097152
  17.8 3.8 %collective-permute-start.3 = (bf16[4,128,640]{2,1,0:T(8,128)(2,1)S(1)}, bf16[4,128,640]{2,1,0:T(8,128)(2,1)S(1)}, u32[]{:S(2)}, u32[]{:S(2)}) collective-permute-start(bf16[4,128,640]{2,1,0:T(8,128)(2,1)S(1)} %attention.2), channel_id=1, source_target_pairs={{0,4},{4,0},{1,5},{5,1},{2,6},{6,2},{3,7},{7,3},{8,12},{12,8},{9,1... | collective-permute-start | bytes 1966088 | tf_op jit(solution)/shard_map/ppermute | solution.py:437
  21.6 11.4 %copy-start = (bf16[16,512,128]{2,1,0:T(8,128)(2,1)S(1)}, bf16[16,512,128]{2,1,0:T(8,128)(2,1)}, u32[]{:S(2)}) copy-start(bf16[16,512,128]{2,1,0:T(8,128)(2,1)} %refs_5_.1) | copy-start | bytes 6291460
  22.4 6.6 %collective-permute-start.7 = (bf16[144,512]{1,0:T(8,128)(2,1)S(1)}, bf16[144,512]{1,0:T(8,128)(2,1)S(1)}, u32[]{:S(2)}, u32[]{:S(2)}) collective-permute-start(bf16[144,512]{1,0:T(8,128)(2,1)S(1)} %get-tuple-element.19), channel_id=1, source_target_pairs={{0,2},{1,3},{2,0},{3,1},{4,6},{5,7},{6,4},{7,5},{8,10},{9,11},{10,... | collective-permute-start | bytes 442376 | tf_op jit(solution)/shard_map/ppermute | solution.py:388
  24.6 8.3 %collective-permute-start.8 = (bf16[144,512]{1,0:T(8,128)(2,1)S(1)}, bf16[144,512]{1,0:T(8,128)(2,1)S(1)}, u32[]{:S(2)}, u32[]{:S(2)}) collective-permute-start(bf16[144,512]{1,0:T(8,128)(2,1)S(1)} %get-tuple-element.20), channel_id=1, source_target_pairs={{0,3},{1,2},{2,1},{3,0},{4,7},{5,6},{6,5},{7,4},{8,11},{9,10},{10,... | collective-permute-start | bytes 442376 | tf_op jit(solution)/shard_map/ppermute | solution.py:388
  26.2 6.8 %collective-permute-start.9 = (bf16[144,512]{1,0:T(8,128)(2,1)S(1)}, bf16[144,512]{1,0:T(8,128)(2,1)S(1)}, u32[]{:S(2)}, u32[]{:S(2)}) collective-permute-start(bf16[144,512]{1,0:T(8,128)(2,1)S(1)} %get-tuple-element.21), channel_id=1, source_target_pairs={{0,1},{1,0},{2,3},{3,2},{4,5},{5,4},{6,7},{7,6},{8,9},{9,8},{10,11... | collective-permute-start | bytes 442376 | tf_op jit(solution)/shard_map/ppermute | solution.py:388
  34.0 6.0 %collective-permute-start.10 = (bf16[144,128]{1,0:T(8,128)(2,1)S(1)}, bf16[144,128]{1,0:T(8,128)(2,1)S(1)}, u32[]{:S(2)}, u32[]{:S(2)}) collective-permute-start(bf16[144,128]{1,0:T(8,128)(2,1)S(1)} %project.1), channel_id=1, source_target_pairs={{0,68},{4,64},{32,100},{36,96},{64,4},{68,0},{96,36},{100,32},{1,6... | collective-permute-start | bytes 110600 | tf_op jit(solution)/shard_map/ppermute | solution.py:465
  38.4 4.6 %collective-permute-start.11 = (bf16[144,128]{1,0:T(8,128)(2,1)S(1)}, bf16[144,128]{1,0:T(8,128)(2,1)S(1)}, u32[]{:S(2)}, u32[]{:S(2)}) collective-permute-start(bf16[144,128]{1,0:T(8,128)(2,1)S(1)} %project.1), channel_id=1, source_target_pairs={{0,100},{4,96},{32,68},{36,64},{64,36},{68,32},{96,4},{100,0},{1,1... | collective-permute-start | bytes 110600 | tf_op jit(solution)/shard_map/ppermute | solution.py:465
  38.6 4.4 %collective-permute-start.12 = (bf16[144,128]{1,0:T(8,128)(2,1)S(1)}, bf16[144,128]{1,0:T(8,128)(2,1)S(1)}, u32[]{:S(2)}, u32[]{:S(2)}) collective-permute-start(bf16[144,128]{1,0:T(8,128)(2,1)S(1)} %project.1), channel_id=1, source_target_pairs={{0,36},{4,32},{32,4},{36,0},{64,100},{68,96},{96,68},{100,64},{1,3... | collective-permute-start | bytes 110600 | tf_op jit(solution)/shard_map/ppermute | solution.py:465
  38.7 4.3 %collective-permute-start.13 = (bf16[144,128]{1,0:T(8,128)(2,1)S(1)}, bf16[144,128]{1,0:T(8,128)(2,1)S(1)}, u32[]{:S(2)}, u32[]{:S(2)}) collective-permute-start(bf16[144,128]{1,0:T(8,128)(2,1)S(1)} %project.1), channel_id=1, source_target_pairs={{0,4},{4,0},{1,5},{5,1},{2,6},{6,2},{3,7},{7,3},{8,12},{12,8},{9,1... | collective-permute-start | bytes 110600 | tf_op jit(solution)/shard_map/ppermute | solution.py:468
  43.3 5.0 %collective-permute-start.14 = (bf16[144,128]{1,0:T(8,128)(2,1)S(1)}, bf16[144,128]{1,0:T(8,128)(2,1)S(1)}, u32[]{:S(2)}, u32[]{:S(2)}) collective-permute-start(bf16[144,128]{1,0:T(8,128)(2,1)S(1)} %middle_merge.1), channel_id=1, source_target_pairs={{0,20},{4,16},{8,28},{12,24},{16,4},{20,0},{24,12},{28,8},{1,21},{... | collective-permute-start | bytes 110600 | tf_op jit(solution)/shard_map/ppermute | solution.py:465
  45.9 5.1 %collective-permute-start.15 = (bf16[144,128]{1,0:T(8,128)(2,1)S(1)}, bf16[144,128]{1,0:T(8,128)(2,1)S(1)}, u32[]{:S(2)}, u32[]{:S(2)}) collective-permute-start(bf16[144,128]{1,0:T(8,128)(2,1)S(1)} %middle_merge.1), channel_id=1, source_target_pairs={{0,28},{4,24},{8,20},{12,16},{16,12},{20,8},{24,4},{28,0},{1,29},{... | collective-permute-start | bytes 110600 | tf_op jit(solution)/shard_map/ppermute | solution.py:465
  47.2 3.8 %collective-permute-start.16 = (bf16[144,128]{1,0:T(8,128)(2,1)S(1)}, bf16[144,128]{1,0:T(8,128)(2,1)S(1)}, u32[]{:S(2)}, u32[]{:S(2)}) collective-permute-start(bf16[144,128]{1,0:T(8,128)(2,1)S(1)} %middle_merge.1), channel_id=1, source_target_pairs={{0,12},{4,8},{8,4},{12,0},{16,28},{20,24},{24,20},{28,16},{1,13},{... | collective-permute-start | bytes 110600 | tf_op jit(solution)/shard_map/ppermute | solution.py:465
  47.2 3.8 %collective-permute-start.17 = (bf16[144,128]{1,0:T(8,128)(2,1)S(1)}, bf16[144,128]{1,0:T(8,128)(2,1)S(1)}, u32[]{:S(2)}, u32[]{:S(2)}) collective-permute-start(bf16[144,128]{1,0:T(8,128)(2,1)S(1)} %middle_merge.1), channel_id=1, source_target_pairs={{0,4},{4,0},{1,5},{5,1},{2,6},{6,2},{3,7},{7,3},{8,12},{12,8},{9,1... | collective-permute-start | bytes 110600 | tf_op jit(solution)/shard_map/ppermute | solution.py:468
  51.3 1.3 %collective-permute-start.18 = (bf16[4,2,16,128]{3,2,1,0:T(8,128)(2,1)S(1)}, bf16[4,2,16,128]{3,2,1,0:T(8,128)(2,1)S(1)}, u32[]{:S(2)}, u32[]{:S(2)}) collective-permute-start(bf16[4,2,16,128]{3,2,1,0:T(8,128)(2,1)S(1)} %finish.1.own_ref), channel_id=1, source_target_pairs={{0,4},{4,0},{1,5},{5,1},{2,6},{6,2},{3,7},{7,3},{8,12},{12,8},{9,1... | collective-permute-start | bytes 98312 | tf_op jit(solution)/shard_map/ppermute | solution.py:486

commit v16 on v15

--- a/solution.py
+++ b/solution.py
@@ -474,7 +474,7 @@
         out_shape=jax.ShapeDtypeStruct(part.shape, bf16),
         compiler_params=small,
         name="middle_merge",
-    )(*crossing(part, "z"))
+    )(*crossing(part, "x"))
     own = pl.pallas_call(
         finish_kernel,
         in_specs=[vmem] * 4,
@@ -482,7 +482,7 @@
         out_shape=jax.ShapeDtypeStruct((steps, half, heads, value_width), bf16),
         compiler_params=small,
         name="finish",
-    )(*crossing(part, "x"))
+    )(*crossing(part, "z"))
     theirs = lax.ppermute(own, "core", swap)
     return pl.pallas_call(
         place_kernel,

time: 53.4 us -> 53.2 us (level)
  no operation moved by 1% of the time
where the time goes in v16:
time: 53.2 us; the launch traced here: 53.1 us
  starting transfers between devices  22.1 us (42%)
  Pallas kernels  15.6 us (29%)
  waiting for transfers between devices  15.3 us (29%)
    ppermute x6, starting transfers between devices, crossing(): lax.ppermute(array, (axis, 'core'), [(2 * i + c, 2 * (i ^ k) + 1 - c) for...  8.66 us
    ppermute x6, starting transfers between devices, over_head(): return lax.ppermute(array, 'head', [(i, i ^ k) for i in range(owners)])  8.4 us
    ppermute x6, waiting for transfers between devices, over_head(): return lax.ppermute(array, 'head', [(i, i ^ k) for i in range(owners)])  7.52 us
    pallas_call x2, Pallas kernels, attend(): pl.pallas_call(functools.partial(attention_kernel, scale), in_specs=[smem...  7.03 us
    ppermute x6, waiting for transfers between devices, crossing(): lax.ppermute(array, (axis, 'core'), [(2 * i + c, 2 * (i ^ k) + 1 - c) for...  6.78 us
    ppermute x3, starting transfers between devices, on_device(): passed = [lax.ppermute(g, 'core', swap) for g in got]  3.38 us
    pallas_call x1, Pallas kernels, on_device(): pl.pallas_call(stage_kernel, in_specs=[smem, anywhere], out_specs=vmem, o...  2.54 us
    pallas_call x1, Pallas kernels, on_device(): pl.pallas_call(functools.partial(queries_kernel, steps), in_specs=[smem]...  2.08 us
  transfers between devices with their start and end apart: 19, of which 9 were waited for; matrix products, arithmetic and copies ran while one was open for 0% of the time, Pallas kernels for 20%

profile of v16, /device:TPU:1, one launch (start us, length us, event | category | flops | bytes accessed | tf_op | source)
XLA Modules:
  0.0 53.1 jit_solution(14974431345836517776)
XLA Ops:
  0.0 2.1 %queries.1 = (bf16[4,64,640]{2,1,0:T(8,128)(2,1)S(1)}, bf16[64,1152]{1,0:T(8,128)(2,1)S(1)}, bf16[16,576]{1,0:T(8,128)(2,1)S(1)}, s32[8,128]{1,0:T(8,128)S(1)}) custom-call(s32[1]{0:T(128)} %bitcast.1.info_ref, s32[1]{0:T(128)} %bitcast.own_first_ref.info_ref, s32[1]{0:T(128)} %bitcast.2.row_ref, s32[1]{0:T(128)} %bitcast.3.place_ref, s32[4]{0:T(128)} %positions_hbm.1, ...), custom_call_target="tpu_custom_call" | custom-call | tf_op jit(solution)/shard_map/queries/pallas_call | solution.py:354
  2.1 3.8 %collective-permute-start = (bf16[64,1152]{1,0:T(8,128)(2,1)S(1)}, bf16[64,1152]{1,0:T(8,128)(2,1)S(1)}, u32[]{:S(2)}, u32[]{:S(2)}) collective-permute-start(bf16[64,1152]{1,0:T(8,128)(2,1)S(1)} %get-tuple-element.16), channel_id=1, source_target_pairs={{0,2},{1,3},{2,0},{3,1},{4,6},{5,7},{6,4},{7,5},{8,10},{9,11},{10,... | collective-permute-start | bytes 442376 | tf_op jit(solution)/shard_map/ppermute | solution.py:388
  5.9 0.8 %collective-permute-start.1 = (bf16[64,1152]{1,0:T(8,128)(2,1)S(1)}, bf16[64,1152]{1,0:T(8,128)(2,1)S(1)}, u32[]{:S(2)}, u32[]{:S(2)}) collective-permute-start(bf16[64,1152]{1,0:T(8,128)(2,1)S(1)} %get-tuple-element.16), channel_id=1, source_target_pairs={{0,3},{1,2},{2,1},{3,0},{4,7},{5,6},{6,5},{7,4},{8,11},{9,10},{10,... | collective-permute-start | bytes 442376 | tf_op jit(solution)/shard_map/ppermute | solution.py:388
  6.7 2.5 %stage.1.k_ref = bf16[2,576,2048]{2,1,0:T(8,128)(2,1)S(1)} custom-call(s32[1]{0:T(128)} %bitcast.1.info_ref, bf16[4,576,2048]{2,1,0:T(8,128)(2,1)} %bitcast.6), custom_call_target="tpu_custom_call" | custom-call | bytes 4718592 | tf_op jit(solution)/shard_map/stage/pallas_call | solution.py:405
  9.2 1.9 %collective-permute-start.4 = (bf16[64,1152]{1,0:T(8,128)(2,1)S(1)}, bf16[64,1152]{1,0:T(8,128)(2,1)S(1)}, u32[]{:S(2)}, u32[]{:S(2)}) collective-permute-start(bf16[64,1152]{1,0:T(8,128)(2,1)S(1)} %collective-permute-done.q1_ref), channel_id=1, source_target_pairs={{0,4},{4,0},{1,5},{5,1},{2,6},{6,2},{3,7},{7,3},{8,12},{12,8},{9,1... | collective-permute-start | bytes 442376 | tf_op jit(solution)/shard_map/ppermute | solution.py:416
  11.1 1.6 %collective-permute-done.1.q2_ref = bf16[64,1152]{1,0:T(8,128)(2,1)S(1)} collective-permute-done((bf16[64,1152]{1,0:T(8,128)(2,1)S(1)}, bf16[64,1152]{1,0:T(8,128)(2,1)S(1)}, u32[]{:S(2)}, u32[]{:S(2)}) %collective-permute-start.1) | collective-permute-done | bytes 147488 | tf_op jit(solution)/shard_map/ppermute | solution.py:388
  12.8 1.1 %collective-permute-start.5 = (bf16[64,1152]{1,0:T(8,128)(2,1)S(1)}, bf16[64,1152]{1,0:T(8,128)(2,1)S(1)}, u32[]{:S(2)}, u32[]{:S(2)}) collective-permute-start(bf16[64,1152]{1,0:T(8,128)(2,1)S(1)} %collective-permute-done.1.q2_ref), channel_id=1, source_target_pairs={{0,4},{4,0},{1,5},{5,1},{2,6},{6,2},{3,7},{7,3},{8,12},{12,8},{9,1... | collective-permute-start | bytes 442376 | tf_op jit(solution)/shard_map/ppermute | solution.py:416
  14.3 3.5 %attention.2 = bf16[4,128,640]{2,1,0:T(8,128)(2,1)S(1)} custom-call(s32[1]{0:T(128)} %bitcast.1.info_ref, s32[8,128]{1,0:T(8,128)S(1)} %get-tuple-element.14.limits_ref, bf16[4,64,640]{2,1,0:T(8,128)(2,1)S(1)} %get-tuple-element.15.own_ref, bf16[64,1152]{1,0:T(8,128)(2,1)S(1)} %collective-permute-done.q1_ref, ...), custom_call_target="tpu_custom_call" | custom-call | flops 22817013760 | bytes 4718592 | tf_op jit(solution)/shard_map/attention/pallas_call | solution.py:421
  18.0 3.5 %attention.3.b_ref = bf16[4,128,640]{2,1,0:T(8,128)(2,1)S(1)} custom-call(s32[1]{0:T(128)} %bitcast.own_first_ref.info_ref, s32[8,128]{1,0:T(8,128)S(1)} %get-tuple-element.14.limits_ref, bf16[4,64,640]{2,1,0:T(8,128)(2,1)S(1)} %get-tuple-element.15.own_ref, bf16[64,1152]{1,0:T(8,128)(2,1)S(1)} %collective-permute-done.4.q1_ref, ...), custom_call_target="tpu_custom_call" | custom-call | flops 22817013760 | bytes 4718592 | tf_op jit(solution)/shard_map/attention/pallas_call | solution.py:421
  21.6 0.8 %pair_merge.3 = (bf16[144,512]{1,0:T(8,128)(2,1)S(1)}, bf16[144,512]{1,0:T(8,128)(2,1)S(1)}, bf16[144,512]{1,0:T(8,128)(2,1)S(1)}) custom-call(bf16[4,128,640]{2,1,0:T(8,128)(2,1)S(1)} %collective-permute-done.3.a_ref, bf16[4,128,640]{2,1,0:T(8,128)(2,1)S(1)} %attention.3.b_ref), custom_call_target="tpu_custom_call" | custom-call | tf_op jit(solution)/shard_map/pair_merge/pallas_call | solution.py:440
  22.4 2.2 %collective-permute-start.7 = (bf16[144,512]{1,0:T(8,128)(2,1)S(1)}, bf16[144,512]{1,0:T(8,128)(2,1)S(1)}, u32[]{:S(2)}, u32[]{:S(2)}) collective-permute-start(bf16[144,512]{1,0:T(8,128)(2,1)S(1)} %get-tuple-element.19), channel_id=1, source_target_pairs={{0,2},{1,3},{2,0},{3,1},{4,6},{5,7},{6,4},{7,5},{8,10},{9,11},{10,... | collective-permute-start | bytes 442376 | tf_op jit(solution)/shard_map/ppermute | solution.py:388
  24.6 1.6 %collective-permute-start.8 = (bf16[144,512]{1,0:T(8,128)(2,1)S(1)}, bf16[144,512]{1,0:T(8,128)(2,1)S(1)}, u32[]{:S(2)}, u32[]{:S(2)}) collective-permute-start(bf16[144,512]{1,0:T(8,128)(2,1)S(1)} %get-tuple-element.20), channel_id=1, source_target_pairs={{0,3},{1,2},{2,1},{3,0},{4,7},{5,6},{6,5},{7,4},{8,11},{9,10},{10,... | collective-permute-start | bytes 442376 | tf_op jit(solution)/shard_map/ppermute | solution.py:388
  26.2 0.6 %fresh.1.refs_4_ = bf16[144,512]{1,0:T(8,128)(2,1)S(1)} custom-call(s32[1]{0:T(128)} %bitcast.own_first_ref.info_ref, s32[8,128]{1,0:T(8,128)S(1)} %get-tuple-element.14.limits_ref, bf16[4,64,640]{2,1,0:T(8,128)(2,1)S(1)} %get-tuple-element.15.own_ref, bf16[16,576]{1,0:T(8,128)(2,1)S(1)} %get-tuple-element.22.new_ref), custom_call_target="tpu_custom_call" | custom-call | flops 1000000000 | bytes 4000000 | tf_op jit(solution)/shard_map/fresh/pallas_call | solution.py:393
  27.1 1.9 %collective-permute-done.7.refs_1_ = bf16[144,512]{1,0:T(8,128)(2,1)S(1)} collective-permute-done((bf16[144,512]{1,0:T(8,128)(2,1)S(1)}, bf16[144,512]{1,0:T(8,128)(2,1)S(1)}, u32[]{:S(2)}, u32[]{:S(2)}) %collective-permute-start.7) | collective-permute-done | bytes 147488 | tf_op jit(solution)/shard_map/ppermute | solution.py:388
  29.0 3.9 %collective-permute-done.8.refs_2_ = bf16[144,512]{1,0:T(8,128)(2,1)S(1)} collective-permute-done((bf16[144,512]{1,0:T(8,128)(2,1)S(1)}, bf16[144,512]{1,0:T(8,128)(2,1)S(1)}, u32[]{:S(2)}, u32[]{:S(2)}) %collective-permute-start.8) | collective-permute-done | bytes 147488 | tf_op jit(solution)/shard_map/ppermute | solution.py:388
  33.0 1.0 %project.1 = bf16[144,128]{1,0:T(8,128)(2,1)S(1)} custom-call(bf16[144,512]{1,0:T(8,128)(2,1)S(1)} %pair_merge.2.refs_0_, bf16[144,512]{1,0:T(8,128)(2,1)S(1)} %collective-permute-done.7.refs_1_, bf16[144,512]{1,0:T(8,128)(2,1)S(1)} %collective-permute-done.8.refs_2_, bf16[144,512]{1,0:T(8,128)(2,1)S(1)} %collective-permute-done.9.refs_3_, ...), custom_call_target="tpu_custom_call" | custom-call | tf_op jit(solution)/shard_map/project/pallas_call | solution.py:452
  34.0 3.5 %collective-permute-start.10 = (bf16[144,128]{1,0:T(8,128)(2,1)S(1)}, bf16[144,128]{1,0:T(8,128)(2,1)S(1)}, u32[]{:S(2)}, u32[]{:S(2)}) collective-permute-start(bf16[144,128]{1,0:T(8,128)(2,1)S(1)} %project.1), channel_id=1, source_target_pairs={{0,20},{4,16},{8,28},{12,24},{16,4},{20,0},{24,12},{28,8},{1,21},{... | collective-permute-start | bytes 110600 | tf_op jit(solution)/shard_map/ppermute | solution.py:465
  38.0 0.8 %collective-permute-start.13 = (bf16[144,128]{1,0:T(8,128)(2,1)S(1)}, bf16[144,128]{1,0:T(8,128)(2,1)S(1)}, u32[]{:S(2)}, u32[]{:S(2)}) collective-permute-start(bf16[144,128]{1,0:T(8,128)(2,1)S(1)} %project.1), channel_id=1, source_target_pairs={{0,4},{4,0},{1,5},{5,1},{2,6},{6,2},{3,7},{7,3},{8,12},{12,8},{9,1... | collective-permute-start | bytes 110600 | tf_op jit(solution)/shard_map/ppermute | solution.py:468
  38.8 0.9 %collective-permute-done.10.refs_0_ = bf16[144,128]{1,0:T(8,128)(2,1)S(1)} collective-permute-done((bf16[144,128]{1,0:T(8,128)(2,1)S(1)}, bf16[144,128]{1,0:T(8,128)(2,1)S(1)}, u32[]{:S(2)}, u32[]{:S(2)}) %collective-permute-start.10) | collective-permute-done | bytes 36896 | tf_op jit(solution)/shard_map/ppermute | solution.py:465
  39.7 2.4 %collective-permute-done.11.refs_1_ = bf16[144,128]{1,0:T(8,128)(2,1)S(1)} collective-permute-done((bf16[144,128]{1,0:T(8,128)(2,1)S(1)}, bf16[144,128]{1,0:T(8,128)(2,1)S(1)}, u32[]{:S(2)}, u32[]{:S(2)}) %collective-permute-start.11) | collective-permute-done | bytes 36896 | tf_op jit(solution)/shard_map/ppermute | solution.py:465
  42.4 3.9 %collective-permute-start.14 = (bf16[144,128]{1,0:T(8,128)(2,1)S(1)}, bf16[144,128]{1,0:T(8,128)(2,1)S(1)}, u32[]{:S(2)}, u32[]{:S(2)}) collective-permute-start(bf16[144,128]{1,0:T(8,128)(2,1)S(1)} %middle_merge.1), channel_id=1, source_target_pairs={{0,68},{4,64},{32,100},{36,96},{64,4},{68,0},{96,36},{100,32},{1,6... | collective-permute-start | bytes 110600 | tf_op jit(solution)/shard_map/ppermute | solution.py:465
  47.9 3.0 %collective-permute-done.15.refs_1_ = bf16[144,128]{1,0:T(8,128)(2,1)S(1)} collective-permute-done((bf16[144,128]{1,0:T(8,128)(2,1)S(1)}, bf16[144,128]{1,0:T(8,128)(2,1)S(1)}, u32[]{:S(2)}, u32[]{:S(2)}) %collective-permute-start.15) | collective-permute-done | bytes 36896 | tf_op jit(solution)/shard_map/ppermute | solution.py:465
  51.5 1.0 %collective-permute-done.18.other_ref = bf16[4,2,16,128]{3,2,1,0:T(8,128)(2,1)S(1)} collective-permute-done((bf16[4,2,16,128]{3,2,1,0:T(8,128)(2,1)S(1)}, bf16[4,2,16,128]{3,2,1,0:T(8,128)(2,1)S(1)}, u32[]{:S(2)}, u32[]{:S(2)}) %collective-permute-start.18) | collective-permute-done | bytes 32800 | tf_op jit(solution)/shard_map/ppermute | solution.py:486
  52.4 0.6 %place.1 = bf16[4,4,16,128]{3,2,1,0:T(8,128)(2,1)} custom-call(s32[1]{0:T(128)} %bitcast.own_first_ref.info_ref, bf16[4,2,16,128]{3,2,1,0:T(8,128)(2,1)S(1)} %finish.1.own_ref, bf16[4,2,16,128]{3,2,1,0:T(8,128)(2,1)S(1)} %collective-permute-done.18.other_ref), custom_call_target="tpu_custom_call" | custom-call | tf_op jit(solution)/shard_map/place/pallas_call | solution.py:487
  (34 shorter events, 4.0 us)
Async XLA Ops:
  2.1 7.2 %collective-permute-start = (bf16[64,1152]{1,0:T(8,128)(2,1)S(1)}, bf16[64,1152]{1,0:T(8,128)(2,1)S(1)}, u32[]{:S(2)}, u32[]{:S(2)}) collective-permute-start(bf16[64,1152]{1,0:T(8,128)(2,1)S(1)} %get-tuple-element.16), channel_id=1, source_target_pairs={{0,2},{1,3},{2,0},{3,1},{4,6},{5,7},{6,4},{7,5},{8,10},{9,11},{10,... | collective-permute-start | bytes 442376 | tf_op jit(solution)/shard_map/ppermute | solution.py:388
  5.9 6.8 %collective-permute-start.1 = (bf16[64,1152]{1,0:T(8,128)(2,1)S(1)}, bf16[64,1152]{1,0:T(8,128)(2,1)S(1)}, u32[]{:S(2)}, u32[]{:S(2)}) collective-permute-start(bf16[64,1152]{1,0:T(8,128)(2,1)S(1)} %get-tuple-element.16), channel_id=1, source_target_pairs={{0,3},{1,2},{2,1},{3,0},{4,7},{5,6},{6,5},{7,4},{8,11},{9,10},{10,... | collective-permute-start | bytes 442376 | tf_op jit(solution)/shard_map/ppermute | solution.py:388
  6.7 7.2 %collective-permute-start.2 = (bf16[64,1152]{1,0:T(8,128)(2,1)S(1)}, bf16[64,1152]{1,0:T(8,128)(2,1)S(1)}, u32[]{:S(2)}, u32[]{:S(2)}) collective-permute-start(bf16[64,1152]{1,0:T(8,128)(2,1)S(1)} %get-tuple-element.16), channel_id=1, source_target_pairs={{0,1},{1,0},{2,3},{3,2},{4,5},{5,4},{6,7},{7,6},{8,9},{9,8},{10,11... | collective-permute-start | bytes 442376 | tf_op jit(solution)/shard_map/ppermute | solution.py:388
  6.7 11.3 %slice-start = ((s8[9437184]{0:T(1024)(128)(4,1)}), s8[4194304]{0:T(1024)(128)(4,1)S(1)}, s32[]{:S(2)}) async-start(s8[9437184]{0:T(1024)(128)(4,1)} %bitcast.7), calls=%async_computation | async-start | bytes 8388608
  9.2 8.7 %collective-permute-start.4 = (bf16[64,1152]{1,0:T(8,128)(2,1)S(1)}, bf16[64,1152]{1,0:T(8,128)(2,1)S(1)}, u32[]{:S(2)}, u32[]{:S(2)}) collective-permute-start(bf16[64,1152]{1,0:T(8,128)(2,1)S(1)} %collective-permute-done.q1_ref), channel_id=1, source_target_pairs={{0,4},{4,0},{1,5},{5,1},{2,6},{6,2},{3,7},{7,3},{8,12},{12,8},{9,1... | collective-permute-start | bytes 442376 | tf_op jit(solution)/shard_map/ppermute | solution.py:416
  12.8 5.2 %collective-permute-start.5 = (bf16[64,1152]{1,0:T(8,128)(2,1)S(1)}, bf16[64,1152]{1,0:T(8,128)(2,1)S(1)}, u32[]{:S(2)}, u32[]{:S(2)}) collective-permute-start(bf16[64,1152]{1,0:T(8,128)(2,1)S(1)} %collective-permute-done.1.q2_ref), channel_id=1, source_target_pairs={{0,4},{4,0},{1,5},{5,1},{2,6},{6,2},{3,7},{7,3},{8,12},{12,8},{9,1... | collective-permute-start | bytes 442376 | tf_op jit(solution)/shard_map/ppermute | solution.py:416
  13.9 4.1 %collective-permute-start.6 = (bf16[64,1152]{1,0:T(8,128)(2,1)S(1)}, bf16[64,1152]{1,0:T(8,128)(2,1)S(1)}, u32[]{:S(2)}, u32[]{:S(2)}) collective-permute-start(bf16[64,1152]{1,0:T(8,128)(2,1)S(1)} %collective-permute-done.2.q3_ref), channel_id=1, source_target_pairs={{0,4},{4,0},{1,5},{5,1},{2,6},{6,2},{3,7},{7,3},{8,12},{12,8},{9,1... | collective-permute-start | bytes 442376 | tf_op jit(solution)/shard_map/ppermute | solution.py:416
  14.3 3.8 %slice-start.1 = ((s8[9437184]{0:T(1024)(128)(4,1)}), s8[4194304]{0:T(1024)(128)(4,1)S(1)}, s32[]{:S(2)}) async-start(s8[9437184]{0:T(1024)(128)(4,1)} %bitcast.7), calls=%async_computation.1 | async-start | bytes 8388608
  14.3 3.8 %slice-start.2 = ((s8[9437184]{0:T(1024)(128)(4,1)}), s8[1048576]{0:T(1024)(128)(4,1)S(1)}, s32[]{:S(2)}) async-start(s8[9437184]{0:T(1024)(128)(4,1)} %bitcast.7), calls=%async_computation.2 | async-start | bytes 2097152
  17.8 3.8 %collective-permute-start.3 = (bf16[4,128,640]{2,1,0:T(8,128)(2,1)S(1)}, bf16[4,128,640]{2,1,0:T(8,128)(2,1)S(1)}, u32[]{:S(2)}, u32[]{:S(2)}) collective-permute-start(bf16[4,128,640]{2,1,0:T(8,128)(2,1)S(1)} %attention.2), channel_id=1, source_target_pairs={{0,4},{4,0},{1,5},{5,1},{2,6},{6,2},{3,7},{7,3},{8,12},{12,8},{9,1... | collective-permute-start | bytes 1966088 | tf_op jit(solution)/shard_map/ppermute | solution.py:437
  21.6 11.4 %copy-start = (bf16[16,512,128]{2,1,0:T(8,128)(2,1)S(1)}, bf16[16,512,128]{2,1,0:T(8,128)(2,1)}, u32[]{:S(2)}) copy-start(bf16[16,512,128]{2,1,0:T(8,128)(2,1)} %refs_5_.1) | copy-start | bytes 6291460
  22.4 6.6 %collective-permute-start.7 = (bf16[144,512]{1,0:T(8,128)(2,1)S(1)}, bf16[144,512]{1,0:T(8,128)(2,1)S(1)}, u32[]{:S(2)}, u32[]{:S(2)}) collective-permute-start(bf16[144,512]{1,0:T(8,128)(2,1)S(1)} %get-tuple-element.19), channel_id=1, source_target_pairs={{0,2},{1,3},{2,0},{3,1},{4,6},{5,7},{6,4},{7,5},{8,10},{9,11},{10,... | collective-permute-start | bytes 442376 | tf_op jit(solution)/shard_map/ppermute | solution.py:388
  24.6 8.3 %collective-permute-start.8 = (bf16[144,512]{1,0:T(8,128)(2,1)S(1)}, bf16[144,512]{1,0:T(8,128)(2,1)S(1)}, u32[]{:S(2)}, u32[]{:S(2)}) collective-permute-start(bf16[144,512]{1,0:T(8,128)(2,1)S(1)} %get-tuple-element.20), channel_id=1, source_target_pairs={{0,3},{1,2},{2,1},{3,0},{4,7},{5,6},{6,5},{7,4},{8,11},{9,10},{10,... | collective-permute-start | bytes 442376 | tf_op jit(solution)/shard_map/ppermute | solution.py:388
  26.2 6.8 %collective-permute-start.9 = (bf16[144,512]{1,0:T(8,128)(2,1)S(1)}, bf16[144,512]{1,0:T(8,128)(2,1)S(1)}, u32[]{:S(2)}, u32[]{:S(2)}) collective-permute-start(bf16[144,512]{1,0:T(8,128)(2,1)S(1)} %get-tuple-element.21), channel_id=1, source_target_pairs={{0,1},{1,0},{2,3},{3,2},{4,5},{5,4},{6,7},{7,6},{8,9},{9,8},{10,11... | collective-permute-start | bytes 442376 | tf_op jit(solution)/shard_map/ppermute | solution.py:388
  34.0 5.7 %collective-permute-start.10 = (bf16[144,128]{1,0:T(8,128)(2,1)S(1)}, bf16[144,128]{1,0:T(8,128)(2,1)S(1)}, u32[]{:S(2)}, u32[]{:S(2)}) collective-permute-start(bf16[144,128]{1,0:T(8,128)(2,1)S(1)} %project.1), channel_id=1, source_target_pairs={{0,20},{4,16},{8,28},{12,24},{16,4},{20,0},{24,12},{28,8},{1,21},{... | collective-permute-start | bytes 110600 | tf_op jit(solution)/shard_map/ppermute | solution.py:465
  37.5 4.6 %collective-permute-start.11 = (bf16[144,128]{1,0:T(8,128)(2,1)S(1)}, bf16[144,128]{1,0:T(8,128)(2,1)S(1)}, u32[]{:S(2)}, u32[]{:S(2)}) collective-permute-start(bf16[144,128]{1,0:T(8,128)(2,1)S(1)} %project.1), channel_id=1, source_target_pairs={{0,28},{4,24},{8,20},{12,16},{16,12},{20,8},{24,4},{28,0},{1,29},{... | collective-permute-start | bytes 110600 | tf_op jit(solution)/shard_map/ppermute | solution.py:465
  38.0 4.2 %collective-permute-start.12 = (bf16[144,128]{1,0:T(8,128)(2,1)S(1)}, bf16[144,128]{1,0:T(8,128)(2,1)S(1)}, u32[]{:S(2)}, u32[]{:S(2)}) collective-permute-start(bf16[144,128]{1,0:T(8,128)(2,1)S(1)} %project.1), channel_id=1, source_target_pairs={{0,12},{4,8},{8,4},{12,0},{16,28},{20,24},{24,20},{28,16},{1,13},{... | collective-permute-start | bytes 110600 | tf_op jit(solution)/shard_map/ppermute | solution.py:465
  38.0 4.2 %collective-permute-start.13 = (bf16[144,128]{1,0:T(8,128)(2,1)S(1)}, bf16[144,128]{1,0:T(8,128)(2,1)S(1)}, u32[]{:S(2)}, u32[]{:S(2)}) collective-permute-start(bf16[144,128]{1,0:T(8,128)(2,1)S(1)} %project.1), channel_id=1, source_target_pairs={{0,4},{4,0},{1,5},{5,1},{2,6},{6,2},{3,7},{7,3},{8,12},{12,8},{9,1... | collective-permute-start | bytes 110600 | tf_op jit(solution)/shard_map/ppermute | solution.py:468
  42.4 5.5 %collective-permute-start.14 = (bf16[144,128]{1,0:T(8,128)(2,1)S(1)}, bf16[144,128]{1,0:T(8,128)(2,1)S(1)}, u32[]{:S(2)}, u32[]{:S(2)}) collective-permute-start(bf16[144,128]{1,0:T(8,128)(2,1)S(1)} %middle_merge.1), channel_id=1, source_target_pairs={{0,68},{4,64},{32,100},{36,96},{64,4},{68,0},{96,36},{100,32},{1,6... | collective-permute-start | bytes 110600 | tf_op jit(solution)/shard_map/ppermute | solution.py:465
  46.3 4.6 %collective-permute-start.15 = (bf16[144,128]{1,0:T(8,128)(2,1)S(1)}, bf16[144,128]{1,0:T(8,128)(2,1)S(1)}, u32[]{:S(2)}, u32[]{:S(2)}) collective-permute-start(bf16[144,128]{1,0:T(8,128)(2,1)S(1)} %middle_merge.1), channel_id=1, source_target_pairs={{0,100},{4,96},{32,68},{36,64},{64,36},{68,32},{96,4},{100,0},{1,1... | collective-permute-start | bytes 110600 | tf_op jit(solution)/shard_map/ppermute | solution.py:465
  46.8 4.1 %collective-permute-start.16 = (bf16[144,128]{1,0:T(8,128)(2,1)S(1)}, bf16[144,128]{1,0:T(8,128)(2,1)S(1)}, u32[]{:S(2)}, u32[]{:S(2)}) collective-permute-start(bf16[144,128]{1,0:T(8,128)(2,1)S(1)} %middle_merge.1), channel_id=1, source_target_pairs={{0,36},{4,32},{32,4},{36,0},{64,100},{68,96},{96,68},{100,64},{1,3... | collective-permute-start | bytes 110600 | tf_op jit(solution)/shard_map/ppermute | solution.py:465
  47.1 3.8 %collective-permute-start.17 = (bf16[144,128]{1,0:T(8,128)(2,1)S(1)}, bf16[144,128]{1,0:T(8,128)(2,1)S(1)}, u32[]{:S(2)}, u32[]{:S(2)}) collective-permute-start(bf16[144,128]{1,0:T(8,128)(2,1)S(1)} %middle_merge.1), channel_id=1, source_target_pairs={{0,4},{4,0},{1,5},{5,1},{2,6},{6,2},{3,7},{7,3},{8,12},{12,8},{9,1... | collective-permute-start | bytes 110600 | tf_op jit(solution)/shard_map/ppermute | solution.py:468
  51.2 1.3 %collective-permute-start.18 = (bf16[4,2,16,128]{3,2,1,0:T(8,128)(2,1)S(1)}, bf16[4,2,16,128]{3,2,1,0:T(8,128)(2,1)S(1)}, u32[]{:S(2)}, u32[]{:S(2)}) collective-permute-start(bf16[4,2,16,128]{3,2,1,0:T(8,128)(2,1)S(1)} %finish.1.own_ref), channel_id=1, source_target_pairs={{0,4},{4,0},{1,5},{5,1},{2,6},{6,2},{3,7},{7,3},{8,12},{12,8},{9,1... | collective-permute-start | bytes 98312 | tf_op jit(solution)/shard_map/ppermute | solution.py:486

commit v17 on v15

--- a/solution.py
+++ b/solution.py
@@ -105,7 +105,7 @@
     for s in range(steps):
         for b in range(requests):
             own_ref[b, s * heads : (s + 1) * heads, :width] = lat[s * requests + b].astype(bf16)
-    packed = [own_ref[info_ref[0] + i] for i in range(sent_ref.shape[1] // key_width)]
+    packed = [own_ref[own_first_ref[0] + i] for i in range(sent_ref.shape[1] // key_width)]
     latents = [row[:, :width] for row in packed]
     sent_ref[...] = jnp.concatenate(latents + [row[:, width:key_width] for row in packed], axis=-1)
 
@@ -389,7 +389,13 @@
 
     swap = [(0, 1), (1, 0)]
     partners = (2, 3, 1)
-    got = [over_head(sent_queries, k) for k in partners]
+    sides = [(c, i) for c in range(2) for i in range(owners)]
+    got = [
+        lax.ppermute(
+            sent_queries, ("core", "head"), [(c * owners + i, (1 - c) * owners + (i ^ k)) for c, i in sides]
+        )
+        for k in partners
+    ]
     fresh = pl.pallas_call(
         functools.partial(fresh_kernel, scale, steps, heads),
         in_specs=[smem, vmem, vmem, vmem],

time: 53.4 us -> 53.9 us (level)
  waiting for transfers between devices: 15.6 us -> 18.2 us
  starting transfers between devices: 21.9 us -> 19.9 us
    ppermute x0 -> x3, starting transfers between devices: none -> 4.88 us  [on_device(): lax.ppermute(sent_queries, ('core', 'head'), [(c * owners + i, (1 - c) *...]
    ppermute x6 -> x3, starting transfers between devices: 8.4 us -> 3.7 us  [over_head(): return lax.ppermute(array, 'head', [(i, i ^ k) for i in range(owners)])]
    ppermute x0 -> x3, waiting for transfers between devices: none -> 4.21 us  [on_device(): lax.ppermute(sent_queries, ('core', 'head'), [(c * owners + i, (1 - c) *...]
    ppermute x3, starting transfers between devices: 3.38 us -> 1.12 us  [on_device(): passed = [lax.ppermute(g, 'core', swap) for g in got]]
    ppermute x6 -> x3, waiting for transfers between devices: 7.52 us -> 5.88 us  [over_head(): return lax.ppermute(array, 'head', [(i, i ^ k) for i in range(owners)])]
  transfers between devices with their start and end apart: 19 -> 19, of which waited for: 9 -> 10; matrix products, arithmetic and copies ran while one was open for 0% -> 0% of each run, Pallas kernels for 20% -> 20%
where the time goes in v17:
time: 53.9 us; the launch traced here: 53.7 us
  starting transfers between devices  19.9 us (37%)
  waiting for transfers between devices  18.2 us (34%)
  Pallas kernels  15.5 us (29%)
    ppermute x6, starting transfers between devices, crossing(): lax.ppermute(array, (axis, 'core'), [(2 * i + c, 2 * (i ^ k) + 1 - c) for...  8.68 us
    ppermute x6, waiting for transfers between devices, crossing(): lax.ppermute(array, (axis, 'core'), [(2 * i + c, 2 * (i ^ k) + 1 - c) for...  7.22 us
    pallas_call x2, Pallas kernels, attend(): pl.pallas_call(functools.partial(attention_kernel, scale), in_specs=[smem...  7.02 us
    ppermute x3, waiting for transfers between devices, over_head(): return lax.ppermute(array, 'head', [(i, i ^ k) for i in range(owners)])  5.88 us
    ppermute x3, starting transfers between devices, on_device(): lax.ppermute(sent_queries, ('core', 'head'), [(c * owners + i, (1 - c) *...  4.88 us
    ppermute x3, waiting for transfers between devices, on_device(): lax.ppermute(sent_queries, ('core', 'head'), [(c * owners + i, (1 - c) *...  4.21 us
    ppermute x3, starting transfers between devices, over_head(): return lax.ppermute(array, 'head', [(i, i ^ k) for i in range(owners)])  3.7 us
    pallas_call x1, Pallas kernels, on_device(): pl.pallas_call(stage_kernel, in_specs=[smem, anywhere], out_specs=vmem, o...  2.54 us
  transfers between devices with their start and end apart: 19, of which 10 were waited for; matrix products, arithmetic and copies ran while one was open for 0% of the time, Pallas kernels for 20%

profile of v17, /device:TPU:1, one launch (start us, length us, event | category | flops | bytes accessed | tf_op | source)
XLA Modules:
  0.0 53.7 jit_solution(11979494433910267884)
XLA Ops:
  0.0 2.1 %queries.1 = (bf16[4,64,640]{2,1,0:T(8,128)(2,1)S(1)}, bf16[64,1152]{1,0:T(8,128)(2,1)S(1)}, bf16[16,576]{1,0:T(8,128)(2,1)S(1)}, s32[8,128]{1,0:T(8,128)S(1)}) custom-call(s32[1]{0:T(128)} %bitcast.1.info_ref, s32[1]{0:T(128)} %bitcast.own_first_ref.info_ref, s32[1]{0:T(128)} %bitcast.2.row_ref, s32[1]{0:T(128)} %bitcast.3.place_ref, s32[4]{0:T(128)} %positions_hbm.1, ...), custom_call_target="tpu_custom_call" | custom-call | tf_op jit(solution)/shard_map/queries/pallas_call | solution.py:354
  2.1 4.4 %collective-permute-start = (bf16[64,1152]{1,0:T(8,128)(2,1)S(1)}, bf16[64,1152]{1,0:T(8,128)(2,1)S(1)}, u32[]{:S(2)}, u32[]{:S(2)}) collective-permute-start(bf16[64,1152]{1,0:T(8,128)(2,1)S(1)} %get-tuple-element.16), channel_id=1, source_target_pairs={{0,6},{1,7},{2,4},{3,5},{4,2},{5,3},{6,0},{7,1},{8,14},{9,15},{10,... | collective-permute-start | bytes 442376 | tf_op jit(solution)/shard_map/ppermute | solution.py:394
  7.0 2.5 %stage.1.k_ref = bf16[2,576,2048]{2,1,0:T(8,128)(2,1)S(1)} custom-call(s32[1]{0:T(128)} %bitcast.1.info_ref, bf16[4,576,2048]{2,1,0:T(8,128)(2,1)} %bitcast.6), custom_call_target="tpu_custom_call" | custom-call | bytes 4718592 | tf_op jit(solution)/shard_map/stage/pallas_call | solution.py:411
  9.5 1.1 %collective-permute-done.q1_ref = bf16[64,1152]{1,0:T(8,128)(2,1)S(1)} collective-permute-done((bf16[64,1152]{1,0:T(8,128)(2,1)S(1)}, bf16[64,1152]{1,0:T(8,128)(2,1)S(1)}, u32[]{:S(2)}, u32[]{:S(2)}) %collective-permute-start) | collective-permute-done | bytes 147488 | tf_op jit(solution)/shard_map/ppermute | solution.py:394
  11.0 2.9 %collective-permute-done.1.q2_ref = bf16[64,1152]{1,0:T(8,128)(2,1)S(1)} collective-permute-done((bf16[64,1152]{1,0:T(8,128)(2,1)S(1)}, bf16[64,1152]{1,0:T(8,128)(2,1)S(1)}, u32[]{:S(2)}, u32[]{:S(2)}) %collective-permute-start.1) | collective-permute-done | bytes 147488 | tf_op jit(solution)/shard_map/ppermute | solution.py:394
  14.9 3.5 %attention.2 = bf16[4,128,640]{2,1,0:T(8,128)(2,1)S(1)} custom-call(s32[1]{0:T(128)} %bitcast.1.info_ref, s32[8,128]{1,0:T(8,128)S(1)} %get-tuple-element.14.limits_ref, bf16[4,64,640]{2,1,0:T(8,128)(2,1)S(1)} %get-tuple-element.15.own_ref, bf16[64,1152]{1,0:T(8,128)(2,1)S(1)} %collective-permute-done.q1_ref, ...), custom_call_target="tpu_custom_call" | custom-call | flops 22817013760 | bytes 4718592 | tf_op jit(solution)/shard_map/attention/pallas_call | solution.py:427
  18.6 3.5 %attention.3.b_ref = bf16[4,128,640]{2,1,0:T(8,128)(2,1)S(1)} custom-call(s32[1]{0:T(128)} %bitcast.own_first_ref.info_ref, s32[8,128]{1,0:T(8,128)S(1)} %get-tuple-element.14.limits_ref, bf16[4,64,640]{2,1,0:T(8,128)(2,1)S(1)} %get-tuple-element.15.own_ref, bf16[64,1152]{1,0:T(8,128)(2,1)S(1)} %collective-permute-done.4.q1_ref, ...), custom_call_target="tpu_custom_call" | custom-call | flops 22817013760 | bytes 4718592 | tf_op jit(solution)/shard_map/attention/pallas_call | solution.py:427
  22.2 0.8 %pair_merge.3 = (bf16[144,512]{1,0:T(8,128)(2,1)S(1)}, bf16[144,512]{1,0:T(8,128)(2,1)S(1)}, bf16[144,512]{1,0:T(8,128)(2,1)S(1)}) custom-call(bf16[4,128,640]{2,1,0:T(8,128)(2,1)S(1)} %collective-permute-done.3.a_ref, bf16[4,128,640]{2,1,0:T(8,128)(2,1)S(1)} %attention.3.b_ref), custom_call_target="tpu_custom_call" | custom-call | tf_op jit(solution)/shard_map/pair_merge/pallas_call | solution.py:446
  23.0 2.2 %collective-permute-start.7 = (bf16[144,512]{1,0:T(8,128)(2,1)S(1)}, bf16[144,512]{1,0:T(8,128)(2,1)S(1)}, u32[]{:S(2)}, u32[]{:S(2)}) collective-permute-start(bf16[144,512]{1,0:T(8,128)(2,1)S(1)} %get-tuple-element.19), channel_id=1, source_target_pairs={{0,2},{1,3},{2,0},{3,1},{4,6},{5,7},{6,4},{7,5},{8,10},{9,11},{10,... | collective-permute-start | bytes 442376 | tf_op jit(solution)/shard_map/ppermute | solution.py:388
  25.2 1.5 %collective-permute-start.8 = (bf16[144,512]{1,0:T(8,128)(2,1)S(1)}, bf16[144,512]{1,0:T(8,128)(2,1)S(1)}, u32[]{:S(2)}, u32[]{:S(2)}) collective-permute-start(bf16[144,512]{1,0:T(8,128)(2,1)S(1)} %get-tuple-element.20), channel_id=1, source_target_pairs={{0,3},{1,2},{2,1},{3,0},{4,7},{5,6},{6,5},{7,4},{8,11},{9,10},{10,... | collective-permute-start | bytes 442376 | tf_op jit(solution)/shard_map/ppermute | solution.py:388
  26.7 0.6 %fresh.1.refs_4_ = bf16[144,512]{1,0:T(8,128)(2,1)S(1)} custom-call(s32[1]{0:T(128)} %bitcast.own_first_ref.info_ref, s32[8,128]{1,0:T(8,128)S(1)} %get-tuple-element.14.limits_ref, bf16[4,64,640]{2,1,0:T(8,128)(2,1)S(1)} %get-tuple-element.15.own_ref, bf16[16,576]{1,0:T(8,128)(2,1)S(1)} %get-tuple-element.22.new_ref), custom_call_target="tpu_custom_call" | custom-call | flops 1000000000 | bytes 4000000 | tf_op jit(solution)/shard_map/fresh/pallas_call | solution.py:399
  27.6 2.0 %collective-permute-done.7.refs_1_ = bf16[144,512]{1,0:T(8,128)(2,1)S(1)} collective-permute-done((bf16[144,512]{1,0:T(8,128)(2,1)S(1)}, bf16[144,512]{1,0:T(8,128)(2,1)S(1)}, u32[]{:S(2)}, u32[]{:S(2)}) %collective-permute-start.7) | collective-permute-done | bytes 147488 | tf_op jit(solution)/shard_map/ppermute | solution.py:388
  29.6 3.9 %collective-permute-done.8.refs_2_ = bf16[144,512]{1,0:T(8,128)(2,1)S(1)} collective-permute-done((bf16[144,512]{1,0:T(8,128)(2,1)S(1)}, bf16[144,512]{1,0:T(8,128)(2,1)S(1)}, u32[]{:S(2)}, u32[]{:S(2)}) %collective-permute-start.8) | collective-permute-done | bytes 147488 | tf_op jit(solution)/shard_map/ppermute | solution.py:388
  33.5 1.0 %project.1 = bf16[144,128]{1,0:T(8,128)(2,1)S(1)} custom-call(bf16[144,512]{1,0:T(8,128)(2,1)S(1)} %pair_merge.2.refs_0_, bf16[144,512]{1,0:T(8,128)(2,1)S(1)} %collective-permute-done.7.refs_1_, bf16[144,512]{1,0:T(8,128)(2,1)S(1)} %collective-permute-done.8.refs_2_, bf16[144,512]{1,0:T(8,128)(2,1)S(1)} %collective-permute-done.9.refs_3_, ...), custom_call_target="tpu_custom_call" | custom-call | tf_op jit(solution)/shard_map/project/pallas_call | solution.py:458
  34.5 4.4 %collective-permute-start.10 = (bf16[144,128]{1,0:T(8,128)(2,1)S(1)}, bf16[144,128]{1,0:T(8,128)(2,1)S(1)}, u32[]{:S(2)}, u32[]{:S(2)}) collective-permute-start(bf16[144,128]{1,0:T(8,128)(2,1)S(1)} %project.1), channel_id=1, source_target_pairs={{0,68},{4,64},{32,100},{36,96},{64,4},{68,0},{96,36},{100,32},{1,6... | collective-permute-start | bytes 110600 | tf_op jit(solution)/shard_map/ppermute | solution.py:471
  39.2 0.8 %collective-permute-start.13 = (bf16[144,128]{1,0:T(8,128)(2,1)S(1)}, bf16[144,128]{1,0:T(8,128)(2,1)S(1)}, u32[]{:S(2)}, u32[]{:S(2)}) collective-permute-start(bf16[144,128]{1,0:T(8,128)(2,1)S(1)} %project.1), channel_id=1, source_target_pairs={{0,4},{4,0},{1,5},{5,1},{2,6},{6,2},{3,7},{7,3},{8,12},{12,8},{9,1... | collective-permute-start | bytes 110600 | tf_op jit(solution)/shard_map/ppermute | solution.py:474
  40.0 0.5 %collective-permute-done.10.refs_0_ = bf16[144,128]{1,0:T(8,128)(2,1)S(1)} collective-permute-done((bf16[144,128]{1,0:T(8,128)(2,1)S(1)}, bf16[144,128]{1,0:T(8,128)(2,1)S(1)}, u32[]{:S(2)}, u32[]{:S(2)}) %collective-permute-start.10) | collective-permute-done | bytes 36896 | tf_op jit(solution)/shard_map/ppermute | solution.py:471
  40.5 3.0 %collective-permute-done.11.refs_1_ = bf16[144,128]{1,0:T(8,128)(2,1)S(1)} collective-permute-done((bf16[144,128]{1,0:T(8,128)(2,1)S(1)}, bf16[144,128]{1,0:T(8,128)(2,1)S(1)}, u32[]{:S(2)}, u32[]{:S(2)}) %collective-permute-start.11) | collective-permute-done | bytes 36896 | tf_op jit(solution)/shard_map/ppermute | solution.py:471
  43.8 2.6 %collective-permute-start.14 = (bf16[144,128]{1,0:T(8,128)(2,1)S(1)}, bf16[144,128]{1,0:T(8,128)(2,1)S(1)}, u32[]{:S(2)}, u32[]{:S(2)}) collective-permute-start(bf16[144,128]{1,0:T(8,128)(2,1)S(1)} %middle_merge.1), channel_id=1, source_target_pairs={{0,20},{4,16},{8,28},{12,24},{16,4},{20,0},{24,12},{28,8},{1,21},{... | collective-permute-start | bytes 110600 | tf_op jit(solution)/shard_map/ppermute | solution.py:471
  46.3 1.4 %collective-permute-start.15 = (bf16[144,128]{1,0:T(8,128)(2,1)S(1)}, bf16[144,128]{1,0:T(8,128)(2,1)S(1)}, u32[]{:S(2)}, u32[]{:S(2)}) collective-permute-start(bf16[144,128]{1,0:T(8,128)(2,1)S(1)} %middle_merge.1), channel_id=1, source_target_pairs={{0,28},{4,24},{8,20},{12,16},{16,12},{20,8},{24,4},{28,0},{1,29},{... | collective-permute-start | bytes 110600 | tf_op jit(solution)/shard_map/ppermute | solution.py:471
  47.7 1.0 %collective-permute-done.14.refs_0_ = bf16[144,128]{1,0:T(8,128)(2,1)S(1)} collective-permute-done((bf16[144,128]{1,0:T(8,128)(2,1)S(1)}, bf16[144,128]{1,0:T(8,128)(2,1)S(1)}, u32[]{:S(2)}, u32[]{:S(2)}) %collective-permute-start.14) | collective-permute-done | bytes 36896 | tf_op jit(solution)/shard_map/ppermute | solution.py:471
  48.7 2.7 %collective-permute-done.15.refs_1_ = bf16[144,128]{1,0:T(8,128)(2,1)S(1)} collective-permute-done((bf16[144,128]{1,0:T(8,128)(2,1)S(1)}, bf16[144,128]{1,0:T(8,128)(2,1)S(1)}, u32[]{:S(2)}, u32[]{:S(2)}) %collective-permute-start.15) | collective-permute-done | bytes 36896 | tf_op jit(solution)/shard_map/ppermute | solution.py:471
  52.2 0.9 %collective-permute-done.18.other_ref = bf16[4,2,16,128]{3,2,1,0:T(8,128)(2,1)S(1)} collective-permute-done((bf16[4,2,16,128]{3,2,1,0:T(8,128)(2,1)S(1)}, bf16[4,2,16,128]{3,2,1,0:T(8,128)(2,1)S(1)}, u32[]{:S(2)}, u32[]{:S(2)}) %collective-permute-start.18) | collective-permute-done | bytes 32800 | tf_op jit(solution)/shard_map/ppermute | solution.py:492
  53.1 0.6 %place.1 = bf16[4,4,16,128]{3,2,1,0:T(8,128)(2,1)} custom-call(s32[1]{0:T(128)} %bitcast.own_first_ref.info_ref, bf16[4,2,16,128]{3,2,1,0:T(8,128)(2,1)S(1)} %finish.1.own_ref, bf16[4,2,16,128]{3,2,1,0:T(8,128)(2,1)S(1)} %collective-permute-done.18.other_ref), custom_call_target="tpu_custom_call" | custom-call | tf_op jit(solution)/shard_map/place/pallas_call | solution.py:493
  (34 shorter events, 3.7 us)
Async XLA Ops:
  2.1 8.5 %collective-permute-start = (bf16[64,1152]{1,0:T(8,128)(2,1)S(1)}, bf16[64,1152]{1,0:T(8,128)(2,1)S(1)}, u32[]{:S(2)}, u32[]{:S(2)}) collective-permute-start(bf16[64,1152]{1,0:T(8,128)(2,1)S(1)} %get-tuple-element.16), channel_id=1, source_target_pairs={{0,6},{1,7},{2,4},{3,5},{4,2},{5,3},{6,0},{7,1},{8,14},{9,15},{10,... | collective-permute-start | bytes 442376 | tf_op jit(solution)/shard_map/ppermute | solution.py:394
  6.5 7.4 %collective-permute-start.1 = (bf16[64,1152]{1,0:T(8,128)(2,1)S(1)}, bf16[64,1152]{1,0:T(8,128)(2,1)S(1)}, u32[]{:S(2)}, u32[]{:S(2)}) collective-permute-start(bf16[64,1152]{1,0:T(8,128)(2,1)S(1)} %get-tuple-element.16), channel_id=1, source_target_pairs={{0,7},{1,6},{2,5},{3,4},{4,3},{5,2},{6,1},{7,0},{8,15},{9,14},{10,... | collective-permute-start | bytes 442376 | tf_op jit(solution)/shard_map/ppermute | solution.py:394
  7.0 7.5 %collective-permute-start.2 = (bf16[64,1152]{1,0:T(8,128)(2,1)S(1)}, bf16[64,1152]{1,0:T(8,128)(2,1)S(1)}, u32[]{:S(2)}, u32[]{:S(2)}) collective-permute-start(bf16[64,1152]{1,0:T(8,128)(2,1)S(1)} %get-tuple-element.16), channel_id=1, source_target_pairs={{0,5},{1,4},{2,7},{3,6},{4,1},{5,0},{6,3},{7,2},{8,13},{9,12},{10,... | collective-permute-start | bytes 442376 | tf_op jit(solution)/shard_map/ppermute | solution.py:394
  7.0 11.6 %slice-start = ((s8[9437184]{0:T(1024)(128)(4,1)}), s8[4194304]{0:T(1024)(128)(4,1)S(1)}, s32[]{:S(2)}) async-start(s8[9437184]{0:T(1024)(128)(4,1)} %bitcast.7), calls=%async_computation | async-start | bytes 8388608
  10.6 8.0 %collective-permute-start.4 = (bf16[64,1152]{1,0:T(8,128)(2,1)S(1)}, bf16[64,1152]{1,0:T(8,128)(2,1)S(1)}, u32[]{:S(2)}, u32[]{:S(2)}) collective-permute-start(bf16[64,1152]{1,0:T(8,128)(2,1)S(1)} %collective-permute-done.q1_ref), channel_id=1, source_target_pairs={{0,4},{4,0},{1,5},{5,1},{2,6},{6,2},{3,7},{7,3},{8,12},{12,8},{9,1... | collective-permute-start | bytes 442376 | tf_op jit(solution)/shard_map/ppermute | solution.py:422
  13.9 4.7 %collective-permute-start.5 = (bf16[64,1152]{1,0:T(8,128)(2,1)S(1)}, bf16[64,1152]{1,0:T(8,128)(2,1)S(1)}, u32[]{:S(2)}, u32[]{:S(2)}) collective-permute-start(bf16[64,1152]{1,0:T(8,128)(2,1)S(1)} %collective-permute-done.1.q2_ref), channel_id=1, source_target_pairs={{0,4},{4,0},{1,5},{5,1},{2,6},{6,2},{3,7},{7,3},{8,12},{12,8},{9,1... | collective-permute-start | bytes 442376 | tf_op jit(solution)/shard_map/ppermute | solution.py:422
  14.5 4.1 %collective-permute-start.6 = (bf16[64,1152]{1,0:T(8,128)(2,1)S(1)}, bf16[64,1152]{1,0:T(8,128)(2,1)S(1)}, u32[]{:S(2)}, u32[]{:S(2)}) collective-permute-start(bf16[64,1152]{1,0:T(8,128)(2,1)S(1)} %collective-permute-done.2.q3_ref), channel_id=1, source_target_pairs={{0,4},{4,0},{1,5},{5,1},{2,6},{6,2},{3,7},{7,3},{8,12},{12,8},{9,1... | collective-permute-start | bytes 442376 | tf_op jit(solution)/shard_map/ppermute | solution.py:422
  14.9 3.7 %slice-start.1 = ((s8[9437184]{0:T(1024)(128)(4,1)}), s8[4194304]{0:T(1024)(128)(4,1)S(1)}, s32[]{:S(2)}) async-start(s8[9437184]{0:T(1024)(128)(4,1)} %bitcast.7), calls=%async_computation.1 | async-start | bytes 8388608
  14.9 3.8 %slice-start.2 = ((s8[9437184]{0:T(1024)(128)(4,1)}), s8[1048576]{0:T(1024)(128)(4,1)S(1)}, s32[]{:S(2)}) async-start(s8[9437184]{0:T(1024)(128)(4,1)} %bitcast.7), calls=%async_computation.2 | async-start | bytes 2097152
  18.4 3.8 %collective-permute-start.3 = (bf16[4,128,640]{2,1,0:T(8,128)(2,1)S(1)}, bf16[4,128,640]{2,1,0:T(8,128)(2,1)S(1)}, u32[]{:S(2)}, u32[]{:S(2)}) collective-permute-start(bf16[4,128,640]{2,1,0:T(8,128)(2,1)S(1)} %attention.2), channel_id=1, source_target_pairs={{0,4},{4,0},{1,5},{5,1},{2,6},{6,2},{3,7},{7,3},{8,12},{12,8},{9,1... | collective-permute-start | bytes 1966088 | tf_op jit(solution)/shard_map/ppermute | solution.py:443
  22.2 11.3 %copy-start = (bf16[16,512,128]{2,1,0:T(8,128)(2,1)S(1)}, bf16[16,512,128]{2,1,0:T(8,128)(2,1)}, u32[]{:S(2)}) copy-start(bf16[16,512,128]{2,1,0:T(8,128)(2,1)} %refs_5_.1) | copy-start | bytes 6291460
  23.0 6.6 %collective-permute-start.7 = (bf16[144,512]{1,0:T(8,128)(2,1)S(1)}, bf16[144,512]{1,0:T(8,128)(2,1)S(1)}, u32[]{:S(2)}, u32[]{:S(2)}) collective-permute-start(bf16[144,512]{1,0:T(8,128)(2,1)S(1)} %get-tuple-element.19), channel_id=1, source_target_pairs={{0,2},{1,3},{2,0},{3,1},{4,6},{5,7},{6,4},{7,5},{8,10},{9,11},{10,... | collective-permute-start | bytes 442376 | tf_op jit(solution)/shard_map/ppermute | solution.py:388
  25.2 8.3 %collective-permute-start.8 = (bf16[144,512]{1,0:T(8,128)(2,1)S(1)}, bf16[144,512]{1,0:T(8,128)(2,1)S(1)}, u32[]{:S(2)}, u32[]{:S(2)}) collective-permute-start(bf16[144,512]{1,0:T(8,128)(2,1)S(1)} %get-tuple-element.20), channel_id=1, source_target_pairs={{0,3},{1,2},{2,1},{3,0},{4,7},{5,6},{6,5},{7,4},{8,11},{9,10},{10,... | collective-permute-start | bytes 442376 | tf_op jit(solution)/shard_map/ppermute | solution.py:388
  26.7 6.8 %collective-permute-start.9 = (bf16[144,512]{1,0:T(8,128)(2,1)S(1)}, bf16[144,512]{1,0:T(8,128)(2,1)S(1)}, u32[]{:S(2)}, u32[]{:S(2)}) collective-permute-start(bf16[144,512]{1,0:T(8,128)(2,1)S(1)} %get-tuple-element.21), channel_id=1, source_target_pairs={{0,1},{1,0},{2,3},{3,2},{4,5},{5,4},{6,7},{7,6},{8,9},{9,8},{10,11... | collective-permute-start | bytes 442376 | tf_op jit(solution)/shard_map/ppermute | solution.py:388
  34.5 6.1 %collective-permute-start.10 = (bf16[144,128]{1,0:T(8,128)(2,1)S(1)}, bf16[144,128]{1,0:T(8,128)(2,1)S(1)}, u32[]{:S(2)}, u32[]{:S(2)}) collective-permute-start(bf16[144,128]{1,0:T(8,128)(2,1)S(1)} %project.1), channel_id=1, source_target_pairs={{0,68},{4,64},{32,100},{36,96},{64,4},{68,0},{96,36},{100,32},{1,6... | collective-permute-start | bytes 110600 | tf_op jit(solution)/shard_map/ppermute | solution.py:471
  38.9 4.6 %collective-permute-start.11 = (bf16[144,128]{1,0:T(8,128)(2,1)S(1)}, bf16[144,128]{1,0:T(8,128)(2,1)S(1)}, u32[]{:S(2)}, u32[]{:S(2)}) collective-permute-start(bf16[144,128]{1,0:T(8,128)(2,1)S(1)} %project.1), channel_id=1, source_target_pairs={{0,100},{4,96},{32,68},{36,64},{64,36},{68,32},{96,4},{100,0},{1,1... | collective-permute-start | bytes 110600 | tf_op jit(solution)/shard_map/ppermute | solution.py:471
  39.1 4.4 %collective-permute-start.12 = (bf16[144,128]{1,0:T(8,128)(2,1)S(1)}, bf16[144,128]{1,0:T(8,128)(2,1)S(1)}, u32[]{:S(2)}, u32[]{:S(2)}) collective-permute-start(bf16[144,128]{1,0:T(8,128)(2,1)S(1)} %project.1), channel_id=1, source_target_pairs={{0,36},{4,32},{32,4},{36,0},{64,100},{68,96},{96,68},{100,64},{1,3... | collective-permute-start | bytes 110600 | tf_op jit(solution)/shard_map/ppermute | solution.py:471
  39.2 4.3 %collective-permute-start.13 = (bf16[144,128]{1,0:T(8,128)(2,1)S(1)}, bf16[144,128]{1,0:T(8,128)(2,1)S(1)}, u32[]{:S(2)}, u32[]{:S(2)}) collective-permute-start(bf16[144,128]{1,0:T(8,128)(2,1)S(1)} %project.1), channel_id=1, source_target_pairs={{0,4},{4,0},{1,5},{5,1},{2,6},{6,2},{3,7},{7,3},{8,12},{12,8},{9,1... | collective-permute-start | bytes 110600 | tf_op jit(solution)/shard_map/ppermute | solution.py:474
  43.8 5.0 %collective-permute-start.14 = (bf16[144,128]{1,0:T(8,128)(2,1)S(1)}, bf16[144,128]{1,0:T(8,128)(2,1)S(1)}, u32[]{:S(2)}, u32[]{:S(2)}) collective-permute-start(bf16[144,128]{1,0:T(8,128)(2,1)S(1)} %middle_merge.1), channel_id=1, source_target_pairs={{0,20},{4,16},{8,28},{12,24},{16,4},{20,0},{24,12},{28,8},{1,21},{... | collective-permute-start | bytes 110600 | tf_op jit(solution)/shard_map/ppermute | solution.py:471
  46.3 5.1 %collective-permute-start.15 = (bf16[144,128]{1,0:T(8,128)(2,1)S(1)}, bf16[144,128]{1,0:T(8,128)(2,1)S(1)}, u32[]{:S(2)}, u32[]{:S(2)}) collective-permute-start(bf16[144,128]{1,0:T(8,128)(2,1)S(1)} %middle_merge.1), channel_id=1, source_target_pairs={{0,28},{4,24},{8,20},{12,16},{16,12},{20,8},{24,4},{28,0},{1,29},{... | collective-permute-start | bytes 110600 | tf_op jit(solution)/shard_map/ppermute | solution.py:471
  47.7 3.7 %collective-permute-start.16 = (bf16[144,128]{1,0:T(8,128)(2,1)S(1)}, bf16[144,128]{1,0:T(8,128)(2,1)S(1)}, u32[]{:S(2)}, u32[]{:S(2)}) collective-permute-start(bf16[144,128]{1,0:T(8,128)(2,1)S(1)} %middle_merge.1), channel_id=1, source_target_pairs={{0,12},{4,8},{8,4},{12,0},{16,28},{20,24},{24,20},{28,16},{1,13},{... | collective-permute-start | bytes 110600 | tf_op jit(solution)/shard_map/ppermute | solution.py:471
  47.7 3.7 %collective-permute-start.17 = (bf16[144,128]{1,0:T(8,128)(2,1)S(1)}, bf16[144,128]{1,0:T(8,128)(2,1)S(1)}, u32[]{:S(2)}, u32[]{:S(2)}) collective-permute-start(bf16[144,128]{1,0:T(8,128)(2,1)S(1)} %middle_merge.1), channel_id=1, source_target_pairs={{0,4},{4,0},{1,5},{5,1},{2,6},{6,2},{3,7},{7,3},{8,12},{12,8},{9,1... | collective-permute-start | bytes 110600 | tf_op jit(solution)/shard_map/ppermute | solution.py:474
  51.8 1.3 %collective-permute-start.18 = (bf16[4,2,16,128]{3,2,1,0:T(8,128)(2,1)S(1)}, bf16[4,2,16,128]{3,2,1,0:T(8,128)(2,1)S(1)}, u32[]{:S(2)}, u32[]{:S(2)}) collective-permute-start(bf16[4,2,16,128]{3,2,1,0:T(8,128)(2,1)S(1)} %finish.1.own_ref), channel_id=1, source_target_pairs={{0,4},{4,0},{1,5},{5,1},{2,6},{6,2},{3,7},{7,3},{8,12},{12,8},{9,1... | collective-permute-start | bytes 98312 | tf_op jit(solution)/shard_map/ppermute | solution.py:492

commit v18 on v15

--- a/solution.py
+++ b/solution.py
@@ -313,11 +313,17 @@
         out_ref[:, b] = result[b]
 
 
-def place_kernel(info_ref, own_ref, other_ref, out_ref):
+def place_kernel(info_ref, own_ref, other_ref, out_hbm, sems):
     half = own_ref.shape[1]
     first = info_ref[0]
-    out_ref[:, pl.ds(first, half)] = own_ref[...]
-    out_ref[:, pl.ds(half - first, half)] = other_ref[...]
+    copies = [
+        pltpu.make_async_copy(own_ref, out_hbm.at[:, pl.ds(first, half)], sems.at[0]),
+        pltpu.make_async_copy(other_ref, out_hbm.at[:, pl.ds(half - first, half)], sems.at[1]),
+    ]
+    for copy in copies:
+        copy.start()
+    for copy in copies:
+        copy.wait()
 
 
 def on_device(
@@ -487,7 +493,8 @@
     return pl.pallas_call(
         place_kernel,
         in_specs=[smem, vmem, vmem],
-        out_specs=vmem,
+        out_specs=anywhere,
+        scratch_shapes=[pltpu.SemaphoreType.DMA((2,))],
         out_shape=jax.ShapeDtypeStruct((steps, requests, heads, value_width), bf16),
         compiler_params=small,
         name="place",

time: 53.4 us -> 53.4 us (level)
  no operation moved by 1% of the time
where the time goes in v18:
time: 53.4 us; the launch traced here: 53.3 us
  starting transfers between devices  21.9 us (41%)
  Pallas kernels  15.6 us (29%)
  waiting for transfers between devices  15.6 us (29%)
    ppermute x6, starting transfers between devices, crossing(): lax.ppermute(array, (axis, 'core'), [(2 * i + c, 2 * (i ^ k) + 1 - c) for...  8.65 us
    ppermute x6, starting transfers between devices, over_head(): return lax.ppermute(array, 'head', [(i, i ^ k) for i in range(owners)])  8.4 us
    ppermute x6, waiting for transfers between devices, over_head(): return lax.ppermute(array, 'head', [(i, i ^ k) for i in range(owners)])  7.52 us
    ppermute x6, waiting for transfers between devices, crossing(): lax.ppermute(array, (axis, 'core'), [(2 * i + c, 2 * (i ^ k) + 1 - c) for...  7.25 us
    pallas_call x2, Pallas kernels, attend(): pl.pallas_call(functools.partial(attention_kernel, scale), in_specs=[smem...  7.03 us
    ppermute x3, starting transfers between devices, on_device(): passed = [lax.ppermute(g, 'core', swap) for g in got]  3.38 us
    pallas_call x1, Pallas kernels, on_device(): pl.pallas_call(stage_kernel, in_specs=[smem, anywhere], out_specs=vmem, o...  2.54 us
    pallas_call x1, Pallas kernels, on_device(): pl.pallas_call(functools.partial(queries_kernel, steps), in_specs=[smem]...  2.08 us
  transfers between devices with their start and end apart: 19, of which 9 were waited for; matrix products, arithmetic and copies ran while one was open for 0% of the time, Pallas kernels for 20%

profile of v18, /device:TPU:1, one launch (start us, length us, event | category | flops | bytes accessed | tf_op | source)
XLA Modules:
  0.0 53.3 jit_solution(1348703687033458642)
XLA Ops:
  0.0 2.1 %queries.1 = (bf16[4,64,640]{2,1,0:T(8,128)(2,1)S(1)}, bf16[64,1152]{1,0:T(8,128)(2,1)S(1)}, bf16[16,576]{1,0:T(8,128)(2,1)S(1)}, s32[8,128]{1,0:T(8,128)S(1)}) custom-call(s32[1]{0:T(128)} %bitcast.1.info_ref, s32[1]{0:T(128)} %bitcast.own_first_ref.info_ref, s32[1]{0:T(128)} %bitcast.2.row_ref, s32[1]{0:T(128)} %bitcast.3.place_ref, s32[4]{0:T(128)} %positions_hbm.1, ...), custom_call_target="tpu_custom_call" | custom-call | tf_op jit(solution)/shard_map/queries/pallas_call | solution.py:360
  2.1 3.8 %collective-permute-start = (bf16[64,1152]{1,0:T(8,128)(2,1)S(1)}, bf16[64,1152]{1,0:T(8,128)(2,1)S(1)}, u32[]{:S(2)}, u32[]{:S(2)}) collective-permute-start(bf16[64,1152]{1,0:T(8,128)(2,1)S(1)} %get-tuple-element.16), channel_id=1, source_target_pairs={{0,2},{1,3},{2,0},{3,1},{4,6},{5,7},{6,4},{7,5},{8,10},{9,11},{10,... | collective-permute-start | bytes 442376 | tf_op jit(solution)/shard_map/ppermute | solution.py:394
  5.9 0.8 %collective-permute-start.1 = (bf16[64,1152]{1,0:T(8,128)(2,1)S(1)}, bf16[64,1152]{1,0:T(8,128)(2,1)S(1)}, u32[]{:S(2)}, u32[]{:S(2)}) collective-permute-start(bf16[64,1152]{1,0:T(8,128)(2,1)S(1)} %get-tuple-element.16), channel_id=1, source_target_pairs={{0,3},{1,2},{2,1},{3,0},{4,7},{5,6},{6,5},{7,4},{8,11},{9,10},{10,... | collective-permute-start | bytes 442376 | tf_op jit(solution)/shard_map/ppermute | solution.py:394
  6.7 2.5 %stage.1.k_ref = bf16[2,576,2048]{2,1,0:T(8,128)(2,1)S(1)} custom-call(s32[1]{0:T(128)} %bitcast.1.info_ref, bf16[4,576,2048]{2,1,0:T(8,128)(2,1)} %bitcast.6), custom_call_target="tpu_custom_call" | custom-call | bytes 4718592 | tf_op jit(solution)/shard_map/stage/pallas_call | solution.py:411
  9.2 1.9 %collective-permute-start.4 = (bf16[64,1152]{1,0:T(8,128)(2,1)S(1)}, bf16[64,1152]{1,0:T(8,128)(2,1)S(1)}, u32[]{:S(2)}, u32[]{:S(2)}) collective-permute-start(bf16[64,1152]{1,0:T(8,128)(2,1)S(1)} %collective-permute-done.q1_ref), channel_id=1, source_target_pairs={{0,4},{4,0},{1,5},{5,1},{2,6},{6,2},{3,7},{7,3},{8,12},{12,8},{9,1... | collective-permute-start | bytes 442376 | tf_op jit(solution)/shard_map/ppermute | solution.py:422
  11.1 1.6 %collective-permute-done.1.q2_ref = bf16[64,1152]{1,0:T(8,128)(2,1)S(1)} collective-permute-done((bf16[64,1152]{1,0:T(8,128)(2,1)S(1)}, bf16[64,1152]{1,0:T(8,128)(2,1)S(1)}, u32[]{:S(2)}, u32[]{:S(2)}) %collective-permute-start.1) | collective-permute-done | bytes 147488 | tf_op jit(solution)/shard_map/ppermute | solution.py:394
  12.8 1.1 %collective-permute-start.5 = (bf16[64,1152]{1,0:T(8,128)(2,1)S(1)}, bf16[64,1152]{1,0:T(8,128)(2,1)S(1)}, u32[]{:S(2)}, u32[]{:S(2)}) collective-permute-start(bf16[64,1152]{1,0:T(8,128)(2,1)S(1)} %collective-permute-done.1.q2_ref), channel_id=1, source_target_pairs={{0,4},{4,0},{1,5},{5,1},{2,6},{6,2},{3,7},{7,3},{8,12},{12,8},{9,1... | collective-permute-start | bytes 442376 | tf_op jit(solution)/shard_map/ppermute | solution.py:422
  14.3 3.5 %attention.2 = bf16[4,128,640]{2,1,0:T(8,128)(2,1)S(1)} custom-call(s32[1]{0:T(128)} %bitcast.1.info_ref, s32[8,128]{1,0:T(8,128)S(1)} %get-tuple-element.14.limits_ref, bf16[4,64,640]{2,1,0:T(8,128)(2,1)S(1)} %get-tuple-element.15.own_ref, bf16[64,1152]{1,0:T(8,128)(2,1)S(1)} %collective-permute-done.q1_ref, ...), custom_call_target="tpu_custom_call" | custom-call | flops 22817013760 | bytes 4718592 | tf_op jit(solution)/shard_map/attention/pallas_call | solution.py:427
  18.0 3.5 %attention.3.b_ref = bf16[4,128,640]{2,1,0:T(8,128)(2,1)S(1)} custom-call(s32[1]{0:T(128)} %bitcast.own_first_ref.info_ref, s32[8,128]{1,0:T(8,128)S(1)} %get-tuple-element.14.limits_ref, bf16[4,64,640]{2,1,0:T(8,128)(2,1)S(1)} %get-tuple-element.15.own_ref, bf16[64,1152]{1,0:T(8,128)(2,1)S(1)} %collective-permute-done.4.q1_ref, ...), custom_call_target="tpu_custom_call" | custom-call | flops 22817013760 | bytes 4718592 | tf_op jit(solution)/shard_map/attention/pallas_call | solution.py:427
  21.6 0.8 %pair_merge.3 = (bf16[144,512]{1,0:T(8,128)(2,1)S(1)}, bf16[144,512]{1,0:T(8,128)(2,1)S(1)}, bf16[144,512]{1,0:T(8,128)(2,1)S(1)}) custom-call(bf16[4,128,640]{2,1,0:T(8,128)(2,1)S(1)} %collective-permute-done.3.a_ref, bf16[4,128,640]{2,1,0:T(8,128)(2,1)S(1)} %attention.3.b_ref), custom_call_target="tpu_custom_call" | custom-call | tf_op jit(solution)/shard_map/pair_merge/pallas_call | solution.py:446
  22.4 2.2 %collective-permute-start.7 = (bf16[144,512]{1,0:T(8,128)(2,1)S(1)}, bf16[144,512]{1,0:T(8,128)(2,1)S(1)}, u32[]{:S(2)}, u32[]{:S(2)}) collective-permute-start(bf16[144,512]{1,0:T(8,128)(2,1)S(1)} %get-tuple-element.19), channel_id=1, source_target_pairs={{0,2},{1,3},{2,0},{3,1},{4,6},{5,7},{6,4},{7,5},{8,10},{9,11},{10,... | collective-permute-start | bytes 442376 | tf_op jit(solution)/shard_map/ppermute | solution.py:394
  24.6 1.6 %collective-permute-start.8 = (bf16[144,512]{1,0:T(8,128)(2,1)S(1)}, bf16[144,512]{1,0:T(8,128)(2,1)S(1)}, u32[]{:S(2)}, u32[]{:S(2)}) collective-permute-start(bf16[144,512]{1,0:T(8,128)(2,1)S(1)} %get-tuple-element.20), channel_id=1, source_target_pairs={{0,3},{1,2},{2,1},{3,0},{4,7},{5,6},{6,5},{7,4},{8,11},{9,10},{10,... | collective-permute-start | bytes 442376 | tf_op jit(solution)/shard_map/ppermute | solution.py:394
  27.1 1.9 %collective-permute-done.7.refs_1_ = bf16[144,512]{1,0:T(8,128)(2,1)S(1)} collective-permute-done((bf16[144,512]{1,0:T(8,128)(2,1)S(1)}, bf16[144,512]{1,0:T(8,128)(2,1)S(1)}, u32[]{:S(2)}, u32[]{:S(2)}) %collective-permute-start.7) | collective-permute-done | bytes 147488 | tf_op jit(solution)/shard_map/ppermute | solution.py:394
  29.0 3.9 %collective-permute-done.8.refs_2_ = bf16[144,512]{1,0:T(8,128)(2,1)S(1)} collective-permute-done((bf16[144,512]{1,0:T(8,128)(2,1)S(1)}, bf16[144,512]{1,0:T(8,128)(2,1)S(1)}, u32[]{:S(2)}, u32[]{:S(2)}) %collective-permute-start.8) | collective-permute-done | bytes 147488 | tf_op jit(solution)/shard_map/ppermute | solution.py:394
  33.0 1.0 %project.1 = bf16[144,128]{1,0:T(8,128)(2,1)S(1)} custom-call(bf16[144,512]{1,0:T(8,128)(2,1)S(1)} %pair_merge.2.refs_0_, bf16[144,512]{1,0:T(8,128)(2,1)S(1)} %collective-permute-done.7.refs_1_, bf16[144,512]{1,0:T(8,128)(2,1)S(1)} %collective-permute-done.8.refs_2_, bf16[144,512]{1,0:T(8,128)(2,1)S(1)} %collective-permute-done.9.refs_3_, ...), custom_call_target="tpu_custom_call" | custom-call | tf_op jit(solution)/shard_map/project/pallas_call | solution.py:458
  34.0 4.4 %collective-permute-start.10 = (bf16[144,128]{1,0:T(8,128)(2,1)S(1)}, bf16[144,128]{1,0:T(8,128)(2,1)S(1)}, u32[]{:S(2)}, u32[]{:S(2)}) collective-permute-start(bf16[144,128]{1,0:T(8,128)(2,1)S(1)} %project.1), channel_id=1, source_target_pairs={{0,68},{4,64},{32,100},{36,96},{64,4},{68,0},{96,36},{100,32},{1,6... | collective-permute-start | bytes 110600 | tf_op jit(solution)/shard_map/ppermute | solution.py:471
  38.7 0.8 %collective-permute-start.13 = (bf16[144,128]{1,0:T(8,128)(2,1)S(1)}, bf16[144,128]{1,0:T(8,128)(2,1)S(1)}, u32[]{:S(2)}, u32[]{:S(2)}) collective-permute-start(bf16[144,128]{1,0:T(8,128)(2,1)S(1)} %project.1), channel_id=1, source_target_pairs={{0,4},{4,0},{1,5},{5,1},{2,6},{6,2},{3,7},{7,3},{8,12},{12,8},{9,1... | collective-permute-start | bytes 110600 | tf_op jit(solution)/shard_map/ppermute | solution.py:474
  40.0 3.0 %collective-permute-done.11.refs_1_ = bf16[144,128]{1,0:T(8,128)(2,1)S(1)} collective-permute-done((bf16[144,128]{1,0:T(8,128)(2,1)S(1)}, bf16[144,128]{1,0:T(8,128)(2,1)S(1)}, u32[]{:S(2)}, u32[]{:S(2)}) %collective-permute-start.11) | collective-permute-done | bytes 36896 | tf_op jit(solution)/shard_map/ppermute | solution.py:471
  43.3 2.6 %collective-permute-start.14 = (bf16[144,128]{1,0:T(8,128)(2,1)S(1)}, bf16[144,128]{1,0:T(8,128)(2,1)S(1)}, u32[]{:S(2)}, u32[]{:S(2)}) collective-permute-start(bf16[144,128]{1,0:T(8,128)(2,1)S(1)} %middle_merge.1), channel_id=1, source_target_pairs={{0,20},{4,16},{8,28},{12,24},{16,4},{20,0},{24,12},{28,8},{1,21},{... | collective-permute-start | bytes 110600 | tf_op jit(solution)/shard_map/ppermute | solution.py:471
  45.9 1.4 %collective-permute-start.15 = (bf16[144,128]{1,0:T(8,128)(2,1)S(1)}, bf16[144,128]{1,0:T(8,128)(2,1)S(1)}, u32[]{:S(2)}, u32[]{:S(2)}) collective-permute-start(bf16[144,128]{1,0:T(8,128)(2,1)S(1)} %middle_merge.1), channel_id=1, source_target_pairs={{0,28},{4,24},{8,20},{12,16},{16,12},{20,8},{24,4},{28,0},{1,29},{... | collective-permute-start | bytes 110600 | tf_op jit(solution)/shard_map/ppermute | solution.py:471
  47.2 1.0 %collective-permute-done.14.refs_0_ = bf16[144,128]{1,0:T(8,128)(2,1)S(1)} collective-permute-done((bf16[144,128]{1,0:T(8,128)(2,1)S(1)}, bf16[144,128]{1,0:T(8,128)(2,1)S(1)}, u32[]{:S(2)}, u32[]{:S(2)}) %collective-permute-start.14) | collective-permute-done | bytes 36896 | tf_op jit(solution)/shard_map/ppermute | solution.py:471
  48.2 2.8 %collective-permute-done.15.refs_1_ = bf16[144,128]{1,0:T(8,128)(2,1)S(1)} collective-permute-done((bf16[144,128]{1,0:T(8,128)(2,1)S(1)}, bf16[144,128]{1,0:T(8,128)(2,1)S(1)}, u32[]{:S(2)}, u32[]{:S(2)}) %collective-permute-start.15) | collective-permute-done | bytes 36896 | tf_op jit(solution)/shard_map/ppermute | solution.py:471
  51.8 0.9 %collective-permute-done.18.other_ref = bf16[4,2,16,128]{3,2,1,0:T(8,128)(2,1)S(1)} collective-permute-done((bf16[4,2,16,128]{3,2,1,0:T(8,128)(2,1)S(1)}, bf16[4,2,16,128]{3,2,1,0:T(8,128)(2,1)S(1)}, u32[]{:S(2)}, u32[]{:S(2)}) %collective-permute-start.18) | collective-permute-done | bytes 32800 | tf_op jit(solution)/shard_map/ppermute | solution.py:492
  52.6 0.6 %place.1 = bf16[4,4,16,128]{3,2,1,0:T(8,128)(2,1)} custom-call(s32[1]{0:T(128)} %bitcast.own_first_ref.info_ref, bf16[4,2,16,128]{3,2,1,0:T(8,128)(2,1)S(1)} %finish.1.own_ref, bf16[4,2,16,128]{3,2,1,0:T(8,128)(2,1)S(1)} %collective-permute-done.18.other_ref), custom_call_target="tpu_custom_call" | custom-call | tf_op jit(solution)/shard_map/place/pallas_call | solution.py:493
  (34 shorter events, 3.5 us)
Async XLA Ops:
  2.1 7.2 %collective-permute-start = (bf16[64,1152]{1,0:T(8,128)(2,1)S(1)}, bf16[64,1152]{1,0:T(8,128)(2,1)S(1)}, u32[]{:S(2)}, u32[]{:S(2)}) collective-permute-start(bf16[64,1152]{1,0:T(8,128)(2,1)S(1)} %get-tuple-element.16), channel_id=1, source_target_pairs={{0,2},{1,3},{2,0},{3,1},{4,6},{5,7},{6,4},{7,5},{8,10},{9,11},{10,... | collective-permute-start | bytes 442376 | tf_op jit(solution)/shard_map/ppermute | solution.py:394
  5.9 6.8 %collective-permute-start.1 = (bf16[64,1152]{1,0:T(8,128)(2,1)S(1)}, bf16[64,1152]{1,0:T(8,128)(2,1)S(1)}, u32[]{:S(2)}, u32[]{:S(2)}) collective-permute-start(bf16[64,1152]{1,0:T(8,128)(2,1)S(1)} %get-tuple-element.16), channel_id=1, source_target_pairs={{0,3},{1,2},{2,1},{3,0},{4,7},{5,6},{6,5},{7,4},{8,11},{9,10},{10,... | collective-permute-start | bytes 442376 | tf_op jit(solution)/shard_map/ppermute | solution.py:394
  6.7 7.2 %collective-permute-start.2 = (bf16[64,1152]{1,0:T(8,128)(2,1)S(1)}, bf16[64,1152]{1,0:T(8,128)(2,1)S(1)}, u32[]{:S(2)}, u32[]{:S(2)}) collective-permute-start(bf16[64,1152]{1,0:T(8,128)(2,1)S(1)} %get-tuple-element.16), channel_id=1, source_target_pairs={{0,1},{1,0},{2,3},{3,2},{4,5},{5,4},{6,7},{7,6},{8,9},{9,8},{10,11... | collective-permute-start | bytes 442376 | tf_op jit(solution)/shard_map/ppermute | solution.py:394
  6.7 11.3 %slice-start = ((s8[9437184]{0:T(1024)(128)(4,1)}), s8[4194304]{0:T(1024)(128)(4,1)S(1)}, s32[]{:S(2)}) async-start(s8[9437184]{0:T(1024)(128)(4,1)} %bitcast.7), calls=%async_computation | async-start | bytes 8388608
  9.2 8.7 %collective-permute-start.4 = (bf16[64,1152]{1,0:T(8,128)(2,1)S(1)}, bf16[64,1152]{1,0:T(8,128)(2,1)S(1)}, u32[]{:S(2)}, u32[]{:S(2)}) collective-permute-start(bf16[64,1152]{1,0:T(8,128)(2,1)S(1)} %collective-permute-done.q1_ref), channel_id=1, source_target_pairs={{0,4},{4,0},{1,5},{5,1},{2,6},{6,2},{3,7},{7,3},{8,12},{12,8},{9,1... | collective-permute-start | bytes 442376 | tf_op jit(solution)/shard_map/ppermute | solution.py:422
  12.8 5.2 %collective-permute-start.5 = (bf16[64,1152]{1,0:T(8,128)(2,1)S(1)}, bf16[64,1152]{1,0:T(8,128)(2,1)S(1)}, u32[]{:S(2)}, u32[]{:S(2)}) collective-permute-start(bf16[64,1152]{1,0:T(8,128)(2,1)S(1)} %collective-permute-done.1.q2_ref), channel_id=1, source_target_pairs={{0,4},{4,0},{1,5},{5,1},{2,6},{6,2},{3,7},{7,3},{8,12},{12,8},{9,1... | collective-permute-start | bytes 442376 | tf_op jit(solution)/shard_map/ppermute | solution.py:422
  13.9 4.1 %collective-permute-start.6 = (bf16[64,1152]{1,0:T(8,128)(2,1)S(1)}, bf16[64,1152]{1,0:T(8,128)(2,1)S(1)}, u32[]{:S(2)}, u32[]{:S(2)}) collective-permute-start(bf16[64,1152]{1,0:T(8,128)(2,1)S(1)} %collective-permute-done.2.q3_ref), channel_id=1, source_target_pairs={{0,4},{4,0},{1,5},{5,1},{2,6},{6,2},{3,7},{7,3},{8,12},{12,8},{9,1... | collective-permute-start | bytes 442376 | tf_op jit(solution)/shard_map/ppermute | solution.py:422
  14.3 3.8 %slice-start.1 = ((s8[9437184]{0:T(1024)(128)(4,1)}), s8[4194304]{0:T(1024)(128)(4,1)S(1)}, s32[]{:S(2)}) async-start(s8[9437184]{0:T(1024)(128)(4,1)} %bitcast.7), calls=%async_computation.1 | async-start | bytes 8388608
  14.3 3.8 %slice-start.2 = ((s8[9437184]{0:T(1024)(128)(4,1)}), s8[1048576]{0:T(1024)(128)(4,1)S(1)}, s32[]{:S(2)}) async-start(s8[9437184]{0:T(1024)(128)(4,1)} %bitcast.7), calls=%async_computation.2 | async-start | bytes 2097152
  17.8 3.8 %collective-permute-start.3 = (bf16[4,128,640]{2,1,0:T(8,128)(2,1)S(1)}, bf16[4,128,640]{2,1,0:T(8,128)(2,1)S(1)}, u32[]{:S(2)}, u32[]{:S(2)}) collective-permute-start(bf16[4,128,640]{2,1,0:T(8,128)(2,1)S(1)} %attention.2), channel_id=1, source_target_pairs={{0,4},{4,0},{1,5},{5,1},{2,6},{6,2},{3,7},{7,3},{8,12},{12,8},{9,1... | collective-permute-start | bytes 1966088 | tf_op jit(solution)/shard_map/ppermute | solution.py:443
  21.6 11.4 %copy-start = (bf16[16,512,128]{2,1,0:T(8,128)(2,1)S(1)}, bf16[16,512,128]{2,1,0:T(8,128)(2,1)}, u32[]{:S(2)}) copy-start(bf16[16,512,128]{2,1,0:T(8,128)(2,1)} %refs_5_.1) | copy-start | bytes 6291460
  22.4 6.6 %collective-permute-start.7 = (bf16[144,512]{1,0:T(8,128)(2,1)S(1)}, bf16[144,512]{1,0:T(8,128)(2,1)S(1)}, u32[]{:S(2)}, u32[]{:S(2)}) collective-permute-start(bf16[144,512]{1,0:T(8,128)(2,1)S(1)} %get-tuple-element.19), channel_id=1, source_target_pairs={{0,2},{1,3},{2,0},{3,1},{4,6},{5,7},{6,4},{7,5},{8,10},{9,11},{10,... | collective-permute-start | bytes 442376 | tf_op jit(solution)/shard_map/ppermute | solution.py:394
  24.6 8.3 %collective-permute-start.8 = (bf16[144,512]{1,0:T(8,128)(2,1)S(1)}, bf16[144,512]{1,0:T(8,128)(2,1)S(1)}, u32[]{:S(2)}, u32[]{:S(2)}) collective-permute-start(bf16[144,512]{1,0:T(8,128)(2,1)S(1)} %get-tuple-element.20), channel_id=1, source_target_pairs={{0,3},{1,2},{2,1},{3,0},{4,7},{5,6},{6,5},{7,4},{8,11},{9,10},{10,... | collective-permute-start | bytes 442376 | tf_op jit(solution)/shard_map/ppermute | solution.py:394
  26.2 6.8 %collective-permute-start.9 = (bf16[144,512]{1,0:T(8,128)(2,1)S(1)}, bf16[144,512]{1,0:T(8,128)(2,1)S(1)}, u32[]{:S(2)}, u32[]{:S(2)}) collective-permute-start(bf16[144,512]{1,0:T(8,128)(2,1)S(1)} %get-tuple-element.21), channel_id=1, source_target_pairs={{0,1},{1,0},{2,3},{3,2},{4,5},{5,4},{6,7},{7,6},{8,9},{9,8},{10,11... | collective-permute-start | bytes 442376 | tf_op jit(solution)/shard_map/ppermute | solution.py:394
  34.0 6.0 %collective-permute-start.10 = (bf16[144,128]{1,0:T(8,128)(2,1)S(1)}, bf16[144,128]{1,0:T(8,128)(2,1)S(1)}, u32[]{:S(2)}, u32[]{:S(2)}) collective-permute-start(bf16[144,128]{1,0:T(8,128)(2,1)S(1)} %project.1), channel_id=1, source_target_pairs={{0,68},{4,64},{32,100},{36,96},{64,4},{68,0},{96,36},{100,32},{1,6... | collective-permute-start | bytes 110600 | tf_op jit(solution)/shard_map/ppermute | solution.py:471
  38.4 4.6 %collective-permute-start.11 = (bf16[144,128]{1,0:T(8,128)(2,1)S(1)}, bf16[144,128]{1,0:T(8,128)(2,1)S(1)}, u32[]{:S(2)}, u32[]{:S(2)}) collective-permute-start(bf16[144,128]{1,0:T(8,128)(2,1)S(1)} %project.1), channel_id=1, source_target_pairs={{0,100},{4,96},{32,68},{36,64},{64,36},{68,32},{96,4},{100,0},{1,1... | collective-permute-start | bytes 110600 | tf_op jit(solution)/shard_map/ppermute | solution.py:471
  38.6 4.4 %collective-permute-start.12 = (bf16[144,128]{1,0:T(8,128)(2,1)S(1)}, bf16[144,128]{1,0:T(8,128)(2,1)S(1)}, u32[]{:S(2)}, u32[]{:S(2)}) collective-permute-start(bf16[144,128]{1,0:T(8,128)(2,1)S(1)} %project.1), channel_id=1, source_target_pairs={{0,36},{4,32},{32,4},{36,0},{64,100},{68,96},{96,68},{100,64},{1,3... | collective-permute-start | bytes 110600 | tf_op jit(solution)/shard_map/ppermute | solution.py:471
  38.7 4.3 %collective-permute-start.13 = (bf16[144,128]{1,0:T(8,128)(2,1)S(1)}, bf16[144,128]{1,0:T(8,128)(2,1)S(1)}, u32[]{:S(2)}, u32[]{:S(2)}) collective-permute-start(bf16[144,128]{1,0:T(8,128)(2,1)S(1)} %project.1), channel_id=1, source_target_pairs={{0,4},{4,0},{1,5},{5,1},{2,6},{6,2},{3,7},{7,3},{8,12},{12,8},{9,1... | collective-permute-start | bytes 110600 | tf_op jit(solution)/shard_map/ppermute | solution.py:474
  43.3 5.0 %collective-permute-start.14 = (bf16[144,128]{1,0:T(8,128)(2,1)S(1)}, bf16[144,128]{1,0:T(8,128)(2,1)S(1)}, u32[]{:S(2)}, u32[]{:S(2)}) collective-permute-start(bf16[144,128]{1,0:T(8,128)(2,1)S(1)} %middle_merge.1), channel_id=1, source_target_pairs={{0,20},{4,16},{8,28},{12,24},{16,4},{20,0},{24,12},{28,8},{1,21},{... | collective-permute-start | bytes 110600 | tf_op jit(solution)/shard_map/ppermute | solution.py:471
  45.9 5.1 %collective-permute-start.15 = (bf16[144,128]{1,0:T(8,128)(2,1)S(1)}, bf16[144,128]{1,0:T(8,128)(2,1)S(1)}, u32[]{:S(2)}, u32[]{:S(2)}) collective-permute-start(bf16[144,128]{1,0:T(8,128)(2,1)S(1)} %middle_merge.1), channel_id=1, source_target_pairs={{0,28},{4,24},{8,20},{12,16},{16,12},{20,8},{24,4},{28,0},{1,29},{... | collective-permute-start | bytes 110600 | tf_op jit(solution)/shard_map/ppermute | solution.py:471
  47.2 3.8 %collective-permute-start.16 = (bf16[144,128]{1,0:T(8,128)(2,1)S(1)}, bf16[144,128]{1,0:T(8,128)(2,1)S(1)}, u32[]{:S(2)}, u32[]{:S(2)}) collective-permute-start(bf16[144,128]{1,0:T(8,128)(2,1)S(1)} %middle_merge.1), channel_id=1, source_target_pairs={{0,12},{4,8},{8,4},{12,0},{16,28},{20,24},{24,20},{28,16},{1,13},{... | collective-permute-start | bytes 110600 | tf_op jit(solution)/shard_map/ppermute | solution.py:471
  47.2 3.8 %collective-permute-start.17 = (bf16[144,128]{1,0:T(8,128)(2,1)S(1)}, bf16[144,128]{1,0:T(8,128)(2,1)S(1)}, u32[]{:S(2)}, u32[]{:S(2)}) collective-permute-start(bf16[144,128]{1,0:T(8,128)(2,1)S(1)} %middle_merge.1), channel_id=1, source_target_pairs={{0,4},{4,0},{1,5},{5,1},{2,6},{6,2},{3,7},{7,3},{8,12},{12,8},{9,1... | collective-permute-start | bytes 110600 | tf_op jit(solution)/shard_map/ppermute | solution.py:474
  51.3 1.3 %collective-permute-start.18 = (bf16[4,2,16,128]{3,2,1,0:T(8,128)(2,1)S(1)}, bf16[4,2,16,128]{3,2,1,0:T(8,128)(2,1)S(1)}, u32[]{:S(2)}, u32[]{:S(2)}) collective-permute-start(bf16[4,2,16,128]{3,2,1,0:T(8,128)(2,1)S(1)} %finish.1.own_ref), channel_id=1, source_target_pairs={{0,4},{4,0},{1,5},{5,1},{2,6},{6,2},{3,7},{7,3},{8,12},{12,8},{9,1... | collective-permute-start | bytes 98312 | tf_op jit(solution)/shard_map/ppermute | solution.py:492

commit v19 on v15

--- a/solution.py
+++ b/solution.py
@@ -461,11 +461,12 @@
     def crossing(array, axis):
         size = lax.axis_size(axis)
         sides = [(i, c) for i in range(size) for c in range(2)]
+        sibling = [lax.ppermute(array, "core", swap)]
         got = [
             lax.ppermute(array, (axis, "core"), [(2 * i + c, 2 * (i ^ k) + 1 - c) for i, c in sides])
             for k in (2, 3, 1)
         ]
-        return got + [lax.ppermute(array, "core", swap)]
+        return sibling + got
 
     part = pl.pallas_call(
         middle_kernel,

time: 53.4 us -> 53.8 us (level)
    ppermute x2, starting transfers between devices: 0.82 us -> 1.37 us  [crossing(): sibling = [lax.ppermute(array, 'core', swap)]]
where the time goes in v19:
time: 53.8 us; the launch traced here: 53.7 us
  starting transfers between devices  22.3 us (41%)
  waiting for transfers between devices  15.7 us (29%)
  Pallas kernels  15.6 us (29%)
    ppermute x6, starting transfers between devices, crossing(): lax.ppermute(array, (axis, 'core'), [(2 * i + c, 2 * (i ^ k) + 1 - c) for...  8.5 us
    ppermute x6, starting transfers between devices, over_head(): return lax.ppermute(array, 'head', [(i, i ^ k) for i in range(owners)])  8.4 us
    ppermute x6, waiting for transfers between devices, over_head(): return lax.ppermute(array, 'head', [(i, i ^ k) for i in range(owners)])  7.52 us
    ppermute x6, waiting for transfers between devices, crossing(): lax.ppermute(array, (axis, 'core'), [(2 * i + c, 2 * (i ^ k) + 1 - c) for...  7.27 us
    pallas_call x2, Pallas kernels, attend(): pl.pallas_call(functools.partial(attention_kernel, scale), in_specs=[smem...  7.03 us
    ppermute x3, starting transfers between devices, on_device(): passed = [lax.ppermute(g, 'core', swap) for g in got]  3.38 us
    pallas_call x1, Pallas kernels, on_device(): pl.pallas_call(stage_kernel, in_specs=[smem, anywhere], out_specs=vmem, o...  2.54 us
    pallas_call x1, Pallas kernels, on_device(): pl.pallas_call(functools.partial(queries_kernel, steps), in_specs=[smem]...  2.08 us
  transfers between devices with their start and end apart: 19, of which 9 were waited for; matrix products, arithmetic and copies ran while one was open for 0% of the time, Pallas kernels for 20%

profile of v19, /device:TPU:1, one launch (start us, length us, event | category | flops | bytes accessed | tf_op | source)
XLA Modules:
  0.0 53.7 jit_solution(9823285961307056025)
XLA Ops:
  0.0 2.1 %queries.1 = (bf16[4,64,640]{2,1,0:T(8,128)(2,1)S(1)}, bf16[64,1152]{1,0:T(8,128)(2,1)S(1)}, bf16[16,576]{1,0:T(8,128)(2,1)S(1)}, s32[8,128]{1,0:T(8,128)S(1)}) custom-call(s32[1]{0:T(128)} %bitcast.1.info_ref, s32[1]{0:T(128)} %bitcast.own_first_ref.info_ref, s32[1]{0:T(128)} %bitcast.2.row_ref, s32[1]{0:T(128)} %bitcast.3.place_ref, s32[4]{0:T(128)} %positions_hbm.1, ...), custom_call_target="tpu_custom_call" | custom-call | tf_op jit(solution)/shard_map/queries/pallas_call | solution.py:354
  2.1 3.8 %collective-permute-start = (bf16[64,1152]{1,0:T(8,128)(2,1)S(1)}, bf16[64,1152]{1,0:T(8,128)(2,1)S(1)}, u32[]{:S(2)}, u32[]{:S(2)}) collective-permute-start(bf16[64,1152]{1,0:T(8,128)(2,1)S(1)} %get-tuple-element.16), channel_id=1, source_target_pairs={{0,2},{1,3},{2,0},{3,1},{4,6},{5,7},{6,4},{7,5},{8,10},{9,11},{10,... | collective-permute-start | bytes 442376 | tf_op jit(solution)/shard_map/ppermute | solution.py:388
  5.9 0.8 %collective-permute-start.1 = (bf16[64,1152]{1,0:T(8,128)(2,1)S(1)}, bf16[64,1152]{1,0:T(8,128)(2,1)S(1)}, u32[]{:S(2)}, u32[]{:S(2)}) collective-permute-start(bf16[64,1152]{1,0:T(8,128)(2,1)S(1)} %get-tuple-element.16), channel_id=1, source_target_pairs={{0,3},{1,2},{2,1},{3,0},{4,7},{5,6},{6,5},{7,4},{8,11},{9,10},{10,... | collective-permute-start | bytes 442376 | tf_op jit(solution)/shard_map/ppermute | solution.py:388
  6.7 2.5 %stage.1.k_ref = bf16[2,576,2048]{2,1,0:T(8,128)(2,1)S(1)} custom-call(s32[1]{0:T(128)} %bitcast.1.info_ref, bf16[4,576,2048]{2,1,0:T(8,128)(2,1)} %bitcast.6), custom_call_target="tpu_custom_call" | custom-call | bytes 4718592 | tf_op jit(solution)/shard_map/stage/pallas_call | solution.py:405
  9.2 1.9 %collective-permute-start.4 = (bf16[64,1152]{1,0:T(8,128)(2,1)S(1)}, bf16[64,1152]{1,0:T(8,128)(2,1)S(1)}, u32[]{:S(2)}, u32[]{:S(2)}) collective-permute-start(bf16[64,1152]{1,0:T(8,128)(2,1)S(1)} %collective-permute-done.q1_ref), channel_id=1, source_target_pairs={{0,4},{4,0},{1,5},{5,1},{2,6},{6,2},{3,7},{7,3},{8,12},{12,8},{9,1... | collective-permute-start | bytes 442376 | tf_op jit(solution)/shard_map/ppermute | solution.py:416
  11.1 1.6 %collective-permute-done.1.q2_ref = bf16[64,1152]{1,0:T(8,128)(2,1)S(1)} collective-permute-done((bf16[64,1152]{1,0:T(8,128)(2,1)S(1)}, bf16[64,1152]{1,0:T(8,128)(2,1)S(1)}, u32[]{:S(2)}, u32[]{:S(2)}) %collective-permute-start.1) | collective-permute-done | bytes 147488 | tf_op jit(solution)/shard_map/ppermute | solution.py:388
  12.8 1.1 %collective-permute-start.5 = (bf16[64,1152]{1,0:T(8,128)(2,1)S(1)}, bf16[64,1152]{1,0:T(8,128)(2,1)S(1)}, u32[]{:S(2)}, u32[]{:S(2)}) collective-permute-start(bf16[64,1152]{1,0:T(8,128)(2,1)S(1)} %collective-permute-done.1.q2_ref), channel_id=1, source_target_pairs={{0,4},{4,0},{1,5},{5,1},{2,6},{6,2},{3,7},{7,3},{8,12},{12,8},{9,1... | collective-permute-start | bytes 442376 | tf_op jit(solution)/shard_map/ppermute | solution.py:416
  14.3 3.5 %attention.2 = bf16[4,128,640]{2,1,0:T(8,128)(2,1)S(1)} custom-call(s32[1]{0:T(128)} %bitcast.1.info_ref, s32[8,128]{1,0:T(8,128)S(1)} %get-tuple-element.14.limits_ref, bf16[4,64,640]{2,1,0:T(8,128)(2,1)S(1)} %get-tuple-element.15.own_ref, bf16[64,1152]{1,0:T(8,128)(2,1)S(1)} %collective-permute-done.q1_ref, ...), custom_call_target="tpu_custom_call" | custom-call | flops 22817013760 | bytes 4718592 | tf_op jit(solution)/shard_map/attention/pallas_call | solution.py:421
  18.0 3.5 %attention.3.b_ref = bf16[4,128,640]{2,1,0:T(8,128)(2,1)S(1)} custom-call(s32[1]{0:T(128)} %bitcast.own_first_ref.info_ref, s32[8,128]{1,0:T(8,128)S(1)} %get-tuple-element.14.limits_ref, bf16[4,64,640]{2,1,0:T(8,128)(2,1)S(1)} %get-tuple-element.15.own_ref, bf16[64,1152]{1,0:T(8,128)(2,1)S(1)} %collective-permute-done.4.q1_ref, ...), custom_call_target="tpu_custom_call" | custom-call | flops 22817013760 | bytes 4718592 | tf_op jit(solution)/shard_map/attention/pallas_call | solution.py:421
  21.6 0.8 %pair_merge.3 = (bf16[144,512]{1,0:T(8,128)(2,1)S(1)}, bf16[144,512]{1,0:T(8,128)(2,1)S(1)}, bf16[144,512]{1,0:T(8,128)(2,1)S(1)}) custom-call(bf16[4,128,640]{2,1,0:T(8,128)(2,1)S(1)} %collective-permute-done.3.a_ref, bf16[4,128,640]{2,1,0:T(8,128)(2,1)S(1)} %attention.3.b_ref), custom_call_target="tpu_custom_call" | custom-call | tf_op jit(solution)/shard_map/pair_merge/pallas_call | solution.py:440
  22.4 2.2 %collective-permute-start.7 = (bf16[144,512]{1,0:T(8,128)(2,1)S(1)}, bf16[144,512]{1,0:T(8,128)(2,1)S(1)}, u32[]{:S(2)}, u32[]{:S(2)}) collective-permute-start(bf16[144,512]{1,0:T(8,128)(2,1)S(1)} %get-tuple-element.19), channel_id=1, source_target_pairs={{0,2},{1,3},{2,0},{3,1},{4,6},{5,7},{6,4},{7,5},{8,10},{9,11},{10,... | collective-permute-start | bytes 442376 | tf_op jit(solution)/shard_map/ppermute | solution.py:388
  24.6 1.6 %collective-permute-start.8 = (bf16[144,512]{1,0:T(8,128)(2,1)S(1)}, bf16[144,512]{1,0:T(8,128)(2,1)S(1)}, u32[]{:S(2)}, u32[]{:S(2)}) collective-permute-start(bf16[144,512]{1,0:T(8,128)(2,1)S(1)} %get-tuple-element.20), channel_id=1, source_target_pairs={{0,3},{1,2},{2,1},{3,0},{4,7},{5,6},{6,5},{7,4},{8,11},{9,10},{10,... | collective-permute-start | bytes 442376 | tf_op jit(solution)/shard_map/ppermute | solution.py:388
  27.1 1.9 %collective-permute-done.7.refs_1_ = bf16[144,512]{1,0:T(8,128)(2,1)S(1)} collective-permute-done((bf16[144,512]{1,0:T(8,128)(2,1)S(1)}, bf16[144,512]{1,0:T(8,128)(2,1)S(1)}, u32[]{:S(2)}, u32[]{:S(2)}) %collective-permute-start.7) | collective-permute-done | bytes 147488 | tf_op jit(solution)/shard_map/ppermute | solution.py:388
  29.0 3.9 %collective-permute-done.8.refs_2_ = bf16[144,512]{1,0:T(8,128)(2,1)S(1)} collective-permute-done((bf16[144,512]{1,0:T(8,128)(2,1)S(1)}, bf16[144,512]{1,0:T(8,128)(2,1)S(1)}, u32[]{:S(2)}, u32[]{:S(2)}) %collective-permute-start.8) | collective-permute-done | bytes 147488 | tf_op jit(solution)/shard_map/ppermute | solution.py:388
  33.0 1.0 %project.1 = bf16[144,128]{1,0:T(8,128)(2,1)S(1)} custom-call(bf16[144,512]{1,0:T(8,128)(2,1)S(1)} %pair_merge.2.refs_0_, bf16[144,512]{1,0:T(8,128)(2,1)S(1)} %collective-permute-done.7.refs_1_, bf16[144,512]{1,0:T(8,128)(2,1)S(1)} %collective-permute-done.8.refs_2_, bf16[144,512]{1,0:T(8,128)(2,1)S(1)} %collective-permute-done.9.refs_3_, ...), custom_call_target="tpu_custom_call" | custom-call | tf_op jit(solution)/shard_map/project/pallas_call | solution.py:452
  34.0 0.9 %collective-permute-start.10 = (bf16[144,128]{1,0:T(8,128)(2,1)S(1)}, bf16[144,128]{1,0:T(8,128)(2,1)S(1)}, u32[]{:S(2)}, u32[]{:S(2)}) collective-permute-start(bf16[144,128]{1,0:T(8,128)(2,1)S(1)} %project.1), channel_id=1, source_target_pairs={{0,4},{4,0},{1,5},{5,1},{2,6},{6,2},{3,7},{7,3},{8,12},{12,8},{9,1... | collective-permute-start | bytes 110600 | tf_op jit(solution)/shard_map/ppermute | solution.py:464
  34.9 3.6 %collective-permute-start.11 = (bf16[144,128]{1,0:T(8,128)(2,1)S(1)}, bf16[144,128]{1,0:T(8,128)(2,1)S(1)}, u32[]{:S(2)}, u32[]{:S(2)}) collective-permute-start(bf16[144,128]{1,0:T(8,128)(2,1)S(1)} %project.1), channel_id=1, source_target_pairs={{0,68},{4,64},{32,100},{36,96},{64,4},{68,0},{96,36},{100,32},{1,6... | collective-permute-start | bytes 110600 | tf_op jit(solution)/shard_map/ppermute | solution.py:466
  38.5 0.7 %collective-permute-start.12 = (bf16[144,128]{1,0:T(8,128)(2,1)S(1)}, bf16[144,128]{1,0:T(8,128)(2,1)S(1)}, u32[]{:S(2)}, u32[]{:S(2)}) collective-permute-start(bf16[144,128]{1,0:T(8,128)(2,1)S(1)} %project.1), channel_id=1, source_target_pairs={{0,100},{4,96},{32,68},{36,64},{64,36},{68,32},{96,4},{100,0},{1,1... | collective-permute-start | bytes 110600 | tf_op jit(solution)/shard_map/ppermute | solution.py:466
  40.3 3.0 %collective-permute-done.12.refs_2_ = bf16[144,128]{1,0:T(8,128)(2,1)S(1)} collective-permute-done((bf16[144,128]{1,0:T(8,128)(2,1)S(1)}, bf16[144,128]{1,0:T(8,128)(2,1)S(1)}, u32[]{:S(2)}, u32[]{:S(2)}) %collective-permute-start.12) | collective-permute-done | bytes 36896 | tf_op jit(solution)/shard_map/ppermute | solution.py:466
  44.0 2.8 %collective-permute-start.15 = (bf16[144,128]{1,0:T(8,128)(2,1)S(1)}, bf16[144,128]{1,0:T(8,128)(2,1)S(1)}, u32[]{:S(2)}, u32[]{:S(2)}) collective-permute-start(bf16[144,128]{1,0:T(8,128)(2,1)S(1)} %middle_merge.1), channel_id=1, source_target_pairs={{0,20},{4,16},{8,28},{12,24},{16,4},{20,0},{24,12},{28,8},{1,21},{... | collective-permute-start | bytes 110600 | tf_op jit(solution)/shard_map/ppermute | solution.py:466
  46.8 1.1 %collective-permute-start.16 = (bf16[144,128]{1,0:T(8,128)(2,1)S(1)}, bf16[144,128]{1,0:T(8,128)(2,1)S(1)}, u32[]{:S(2)}, u32[]{:S(2)}) collective-permute-start(bf16[144,128]{1,0:T(8,128)(2,1)S(1)} %middle_merge.1), channel_id=1, source_target_pairs={{0,28},{4,24},{8,20},{12,16},{16,12},{20,8},{24,4},{28,0},{1,29},{... | collective-permute-start | bytes 110600 | tf_op jit(solution)/shard_map/ppermute | solution.py:466
  47.9 1.0 %collective-permute-done.15.refs_1_ = bf16[144,128]{1,0:T(8,128)(2,1)S(1)} collective-permute-done((bf16[144,128]{1,0:T(8,128)(2,1)S(1)}, bf16[144,128]{1,0:T(8,128)(2,1)S(1)}, u32[]{:S(2)}, u32[]{:S(2)}) %collective-permute-start.15) | collective-permute-done | bytes 36896 | tf_op jit(solution)/shard_map/ppermute | solution.py:466
  48.9 2.5 %collective-permute-done.16.refs_2_ = bf16[144,128]{1,0:T(8,128)(2,1)S(1)} collective-permute-done((bf16[144,128]{1,0:T(8,128)(2,1)S(1)}, bf16[144,128]{1,0:T(8,128)(2,1)S(1)}, u32[]{:S(2)}, u32[]{:S(2)}) %collective-permute-start.16) | collective-permute-done | bytes 36896 | tf_op jit(solution)/shard_map/ppermute | solution.py:466
  52.2 0.9 %collective-permute-done.18.other_ref = bf16[4,2,16,128]{3,2,1,0:T(8,128)(2,1)S(1)} collective-permute-done((bf16[4,2,16,128]{3,2,1,0:T(8,128)(2,1)S(1)}, bf16[4,2,16,128]{3,2,1,0:T(8,128)(2,1)S(1)}, u32[]{:S(2)}, u32[]{:S(2)}) %collective-permute-start.18) | collective-permute-done | bytes 32800 | tf_op jit(solution)/shard_map/ppermute | solution.py:487
  (34 shorter events, 4.8 us)
Async XLA Ops:
  2.1 7.2 %collective-permute-start = (bf16[64,1152]{1,0:T(8,128)(2,1)S(1)}, bf16[64,1152]{1,0:T(8,128)(2,1)S(1)}, u32[]{:S(2)}, u32[]{:S(2)}) collective-permute-start(bf16[64,1152]{1,0:T(8,128)(2,1)S(1)} %get-tuple-element.16), channel_id=1, source_target_pairs={{0,2},{1,3},{2,0},{3,1},{4,6},{5,7},{6,4},{7,5},{8,10},{9,11},{10,... | collective-permute-start | bytes 442376 | tf_op jit(solution)/shard_map/ppermute | solution.py:388
  5.9 6.8 %collective-permute-start.1 = (bf16[64,1152]{1,0:T(8,128)(2,1)S(1)}, bf16[64,1152]{1,0:T(8,128)(2,1)S(1)}, u32[]{:S(2)}, u32[]{:S(2)}) collective-permute-start(bf16[64,1152]{1,0:T(8,128)(2,1)S(1)} %get-tuple-element.16), channel_id=1, source_target_pairs={{0,3},{1,2},{2,1},{3,0},{4,7},{5,6},{6,5},{7,4},{8,11},{9,10},{10,... | collective-permute-start | bytes 442376 | tf_op jit(solution)/shard_map/ppermute | solution.py:388
  6.7 7.2 %collective-permute-start.2 = (bf16[64,1152]{1,0:T(8,128)(2,1)S(1)}, bf16[64,1152]{1,0:T(8,128)(2,1)S(1)}, u32[]{:S(2)}, u32[]{:S(2)}) collective-permute-start(bf16[64,1152]{1,0:T(8,128)(2,1)S(1)} %get-tuple-element.16), channel_id=1, source_target_pairs={{0,1},{1,0},{2,3},{3,2},{4,5},{5,4},{6,7},{7,6},{8,9},{9,8},{10,11... | collective-permute-start | bytes 442376 | tf_op jit(solution)/shard_map/ppermute | solution.py:388
  6.7 11.3 %slice-start = ((s8[9437184]{0:T(1024)(128)(4,1)}), s8[4194304]{0:T(1024)(128)(4,1)S(1)}, s32[]{:S(2)}) async-start(s8[9437184]{0:T(1024)(128)(4,1)} %bitcast.7), calls=%async_computation | async-start | bytes 8388608
  9.2 8.7 %collective-permute-start.4 = (bf16[64,1152]{1,0:T(8,128)(2,1)S(1)}, bf16[64,1152]{1,0:T(8,128)(2,1)S(1)}, u32[]{:S(2)}, u32[]{:S(2)}) collective-permute-start(bf16[64,1152]{1,0:T(8,128)(2,1)S(1)} %collective-permute-done.q1_ref), channel_id=1, source_target_pairs={{0,4},{4,0},{1,5},{5,1},{2,6},{6,2},{3,7},{7,3},{8,12},{12,8},{9,1... | collective-permute-start | bytes 442376 | tf_op jit(solution)/shard_map/ppermute | solution.py:416
  12.8 5.2 %collective-permute-start.5 = (bf16[64,1152]{1,0:T(8,128)(2,1)S(1)}, bf16[64,1152]{1,0:T(8,128)(2,1)S(1)}, u32[]{:S(2)}, u32[]{:S(2)}) collective-permute-start(bf16[64,1152]{1,0:T(8,128)(2,1)S(1)} %collective-permute-done.1.q2_ref), channel_id=1, source_target_pairs={{0,4},{4,0},{1,5},{5,1},{2,6},{6,2},{3,7},{7,3},{8,12},{12,8},{9,1... | collective-permute-start | bytes 442376 | tf_op jit(solution)/shard_map/ppermute | solution.py:416
  13.9 4.1 %collective-permute-start.6 = (bf16[64,1152]{1,0:T(8,128)(2,1)S(1)}, bf16[64,1152]{1,0:T(8,128)(2,1)S(1)}, u32[]{:S(2)}, u32[]{:S(2)}) collective-permute-start(bf16[64,1152]{1,0:T(8,128)(2,1)S(1)} %collective-permute-done.2.q3_ref), channel_id=1, source_target_pairs={{0,4},{4,0},{1,5},{5,1},{2,6},{6,2},{3,7},{7,3},{8,12},{12,8},{9,1... | collective-permute-start | bytes 442376 | tf_op jit(solution)/shard_map/ppermute | solution.py:416
  14.3 3.8 %slice-start.1 = ((s8[9437184]{0:T(1024)(128)(4,1)}), s8[4194304]{0:T(1024)(128)(4,1)S(1)}, s32[]{:S(2)}) async-start(s8[9437184]{0:T(1024)(128)(4,1)} %bitcast.7), calls=%async_computation.1 | async-start | bytes 8388608
  14.3 3.8 %slice-start.2 = ((s8[9437184]{0:T(1024)(128)(4,1)}), s8[1048576]{0:T(1024)(128)(4,1)S(1)}, s32[]{:S(2)}) async-start(s8[9437184]{0:T(1024)(128)(4,1)} %bitcast.7), calls=%async_computation.2 | async-start | bytes 2097152
  17.8 3.8 %collective-permute-start.3 = (bf16[4,128,640]{2,1,0:T(8,128)(2,1)S(1)}, bf16[4,128,640]{2,1,0:T(8,128)(2,1)S(1)}, u32[]{:S(2)}, u32[]{:S(2)}) collective-permute-start(bf16[4,128,640]{2,1,0:T(8,128)(2,1)S(1)} %attention.2), channel_id=1, source_target_pairs={{0,4},{4,0},{1,5},{5,1},{2,6},{6,2},{3,7},{7,3},{8,12},{12,8},{9,1... | collective-permute-start | bytes 1966088 | tf_op jit(solution)/shard_map/ppermute | solution.py:437
  21.6 11.4 %copy-start = (bf16[16,512,128]{2,1,0:T(8,128)(2,1)S(1)}, bf16[16,512,128]{2,1,0:T(8,128)(2,1)}, u32[]{:S(2)}) copy-start(bf16[16,512,128]{2,1,0:T(8,128)(2,1)} %refs_5_.1) | copy-start | bytes 6291460
  22.4 6.6 %collective-permute-start.7 = (bf16[144,512]{1,0:T(8,128)(2,1)S(1)}, bf16[144,512]{1,0:T(8,128)(2,1)S(1)}, u32[]{:S(2)}, u32[]{:S(2)}) collective-permute-start(bf16[144,512]{1,0:T(8,128)(2,1)S(1)} %get-tuple-element.19), channel_id=1, source_target_pairs={{0,2},{1,3},{2,0},{3,1},{4,6},{5,7},{6,4},{7,5},{8,10},{9,11},{10,... | collective-permute-start | bytes 442376 | tf_op jit(solution)/shard_map/ppermute | solution.py:388
  24.6 8.3 %collective-permute-start.8 = (bf16[144,512]{1,0:T(8,128)(2,1)S(1)}, bf16[144,512]{1,0:T(8,128)(2,1)S(1)}, u32[]{:S(2)}, u32[]{:S(2)}) collective-permute-start(bf16[144,512]{1,0:T(8,128)(2,1)S(1)} %get-tuple-element.20), channel_id=1, source_target_pairs={{0,3},{1,2},{2,1},{3,0},{4,7},{5,6},{6,5},{7,4},{8,11},{9,10},{10,... | collective-permute-start | bytes 442376 | tf_op jit(solution)/shard_map/ppermute | solution.py:388
  26.2 6.8 %collective-permute-start.9 = (bf16[144,512]{1,0:T(8,128)(2,1)S(1)}, bf16[144,512]{1,0:T(8,128)(2,1)S(1)}, u32[]{:S(2)}, u32[]{:S(2)}) collective-permute-start(bf16[144,512]{1,0:T(8,128)(2,1)S(1)} %get-tuple-element.21), channel_id=1, source_target_pairs={{0,1},{1,0},{2,3},{3,2},{4,5},{5,4},{6,7},{7,6},{8,9},{9,8},{10,11... | collective-permute-start | bytes 442376 | tf_op jit(solution)/shard_map/ppermute | solution.py:388
  34.0 5.5 %collective-permute-start.10 = (bf16[144,128]{1,0:T(8,128)(2,1)S(1)}, bf16[144,128]{1,0:T(8,128)(2,1)S(1)}, u32[]{:S(2)}, u32[]{:S(2)}) collective-permute-start(bf16[144,128]{1,0:T(8,128)(2,1)S(1)} %project.1), channel_id=1, source_target_pairs={{0,4},{4,0},{1,5},{5,1},{2,6},{6,2},{3,7},{7,3},{8,12},{12,8},{9,1... | collective-permute-start | bytes 110600 | tf_op jit(solution)/shard_map/ppermute | solution.py:464
  34.9 5.4 %collective-permute-start.11 = (bf16[144,128]{1,0:T(8,128)(2,1)S(1)}, bf16[144,128]{1,0:T(8,128)(2,1)S(1)}, u32[]{:S(2)}, u32[]{:S(2)}) collective-permute-start(bf16[144,128]{1,0:T(8,128)(2,1)S(1)} %project.1), channel_id=1, source_target_pairs={{0,68},{4,64},{32,100},{36,96},{64,4},{68,0},{96,36},{100,32},{1,6... | collective-permute-start | bytes 110600 | tf_op jit(solution)/shard_map/ppermute | solution.py:466
  38.5 4.8 %collective-permute-start.12 = (bf16[144,128]{1,0:T(8,128)(2,1)S(1)}, bf16[144,128]{1,0:T(8,128)(2,1)S(1)}, u32[]{:S(2)}, u32[]{:S(2)}) collective-permute-start(bf16[144,128]{1,0:T(8,128)(2,1)S(1)} %project.1), channel_id=1, source_target_pairs={{0,100},{4,96},{32,68},{36,64},{64,36},{68,32},{96,4},{100,0},{1,1... | collective-permute-start | bytes 110600 | tf_op jit(solution)/shard_map/ppermute | solution.py:466
  39.2 4.0 %collective-permute-start.13 = (bf16[144,128]{1,0:T(8,128)(2,1)S(1)}, bf16[144,128]{1,0:T(8,128)(2,1)S(1)}, u32[]{:S(2)}, u32[]{:S(2)}) collective-permute-start(bf16[144,128]{1,0:T(8,128)(2,1)S(1)} %project.1), channel_id=1, source_target_pairs={{0,36},{4,32},{32,4},{36,0},{64,100},{68,96},{96,68},{100,64},{1,3... | collective-permute-start | bytes 110600 | tf_op jit(solution)/shard_map/ppermute | solution.py:466
  43.5 4.4 %collective-permute-start.14 = (bf16[144,128]{1,0:T(8,128)(2,1)S(1)}, bf16[144,128]{1,0:T(8,128)(2,1)S(1)}, u32[]{:S(2)}, u32[]{:S(2)}) collective-permute-start(bf16[144,128]{1,0:T(8,128)(2,1)S(1)} %middle_merge.1), channel_id=1, source_target_pairs={{0,4},{4,0},{1,5},{5,1},{2,6},{6,2},{3,7},{7,3},{8,12},{12,8},{9,1... | collective-permute-start | bytes 110600 | tf_op jit(solution)/shard_map/ppermute | solution.py:464
  44.0 4.9 %collective-permute-start.15 = (bf16[144,128]{1,0:T(8,128)(2,1)S(1)}, bf16[144,128]{1,0:T(8,128)(2,1)S(1)}, u32[]{:S(2)}, u32[]{:S(2)}) collective-permute-start(bf16[144,128]{1,0:T(8,128)(2,1)S(1)} %middle_merge.1), channel_id=1, source_target_pairs={{0,20},{4,16},{8,28},{12,24},{16,4},{20,0},{24,12},{28,8},{1,21},{... | collective-permute-start | bytes 110600 | tf_op jit(solution)/shard_map/ppermute | solution.py:466
  46.8 4.7 %collective-permute-start.16 = (bf16[144,128]{1,0:T(8,128)(2,1)S(1)}, bf16[144,128]{1,0:T(8,128)(2,1)S(1)}, u32[]{:S(2)}, u32[]{:S(2)}) collective-permute-start(bf16[144,128]{1,0:T(8,128)(2,1)S(1)} %middle_merge.1), channel_id=1, source_target_pairs={{0,28},{4,24},{8,20},{12,16},{16,12},{20,8},{24,4},{28,0},{1,29},{... | collective-permute-start | bytes 110600 | tf_op jit(solution)/shard_map/ppermute | solution.py:466
  47.9 3.6 %collective-permute-start.17 = (bf16[144,128]{1,0:T(8,128)(2,1)S(1)}, bf16[144,128]{1,0:T(8,128)(2,1)S(1)}, u32[]{:S(2)}, u32[]{:S(2)}) collective-permute-start(bf16[144,128]{1,0:T(8,128)(2,1)S(1)} %middle_merge.1), channel_id=1, source_target_pairs={{0,12},{4,8},{8,4},{12,0},{16,28},{20,24},{24,20},{28,16},{1,13},{... | collective-permute-start | bytes 110600 | tf_op jit(solution)/shard_map/ppermute | solution.py:466
  51.7 1.3 %collective-permute-start.18 = (bf16[4,2,16,128]{3,2,1,0:T(8,128)(2,1)S(1)}, bf16[4,2,16,128]{3,2,1,0:T(8,128)(2,1)S(1)}, u32[]{:S(2)}, u32[]{:S(2)}) collective-permute-start(bf16[4,2,16,128]{3,2,1,0:T(8,128)(2,1)S(1)} %finish.1.own_ref), channel_id=1, source_target_pairs={{0,4},{4,0},{1,5},{5,1},{2,6},{6,2},{3,7},{7,3},{8,12},{12,8},{9,1... | collective-permute-start | bytes 98312 | tf_op jit(solution)/shard_map/ppermute | solution.py:487
